TPU v7x, 128 devices: a whole 4x4x4 slice. The times are simulated.
128 devices in a mesh: shell: 16 (over y, x), order: 8 (over z, core).
Axes of the slice: x: 4, y: 4, z: 4, core: 2. Of those that a mesh axis runs over, the one named last changes fastest.
Arguments:
- velocity: bfloat16 [3, 32, 2, 512, 512], P(None, 'shell', None, 'order'), may hold values from -6 to 6
- vorticity: bfloat16 [3, 32, 2, 512, 512], P(None, 'shell', None, 'order'), may hold values from -6 to 6
- magnetic: bfloat16 [3, 32, 2, 512, 512], P(None, 'shell', None, 'order'), may hold values from -6 to 6
- current: bfloat16 [3, 32, 2, 512, 512], P(None, 'shell', None, 'order'), may hold values from -6 to 6
- potential: bfloat16 [3, 32, 2, 512, 512], P(None, 'shell', None, 'order'), may hold values from -6 to 6
- order_slots: int32 [512], replicated, may hold values from 0 to 511, as said below
- legendre_values: bfloat16 [256, 513, 256], P('order'), as said below
- block_lengths: int32 [4], replicated, may hold values from 1 to 16, 32 in all
- coupling: float32 [2, 32], P(None, 'shell'), may hold values from 50 to 500
- angular: float32 [2, 32], P(None, 'shell'), may hold values from 3.8146973e-05 to 0.00038146973
Outputs:
- velocity_next: float32 [3, 32, 2, 512, 512], P(None, 'shell', None, 'order')
- potential_next: float32 [3, 32, 2, 512, 512], P(None, 'shell', None, 'order')
Inputs may be any that keep to these rules, and one draw needn't show every extreme that they name: `order_slots`: slots 2 i and 2 i + 1 hold an order m < 256 and 511 - m; every order from 0 to 511 is held once. `legendre_values`: the orthonormal associated Legendre functions (the squared harmonic integrates to 1 over the sphere), without Condon-Shortley phase, of the orders in order_slots, at cos(theta_j), packed as the first step says; entries beyond a slot's degrees are unused. `block_lengths`: the 4 lengths sum to 32; the largest is exactly 16.
All inputs are finite; a program needn't handle non-finite values.
Results may differ from a plain program's by a relative error of at most 0.004.
Values may be sent and summed in bfloat16 or wider, within the bound.
No kernel may reach another device: no remote copies, remote signals or barrier semaphores. Data moves between devices by JAX's collectives and lax.ppermute only.
A program may use at most 128 MiB of HBM per device.

v0:
```python
import math

import jax
import jax.numpy as jnp
from jax import lax
from jax.sharding import PartitionSpec as P

L = 512
NLAT = 512
NPHI = 1024
NH = 256


time_step = 0.5
rotation_rate = 2.0


def passed_along(shard, axis, by):
    devices = lax.axis_size(axis)
    pairs = [(i, i + by) for i in range(devices) if 0 <= i + by < devices]
    return lax.ppermute(shard, axis, pairs)


def prefix_2(part, axis, combine, identity, reverse):
    count = lax.axis_size(axis)
    place = lax.axis_index(axis)
    ahead = count - 1 - place if reverse else place
    gathered = jax.tree.map(lambda a: lax.all_gather(a, axis), part)
    state = jax.tree.map(lambda a, e: jnp.zeros_like(a) + jnp.asarray(e, a.dtype), part, identity)

    def one(hop, state):
        source = count - 1 - hop if reverse else hop
        return combine(
            state, jax.tree.map(lambda a: lax.dynamic_index_in_dim(a, source, 0, False), gathered)
        )

    return lax.fori_loop(0, ahead, one, state)


def unpack_table(packed, orders):
    pair_count = packed.shape[0]
    degree_count = packed.shape[1] - 1
    lower = orders.reshape(pair_count, 2)[:, 0]
    padded = jnp.concatenate(
        [jnp.zeros((pair_count, degree_count, packed.shape[2]), packed.dtype), packed], axis=1
    )
    starts = degree_count - lower
    even_rows = jax.vmap(lambda row, begin: lax.dynamic_slice_in_dim(row, begin, degree_count, 0))(
        padded, starts
    )
    degree_ids = jnp.arange(degree_count, dtype=jnp.int32)
    odd_rows = jnp.where(
        degree_ids[None, :, None] >= (degree_count - 1 - lower)[:, None, None],
        packed[:, 1:, :],
        jnp.zeros_like(packed[:, 1:, :]),
    )
    table = jnp.stack([even_rows, odd_rows], axis=1).reshape(
        2 * pair_count, degree_count, packed.shape[2]
    )
    return jnp.transpose(table, (1, 0, 2))


def parity_sign(orders, degrees_count):
    parity = (jnp.arange(degrees_count, dtype=jnp.int32)[None, :] + orders[:, None]) % 2
    return 1.0 - 2.0 * parity.astype(jnp.float32)


def latitude_weight(row_ids, lat_count, degrees_count):
    colatitude = math.pi * (row_ids.astype(jnp.float32) + 0.5) / lat_count
    return math.sqrt(2.0 * math.pi) * degrees_count * math.pi / lat_count * jnp.sin(colatitude)


def split_table(table):
    high_part = table.astype(jnp.bfloat16)
    low_part = (table - high_part.astype(jnp.float32)).astype(jnp.bfloat16)
    return (high_part, low_part)


def fourier_tables(orders_grid, lon_count, degrees_count):
    points = jnp.arange(lon_count, dtype=jnp.int32)
    phases = orders_grid[:, :, None] * points[None, None, :] % lon_count
    angles = 2.0 * math.pi / lon_count * phases.astype(jnp.float32)
    cosines = jnp.cos(angles)
    sines = jnp.sin(angles)
    doubled = jnp.where(orders_grid == 0, 1.0, 2.0)[:, :, None] * (
        math.sqrt(2.0 * math.pi) / degrees_count
    )
    synthesis = jnp.stack([doubled * cosines, -doubled * sines], axis=1).reshape(-1, lon_count)
    analysis = (jnp.stack([cosines, -sines], axis=1) / lon_count).reshape(-1, lon_count)
    return (split_table(synthesis), split_table(analysis))


def cross_product(first, second):
    return jnp.stack(
        [
            first[1] * second[2] - first[2] * second[1],
            first[2] * second[0] - first[0] * second[2],
            first[0] * second[1] - first[1] * second[0],
        ]
    )


def nonlinear_terms(field_grid):
    flow_grid = field_grid[0:3]
    vorticity_grid = field_grid[3:6]
    magnetic_grid = field_grid[6:9]
    current_grid = field_grid[9:12]
    rotation = jnp.stack(
        [rotation_rate * flow_grid[1], -rotation_rate * flow_grid[0], jnp.zeros_like(flow_grid[0])]
    )
    momentum = (
        cross_product(flow_grid, vorticity_grid)
        + cross_product(current_grid, magnetic_grid)
        + rotation
    )
    induction = cross_product(flow_grid, magnetic_grid)
    return jnp.concatenate([momentum, induction], axis=0)


def widen(factor):
    return factor[:, None, :, None]


def compose_factor(earlier, later):
    product = jnp.sum(later[:, :, None] * earlier[None, :, :], axis=1)
    return product / product[1:2, 1:2]


def compose_affine(earlier, later):
    return (later[0] * earlier[0], widen(later[0]) * earlier[1] + later[1])


def solve_along_shells(right_side, coupling_below, angular, degree_term):
    shells = right_side.shape[2]
    width = degree_term.shape[0]
    next_first = passed_along(coupling_below[:, :1], "shell", -1)
    coupling_above = jnp.concatenate([coupling_below[:, 1:], next_first], axis=1)
    diagonal = (
        1.0
        + coupling_below[:, :, None]
        + coupling_above[:, :, None]
        + angular[:, :, None] * degree_term
    )
    all_ones = jnp.ones((2, width), jnp.float32)
    all_zeros = jnp.zeros((2, width), jnp.float32)
    identity = jnp.stack([jnp.stack([all_ones, all_zeros]), jnp.stack([all_zeros, all_ones])])
    composite = identity
    for position in range(shells):
        above_row = jnp.broadcast_to(coupling_above[:, position, None], (2, width))
        below_row = jnp.broadcast_to(coupling_below[:, position, None], (2, width))
        shell_map = jnp.stack(
            [jnp.stack([all_zeros, above_row]), jnp.stack([-below_row, diagonal[:, position]])]
        )
        composite = compose_factor(composite, shell_map)
    prefix = prefix_2(composite, "shell", compose_factor, identity, False)
    carried = prefix[0, 1] / prefix[1, 1]
    denominators, slopes, factors = ([], [], [])
    for position in range(shells):
        denominator = diagonal[:, position] - coupling_below[:, position, None] * carried
        carried = coupling_above[:, position, None] / denominator
        denominators.append(denominator)
        slopes.append(carried)
        factors.append(coupling_below[:, position, None] / denominator)
    offset = jnp.zeros_like(right_side[:, :, 0])
    total_factor = all_ones
    for position in range(shells):
        offset = widen(factors[position]) * offset + right_side[:, :, position] / widen(
            denominators[position]
        )
        total_factor = factors[position] * total_factor
    _, running = prefix_2(
        (total_factor, offset), "shell", compose_affine, (all_ones, jnp.zeros_like(offset)), False
    )
    reduced = []
    for position in range(shells):
        running = widen(factors[position]) * running + right_side[:, :, position] / widen(
            denominators[position]
        )
        reduced.append(running)
    intercept = jnp.zeros_like(offset)
    total_slope = all_ones
    for position in reversed(range(shells)):
        intercept = reduced[position] + widen(slopes[position]) * intercept
        total_slope = slopes[position] * total_slope
    _, beyond = prefix_2(
        (total_slope, intercept), "shell", compose_affine, (all_ones, jnp.zeros_like(offset)), True
    )
    outputs = [None] * shells
    carried_value = beyond
    for position in reversed(range(shells)):
        carried_value = reduced[position] + widen(slopes[position]) * carried_value
        outputs[position] = carried_value
    return jnp.stack(outputs, axis=2)


def body(
    velocity,
    vorticity,
    magnetic,
    current,
    potential,
    order_slots,
    legendre_values,
    block_lengths,
    coupling,
    angular,
):
    shells = velocity.shape[1]
    slot_count = velocity.shape[3]
    order_count = lax.axis_size("order")
    order_rank = lax.axis_index("order")
    shell_rank = lax.axis_index("shell")
    own_orders = lax.dynamic_slice_in_dim(order_slots, order_rank * slot_count, slot_count)
    legendre = unpack_table(legendre_values, own_orders)
    parity = parity_sign(own_orders, L)
    spectral = jnp.concatenate([velocity, vorticity, magnetic, current], axis=0)
    zero_block = jnp.zeros_like(spectral)
    even_part = jnp.where(parity > 0, spectral, zero_block)
    odd_part = jnp.where(parity > 0, zero_block, spectral)
    even_sum = jnp.einsum(
        "cspkl,lkj->csjpk", even_part, legendre, preferred_element_type=jnp.float32
    )
    odd_sum = jnp.einsum("cspkl,lkj->csjpk", odd_part, legendre, preferred_element_type=jnp.float32)
    latitude = jnp.stack([even_sum + odd_sum, even_sum - odd_sum], axis=2).astype(jnp.bfloat16)
    latitude = latitude.reshape(spectral.shape[0], shells, 2, NH, 2 * slot_count)
    row_count = NH // order_count
    row_ids = order_rank * row_count + jnp.arange(row_count, dtype=jnp.int32)
    row_weight = latitude_weight(row_ids, NLAT, L)[:, None]
    (synthesis_high, synthesis_low), (analysis_high, analysis_low) = fourier_tables(
        order_slots.reshape(order_count, slot_count), NPHI, L
    )
    incoming = lax.all_to_all(latitude, "order", split_axis=3, concat_axis=4, tiled=True)
    field_grid = jnp.einsum(
        "cshjq,qi->cshji", incoming, synthesis_high, preferred_element_type=jnp.float32
    )
    field_grid = field_grid + jnp.einsum(
        "cshjq,qi->cshji", incoming, synthesis_low, preferred_element_type=jnp.float32
    )
    products = nonlinear_terms(field_grid)
    products_high = products.astype(jnp.bfloat16)
    products_low = (products - products_high.astype(jnp.float32)).astype(jnp.bfloat16)
    coeffs = jnp.einsum(
        "cshji,qi->cshjq", products_high, analysis_high, preferred_element_type=jnp.float32
    )
    coeffs = coeffs + jnp.einsum(
        "cshji,qi->cshjq", products_high, analysis_low, preferred_element_type=jnp.float32
    )
    coeffs = coeffs + jnp.einsum(
        "cshji,qi->cshjq", products_low, analysis_high, preferred_element_type=jnp.float32
    )
    coeffs = (coeffs * row_weight).astype(jnp.bfloat16)
    returned = lax.all_to_all(coeffs, "order", split_axis=4, concat_axis=3, tiled=True)
    returned = returned.reshape(6, shells, 2, NH, 2, slot_count)
    northern = jnp.einsum(
        "csjpk,lkj->cslpk", returned[:, :, 0], legendre, preferred_element_type=jnp.float32
    )
    southern = jnp.einsum(
        "csjpk,lkj->cslpk", returned[:, :, 1], legendre, preferred_element_type=jnp.float32
    )
    analysed_terms = northern + jnp.transpose(parity)[:, None, :] * southern
    state_rows = (
        jnp.stack([velocity, potential], axis=0)
        .transpose(0, 1, 2, 5, 3, 4)
        .reshape(2, 3, shells, L, 2 * slot_count)
    )
    right_side = state_rows.astype(jnp.float32) + time_step * analysed_terms.reshape(
        2, 3, shells, L, 2 * slot_count
    )
    shell_ids = shell_rank * shells + jnp.arange(shells, dtype=jnp.int32)
    starts = jnp.cumsum(block_lengths) - block_lengths
    is_start = jnp.any(shell_ids[:, None] == starts[None, :], axis=1)
    coupling_below = jnp.where(is_start[None, :], 0.0, coupling)
    degree_real = jnp.arange(L, dtype=jnp.float32)
    degree_term = degree_real * (degree_real + 1.0)
    solution = solve_along_shells(right_side, coupling_below, angular, degree_term)
    solution = solution.reshape(2, 3, shells, L, 2, slot_count).transpose(0, 1, 2, 4, 5, 3)
    return (solution[0], solution[1])


def solution(mesh):
    in_specs = (
        P(None, "shell", None, "order", None),
        P(None, "shell", None, "order", None),
        P(None, "shell", None, "order", None),
        P(None, "shell", None, "order", None),
        P(None, "shell", None, "order", None),
        P(),
        P("order", None, None),
        P(),
        P(None, "shell"),
        P(None, "shell"),
    )
    out_specs = (P(None, "shell", None, "order", None), P(None, "shell", None, "order", None))
    return jax.shard_map(body, mesh=mesh, in_specs=in_specs, out_specs=out_specs, check_vma=False)
```

profile of v0, /device:TPU:0, one launch (start us, length us, event | category | flops | bytes accessed | tf_op | source)
XLA Modules:
  0.0 772.3 jit_solution(5094821844200421002)
XLA Ops:
  12.1 11.5 %copy.73 = bf16[32,513,256]{2,1,0:T(8,128)(2,1)} copy(bf16[32,513,256]{2,0,1:T(8,128)(2,1)} %param.22) | data formatting | bytes 16809984 | tf_op args[6]
  23.8 9.6 %fusion = bf16[32,1,512,256]{3,2,0,1:T(8,128)(2,1)} fusion(bf16[32,513,256]{2,1,0:T(8,128)(2,1)} %copy.73, pred[32,512]{1,0:T(8,128)(4,1)S(1)} %iota_compare_fusion), kind=kLoop, calls=%fused_computation.12 | loop fusion | flops 4194304 | bytes 16793600 | tf_op jit(solution)/shard_map/stack | solution.py:57
  33.4 6.6 concatenate.19
  40.1 118.9 %while.44 = (s32[]{:T(128)}, bf16[32,1025,256]{2,1,0:T(8,128)(2,1)}, s32[32,3]{0,1:T(4,128)S(1)}, bf16[32,512,256]{2,1,0:T(8,128)(2,1)}) while((s32[]{:T(128)}, bf16[32,1025,256]{2,1,0:T(8,128)(2,1)}, s32[32,3]{0,1:T(4,128)S(1)}, bf16[32,512,256]{2,1,0:T(8,128)(2,1)}) %tuple.127), condition=%wide.while_cond.clone, body=%wide.while_body.sunk.clone | while | flops 2 | bytes 525421 | solution.py:48
  40.8 3.1 dynamic-slice_dynamic-update-slice_fusion.3
  44.5 3.1 dynamic-slice_dynamic-update-slice_fusion.3
  48.2 3.1 dynamic-slice_dynamic-update-slice_fusion.3
  51.9 3.1 dynamic-slice_dynamic-update-slice_fusion.3
  55.7 3.1 dynamic-slice_dynamic-update-slice_fusion.3
  59.4 3.1 dynamic-slice_dynamic-update-slice_fusion.3
  63.1 3.1 dynamic-slice_dynamic-update-slice_fusion.3
  66.8 3.1 dynamic-slice_dynamic-update-slice_fusion.3
  70.5 3.1 dynamic-slice_dynamic-update-slice_fusion.3
  74.3 3.0 dynamic-slice_dynamic-update-slice_fusion.3
  78.0 3.0 dynamic-slice_dynamic-update-slice_fusion.3
  81.7 3.0 dynamic-slice_dynamic-update-slice_fusion.3
  85.4 3.1 dynamic-slice_dynamic-update-slice_fusion.3
  89.1 3.1 dynamic-slice_dynamic-update-slice_fusion.3
  92.8 3.1 dynamic-slice_dynamic-update-slice_fusion.3
  96.5 3.1 dynamic-slice_dynamic-update-slice_fusion.3
  100.3 3.1 dynamic-slice_dynamic-update-slice_fusion.3
  104.0 3.0 dynamic-slice_dynamic-update-slice_fusion.3
  107.7 3.0 dynamic-slice_dynamic-update-slice_fusion.3
  111.4 3.1 dynamic-slice_dynamic-update-slice_fusion.3
  115.1 3.1 dynamic-slice_dynamic-update-slice_fusion.3
  118.8 3.0 dynamic-slice_dynamic-update-slice_fusion.3
  122.5 3.1 dynamic-slice_dynamic-update-slice_fusion.3
  126.3 3.1 dynamic-slice_dynamic-update-slice_fusion.3
  130.0 3.1 dynamic-slice_dynamic-update-slice_fusion.3
  133.7 3.1 dynamic-slice_dynamic-update-slice_fusion.3
  137.4 3.1 dynamic-slice_dynamic-update-slice_fusion.3
  141.1 3.1 dynamic-slice_dynamic-update-slice_fusion.3
  144.8 3.1 dynamic-slice_dynamic-update-slice_fusion.3
  148.6 3.0 dynamic-slice_dynamic-update-slice_fusion.3
  152.3 3.0 dynamic-slice_dynamic-update-slice_fusion.3
  156.0 3.0 dynamic-slice_dynamic-update-slice_fusion.3
  159.0 8.0 %pad_maximum_fusion = bf16[32,2,512,256]{3,2,0,1:T(8,128)(2,1)S(1)} fusion(bf16[32,1,512,256]{3,2,0,1:T(8,128)(2,1)} %fusion, bf16[32,1,512,256]{3,2,0,1:T(8,128)(2,1)} %bitcast.231), kind=kLoop, calls=%fused_computation.10 | loop fusion | flops 8388608 | bytes 33554432 | tf_op jit(solution)/shard_map/stack | solution.py:57
  167.0 6.6 copy.76
  175.8 9.6 %fusion.4 = f32[64,256,12,2,2]{1,2,4,3,0:T(8,128)} fusion(bf16[512,64,256,1,1]{2,0,4,3,1:T(8,128)(2,1)} %bitcast.224, bf16[12,2,2,64,512]{4,3,2,1,0:T(8,128)(2,1)S(1)} %get-tuple-element.248), kind=kOutput, calls=%fused_computation.21 | convolution fusion | flops 805306368 | bytes 23068672 | tf_op jit(solution)/shard_map/cspkl,lkj->csjpk/dot_general | solution.py:223
  185.4 11.5 %fusion.21 = (bf16[12,2,256,2,64]{2,0,3,1,4:T(8,128)(2,1)}, bf16[12,2,256,2,64]{2,0,3,1,4:T(8,128)(2,1)}) fusion(f32[64,256,12,2,2]{1,2,4,3,0:T(8,128)} %fusion.4, bf16[512,64,256,1,1]{2,0,4,3,1:T(8,128)(2,1)} %bitcast.225, bf16[12,2,2,64,512]{4,3,2,1,0:T(8,128)(2,1)S(1)} %get-tuple-element.249), kind=kOutput, calls=%fused_computation.50 | convolution fusion | flops 808452096 | bytes 26214400 | tf_op jit(solution)/shard_map/cspkl,lkj->csjpk/dot_general | solution.py:220
  200.7 6.0 copy.81
  206.7 5.5 all-to-all-start
  212.4 10.9 %broadcast_multiply_fusion.1 = (f32[8,1,64,1024]{3,2,1,0:T(8,128)S(1)}, f32[8,1,64,1024]{3,2,1,0:T(8,128)}, f32[8,1,64,1024]{3,2,1,0:T(8,128)S(1)}, f32[8,1,64,1024]{3,2,1,0:T(8,128)}) fusion(f32[8,64]{1,0:T(8,128)S(1)} %get-tuple-element.262, s32[8,64]{1,0:T(8,128)S(1)} %reshape.950, f32[8,64]{1,0:T(8,128)S(1)} %get-tuple-element.263), kind=kLoop, calls=%fused_computation.86 | loop fusion | flops 8912896 | bytes 8394752 | tf_op jit(solution)/shard_map/mul | solution.py:88
  234.5 3.4 maximum_convert_fusion
  240.9 27.6 %all_gather.22 = f32[16,2,2,2,512]{4,3,2,1,0:T(2,128)S(1)} all-gather(f32[1,2,2,2,512]{4,3,2,1,0:T(2,128)S(1)} %bitcast_divide_fusion.4), channel_id=1, replica_groups=mesh['shell'=16,'order'=8] {'shell'}, dimensions={0}, use_global_device_ids=true | all-gather | bytes 278528 | tf_op jit(solution)/shard_map/all_gather | solution.py:28
  270.1 3.5 fusion.9
  273.6 3.4 fusion.15
  285.8 11.4 %copy.84 = bf16[6,2,2,32,1024]{3,2,1,0,4:T(2,128)(2,1)} copy(bf16[6,2,2,32,1024]{4,3,2,1,0:T(8,128)(2,1)S(1)} %multiply_convert_fusion) | data formatting | bytes 3145728 | tf_op jit(solution)/shard_map/convert_element_type | solution.py:251
  297.2 9.5 %reshape.987 = bf16[8,2,49152]{2,1,0:T(2,128)(2,1)} reshape(bf16[1024,6,2,2,32]{4,3,2,1,0:T(2,128)(2,1)} %bitcast.228) | data formatting | bytes 3145728
  306.7 5.0 all-to-all-start.1
  312.0 21.3 %all-to-all-done.1 = bf16[8,2,49152]{2,1,0:T(2,128)(2,1)S(1)} async-done(((bf16[8,2,49152]{2,1,0:T(2,128)(2,1)}), bf16[8,2,49152]{2,1,0:T(2,128)(2,1)S(1)}, u32[]{:S(2)}, u32[]{:S(2)}) %all-to-all-start.1) | async-done | bytes 1572896 | tf_op jit(solution)/shard_map/all_to_all | solution.py:252
  333.3 5.4 reshape.988
  338.7 15.0 %copy.85 = bf16[6,2,2,32,8,128]{5,3,4,2,1,0:T(8,128)(2,1)} copy(bf16[6,2,2,32,8,128]{3,2,1,0,5,4:T(2,128)(2,1)} %bitcast.229) | data formatting | bytes 3145728 | tf_op jit(solution)/shard_map/all_to_all | solution.py:252
  353.7 5.4 reshape.951
  359.0 3.4 fusion.72
  362.4 3.4 copy.101
  365.8 9.8 %fusion.42 = f32[64,512,6,2,2]{1,2,4,3,0:T(8,128)} fusion(bf16[512,64,256,1,1]{2,0,4,3,1:T(8,128)(2,1)} %bitcast.226, bf16[6,2,1,256,2,64]{3,0,4,1,5,2:T(8,128)(2,1)S(1)} %copy.101), kind=kOutput, calls=%fused_computation.80 | convolution fusion | flops 402653184 | bytes 20709376 | tf_op jit(solution)/shard_map/csjpk,lkj->cslpk/dot_general | solution.py:254
  377.1 9.5 %fusion.2 = f32[6,2,512,2,64]{2,0,3,1,4:T(8,128)S(1)} fusion(f32[64,512,6,2,2]{1,2,4,3,0:T(8,128)} %fusion.42, bf16[512,64,256,1,1]{2,0,4,3,1:T(8,128)(2,1)} %bitcast.227, f32[512,64]{0,1:T(8,128)S(1)} %fusion.55, bf16[6,2,1,256,2,64]{3,0,4,1,5,2:T(8,128)(2,1)S(1)} %copy.102), kind=kOutput, calls=%fused_computation.17 | convolution fusion | flops 405012480 | bytes 23986176 | tf_op jit(solution)/shard_map/csjpk,lkj->cslpk/dot_general | solution.py:257
  393.2 21.8 %all_gather.23 = f32[16,2,512]{2,1,0:T(2,128)S(1)} all-gather(f32[1,2,512]{2,1,0:T(2,128)S(1)} %get-tuple-element.232), channel_id=1, replica_groups=mesh['shell'=16,'order'=8] {'shell'}, dimensions={0}, use_global_device_ids=true | all-gather | bytes 69632 | tf_op jit(solution)/shard_map/all_gather | solution.py:28
  414.9 128.8 %all-gather.4.cloned.1.call-done = f32[16,2,3,512,128]{4,3,2,1,0:T(8,128)} async-done(((f32[1,2,3,512,128]{4,3,2,1,0:T(8,128)}), f32[16,2,3,512,128]{4,3,2,1,0:T(8,128)}) %all-gather.4.cloned.1.call-update) | async-done | bytes 25165840 | tf_op jit(solution)/shard_map/all_gather | solution.py:28
  544.3 3.7 multiply_add_fusion.2
  549.7 49.6 %all_gather.25 = f32[16,2,512]{2,1,0:T(2,128)S(1)} all-gather(f32[1,2,512]{2,1,0:T(2,128)S(1)} %divide_multiply_fusion), channel_id=1, replica_groups=mesh['shell'=16,'order'=8] {'shell'}, dimensions={0}, use_global_device_ids=true | all-gather | bytes 69632 | tf_op jit(solution)/shard_map/all_gather | solution.py:28
  599.3 131.9 %all-gather.6.cloned.1.call-done = f32[32,3,512,128]{3,2,1,0:T(8,128)} async-done(((f32[2,3,512,128]{3,2,1,0:T(8,128)}), f32[32,3,512,128]{3,2,1,0:T(8,128)}) %all-gather.6.cloned.1.call-update) | async-done | bytes 25165840 | tf_op jit(solution)/shard_map/all_gather | solution.py:28
  731.3 28.6 %while.43 = (s32[]{:T(128)}, f32[2,3,512,128]{3,2,1,0:T(8,128)S(1)}, s32[]{:T(128)}, f32[16,2,512]{2,1,0:T(2,128)S(1)}, f32[16,2,3,512,128]{4,3,2,1,0:T(8,128)}) while((s32[]{:T(128)}, f32[2,3,512,128]{3,2,1,0:T(8,128)S(1)}, s32[]{:T(128)}, f32[16,2,512]{2,1,0:T(2,128)S(1)}, f32[16,2,3,512,128]{4,3,2,1,0:T(8,128)}) %tuple.140), condition=%wide.region_10.11_spmd.clone, body=%wide.region_9.10_spmd.sunk.clone | while | flops 786438 | bytes 4731003 | solution.py:37
  (253 shorter events, 100.3 us)
Async XLA Ops:
  9.7 217.3 %copy-start.22 = (f32[2]{0:T(128)}, f32[2]{0:T(128)S(1)}, u32[]{:S(2)}) copy-start(f32[2]{0:T(128)S(1)} %get-tuple-element.182) | copy-start | bytes 28
  9.7 217.3 %copy-start.18 = (f32[2]{0:T(128)}, f32[2]{0:T(128)S(1)}, u32[]{:S(2)}) copy-start(f32[2]{0:T(128)S(1)} %get-tuple-element.183) | copy-start | bytes 28
  9.7 230.1 %collective-permute-start = (f32[2,1]{1,0:T(2,128)S(1)}, f32[2,1]{1,0:T(2,128)S(1)}, u32[]{:S(2)}, u32[]{:S(2)}) collective-permute-start(f32[2,1]{1,0:T(2,128)S(1)} %get-tuple-element.265), channel_id=1, source_target_pairs={{8,0},{16,8},{24,16},{32,24},{40,32},{48,40},{56,48},{64,56},{72,6... | collective-permute-start | bytes 32 | tf_op jit(solution)/shard_map/ppermute | solution.py:21
  23.8 9.6 %copy-start = (bf16[32,513,256]{2,1,0:T(8,128)(2,1)S(1)}, bf16[32,513,256]{2,1,0:T(8,128)(2,1)}, u32[]{:S(2)}) copy-start(bf16[32,513,256]{2,1,0:T(8,128)(2,1)} %copy.73) | copy-start | bytes 25214980
  167.0 6.6 copy-start.6
  173.6 1.1 copy-start.12
  173.7 1.4 copy-start.13
  173.7 1.6 copy-start.14
  196.9 2.6 copy-start.11
  206.7 5.5 copy-start.29
  206.7 61.8 %all-to-all-start = ((bf16[12,2,2,256,128]{4,1,0,2,3:T(2,128)(2,1)}), bf16[12,2,2,256,128]{4,1,0,2,3:T(2,128)(2,1)S(1)}, u32[]{:S(2)}, u32[]{:S(2)}) async-start(bf16[12,2,2,256,128]{4,1,0,2,3:T(2,128)(2,1)} %copy.81), calls=%async_computation | async-start | bytes 6291456 | tf_op jit(solution)/shard_map/all_to_all | solution.py:232
  225.2 1.7 copy-start.30
  225.2 1.8 copy-start.21
  229.8 2.0 copy-start.2
  234.5 3.4 copy-start.3
  237.9 1.9 copy-start.28
  240.1 0.5 copy-start.25
  240.3 0.6 copy-start.15
  268.5 1.6 copy-start.10
  270.1 3.5 copy-start.9
  277.7 0.7 copy-start.31
  278.4 1.6 copy-start.7
  280.0 1.8 copy-start.8
  281.9 1.9 copy-start.32
  306.7 5.0 copy-start.16
  306.7 5.0 copy-start.19
  306.7 5.0 copy-start.23
  306.7 5.1 copy-start.26
  306.7 26.5 %all-to-all-start.1 = ((bf16[8,2,49152]{2,1,0:T(2,128)(2,1)}), bf16[8,2,49152]{2,1,0:T(2,128)(2,1)S(1)}, u32[]{:S(2)}, u32[]{:S(2)}) async-start(bf16[8,2,49152]{2,1,0:T(2,128)(2,1)} %reshape.987), calls=%async_computation.1 | async-start | bytes 3145728 | tf_op jit(solution)/shard_map/all_to_all | solution.py:252
  311.7 232.1 %all-gather.4.cloned.1.call-start = ((), (), s32[]{:S(2)}) async-start(), calls=%async_computation.2 | async-start | bytes 26738688 | tf_op jit(solution)/shard_map/all_gather | solution.py:28
  365.8 9.8 %copy-start.5 = (bf16[6,2,1,256,2,64]{5,4,3,2,1,0:T(2,128)(2,1)S(1)}, bf16[6,2,1,256,2,64]{5,4,3,2,1,0:T(2,128)(2,1)}, u32[]{:S(2)}) copy-start(bf16[6,2,1,256,2,64]{5,4,3,2,1,0:T(2,128)(2,1)} %get-tuple-element.252) | copy-start | bytes 2359300
  386.6 1.9 copy-start.4
  389.3 1.6 copy-start.1
  391.3 1.7 copy-start.17
  391.4 1.7 copy-start.20
  391.4 1.7 copy-start.24
  393.0 338.2 %all-gather.6.cloned.1.call-start = ((), (), s32[]{:S(2)}) async-start(), calls=%async_computation.3 | async-start | bytes 26738688 | tf_op jit(solution)/shard_map/all_gather | solution.py:28
  548.0 1.6 copy-start.27
Sparse Core Ops, SparseCore 0:
  393.1 150.5 all-gather.3
  549.8 181.3 all-gather.5
where the time goes:
time: 782 us; the launch traced here: 772 us
  waiting for transfers between devices  282 us (36%)
  local copies, waits for them, and re-layouts  227 us (29%)
  blocking collectives  99 us (13%)
  other arithmetic  83.8 us (11%)
  matrix products  53.1 us (7%)
  between operations  14.9 us (2%)
  starting transfers between devices  11.9 us (2%)
    all_gather x2, waiting for transfers between devices, prefix_2(): gathered = jax.tree.map(lambda a: lax.all_gather(a, axis), part)  261 us
    gather x96, local copies, waits for them, and re-layouts  119 us
    all_gather x3, blocking collectives, prefix_2(): gathered = jax.tree.map(lambda a: lax.all_gather(a, axis), part)  99 us
    unnamed x78, local copies, waits for them, and re-layouts  38.9 us
    add x15, other arithmetic, compose_affine(): return (later[0] * earlier[0], widen(later[0]) * earlier[1] + later[1])  27.9 us
    all_to_all x1, waiting for transfers between devices, body(): lax.all_to_all(coeffs, 'order', split_axis=4, concat_axis=3, tiled=True)  21.3 us
    another operation x2, other arithmetic, unpack_table(): jnp.stack([even_rows, odd_rows], axis=1)  17.6 us
  transfers between devices with their start and end apart: 5, of which 3 were waited for; matrix products, arithmetic and copies ran while one was open for 29% of the time, Pallas kernels for 0%

commit v1 on v0

v1 whole, which is shorter than its diff:
```python
import math

import jax
import jax.numpy as jnp
import numpy as np
from jax import lax
from jax.experimental import pallas as pl
from jax.experimental.pallas import tpu as pltpu
from jax.sharding import PartitionSpec as P

L = 512
NLAT = 512
NPHI = 1024
NH = 256
f32 = jnp.float32
bf16 = jnp.bfloat16
MIB = 1 << 20


def natural_tables():
    phases = (np.arange(L)[:, None] * np.arange(NPHI)[None, :]) % NPHI
    angles = 2.0 * np.pi * phases / NPHI
    rows = np.stack([np.cos(angles), -np.sin(angles)], axis=1)
    weight = np.where(np.arange(L) == 0, 1.0, 2.0) * (math.sqrt(2.0 * math.pi) / L)
    synthesis = (rows * weight[:, None, None]).reshape(2 * L, NPHI)
    analysis = (rows / NPHI).reshape(2 * L, NPHI)
    return synthesis.T.astype(jnp.bfloat16), analysis.astype(jnp.bfloat16)


def load(ref, rows):
    return jnp.concatenate([ref[q, rows, :] for q in range(ref.shape[0])], axis=1)


def store(ref, rows, value):
    for q in range(ref.shape[0]):
        ref[q, rows, :] = value[:, q * 128 : q * 128 + 128]


def synthesis_kernel(lower, vel, vor, mag, cur, table, out, xs, ys):
    step = pl.program_id(0)
    for a, ref in enumerate((vel, vor, mag, cur)):
        for c in range(3):
            for s in range(2):
                for p in range(2):
                    row = (s * 24 + (a * 3 + c) * 2 + p) * 16
                    store(xs, pl.ds(row, 16), ref[c, s, p].astype(f32))
    r = lax.broadcasted_iota(jnp.int32, (1, L), 1)
    sign_a = (1 - 2 * (r & 1)).astype(f32)

    def one_pair(i, _):
        m = lower[step * 8 + i]
        a = load(xs, pl.ds(2 * i, 48, stride=16))
        b = load(xs, pl.ds(2 * i + 1, 48, stride=16))
        a = pltpu.roll(a, (L - m) & (L - 1), 1)
        b_last = b[:, L - 1 : L]
        b = pltpu.roll(b, 1, 1)
        is_a = r < L - m
        sign_b = (1 - 2 * ((r + m) & 1)).astype(f32)
        a = jnp.where(is_a, a, 0.0)
        b = jnp.where(is_a, 0.0, b)
        lhs = jnp.concatenate([a, a * sign_a, b, b * sign_b], axis=0).astype(bf16)
        res = jnp.dot(lhs, table[i, 0:L, :], preferred_element_type=f32)
        last = b_last * table[i, L : L + 1, :].astype(f32)
        last_sign = (1 - 2 * (m & 1)).astype(f32)
        b_n = res[96:144] + last
        b_s = res[144:192] + last * last_sign
        for k, parts in ((2 * i, (res[0:48], res[48:96])), (2 * i + 1, (b_n, b_s))):
            for h in range(2):
                for s in range(2):
                    rows = pl.ds((s * 2 + h) * 384 + k, 24, stride=16)
                    store(ys, rows, parts[h][s * 24 : s * 24 + 24])
        return 0

    lax.fori_loop(0, 8, one_pair, 0)
    for sh in range(4):
        for jh in range(2):
            piece = ys[jh, sh * 384 : sh * 384 + 384, :]
            out[sh * 2 + jh] = piece.reshape(24, 16, 128).astype(bf16)


def legendre_synthesis(lower, velocity, vorticity, magnetic, current, table):
    field = pl.BlockSpec((3, 2, 2, 16, L), lambda g, low: (0, 0, 0, g, 0))
    return pl.pallas_call(
        synthesis_kernel,
        grid_spec=pltpu.PrefetchScalarGridSpec(
            num_scalar_prefetch=1,
            grid=(4,),
            in_specs=[field] * 4 + [pl.BlockSpec((8, L + 1, NH), lambda g, low: (g, 0, 0))],
            out_specs=pl.BlockSpec((8, 24, 16, 128), lambda g, low: (0, 0, g, 0)),
            scratch_shapes=[pltpu.VMEM((4, 768, 128), f32), pltpu.VMEM((2, 1536, 128), f32)],
        ),
        out_shape=jax.ShapeDtypeStruct((8, 24, 64, 128), bf16),
        compiler_params=pltpu.CompilerParams(vmem_limit_bytes=40 * MIB),
        cost_estimate=pl.CostEstimate(flops=int(1.6e9), bytes_accessed=15 * MIB, transcendentals=0),
        name="legendre_synthesis",
    )(lower, velocity, vorticity, magnetic, current, table)


def state_kernel(kappa, angular, vel, pot, out, scr):
    for f, ref in enumerate((vel, pot)):
        for c in range(3):
            for s in range(2):
                for p in range(2):
                    x = ref[c, s, p].astype(f32)
                    row = s * 48 + ((f * 3 + c) * 2 + p) * 4
                    for d in range(4):
                        scr[d, row : row + 4, :] = x[4 * d : 4 * d + 4]
    lane = lax.broadcasted_iota(jnp.int32, (1, L), 1)
    for kind, ref in enumerate((kappa, angular)):
        for f in range(2):
            for s in range(2):
                value = jnp.full((1, L), ref[f, s], f32)
                high = value.astype(bf16).astype(f32)
                rest = value - high
                mid = rest.astype(bf16).astype(f32)
                low = rest - mid
                line = jnp.where(lane < 128, high, jnp.where(lane < 256, mid, low))
                row = 96 + (kind * 2 + f) * 2 + s
                for d in range(4):
                    scr[d, row : row + 1, :] = line
    scr[:, 104:112, :] = jnp.zeros((4, 8, L), f32)
    out[...] = scr[...].astype(bf16)


def state_to_send(kappa, angular, velocity, potential):
    field = pl.BlockSpec((3, 2, 2, 16, L), lambda g: (0, 0, 0, g, 0))
    small = pl.BlockSpec(memory_space=pltpu.SMEM)
    return pl.pallas_call(
        state_kernel,
        grid=(4,),
        in_specs=[small, small, field, field],
        out_specs=pl.BlockSpec((4, 112, L), lambda g: (g, 0, 0)),
        out_shape=jax.ShapeDtypeStruct((16, 112, L), bf16),
        scratch_shapes=[pltpu.VMEM((4, 112, L), f32)],
        compiler_params=pltpu.CompilerParams(vmem_limit_bytes=24 * MIB),
        cost_estimate=pl.CostEstimate(flops=10**6, bytes_accessed=4 * MIB, transcendentals=0),
        name="state_to_send",
    )(kappa, angular, velocity, potential)


def grid_kernel(lat, syn, ana, weight, out, wide, prod, acc):
    step = pl.program_id(0)

    @pl.when(step == 0)
    def _():
        for c in range(12):
            wide[:, c * 128 : c * 128 + 128] = lat[:, 2 * c : 2 * c + 2].reshape(1024, 128)

    g = jnp.dot(syn[...], wide[...], preferred_element_type=f32)
    x = [g[:, c * 128 : c * 128 + 128] for c in range(12)]
    u, w, b, j = x[0:3], x[3:6], x[6:9], x[9:12]

    def cross(p, q):
        return [
            p[1] * q[2] - p[2] * q[1],
            p[2] * q[0] - p[0] * q[2],
            p[0] * q[1] - p[1] * q[0],
        ]

    uw, jb, ub = cross(u, w), cross(j, b), cross(u, b)
    terms = [uw[0] + jb[0] + 2.0 * u[1], uw[1] + jb[1] - 2.0 * u[0], uw[2] + jb[2]] + ub
    for c in range(6):
        prod[:, c * 128 : c * 128 + 128] = terms[c].astype(bf16)
    part = jnp.dot(ana[...], prod[...], preferred_element_type=f32)

    @pl.when(step == 0)
    def _():
        acc[...] = part

    @pl.when(step > 0)
    def _():
        acc[...] += part

    @pl.when(step == pl.num_programs(0) - 1)
    def _():
        wt = weight[...]
        for c in range(6):
            out[:, c * 128 : c * 128 + 128] = (acc[:, c * 128 : c * 128 + 128] * wt).astype(bf16)


def grid_stage(lat, syn, ana, weight):
    rows = 256
    return pl.pallas_call(
        grid_kernel,
        grid=(NPHI // rows,),
        in_specs=[
            pl.BlockSpec((8, 24, 64, 128), lambda i: (0, 0, 0, 0)),
            pl.BlockSpec((rows, 1024), lambda i: (i, 0)),
            pl.BlockSpec((1024, rows), lambda i: (0, i)),
            pl.BlockSpec((1, 128), lambda i: (0, 0)),
        ],
        out_specs=pl.BlockSpec((1024, 768), lambda i: (0, 0)),
        out_shape=jax.ShapeDtypeStruct((1024, 768), bf16),
        scratch_shapes=[
            pltpu.VMEM((1024, 1536), bf16),
            pltpu.VMEM((rows, 768), bf16),
            pltpu.VMEM((1024, 768), f32),
        ],
        compiler_params=pltpu.CompilerParams(vmem_limit_bytes=48 * MIB),
        cost_estimate=pl.CostEstimate(flops=int(4.8e9), bytes_accessed=9 * MIB, transcendentals=0),
        name="grid_stage",
    )(lat, syn, ana, weight)


def prepare_kernel(place, lower, table, extra, table_out, factors, scr):
    l_row = lax.broadcasted_iota(jnp.int32, (1, L), 1)
    for i in range(2):
        m = lower[place[0] * 2 + i]
        scr[...] = table[i].astype(f32)
        a = jnp.transpose(scr[0:L, :])
        a = pltpu.roll(a, m, 1)
        table_out[2 * i] = jnp.where(l_row >= m, a, 0.0).astype(bf16)
        b = jnp.transpose(scr[1 : L + 1, :])
        table_out[2 * i + 1] = jnp.where(l_row >= L - 1 - m, b, 0.0).astype(bf16)
    degree = l_row.astype(f32)
    degree_term = degree * (degree + 1.0)
    below, angle = [[], []], [[], []]
    for d in range(16):
        x = extra[d].astype(f32)
        value = (x[0:8, 0:128] + x[0:8, 128:256]) + x[0:8, 256:384]
        value = jnp.concatenate([value] * 4, axis=1)
        for f in range(2):
            for s in range(2):
                below[f].append(value[f * 2 + s : f * 2 + s + 1])
                angle[f].append(value[4 + f * 2 + s : 4 + f * 2 + s + 1])
    for f in range(2):
        carried = jnp.zeros((1, L), f32)
        for s in range(32):
            under = below[f][s]
            above = below[f][s + 1] if s < 31 else jnp.zeros((1, L), f32)
            diagonal = 1.0 + under + above + angle[f][s] * degree_term
            inverse = 1.0 / (diagonal - under * carried)
            carried = above * inverse
            row = f * 32 + s
            factors[0, row : row + 1, :] = inverse
            factors[1, row : row + 1, :] = under * inverse
            factors[2, row : row + 1, :] = carried


def prepare_solve(place, lower, table, state):
    return pl.pallas_call(
        prepare_kernel,
        grid_spec=pltpu.PrefetchScalarGridSpec(
            num_scalar_prefetch=2,
            grid=(1,),
            in_specs=[
                pl.BlockSpec((2, L + 1, NH), lambda g, place, low: (place[0], 0, 0)),
                pl.BlockSpec((16, 16, L), lambda g, place, low: (0, 6, 0)),
            ],
            out_specs=[
                pl.BlockSpec((4, NH, L), lambda g, place, low: (0, 0, 0)),
                pl.BlockSpec((3, 64, L), lambda g, place, low: (0, 0, 0)),
            ],
            scratch_shapes=[pltpu.VMEM((L + 1, NH), f32)],
        ),
        out_shape=[
            jax.ShapeDtypeStruct((4, NH, L), bf16),
            jax.ShapeDtypeStruct((3, 64, L), f32),
        ],
        compiler_params=pltpu.CompilerParams(vmem_limit_bytes=24 * MIB),
        cost_estimate=pl.CostEstimate(flops=10**7, bytes_accessed=3 * MIB, transcendentals=0),
        name="prepare_solve",
    )(place, lower, table, state)


def solve_kernel(place, lower, coef, state, table, factors, out, cs, lhs, rhs):
    for c in range(6):
        cs[c] = coef[:, c * 128 : c * 128 + 128].astype(f32)
    l_row = lax.broadcasted_iota(jnp.int32, (1, L), 1)
    for k in range(4):
        m = lower[place[0] * 2 + k // 2]
        order = m if k % 2 == 0 else L - 1 - m
        half_sign = 0.5 * (1 - 2 * ((l_row + order) & 1)).astype(f32)
        for h in range(2):
            for c in range(6):
                for p in range(2):
                    row = ((h * 6 + c) * 2 + p) * 32
                    for jh in range(2):
                        start = h * 16 + jh * 8 + k * 2 + p
                        lhs[k % 2, row : row + 32, jh * 128 : jh * 128 + 128] = cs[
                            c, pl.ds(start, 32, stride=32), :
                        ].astype(bf16)
        res = jnp.dot(lhs[k % 2], table[k], preferred_element_type=f32)
        half = 0.5 * res[0:384] + half_sign * res[384:768]
        for cp in range(12):
            store(rhs, pl.ds(cp * 4 + k, 32, stride=48), half[cp * 32 : cp * 32 + 32])

    def factor(kind, f, s):
        return factors[kind, pl.ds(f * 32 + s, 1), :]

    def forward(d, running):
        running = list(running)
        block = state[d].astype(f32)
        for s2 in range(2):
            s = 2 * d + s2
            for f in range(2):
                base = s * 48 + f * 24
                value = load(rhs, pl.ds(base, 24)) + block[s2 * 48 + f * 24 : s2 * 48 + f * 24 + 24]
                running[f] = factor(0, f, s) * value + factor(1, f, s) * running[f]
                store(rhs, pl.ds(base, 24), running[f])
        return tuple(running)

    zero = jnp.zeros((24, L), f32)
    lax.fori_loop(0, 16, forward, (zero, zero))

    def backward(step, carried):
        d = 15 - step
        carried = list(carried)
        pieces = [None] * 4
        for s2 in (1, 0):
            s = 2 * d + s2
            for f in range(2):
                value = load(rhs, pl.ds(s * 48 + f * 24, 24))
                carried[f] = value + factor(2, f, s) * carried[f]
                pieces[s2 * 2 + f] = carried[f]
        out[d] = jnp.concatenate(pieces, axis=0).astype(bf16)
        return tuple(carried)

    lax.fori_loop(0, 16, backward, (zero, zero))


def analysis_and_solve(place, lower, coef, state, table, factors):
    return pl.pallas_call(
        solve_kernel,
        grid_spec=pltpu.PrefetchScalarGridSpec(
            num_scalar_prefetch=2,
            grid=(1,),
            in_specs=[
                pl.BlockSpec((1024, 768), lambda g, place, low: (0, 0)),
                pl.BlockSpec((16, 96, L), lambda g, place, low: (0, 0, 0)),
                pl.BlockSpec((4, NH, L), lambda g, place, low: (0, 0, 0)),
                pl.BlockSpec((3, 64, L), lambda g, place, low: (0, 0, 0)),
            ],
            out_specs=pl.BlockSpec((16, 96, L), lambda g, place, low: (0, 0, 0)),
            scratch_shapes=[
                pltpu.VMEM((6, 1024, 128), f32),
                pltpu.VMEM((2, 768, NH), bf16),
                pltpu.VMEM((4, 32 * 48, 128), f32),
            ],
        ),
        out_shape=jax.ShapeDtypeStruct((16, 96, L), bf16),
        compiler_params=pltpu.CompilerParams(vmem_limit_bytes=48 * MIB),
        cost_estimate=pl.CostEstimate(flops=int(0.9e9), bytes_accessed=6 * MIB, transcendentals=0),
        name="analysis_and_solve",
    )(place, lower, coef, state, table, factors)


def unpack_kernel(got, out_v, out_p, scr, tmp):
    store(scr, pl.ds(0, 768), got[...].astype(f32).reshape(768, L))
    for f, ref in enumerate((out_v, out_p)):
        for c in range(3):
            for p in range(2):
                for k in range(4):
                    row = ((f * 3 + c) * 2 + p) * 4 + k
                    store(tmp, pl.ds(k, 16, stride=4), load(scr, pl.ds(row, 16, stride=48)))
                ref[c, 0, p] = load(tmp, pl.ds(0, 64))


def unpack_solution(got):
    shape = jax.ShapeDtypeStruct((3, 2, 2, 64, L), f32)
    field = pl.BlockSpec((3, 1, 2, 64, L), lambda s: (0, s, 0, 0, 0))
    return pl.pallas_call(
        unpack_kernel,
        grid=(2,),
        in_specs=[pl.BlockSpec((16, 48, L), lambda s: (0, s, 0))],
        out_specs=[field, field],
        out_shape=[shape, shape],
        scratch_shapes=[pltpu.VMEM((4, 768, 128), f32), pltpu.VMEM((4, 64, 128), f32)],
        compiler_params=pltpu.CompilerParams(vmem_limit_bytes=24 * MIB),
        cost_estimate=pl.CostEstimate(flops=10**6, bytes_accessed=5 * MIB, transcendentals=0),
        name="unpack_solution",
    )(got)


def fourier_tables(order_slots):
    natural_s, natural_a = natural_tables()
    ids = jnp.arange(2 * L, dtype=jnp.int32)
    part = jnp.arange(2, dtype=jnp.int32)
    by_source = order_slots.reshape(8, 1, 64) * 2 + part[None, :, None]
    pick_s = (ids[:, None] == by_source.reshape(1, -1)).astype(bf16)
    syn = jnp.dot(jnp.asarray(natural_s), pick_s, preferred_element_type=f32).astype(bf16)
    slots = order_slots.reshape(8, 16, 4).transpose(1, 0, 2)
    by_target = slots[..., None] * 2 + part
    pick_a = (by_target.reshape(-1, 1) == ids[None, :]).astype(bf16)
    ana = jnp.dot(pick_a, jnp.asarray(natural_a), preferred_element_type=f32).astype(bf16)
    return syn, ana


def body(
    velocity,
    vorticity,
    magnetic,
    current,
    potential,
    order_slots,
    legendre_values,
    block_lengths,
    coupling,
    angular,
):
    order_rank = lax.axis_index("order")
    shell_rank = lax.axis_index("shell")
    lower = lax.dynamic_slice_in_dim(order_slots, order_rank * 64, 64).reshape(32, 2)[:, 0]
    place = shell_rank.reshape(1)
    shell_ids = shell_rank * 2 + jnp.arange(2, dtype=jnp.int32)
    starts = jnp.cumsum(block_lengths) - block_lengths
    is_start = jnp.any(shell_ids[:, None] == starts[None, :], axis=1)
    kappa = jnp.where(is_start[None, :], 0.0, coupling)
    rows = (order_rank & 1) * 128 + jnp.arange(128, dtype=jnp.int32)
    colatitude = math.pi * (rows.astype(f32) + 0.5) / NLAT
    weight = (math.sqrt(2.0 * math.pi) * L * math.pi / NLAT * jnp.sin(colatitude))[None, :]

    latitude = legendre_synthesis(
        lower, velocity, vorticity, magnetic, current, legendre_values
    )
    incoming = lax.all_to_all(latitude, "order", 0, 0, tiled=True)

    order_after, vel_after, pot_after, _ = lax.optimization_barrier(
        (order_slots, velocity, potential, latitude)
    )
    state = state_to_send(kappa, angular, vel_after, pot_after)
    state = lax.all_to_all(state, "shell", 0, 0, tiled=True)
    syn, ana = fourier_tables(order_after)
    table, factors = prepare_solve(place, lower, legendre_values, state)

    coefs = grid_stage(incoming, syn, ana, weight)
    coefs = lax.all_to_all(
        coefs.reshape(128, 8, 768), ("shell", "order"), 0, 0, tiled=True
    ).reshape(1024, 768)
    solved = analysis_and_solve(place, lower, coefs, state, table, factors)
    solved = lax.all_to_all(solved, "shell", 0, 0, tiled=True)
    return tuple(unpack_solution(solved))


def solution(mesh):
    spectral = P(None, "shell", None, "order", None)
    in_specs = (
        spectral,
        spectral,
        spectral,
        spectral,
        spectral,
        P(),
        P("order", None, None),
        P(),
        P(None, "shell"),
        P(None, "shell"),
    )
    return jax.shard_map(
        body, mesh=mesh, in_specs=in_specs, out_specs=(spectral, spectral), check_vma=False
    )
```

time: 782 us -> 175 us (0.22); the launches traced: 772 us -> 174 us
  waiting for transfers between devices: 282 us -> 61.8 us
  local copies, waits for them, and re-layouts: 227 us -> 22.9 us
  other arithmetic: 83.8 us -> 0.63 us
  blocking collectives: 99 us -> 25.4 us
  matrix products: 53.1 us -> 6.54 us
  Pallas kernels: 0 us -> 38.5 us
  between operations: 14.9 us -> 0.91 us
    all_gather x2 -> x0, waiting for transfers between devices: 261 us -> none  [prefix_2(): gathered = jax.tree.map(lambda a: lax.all_gather(a, axis), part)]
    gather x96 -> x0, local copies, waits for them, and re-layouts: 119 us -> none
    all_gather x3 -> x0, blocking collectives: 99 us -> none  [prefix_2(): gathered = jax.tree.map(lambda a: lax.all_gather(a, axis), part)]
    dot_general x9 -> x2, matrix products: 53.1 us -> 6.54 us  [the longest x1 4.12 us: fourier_tables(): jnp.dot(pick_a, jnp.asarray(natural_a), preferred_element_type=f32)]
    all_to_all x2 -> x3, waiting for transfers between devices: 21.3 us -> 61.8 us  [the longest x1 34.8 us: body(): incoming = lax.all_to_all(latitude, 'order', 0, 0, tiled=True)]
    pallas_call x0 -> x6, Pallas kernels: none -> 38.5 us  [the longest x1 15.1 us: legendre_synthesis(): pl.pallas_call(synthesis_kernel, grid_spec=pltpu.PrefetchScalarGridSpec(n...]
    add x23 -> x3, other arithmetic: 35.9 us -> 0.21 us  [the longest x1 0.2 us: fourier_tables(): by_target = slots[..., None] * 2 + part]
    all_to_all x0 -> x1, blocking collectives: none -> 25.4 us  [body(): solved = lax.all_to_all(solved, 'shell', 0, 0, tiled=True)]
  transfers between devices with their start and end apart: 5 -> 3, of which waited for: 3 -> 3; matrix products, arithmetic and copies ran while one was open for 29% -> 4% of each run, Pallas kernels for 0% -> 8%
where the time goes in v1:
time: 175 us; the launch traced here: 174 us
  waiting for transfers between devices  61.8 us (35%)
  Pallas kernels  38.5 us (22%)
  blocking collectives  25.4 us (15%)
  local copies, waits for them, and re-layouts  22.9 us (13%)
  starting transfers between devices  17.4 us (10%)
  matrix products  6.54 us (4%)
    all_to_all x1, waiting for transfers between devices, body(): incoming = lax.all_to_all(latitude, 'order', 0, 0, tiled=True)  34.8 us
    all_to_all x1, blocking collectives, body(): solved = lax.all_to_all(solved, 'shell', 0, 0, tiled=True)  25.4 us
    unnamed x37, local copies, waits for them, and re-layouts  21.4 us
    all_to_all x1, waiting for transfers between devices, body(): lax.all_to_all(coefs.reshape(128, 8, 768), ('shell', 'order'), 0, 0, tile...  17.9 us
    pallas_call x1, Pallas kernels, legendre_synthesis(): pl.pallas_call(synthesis_kernel, grid_spec=pltpu.PrefetchScalarGridSpec(n...  15.1 us
    pallas_call x1, Pallas kernels, grid_stage(): pl.pallas_call(grid_kernel, grid=(NPHI // rows,), in_specs=[pl.BlockSpec(...  10.6 us
    all_to_all x1, waiting for transfers between devices, body(): state = lax.all_to_all(state, 'shell', 0, 0, tiled=True)  9.03 us
    pallas_call x1, Pallas kernels, analysis_and_solve(): pl.pallas_call(solve_kernel, grid_spec=pltpu.PrefetchScalarGridSpec(num_s...  7.07 us
  transfers between devices with their start and end apart: 3, of which 3 were waited for; matrix products, arithmetic and copies ran while one was open for 4% of the time, Pallas kernels for 8%

profile of v1, /device:TPU:0, one launch (start us, length us, event | category | flops | bytes accessed | tf_op | source)
XLA Modules:
  0.0 174.1 jit_solution(15330828046153961158)
XLA Ops:
  0.6 0.8 dynamic_slice.3
  1.4 0.1 reshape.116
  1.5 0.1 slice_reduce_fusion.lower
  1.6 0.0 copy-start.3
  1.6 0.0 copy-start.7
  1.6 0.0 copy-start.8
  1.6 0.0 copy-start.9
  1.7 11.6 %copy.22.table = bf16[32,513,256]{2,1,0:T(8,128)(2,1)} copy(bf16[32,513,256]{2,0,1:T(8,128)(2,1)} %param.18) | data formatting | bytes 16809984 | tf_op args[6]
  13.3 0.0 copy-done.3
  13.3 0.0 copy-done.7
  13.3 0.0 copy-done.8
  13.3 0.0 copy-done.9
  13.3 15.1 %legendre_synthesis.1 = bf16[8,24,64,128]{3,2,1,0:T(8,128)(2,1)} custom-call(s32[32]{0:T(128)S(1)} %slice_reduce_fusion.lower, bf16[3,2,2,64,512]{4,3,2,1,0:T(8,128)(2,1)S(1)} %copy-done.3, bf16[3,2,2,64,512]{4,3,2,1,0:T(8,128)(2,1)S(1)} %copy-done.7, bf16[3,2,2,64,512]{4,3,2,1,0:T(8,128)(2,1)S(1)} %copy-done.8, bf16[3,2,2,64,512]{4,3,2,1,0:T(8,128)(2,1)S(1)} %copy-done.9, ...), custom_call_target="tpu_custom_call" | custom-call | flops 1600000000 | bytes 15728640 | tf_op jit(solution)/shard_map/legendre_synthesis/pallas_call | solution.py:83
  28.4 0.0 copy-start.14
  28.4 0.0 copy-start.16
  28.4 0.0 copy-start.15
  28.4 0.0 copy-start.10
  28.4 0.0 copy-start.13
  28.4 5.5 %all-to-all-start = ((bf16[8,24,64,128]{3,2,1,0:T(8,128)(2,1)}), bf16[8,24,64,128]{3,2,1,0:T(8,128)(2,1)}, u32[]{:S(2)}, u32[]{:S(2)}) async-start(bf16[8,24,64,128]{3,2,1,0:T(8,128)(2,1)} %legendre_synthesis.1), calls=%async_computation | async-start | bytes 6291456 | tf_op jit(solution)/shard_map/all_to_all | solution.py:416
  33.9 0.0 copy-done.14
  33.9 0.1 mul.52
  34.1 0.1 mul.51
  34.1 0.0 copy-done.16
  34.1 0.2 reduce-window.9
  34.3 0.2 iota_add_fusion
  34.5 0.2 add.87
  34.8 0.2 compare_reduce_fusion
  35.0 0.0 copy-done.15
  35.0 0.0 copy-done.10
  35.0 0.0 copy-done.13
  35.0 1.4 state_to_send.1
  36.4 0.0 copy-start.2
  36.4 1.2 copy-done.2
  37.7 34.8 %all-to-all-done.lat = bf16[8,24,64,128]{3,2,1,0:T(8,128)(2,1)} async-done(((bf16[8,24,64,128]{3,2,1,0:T(8,128)(2,1)}), bf16[8,24,64,128]{3,2,1,0:T(8,128)(2,1)}, u32[]{:S(2)}, u32[]{:S(2)}) %all-to-all-start) | async-done | bytes 3145760 | tf_op jit(solution)/shard_map/all_to_all | solution.py:416
  72.5 7.0 %all-to-all-start.2 = ((bf16[16,112,512]{2,1,0:T(8,128)(2,1)}), bf16[16,112,512]{2,1,0:T(8,128)(2,1)S(1)}, u32[]{:S(2)}, u32[]{:S(2)}) async-start(bf16[16,112,512]{2,1,0:T(8,128)(2,1)} %copy-done.2), calls=%async_computation.2 | async-start | bytes 3670016 | tf_op jit(solution)/shard_map/all_to_all | solution.py:422
  79.5 0.1 add.83
  79.7 0.0 copy-start.17
  79.7 4.1 %fusion.4.ana = bf16[1024,1024]{1,0:T(8,128)(2,1)S(1)} fusion(bf16[1024,1024]{1,0:T(8,128)(2,1)} %constant.44.clone, s32[1024]{0:T(1024)S(1)} %add.87), kind=kOutput, calls=%fused_computation.7 | convolution fusion | flops 2149580800 | bytes 4198400 | tf_op jit(solution)/shard_map/dot_general | solution.py:385
  83.8 0.0 copy-done.17
  83.8 2.4 %convert_bitcast_fusion.syn = bf16[1024,1024]{1,0:T(8,128)(2,1)S(1)} fusion(bf16[1024,1024]{1,0:T(8,128)(2,1)S(1)} %copy-done.17, s32[1024]{0:T(1024)S(1)} %add.83), kind=kOutput, calls=%fused_computation.5 | convolution fusion | flops 2149580800 | bytes 4198400 | tf_op jit(solution)/shard_map/dot_general | solution.py:381
  86.2 10.6 %grid_stage.1 = bf16[1024,768]{1,0:T(8,128)(2,1)S(1)} custom-call(bf16[8,24,64,128]{3,2,1,0:T(8,128)(2,1)} %all-to-all-done.lat, bf16[1024,1024]{1,0:T(8,128)(2,1)S(1)} %convert_bitcast_fusion.syn, bf16[1024,1024]{1,0:T(8,128)(2,1)S(1)} %fusion.4.ana, f32[1,128]{1,0:T(1,128)S(1)} %sine_multiply_fusion.weight), custom_call_target="tpu_custom_call" | custom-call | flops 4800000000 | bytes 9437184 | tf_op jit(solution)/shard_map/grid_stage/pallas_call | solution.py:183
  96.8 0.0 copy-start.4
  96.8 1.1 copy-done.4
  98.0 9.0 %all-to-all-done.2.extra.state = bf16[16,112,512]{2,1,0:T(8,128)(2,1)S(1)} async-done(((bf16[16,112,512]{2,1,0:T(8,128)(2,1)}), bf16[16,112,512]{2,1,0:T(8,128)(2,1)S(1)}, u32[]{:S(2)}, u32[]{:S(2)}) %all-to-all-start.2) | async-done | bytes 1835040 | tf_op jit(solution)/shard_map/all_to_all | solution.py:422
  107.0 0.0 copy-start.1
  107.0 4.9 %all-to-all-start.1 = ((bf16[128,8,768]{2,1,0:T(8,128)(2,1)}), bf16[128,8,768]{2,1,0:T(8,128)(2,1)S(1)}, u32[]{:S(2)}, u32[]{:S(2)}) async-start(bf16[128,8,768]{2,1,0:T(8,128)(2,1)} %bitcast.12), calls=%async_computation.1 | async-start | bytes 3145728 | tf_op jit(solution)/shard_map/all_to_all | solution.py:427
  111.9 0.0 copy-start
  111.9 3.4 %copy-done = bf16[32,513,256]{2,1,0:T(8,128)(2,1)S(1)} copy-done((bf16[32,513,256]{2,1,0:T(8,128)(2,1)S(1)}, bf16[32,513,256]{2,1,0:T(8,128)(2,1)}, u32[]{:S(2)}) %copy-start) | copy-done | bytes 8405016
  115.3 1.6 prepare_solve.1
  116.9 0.0 copy-done.1
  116.9 0.0 copy-start.5
  116.9 1.0 copy-done.5
  117.9 0.0 copy-start.11
  117.9 0.8 copy-done.11
  118.6 17.9 %all-to-all-done.1 = bf16[128,8,768]{2,1,0:T(8,128)(2,1)S(1)} async-done(((bf16[128,8,768]{2,1,0:T(8,128)(2,1)}), bf16[128,8,768]{2,1,0:T(8,128)(2,1)S(1)}, u32[]{:S(2)}, u32[]{:S(2)}) %all-to-all-start.1) | async-done | bytes 1572896 | tf_op jit(solution)/shard_map/all_to_all | solution.py:427
  136.5 0.0 copy-start.6
  136.5 1.2 copy-done.6
  137.8 0.0 copy-start.12
  137.8 1.0 copy-done.12
  138.7 7.1 %analysis_and_solve.1 = bf16[16,96,512]{2,1,0:T(8,128)(2,1)S(1)} custom-call(s32[1]{0:T(128)} %bitcast.place, s32[32]{0:T(128)S(1)} %slice_reduce_fusion.lower, bf16[1024,768]{1,0:T(8,128)(2,1)S(1)} %bitcast.11, bf16[16,112,512]{2,1,0:T(8,128)(2,1)} %copy-done.1, bf16[4,256,512]{2,1,0:T(8,128)(2,1)S(1)} %copy-done.6, f32[3,64,512]{2,1,0:T(8,128)S(1)} %copy-done.12), custom_call_target="tpu_custom_call" | custom-call | flops 900000000 | bytes 6291456 | tf_op jit(solution)/shard_map/analysis_and_solve/pallas_call | solution.py:323
  145.8 25.4 %all_to_all.20.got = bf16[16,96,512]{2,1,0:T(8,128)(2,1)S(1)} all-to-all(bf16[16,96,512]{2,1,0:T(8,128)(2,1)S(1)} %analysis_and_solve.1), channel_id=1, replica_groups=mesh['shell'=16,'order'=8] {'shell'}, dimensions={0} | all-to-all | bytes 3145728 | tf_op jit(solution)/shard_map/all_to_all | solution.py:431
  171.3 2.8 %unpack_solution.1 = (f32[3,2,2,64,512]{4,3,2,1,0:T(8,128)}, f32[3,2,2,64,512]{4,3,2,1,0:T(8,128)}) custom-call(bf16[16,96,512]{2,1,0:T(8,128)(2,1)S(1)} %all_to_all.20.got), custom_call_target="tpu_custom_call" | custom-call | flops 1000000 | bytes 5242880 | tf_op jit(solution)/shard_map/unpack_solution/pallas_call | solution.py:362
  (7 shorter events, 0.1 us)
Async XLA Ops:
  1.6 11.7 %copy-start.3 = (bf16[3,2,2,64,512]{4,3,2,1,0:T(8,128)(2,1)S(1)}, bf16[3,2,2,64,512]{4,3,2,1,0:T(8,128)(2,1)}, u32[]{:S(2)}) copy-start(bf16[3,2,2,64,512]{4,3,2,1,0:T(8,128)(2,1)} %vel.2) | copy-start | bytes 2359300
  1.6 11.7 %copy-start.7 = (bf16[3,2,2,64,512]{4,3,2,1,0:T(8,128)(2,1)S(1)}, bf16[3,2,2,64,512]{4,3,2,1,0:T(8,128)(2,1)}, u32[]{:S(2)}) copy-start(bf16[3,2,2,64,512]{4,3,2,1,0:T(8,128)(2,1)} %vor.1) | copy-start | bytes 2359300
  1.6 11.6 %copy-start.8 = (bf16[3,2,2,64,512]{4,3,2,1,0:T(8,128)(2,1)S(1)}, bf16[3,2,2,64,512]{4,3,2,1,0:T(8,128)(2,1)}, u32[]{:S(2)}) copy-start(bf16[3,2,2,64,512]{4,3,2,1,0:T(8,128)(2,1)} %mag.1) | copy-start | bytes 2359300
  1.6 11.6 %copy-start.9 = (bf16[3,2,2,64,512]{4,3,2,1,0:T(8,128)(2,1)S(1)}, bf16[3,2,2,64,512]{4,3,2,1,0:T(8,128)(2,1)}, u32[]{:S(2)}) copy-start(bf16[3,2,2,64,512]{4,3,2,1,0:T(8,128)(2,1)} %cur.1) | copy-start | bytes 2359300
  28.4 5.6 %copy-start.14 = (s32[512]{0:T(512)S(1)}, s32[512]{0:T(512)}, u32[]{:S(2)}) copy-start(s32[512]{0:T(512)} %param.17) | copy-start | bytes 6148
  28.4 5.8 %copy-start.16 = (s32[4]{0:T(128)S(1)}, s32[4]{0:T(128)}, u32[]{:S(2)}) copy-start(s32[4]{0:T(128)} %param.19) | copy-start | bytes 52
  28.4 6.6 %copy-start.15 = (f32[2,2]{1,0:T(2,128)S(1)}, f32[2,2]{1,0:T(2,128)}, u32[]{:S(2)}) copy-start(f32[2,2]{1,0:T(2,128)} %param.20) | copy-start | bytes 52
  28.4 6.6 %copy-start.10 = (bf16[3,2,2,64,512]{4,3,2,1,0:T(8,128)(2,1)S(1)}, bf16[3,2,2,64,512]{4,3,2,1,0:T(8,128)(2,1)}, u32[]{:S(2)}) copy-start(bf16[3,2,2,64,512]{4,3,2,1,0:T(8,128)(2,1)} %pot) | copy-start | bytes 2359300
  28.4 6.6 %copy-start.13 = (f32[2,2]{1,0:T(2,128)S(1)}, f32[2,2]{1,0:T(2,128)}, u32[]{:S(2)}) copy-start(f32[2,2]{1,0:T(2,128)} %angular.1) | copy-start | bytes 52
  28.4 44.1 %all-to-all-start = ((bf16[8,24,64,128]{3,2,1,0:T(8,128)(2,1)}), bf16[8,24,64,128]{3,2,1,0:T(8,128)(2,1)}, u32[]{:S(2)}, u32[]{:S(2)}) async-start(bf16[8,24,64,128]{3,2,1,0:T(8,128)(2,1)} %legendre_synthesis.1), calls=%async_computation | async-start | bytes 6291456 | tf_op jit(solution)/shard_map/all_to_all | solution.py:416
  36.4 1.2 copy-start.2
  72.5 34.5 %all-to-all-start.2 = ((bf16[16,112,512]{2,1,0:T(8,128)(2,1)}), bf16[16,112,512]{2,1,0:T(8,128)(2,1)S(1)}, u32[]{:S(2)}, u32[]{:S(2)}) async-start(bf16[16,112,512]{2,1,0:T(8,128)(2,1)} %copy-done.2), calls=%async_computation.2 | async-start | bytes 3670016 | tf_op jit(solution)/shard_map/all_to_all | solution.py:422
  79.7 4.1 %copy-start.17 = (bf16[1024,1024]{1,0:T(8,128)(2,1)S(1)}, bf16[1024,1024]{1,0:T(8,128)(2,1)}, u32[]{:S(2)}) copy-start(bf16[1024,1024]{1,0:T(8,128)(2,1)} %constant.43.clone) | copy-start | bytes 6291460
  96.8 1.1 copy-start.4
  107.0 9.9 %copy-start.1 = (bf16[16,112,512]{2,1,0:T(8,128)(2,1)}, bf16[16,112,512]{2,1,0:T(8,128)(2,1)S(1)}, u32[]{:S(2)}) copy-start(bf16[16,112,512]{2,1,0:T(8,128)(2,1)S(1)} %all-to-all-done.2.extra.state) | copy-start | bytes 5505028
  107.0 29.5 %all-to-all-start.1 = ((bf16[128,8,768]{2,1,0:T(8,128)(2,1)}), bf16[128,8,768]{2,1,0:T(8,128)(2,1)S(1)}, u32[]{:S(2)}, u32[]{:S(2)}) async-start(bf16[128,8,768]{2,1,0:T(8,128)(2,1)} %bitcast.12), calls=%async_computation.1 | async-start | bytes 3145728 | tf_op jit(solution)/shard_map/all_to_all | solution.py:427
  111.9 3.4 %copy-start = (bf16[32,513,256]{2,1,0:T(8,128)(2,1)S(1)}, bf16[32,513,256]{2,1,0:T(8,128)(2,1)}, u32[]{:S(2)}) copy-start(bf16[32,513,256]{2,1,0:T(8,128)(2,1)} %copy.22.table) | copy-start | bytes 25214980
  116.9 1.0 copy-start.5
  117.9 0.8 copy-start.11
  136.5 1.2 copy-start.6
  137.8 1.0 copy-start.12

commit v2 on v1

--- a/solution.py
+++ b/solution.py
@@ -96,17 +96,19 @@
     )(lower, velocity, vorticity, magnetic, current, table)
 
 
-def state_kernel(kappa, angular, vel, pot, out, scr):
+def state_kernel(place, kappa, angular, vel, pot, *refs):
+    outs, scr = refs[:16], refs[16]
     for f, ref in enumerate((vel, pot)):
         for c in range(3):
             for s in range(2):
                 for p in range(2):
                     x = ref[c, s, p].astype(f32)
                     row = s * 48 + ((f * 3 + c) * 2 + p) * 4
-                    for d in range(4):
+                    for d in range(16):
                         scr[d, row : row + 4, :] = x[4 * d : 4 * d + 4]
     lane = lax.broadcasted_iota(jnp.int32, (1, L), 1)
-    for kind, ref in enumerate((kappa, angular)):
+    lines = []
+    for ref in (kappa, angular):
         for f in range(2):
             for s in range(2):
                 value = jnp.full((1, L), ref[f, s], f32)
@@ -114,28 +116,27 @@
                 rest = value - high
                 mid = rest.astype(bf16).astype(f32)
                 low = rest - mid
-                line = jnp.where(lane < 128, high, jnp.where(lane < 256, mid, low))
-                row = 96 + (kind * 2 + f) * 2 + s
-                for d in range(4):
-                    scr[d, row : row + 1, :] = line
-    scr[:, 104:112, :] = jnp.zeros((4, 8, L), f32)
-    out[...] = scr[...].astype(bf16)
-
-
-def state_to_send(kappa, angular, velocity, potential):
-    field = pl.BlockSpec((3, 2, 2, 16, L), lambda g: (0, 0, 0, g, 0))
+                lines.append(jnp.where(lane < 128, high, jnp.where(lane < 256, mid, low)))
+    extra = jnp.concatenate(lines + [jnp.zeros((8, L), f32)], axis=0).astype(bf16)
+    for r in range(16):
+        outs[r][0:96, :] = scr[place[0] ^ r].astype(bf16)
+        outs[r][96:112, :] = extra
+
+
+def state_to_send(place, kappa, angular, velocity, potential):
+    field = pl.BlockSpec((3, 2, 2, 64, L), lambda g: (0, 0, 0, 0, 0))
     small = pl.BlockSpec(memory_space=pltpu.SMEM)
     return pl.pallas_call(
         state_kernel,
-        grid=(4,),
-        in_specs=[small, small, field, field],
-        out_specs=pl.BlockSpec((4, 112, L), lambda g: (g, 0, 0)),
-        out_shape=jax.ShapeDtypeStruct((16, 112, L), bf16),
-        scratch_shapes=[pltpu.VMEM((4, 112, L), f32)],
-        compiler_params=pltpu.CompilerParams(vmem_limit_bytes=24 * MIB),
+        grid=(1,),
+        in_specs=[small, small, small, field, field],
+        out_specs=[pl.BlockSpec((112, L), lambda g: (0, 0))] * 16,
+        out_shape=[jax.ShapeDtypeStruct((112, L), bf16)] * 16,
+        scratch_shapes=[pltpu.VMEM((16, 96, L), f32)],
+        compiler_params=pltpu.CompilerParams(vmem_limit_bytes=32 * MIB),
         cost_estimate=pl.CostEstimate(flops=10**6, bytes_accessed=4 * MIB, transcendentals=0),
         name="state_to_send",
-    )(kappa, angular, velocity, potential)
+    )(place, kappa, angular, velocity, potential)
 
 
 def grid_kernel(lat, syn, ana, weight, out, wide, prod, acc):
@@ -202,7 +203,11 @@
     )(lat, syn, ana, weight)
 
 
-def prepare_kernel(place, lower, table, extra, table_out, factors, scr):
+def prepare_kernel(place, lower, table, *refs):
+    parts, (state_out, table_out, factors, scr, extra) = refs[:16], refs[16:]
+    for r in range(16):
+        state_out[place[0] ^ r] = parts[r][0:96, :]
+        extra[place[0] ^ r] = parts[r][96:112, :].astype(f32)
     l_row = lax.broadcasted_iota(jnp.int32, (1, L), 1)
     for i in range(2):
         m = lower[place[0] * 2 + i]
@@ -216,7 +221,7 @@
     degree_term = degree * (degree + 1.0)
     below, angle = [[], []], [[], []]
     for d in range(16):
-        x = extra[d].astype(f32)
+        x = extra[d]
         value = (x[0:8, 0:128] + x[0:8, 128:256]) + x[0:8, 256:384]
         value = jnp.concatenate([value] * 4, axis=1)
         for f in range(2):
@@ -237,7 +242,7 @@
             factors[2, row : row + 1, :] = carried
 
 
-def prepare_solve(place, lower, table, state):
+def prepare_solve(place, lower, table, parts):
     return pl.pallas_call(
         prepare_kernel,
         grid_spec=pltpu.PrefetchScalarGridSpec(
@@ -245,22 +250,24 @@
             grid=(1,),
             in_specs=[
                 pl.BlockSpec((2, L + 1, NH), lambda g, place, low: (place[0], 0, 0)),
-                pl.BlockSpec((16, 16, L), lambda g, place, low: (0, 6, 0)),
-            ],
+            ]
+            + [pl.BlockSpec((112, L), lambda g, place, low: (0, 0))] * 16,
             out_specs=[
+                pl.BlockSpec((16, 96, L), lambda g, place, low: (0, 0, 0)),
                 pl.BlockSpec((4, NH, L), lambda g, place, low: (0, 0, 0)),
                 pl.BlockSpec((3, 64, L), lambda g, place, low: (0, 0, 0)),
             ],
-            scratch_shapes=[pltpu.VMEM((L + 1, NH), f32)],
+            scratch_shapes=[pltpu.VMEM((L + 1, NH), f32), pltpu.VMEM((16, 16, L), f32)],
         ),
         out_shape=[
+            jax.ShapeDtypeStruct((16, 96, L), bf16),
             jax.ShapeDtypeStruct((4, NH, L), bf16),
             jax.ShapeDtypeStruct((3, 64, L), f32),
         ],
         compiler_params=pltpu.CompilerParams(vmem_limit_bytes=24 * MIB),
         cost_estimate=pl.CostEstimate(flops=10**7, bytes_accessed=3 * MIB, transcendentals=0),
         name="prepare_solve",
-    )(place, lower, table, state)
+    )(place, lower, table, *parts)
 
 
 def solve_kernel(place, lower, coef, state, table, factors, out, cs, lhs, rhs):
@@ -418,15 +425,18 @@
     order_after, vel_after, pot_after, _ = lax.optimization_barrier(
         (order_slots, velocity, potential, latitude)
     )
-    state = state_to_send(kappa, angular, vel_after, pot_after)
-    state = lax.all_to_all(state, "shell", 0, 0, tiled=True)
+    parts = state_to_send(place, kappa, angular, vel_after, pot_after)
+    parts = [parts[0]] + [
+        lax.ppermute(parts[r], "shell", [(i, i ^ r) for i in range(16)]) for r in range(1, 16)
+    ]
     syn, ana = fourier_tables(order_after)
-    table, factors = prepare_solve(place, lower, legendre_values, state)
-
+    early = 12
+    incoming, parts[1:early] = lax.optimization_barrier((incoming, parts[1:early]))
     coefs = grid_stage(incoming, syn, ana, weight)
     coefs = lax.all_to_all(
         coefs.reshape(128, 8, 768), ("shell", "order"), 0, 0, tiled=True
     ).reshape(1024, 768)
+    state, table, factors = prepare_solve(place, lower, legendre_values, parts)
     solved = analysis_and_solve(place, lower, coefs, state, table, factors)
     solved = lax.all_to_all(solved, "shell", 0, 0, tiled=True)
     return tuple(unpack_solution(solved))

time: 175 us -> 180 us (1.029)
  waiting for transfers between devices: 61.8 us -> 22.6 us
  starting transfers between devices: 17.4 us -> 45.2 us
  local copies, waits for them, and re-layouts: 22.9 us -> 33.4 us
  matrix products: 6.54 us -> 10.6 us
  blocking collectives: 25.4 us -> 27.3 us
    all_to_all x1, waiting for transfers between devices: 34.8 us -> 0.23 us  [body(): incoming = lax.all_to_all(latitude, 'order', 0, 0, tiled=True)]
    ppermute x0 -> x15, starting transfers between devices: none -> 31.4 us  [body(): lax.ppermute(parts[r], 'shell', [(i, i ^ r) for i in range(16)])]
    ppermute x0 -> x15, waiting for transfers between devices: none -> 22.4 us  [body(): lax.ppermute(parts[r], 'shell', [(i, i ^ r) for i in range(16)])]
    all_to_all x1, waiting for transfers between devices: 17.9 us -> 0.01 us  [body(): lax.all_to_all(coefs.reshape(128, 8, 768), ('shell', 'order'), 0, 0, tile...]
    unnamed x37 -> x77, local copies, waits for them, and re-layouts: 21.4 us -> 31.9 us
    all_to_all x1 -> x0, waiting for transfers between devices: 9.03 us -> none  [body(): state = lax.all_to_all(state, 'shell', 0, 0, tiled=True)]
    all_to_all x1 -> x0, starting transfers between devices: 7.04 us -> none  [body(): state = lax.all_to_all(state, 'shell', 0, 0, tiled=True)]
    all_to_all x1, starting transfers between devices: 4.86 us -> 8.19 us  [body(): lax.all_to_all(coefs.reshape(128, 8, 768), ('shell', 'order'), 0, 0, tile...]
  transfers between devices with their start and end apart: 3 -> 17, of which waited for: 3 -> 3; matrix products, arithmetic and copies ran while one was open for 4% -> 7% of each run, Pallas kernels for 8% -> 2%
where the time goes in v2:
time: 180 us; the launch traced here: 179 us
  starting transfers between devices  45.2 us (25%)
  Pallas kernels  37.9 us (21%)
  local copies, waits for them, and re-layouts  33.4 us (19%)
  blocking collectives  27.3 us (15%)
  waiting for transfers between devices  22.6 us (13%)
  matrix products  10.6 us (6%)
    unnamed x77, local copies, waits for them, and re-layouts  31.9 us
    ppermute x15, starting transfers between devices, body(): lax.ppermute(parts[r], 'shell', [(i, i ^ r) for i in range(16)])  31.4 us
    all_to_all x1, blocking collectives, body(): solved = lax.all_to_all(solved, 'shell', 0, 0, tiled=True)  27.3 us
    ppermute x15, waiting for transfers between devices, body(): lax.ppermute(parts[r], 'shell', [(i, i ^ r) for i in range(16)])  22.4 us
    pallas_call x1, Pallas kernels, legendre_synthesis(): pl.pallas_call(synthesis_kernel, grid_spec=pltpu.PrefetchScalarGridSpec(n...  15.1 us
    pallas_call x1, Pallas kernels, grid_stage(): pl.pallas_call(grid_kernel, grid=(NPHI // rows,), in_specs=[pl.BlockSpec(...  11.6 us
    all_to_all x1, starting transfers between devices, body(): lax.all_to_all(coefs.reshape(128, 8, 768), ('shell', 'order'), 0, 0, tile...  8.19 us
    pallas_call x1, Pallas kernels, analysis_and_solve(): pl.pallas_call(solve_kernel, grid_spec=pltpu.PrefetchScalarGridSpec(num_s...  5.62 us
  transfers between devices with their start and end apart: 17, of which 3 were waited for; matrix products, arithmetic and copies ran while one was open for 7% of the time, Pallas kernels for 2%

profile of v2, /device:TPU:0, one launch (start us, length us, event | category | flops | bytes accessed | tf_op | source)
XLA Modules:
  0.0 178.6 jit_solution(11819458093862258472)
XLA Ops:
  0.6 0.8 dynamic_slice.3
  1.4 0.1 reshape.116
  1.5 0.1 slice_reduce_fusion.lower
  1.6 0.0 copy-start.1
  1.6 0.0 copy-start.4
  1.6 0.0 copy-start.5
  1.6 0.0 copy-start.6
  1.7 11.7 %copy.22.table = bf16[32,513,256]{2,1,0:T(8,128)(2,1)} copy(bf16[32,513,256]{2,0,1:T(8,128)(2,1)} %param.18) | data formatting | bytes 16809984 | tf_op args[6]
  13.3 15.1 %legendre_synthesis.1 = bf16[8,24,64,128]{3,2,1,0:T(8,128)(2,1)} custom-call(s32[32]{0:T(128)S(1)} %slice_reduce_fusion.lower, bf16[3,2,2,64,512]{4,3,2,1,0:T(8,128)(2,1)S(1)} %copy-done.1, bf16[3,2,2,64,512]{4,3,2,1,0:T(8,128)(2,1)S(1)} %copy-done.4, bf16[3,2,2,64,512]{4,3,2,1,0:T(8,128)(2,1)S(1)} %copy-done.5, bf16[3,2,2,64,512]{4,3,2,1,0:T(8,128)(2,1)S(1)} %copy-done.6, ...), custom_call_target="tpu_custom_call" | custom-call | flops 1600000000 | bytes 15728640 | tf_op jit(solution)/shard_map/legendre_synthesis/pallas_call | solution.py:83
  28.4 0.0 copy-start.35
  28.4 5.5 %all-to-all-start = ((bf16[8,24,64,128]{3,2,1,0:T(8,128)(2,1)}), bf16[8,24,64,128]{3,2,1,0:T(8,128)(2,1)}, u32[]{:S(2)}, u32[]{:S(2)}) async-start(bf16[8,24,64,128]{3,2,1,0:T(8,128)(2,1)} %legendre_synthesis.1), calls=%async_computation | async-start | bytes 6291456 | tf_op jit(solution)/shard_map/all_to_all | solution.py:423
  34.0 0.2 reduce-window.9
  34.2 0.2 compare_reduce_fusion
  34.4 1.1 state_to_send.1
  35.5 0.0 copy-start.8
  35.5 0.6 copy-done.8
  36.2 1.5 collective-permute-start
  37.7 2.7 %collective-permute-start.1 = (bf16[112,512]{1,0:T(8,128)(2,1)S(1)}, bf16[112,512]{1,0:T(8,128)(2,1)S(1)}, u32[]{:S(2)}, u32[]{:S(2)}) collective-permute-start(bf16[112,512]{1,0:T(8,128)(2,1)S(1)} %get-tuple-element.39), channel_id=1, source_target_pairs={{0,16},{8,24},{16,0},{24,8},{32,48},{40,56},{48,32},{56,40},{64,80... | collective-permute-start | bytes 344072 | tf_op jit(solution)/shard_map/ppermute | solution.py:430
  40.4 0.5 collective-permute-start.2
  40.9 1.6 collective-permute-start.3
  42.5 0.2 collective-permute-start.4
  42.6 0.1 mul.53
  42.8 0.2 iota_add_fusion
  43.0 0.2 add.89
  43.2 5.3 %fusion.4.ana = bf16[1024,1024]{1,0:T(8,128)(2,1)} fusion(bf16[1024,1024]{1,0:T(8,128)(2,1)} %constant.44.clone, s32[1024]{0:T(1024)S(1)} %add.89), kind=kOutput, calls=%fused_computation.7 | convolution fusion | flops 2149580800 | bytes 4198400 | tf_op jit(solution)/shard_map/dot_general | solution.py:392
  48.5 0.1 mul.52
  48.6 5.0 %collective-permute-start.5 = (bf16[112,512]{1,0:T(8,128)(2,1)S(1)}, bf16[112,512]{1,0:T(8,128)(2,1)S(1)}, u32[]{:S(2)}, u32[]{:S(2)}) collective-permute-start(bf16[112,512]{1,0:T(8,128)(2,1)S(1)} %get-tuple-element.43), channel_id=1, source_target_pairs={{0,48},{8,56},{16,32},{24,40},{32,16},{40,24},{48,0},{56,8},{64,11... | collective-permute-start | bytes 344072 | tf_op jit(solution)/shard_map/ppermute | solution.py:430
  53.6 0.1 add.85
  53.6 0.4 collective-permute-start.6
  54.0 3.2 %collective-permute-start.7 = (bf16[112,512]{1,0:T(8,128)(2,1)S(1)}, bf16[112,512]{1,0:T(8,128)(2,1)S(1)}, u32[]{:S(2)}, u32[]{:S(2)}) collective-permute-start(bf16[112,512]{1,0:T(8,128)(2,1)S(1)} %get-tuple-element.45), channel_id=1, source_target_pairs={{0,64},{8,72},{16,80},{24,88},{32,96},{40,104},{48,112},{56,120},{... | collective-permute-start | bytes 344072 | tf_op jit(solution)/shard_map/ppermute | solution.py:430
  57.3 6.6 %collective-permute-start.9 = (bf16[112,512]{1,0:T(8,128)(2,1)S(1)}, bf16[112,512]{1,0:T(8,128)(2,1)S(1)}, u32[]{:S(2)}, u32[]{:S(2)}) collective-permute-start(bf16[112,512]{1,0:T(8,128)(2,1)S(1)} %get-tuple-element.47), channel_id=1, source_target_pairs={{0,80},{8,88},{16,64},{24,72},{32,112},{40,120},{48,96},{56,104},{... | collective-permute-start | bytes 344072 | tf_op jit(solution)/shard_map/ppermute | solution.py:430
  63.9 0.3 collective-permute-start.10
  64.1 5.3 %convert_bitcast_fusion.syn = bf16[1024,1024]{1,0:T(8,128)(2,1)} fusion(bf16[1024,1024]{1,0:T(8,128)(2,1)} %constant.43.clone, s32[1024]{0:T(1024)S(1)} %add.85), kind=kOutput, calls=%fused_computation.5 | convolution fusion | flops 2149580800 | bytes 4198400 | tf_op jit(solution)/shard_map/dot_general | solution.py:388
  69.6 2.6 %collective-permute-done.10.refs_11_ = bf16[112,512]{1,0:T(8,128)(2,1)S(1)} collective-permute-done((bf16[112,512]{1,0:T(8,128)(2,1)S(1)}, bf16[112,512]{1,0:T(8,128)(2,1)S(1)}, u32[]{:S(2)}, u32[]{:S(2)}) %collective-permute-start.10) | collective-permute-done | bytes 114720 | tf_op jit(solution)/shard_map/ppermute | solution.py:430
  72.3 0.2 all-to-all-done.lat
  72.5 1.6 copy-done.33
  74.1 1.6 copy-done.34
  75.7 11.6 %grid_stage.1 = bf16[1024,768]{1,0:T(8,128)(2,1)} custom-call(bf16[8,24,64,128]{3,2,1,0:T(8,128)(2,1)} %all-to-all-done.lat, bf16[1024,1024]{1,0:T(8,128)(2,1)S(1)} %copy-done.34, bf16[1024,1024]{1,0:T(8,128)(2,1)S(1)} %copy-done.33, f32[1,128]{1,0:T(1,128)S(1)} %sine_multiply_fusion.weight), custom_call_target="tpu_custom_call" | custom-call | flops 4800000000 | bytes 9437184 | tf_op jit(solution)/shard_map/grid_stage/pallas_call | solution.py:184
  87.4 8.2 %all-to-all-start.1 = ((bf16[128,8,768]{2,1,0:T(8,128)(2,1)}), bf16[128,8,768]{2,1,0:T(8,128)(2,1)S(1)}, u32[]{:S(2)}, u32[]{:S(2)}) async-start(bf16[128,8,768]{2,1,0:T(8,128)(2,1)} %bitcast.5), calls=%async_computation.1 | async-start | bytes 3145728 | tf_op jit(solution)/shard_map/all_to_all | solution.py:436
  95.6 2.3 %collective-permute-start.11 = (bf16[112,512]{1,0:T(8,128)(2,1)S(1)}, bf16[112,512]{1,0:T(8,128)(2,1)S(1)}, u32[]{:S(2)}, u32[]{:S(2)}) collective-permute-start(bf16[112,512]{1,0:T(8,128)(2,1)S(1)} %get-tuple-element.63), channel_id=1, source_target_pairs={{0,96},{8,104},{16,112},{24,120},{32,64},{40,72},{48,80},{56,88},{... | collective-permute-start | bytes 344072 | tf_op jit(solution)/shard_map/ppermute | solution.py:430
  97.9 1.4 collective-permute-start.12
  99.3 4.9 %collective-permute-start.13 = (bf16[112,512]{1,0:T(8,128)(2,1)S(1)}, bf16[112,512]{1,0:T(8,128)(2,1)S(1)}, u32[]{:S(2)}, u32[]{:S(2)}) collective-permute-start(bf16[112,512]{1,0:T(8,128)(2,1)S(1)} %get-tuple-element.65), channel_id=1, source_target_pairs={{0,112},{8,120},{16,96},{24,104},{32,80},{40,88},{48,64},{56,72},{... | collective-permute-start | bytes 344072 | tf_op jit(solution)/shard_map/ppermute | solution.py:430
  104.2 1.0 collective-permute-start.14
  105.1 19.7 %collective-permute-done.11.refs_12_ = bf16[112,512]{1,0:T(8,128)(2,1)S(1)} collective-permute-done((bf16[112,512]{1,0:T(8,128)(2,1)S(1)}, bf16[112,512]{1,0:T(8,128)(2,1)S(1)}, u32[]{:S(2)}, u32[]{:S(2)}) %collective-permute-start.11) | collective-permute-done | bytes 114720 | tf_op jit(solution)/shard_map/ppermute | solution.py:430
  124.8 3.4 %copy-done = bf16[32,513,256]{2,1,0:T(8,128)(2,1)S(1)} copy-done((bf16[32,513,256]{2,1,0:T(8,128)(2,1)S(1)}, bf16[32,513,256]{2,1,0:T(8,128)(2,1)}, u32[]{:S(2)}) %copy-start) | copy-done | bytes 8405016
  128.2 0.9 copy-done.9
  129.1 0.9 copy-done.11
  130.0 0.9 copy-done.13
  130.9 0.9 copy-done.15
  131.8 0.9 copy-done.17
  132.7 0.9 copy-done.19
  133.6 0.9 copy-done.21
  134.5 0.9 copy-done.23
  135.4 0.9 copy-done.25
  136.3 0.9 copy-done.27
  137.2 0.9 copy-done.29
  138.1 0.9 copy-done.31
  139.0 1.6 prepare_solve.1
  140.6 0.0 copy-start.2
  140.7 1.0 copy-done.2
  141.6 1.2 copy-done.3
  142.8 5.6 %analysis_and_solve.1 = bf16[16,96,512]{2,1,0:T(8,128)(2,1)S(1)} custom-call(s32[1]{0:T(128)} %bitcast.place, s32[32]{0:T(128)S(1)} %slice_reduce_fusion.lower, bf16[1024,768]{1,0:T(8,128)(2,1)S(1)} %bitcast.11, bf16[16,96,512]{2,1,0:T(8,128)(2,1)S(1)} %get-tuple-element.67.state, bf16[4,256,512]{2,1,0:T(8,128)(2,1)S(1)} %copy-done.3, ...), custom_call_target="tpu_custom_call" | custom-call | flops 900000000 | bytes 6291456 | tf_op jit(solution)/shard_map/analysis_and_solve/pallas_call | solution.py:330
  148.5 27.3 %all_to_all.15.got = bf16[16,96,512]{2,1,0:T(8,128)(2,1)S(1)} all-to-all(bf16[16,96,512]{2,1,0:T(8,128)(2,1)S(1)} %analysis_and_solve.1), channel_id=1, replica_groups=mesh['shell'=16,'order'=8] {'shell'}, dimensions={0} | all-to-all | bytes 3145728 | tf_op jit(solution)/shard_map/all_to_all | solution.py:441
  175.8 2.8 %unpack_solution.1 = (f32[3,2,2,64,512]{4,3,2,1,0:T(8,128)}, f32[3,2,2,64,512]{4,3,2,1,0:T(8,128)}) custom-call(bf16[16,96,512]{2,1,0:T(8,128)(2,1)S(1)} %all_to_all.15.got), custom_call_target="tpu_custom_call" | custom-call | flops 1000000 | bytes 5242880 | tf_op jit(solution)/shard_map/unpack_solution/pallas_call | solution.py:369
  (73 shorter events, 0.2 us)
Async XLA Ops:
  1.6 11.7 %copy-start.1 = (bf16[3,2,2,64,512]{4,3,2,1,0:T(8,128)(2,1)S(1)}, bf16[3,2,2,64,512]{4,3,2,1,0:T(8,128)(2,1)}, u32[]{:S(2)}) copy-start(bf16[3,2,2,64,512]{4,3,2,1,0:T(8,128)(2,1)} %vel.2) | copy-start | bytes 2359300
  1.6 11.7 %copy-start.4 = (bf16[3,2,2,64,512]{4,3,2,1,0:T(8,128)(2,1)S(1)}, bf16[3,2,2,64,512]{4,3,2,1,0:T(8,128)(2,1)}, u32[]{:S(2)}) copy-start(bf16[3,2,2,64,512]{4,3,2,1,0:T(8,128)(2,1)} %vor.1) | copy-start | bytes 2359300
  1.6 11.7 %copy-start.5 = (bf16[3,2,2,64,512]{4,3,2,1,0:T(8,128)(2,1)S(1)}, bf16[3,2,2,64,512]{4,3,2,1,0:T(8,128)(2,1)}, u32[]{:S(2)}) copy-start(bf16[3,2,2,64,512]{4,3,2,1,0:T(8,128)(2,1)} %mag.1) | copy-start | bytes 2359300
  1.6 11.7 %copy-start.6 = (bf16[3,2,2,64,512]{4,3,2,1,0:T(8,128)(2,1)S(1)}, bf16[3,2,2,64,512]{4,3,2,1,0:T(8,128)(2,1)}, u32[]{:S(2)}) copy-start(bf16[3,2,2,64,512]{4,3,2,1,0:T(8,128)(2,1)} %cur.1) | copy-start | bytes 2359300
  28.4 5.6 %copy-start.37 = (s32[4]{0:T(128)S(1)}, s32[4]{0:T(128)}, u32[]{:S(2)}) copy-start(s32[4]{0:T(128)} %param.19) | copy-start | bytes 52
  28.4 5.9 %copy-start.36 = (f32[2,2]{1,0:T(2,128)S(1)}, f32[2,2]{1,0:T(2,128)}, u32[]{:S(2)}) copy-start(f32[2,2]{1,0:T(2,128)} %param.20) | copy-start | bytes 52
  28.4 6.0 %copy-start.7 = (bf16[3,2,2,64,512]{4,3,2,1,0:T(8,128)(2,1)S(1)}, bf16[3,2,2,64,512]{4,3,2,1,0:T(8,128)(2,1)}, u32[]{:S(2)}) copy-start(bf16[3,2,2,64,512]{4,3,2,1,0:T(8,128)(2,1)} %pot) | copy-start | bytes 2359300
  28.4 6.0 %copy-start.32 = (f32[2,2]{1,0:T(2,128)S(1)}, f32[2,2]{1,0:T(2,128)}, u32[]{:S(2)}) copy-start(f32[2,2]{1,0:T(2,128)} %angular.1) | copy-start | bytes 52
  28.4 14.2 %copy-start.35 = (s32[512]{0:T(512)S(1)}, s32[512]{0:T(512)}, u32[]{:S(2)}) copy-start(s32[512]{0:T(512)} %param.17) | copy-start | bytes 6148
  28.4 44.1 %all-to-all-start = ((bf16[8,24,64,128]{3,2,1,0:T(8,128)(2,1)}), bf16[8,24,64,128]{3,2,1,0:T(8,128)(2,1)}, u32[]{:S(2)}, u32[]{:S(2)}) async-start(bf16[8,24,64,128]{3,2,1,0:T(8,128)(2,1)} %legendre_synthesis.1), calls=%async_computation | async-start | bytes 6291456 | tf_op jit(solution)/shard_map/all_to_all | solution.py:423
  35.5 0.6 copy-start.8
  36.2 12.4 %collective-permute-start = (bf16[112,512]{1,0:T(8,128)(2,1)S(1)}, bf16[112,512]{1,0:T(8,128)(2,1)S(1)}, u32[]{:S(2)}, u32[]{:S(2)}) collective-permute-start(bf16[112,512]{1,0:T(8,128)(2,1)S(1)} %get-tuple-element.38), channel_id=1, source_target_pairs={{0,8},{8,0},{16,24},{24,16},{32,40},{40,32},{48,56},{56,48},{64,72... | collective-permute-start | bytes 344072 | tf_op jit(solution)/shard_map/ppermute | solution.py:430
  37.7 16.0 %collective-permute-start.1 = (bf16[112,512]{1,0:T(8,128)(2,1)S(1)}, bf16[112,512]{1,0:T(8,128)(2,1)S(1)}, u32[]{:S(2)}, u32[]{:S(2)}) collective-permute-start(bf16[112,512]{1,0:T(8,128)(2,1)S(1)} %get-tuple-element.39), channel_id=1, source_target_pairs={{0,16},{8,24},{16,0},{24,8},{32,48},{40,56},{48,32},{56,40},{64,80... | collective-permute-start | bytes 344072 | tf_op jit(solution)/shard_map/ppermute | solution.py:430
  40.4 13.6 %collective-permute-start.2 = (bf16[112,512]{1,0:T(8,128)(2,1)S(1)}, bf16[112,512]{1,0:T(8,128)(2,1)S(1)}, u32[]{:S(2)}, u32[]{:S(2)}) collective-permute-start(bf16[112,512]{1,0:T(8,128)(2,1)S(1)} %get-tuple-element.40), channel_id=1, source_target_pairs={{0,24},{8,16},{16,8},{24,0},{32,56},{40,48},{48,40},{56,32},{64,88... | collective-permute-start | bytes 344072 | tf_op jit(solution)/shard_map/ppermute | solution.py:430
  40.9 16.4 %collective-permute-start.3 = (bf16[112,512]{1,0:T(8,128)(2,1)S(1)}, bf16[112,512]{1,0:T(8,128)(2,1)S(1)}, u32[]{:S(2)}, u32[]{:S(2)}) collective-permute-start(bf16[112,512]{1,0:T(8,128)(2,1)S(1)} %get-tuple-element.41), channel_id=1, source_target_pairs={{0,32},{8,40},{16,48},{24,56},{32,0},{40,8},{48,16},{56,24},{64,96... | collective-permute-start | bytes 344072 | tf_op jit(solution)/shard_map/ppermute | solution.py:430
  42.5 14.8 %collective-permute-start.4 = (bf16[112,512]{1,0:T(8,128)(2,1)S(1)}, bf16[112,512]{1,0:T(8,128)(2,1)S(1)}, u32[]{:S(2)}, u32[]{:S(2)}) collective-permute-start(bf16[112,512]{1,0:T(8,128)(2,1)S(1)} %get-tuple-element.42), channel_id=1, source_target_pairs={{0,40},{8,32},{16,56},{24,48},{32,8},{40,0},{48,24},{56,16},{64,10... | collective-permute-start | bytes 344072 | tf_op jit(solution)/shard_map/ppermute | solution.py:430
  48.6 20.9 %copy-start.10 = (bf16[112,512]{1,0:T(8,128)(2,1)}, bf16[112,512]{1,0:T(8,128)(2,1)S(1)}, u32[]{:S(2)}) copy-start(bf16[112,512]{1,0:T(8,128)(2,1)S(1)} %collective-permute-done.refs_1_) | copy-start | bytes 344068
  48.6 15.3 %collective-permute-start.5 = (bf16[112,512]{1,0:T(8,128)(2,1)S(1)}, bf16[112,512]{1,0:T(8,128)(2,1)S(1)}, u32[]{:S(2)}, u32[]{:S(2)}) collective-permute-start(bf16[112,512]{1,0:T(8,128)(2,1)S(1)} %get-tuple-element.43), channel_id=1, source_target_pairs={{0,48},{8,56},{16,32},{24,40},{32,16},{40,24},{48,0},{56,8},{64,11... | collective-permute-start | bytes 344072 | tf_op jit(solution)/shard_map/ppermute | solution.py:430
  53.6 15.8 %copy-start.12 = (bf16[112,512]{1,0:T(8,128)(2,1)}, bf16[112,512]{1,0:T(8,128)(2,1)S(1)}, u32[]{:S(2)}) copy-start(bf16[112,512]{1,0:T(8,128)(2,1)S(1)} %collective-permute-done.1.refs_2_) | copy-start | bytes 344068
  53.6 15.9 %collective-permute-start.6 = (bf16[112,512]{1,0:T(8,128)(2,1)S(1)}, bf16[112,512]{1,0:T(8,128)(2,1)S(1)}, u32[]{:S(2)}, u32[]{:S(2)}) collective-permute-start(bf16[112,512]{1,0:T(8,128)(2,1)S(1)} %get-tuple-element.44), channel_id=1, source_target_pairs={{0,56},{8,48},{16,40},{24,32},{32,24},{40,16},{48,8},{56,0},{64,12... | collective-permute-start | bytes 344072 | tf_op jit(solution)/shard_map/ppermute | solution.py:430
  54.0 15.4 %copy-start.14 = (bf16[112,512]{1,0:T(8,128)(2,1)}, bf16[112,512]{1,0:T(8,128)(2,1)S(1)}, u32[]{:S(2)}) copy-start(bf16[112,512]{1,0:T(8,128)(2,1)S(1)} %collective-permute-done.2.refs_3_) | copy-start | bytes 344068
  54.0 15.5 %collective-permute-start.7 = (bf16[112,512]{1,0:T(8,128)(2,1)S(1)}, bf16[112,512]{1,0:T(8,128)(2,1)S(1)}, u32[]{:S(2)}, u32[]{:S(2)}) collective-permute-start(bf16[112,512]{1,0:T(8,128)(2,1)S(1)} %get-tuple-element.45), channel_id=1, source_target_pairs={{0,64},{8,72},{16,80},{24,88},{32,96},{40,104},{48,112},{56,120},{... | collective-permute-start | bytes 344072 | tf_op jit(solution)/shard_map/ppermute | solution.py:430
  57.2 12.2 %copy-start.16 = (bf16[112,512]{1,0:T(8,128)(2,1)}, bf16[112,512]{1,0:T(8,128)(2,1)S(1)}, u32[]{:S(2)}) copy-start(bf16[112,512]{1,0:T(8,128)(2,1)S(1)} %collective-permute-done.3.refs_4_) | copy-start | bytes 344068
  57.2 12.4 %collective-permute-start.8 = (bf16[112,512]{1,0:T(8,128)(2,1)S(1)}, bf16[112,512]{1,0:T(8,128)(2,1)S(1)}, u32[]{:S(2)}, u32[]{:S(2)}) collective-permute-start(bf16[112,512]{1,0:T(8,128)(2,1)S(1)} %get-tuple-element.46), channel_id=1, source_target_pairs={{0,72},{8,64},{16,88},{24,80},{32,104},{40,96},{48,120},{56,112},{... | collective-permute-start | bytes 344072 | tf_op jit(solution)/shard_map/ppermute | solution.py:430
  57.3 12.2 %copy-start.18 = (bf16[112,512]{1,0:T(8,128)(2,1)}, bf16[112,512]{1,0:T(8,128)(2,1)S(1)}, u32[]{:S(2)}) copy-start(bf16[112,512]{1,0:T(8,128)(2,1)S(1)} %collective-permute-done.4.refs_5_) | copy-start | bytes 344068
  57.3 12.4 %collective-permute-start.9 = (bf16[112,512]{1,0:T(8,128)(2,1)S(1)}, bf16[112,512]{1,0:T(8,128)(2,1)S(1)}, u32[]{:S(2)}, u32[]{:S(2)}) collective-permute-start(bf16[112,512]{1,0:T(8,128)(2,1)S(1)} %get-tuple-element.47), channel_id=1, source_target_pairs={{0,80},{8,88},{16,64},{24,72},{32,112},{40,120},{48,96},{56,104},{... | collective-permute-start | bytes 344072 | tf_op jit(solution)/shard_map/ppermute | solution.py:430
  63.9 5.6 %copy-start.20 = (bf16[112,512]{1,0:T(8,128)(2,1)}, bf16[112,512]{1,0:T(8,128)(2,1)S(1)}, u32[]{:S(2)}) copy-start(bf16[112,512]{1,0:T(8,128)(2,1)S(1)} %collective-permute-done.5.refs_6_) | copy-start | bytes 344068
  63.9 8.4 %collective-permute-start.10 = (bf16[112,512]{1,0:T(8,128)(2,1)S(1)}, bf16[112,512]{1,0:T(8,128)(2,1)S(1)}, u32[]{:S(2)}, u32[]{:S(2)}) collective-permute-start(bf16[112,512]{1,0:T(8,128)(2,1)S(1)} %get-tuple-element.48), channel_id=1, source_target_pairs={{0,88},{8,80},{16,72},{24,64},{32,120},{40,112},{48,104},{56,96},{... | collective-permute-start | bytes 344072 | tf_op jit(solution)/shard_map/ppermute | solution.py:430
  69.6 17.8 %copy-start.22 = (bf16[112,512]{1,0:T(8,128)(2,1)}, bf16[112,512]{1,0:T(8,128)(2,1)S(1)}, u32[]{:S(2)}) copy-start(bf16[112,512]{1,0:T(8,128)(2,1)S(1)} %collective-permute-done.6.refs_7_) | copy-start | bytes 344068
  69.6 17.7 %copy-start.24 = (bf16[112,512]{1,0:T(8,128)(2,1)}, bf16[112,512]{1,0:T(8,128)(2,1)S(1)}, u32[]{:S(2)}) copy-start(bf16[112,512]{1,0:T(8,128)(2,1)S(1)} %collective-permute-done.7.refs_8_) | copy-start | bytes 344068
  69.6 17.7 %copy-start.26 = (bf16[112,512]{1,0:T(8,128)(2,1)}, bf16[112,512]{1,0:T(8,128)(2,1)S(1)}, u32[]{:S(2)}) copy-start(bf16[112,512]{1,0:T(8,128)(2,1)S(1)} %collective-permute-done.8.refs_9_) | copy-start | bytes 344068
  69.6 17.7 %copy-start.28 = (bf16[112,512]{1,0:T(8,128)(2,1)}, bf16[112,512]{1,0:T(8,128)(2,1)S(1)}, u32[]{:S(2)}) copy-start(bf16[112,512]{1,0:T(8,128)(2,1)S(1)} %collective-permute-done.9.refs_10_) | copy-start | bytes 344068
  72.3 15.1 %copy-start.30 = (bf16[112,512]{1,0:T(8,128)(2,1)}, bf16[112,512]{1,0:T(8,128)(2,1)S(1)}, u32[]{:S(2)}) copy-start(bf16[112,512]{1,0:T(8,128)(2,1)S(1)} %collective-permute-done.10.refs_11_) | copy-start | bytes 344068
  72.5 1.6 copy-start.33
  74.1 1.6 copy-start.34
  87.4 54.3 %all-to-all-start.1 = ((bf16[128,8,768]{2,1,0:T(8,128)(2,1)}), bf16[128,8,768]{2,1,0:T(8,128)(2,1)S(1)}, u32[]{:S(2)}, u32[]{:S(2)}) async-start(bf16[128,8,768]{2,1,0:T(8,128)(2,1)} %bitcast.5), calls=%async_computation.1 | async-start | bytes 3145728 | tf_op jit(solution)/shard_map/all_to_all | solution.py:436
  95.6 29.2 %collective-permute-start.11 = (bf16[112,512]{1,0:T(8,128)(2,1)S(1)}, bf16[112,512]{1,0:T(8,128)(2,1)S(1)}, u32[]{:S(2)}, u32[]{:S(2)}) collective-permute-start(bf16[112,512]{1,0:T(8,128)(2,1)S(1)} %get-tuple-element.63), channel_id=1, source_target_pairs={{0,96},{8,104},{16,112},{24,120},{32,64},{40,72},{48,80},{56,88},{... | collective-permute-start | bytes 344072 | tf_op jit(solution)/shard_map/ppermute | solution.py:430
  97.9 26.9 %collective-permute-start.12 = (bf16[112,512]{1,0:T(8,128)(2,1)S(1)}, bf16[112,512]{1,0:T(8,128)(2,1)S(1)}, u32[]{:S(2)}, u32[]{:S(2)}) collective-permute-start(bf16[112,512]{1,0:T(8,128)(2,1)S(1)} %get-tuple-element.64), channel_id=1, source_target_pairs={{0,104},{8,96},{16,120},{24,112},{32,72},{40,64},{48,88},{56,80},{... | collective-permute-start | bytes 344072 | tf_op jit(solution)/shard_map/ppermute | solution.py:430
  99.3 25.5 %collective-permute-start.13 = (bf16[112,512]{1,0:T(8,128)(2,1)S(1)}, bf16[112,512]{1,0:T(8,128)(2,1)S(1)}, u32[]{:S(2)}, u32[]{:S(2)}) collective-permute-start(bf16[112,512]{1,0:T(8,128)(2,1)S(1)} %get-tuple-element.65), channel_id=1, source_target_pairs={{0,112},{8,120},{16,96},{24,104},{32,80},{40,88},{48,64},{56,72},{... | collective-permute-start | bytes 344072 | tf_op jit(solution)/shard_map/ppermute | solution.py:430
  104.2 20.7 %collective-permute-start.14 = (bf16[112,512]{1,0:T(8,128)(2,1)S(1)}, bf16[112,512]{1,0:T(8,128)(2,1)S(1)}, u32[]{:S(2)}, u32[]{:S(2)}) collective-permute-start(bf16[112,512]{1,0:T(8,128)(2,1)S(1)} %get-tuple-element.66), channel_id=1, source_target_pairs={{0,120},{8,112},{16,104},{24,96},{32,88},{40,80},{48,72},{56,64},{... | collective-permute-start | bytes 344072 | tf_op jit(solution)/shard_map/ppermute | solution.py:430
  124.8 3.4 %copy-start = (bf16[32,513,256]{2,1,0:T(8,128)(2,1)S(1)}, bf16[32,513,256]{2,1,0:T(8,128)(2,1)}, u32[]{:S(2)}) copy-start(bf16[32,513,256]{2,1,0:T(8,128)(2,1)} %copy.22.table) | copy-start | bytes 25214980
  128.2 0.9 copy-start.9
  129.1 0.9 copy-start.11
  130.0 0.9 copy-start.13
  130.9 0.9 copy-start.15
  131.8 0.9 copy-start.17
  132.7 0.9 copy-start.19
  133.6 0.9 copy-start.21
  134.5 0.9 copy-start.23
  135.4 0.9 copy-start.25
  136.3 0.9 copy-start.27
  137.2 0.9 copy-start.29
  138.1 0.9 copy-start.31
  140.6 1.0 copy-start.2
  141.6 1.2 copy-start.3

commit v3 on v2

--- a/solution.py
+++ b/solution.py
@@ -36,21 +36,39 @@
         ref[q, rows, :] = value[:, q * 128 : q * 128 + 128]
 
 
-def synthesis_kernel(lower, vel, vor, mag, cur, table, out, xs, ys):
+PITCH = 33
+TABLE_PITCH = 17
+CHUNK = 171
+
+
+def synthesis_kernel(place, lower, vel, vor, mag, cur, table, out, pairs, xs, ys, ts):
     step = pl.program_id(0)
-    for a, ref in enumerate((vel, vor, mag, cur)):
-        for c in range(3):
-            for s in range(2):
-                for p in range(2):
-                    row = (s * 24 + (a * 3 + c) * 2 + p) * 16
-                    store(xs, pl.ds(row, 16), ref[c, s, p].astype(f32))
+    chunk = pl.program_id(1)
+
+    @pl.when(chunk == 0)
+    def _():
+        for a, ref in enumerate((vel, vor, mag, cur)):
+            for c in range(3):
+                for s in range(2):
+                    for p in range(2):
+                        row = (s * 24 + (a * 3 + c) * 2 + p) * PITCH
+                        store(xs, pl.ds(row, 32), ref[c, s, p].astype(f32))
+
+    for q in range(3):
+
+        @pl.when(chunk == q)
+        def _():
+            for d in range(CHUNK):
+                store(ts, pl.ds((q * CHUNK + d) * TABLE_PITCH, 16), table[d].astype(f32))
+
     r = lax.broadcasted_iota(jnp.int32, (1, L), 1)
     sign_a = (1 - 2 * (r & 1)).astype(f32)
 
     def one_pair(i, _):
-        m = lower[step * 8 + i]
-        a = load(xs, pl.ds(2 * i, 48, stride=16))
-        b = load(xs, pl.ds(2 * i + 1, 48, stride=16))
+        m = lower[step * 16 + i]
+        a = load(xs, pl.ds(2 * i, 48, stride=PITCH))
+        b = load(xs, pl.ds(2 * i + 1, 48, stride=PITCH))
+        rows = load(ts, pl.ds(i, L, stride=TABLE_PITCH)).astype(bf16)
         a = pltpu.roll(a, (L - m) & (L - 1), 1)
         b_last = b[:, L - 1 : L]
         b = pltpu.roll(b, 1, 1)
@@ -59,41 +77,63 @@
         a = jnp.where(is_a, a, 0.0)
         b = jnp.where(is_a, 0.0, b)
         lhs = jnp.concatenate([a, a * sign_a, b, b * sign_b], axis=0).astype(bf16)
-        res = jnp.dot(lhs, table[i, 0:L, :], preferred_element_type=f32)
-        last = b_last * table[i, L : L + 1, :].astype(f32)
+        res = jnp.dot(lhs, rows, preferred_element_type=f32)
+        last = b_last * load(ts, pl.ds(L * TABLE_PITCH + i, 1))
         last_sign = (1 - 2 * (m & 1)).astype(f32)
         b_n = res[96:144] + last
         b_s = res[144:192] + last * last_sign
         for k, parts in ((2 * i, (res[0:48], res[48:96])), (2 * i + 1, (b_n, b_s))):
             for h in range(2):
                 for s in range(2):
-                    rows = pl.ds((s * 2 + h) * 384 + k, 24, stride=16)
-                    store(ys, rows, parts[h][s * 24 : s * 24 + 24])
+                    at = pl.ds((s * 2 + h) * 24 * PITCH + k, 24, stride=PITCH)
+                    store(ys, at, parts[h][s * 24 : s * 24 + 24])
         return 0
 
-    lax.fori_loop(0, 8, one_pair, 0)
-    for sh in range(4):
-        for jh in range(2):
-            piece = ys[jh, sh * 384 : sh * 384 + 384, :]
-            out[sh * 2 + jh] = piece.reshape(24, 16, 128).astype(bf16)
-
-
-def legendre_synthesis(lower, velocity, vorticity, magnetic, current, table):
-    field = pl.BlockSpec((3, 2, 2, 16, L), lambda g, low: (0, 0, 0, g, 0))
+    @pl.when(chunk == 2)
+    def _():
+        lax.fori_loop(0, 16, one_pair, 0, unroll=8)
+        for sh in range(4):
+            for jh in range(2):
+                for cp in range(24):
+                    row = (sh * 24 + cp) * PITCH
+                    out[sh * 2 + jh, cp] = ys[jh, row : row + 32, :].astype(bf16)
+
+    @pl.when((chunk == 2) & (step == place[0] // 8))
+    def _():
+        for i in range(2):
+            at = (place[0] & 7) * 2 + i
+            pairs[i, 0:L, :] = load(ts, pl.ds(at, L, stride=TABLE_PITCH)).astype(bf16)
+            last = load(ts, pl.ds(L * TABLE_PITCH + at, 1))
+            pairs[i, L : L + 16, :] = jnp.broadcast_to(last, (16, NH)).astype(bf16)
+
+
+def legendre_synthesis(place, lower, velocity, vorticity, magnetic, current, table):
+    field = pl.BlockSpec((3, 2, 2, 32, L), lambda g, q, place, low: (0, 0, 0, g, 0))
     return pl.pallas_call(
         synthesis_kernel,
         grid_spec=pltpu.PrefetchScalarGridSpec(
-            num_scalar_prefetch=1,
-            grid=(4,),
-            in_specs=[field] * 4 + [pl.BlockSpec((8, L + 1, NH), lambda g, low: (g, 0, 0))],
-            out_specs=pl.BlockSpec((8, 24, 16, 128), lambda g, low: (0, 0, g, 0)),
-            scratch_shapes=[pltpu.VMEM((4, 768, 128), f32), pltpu.VMEM((2, 1536, 128), f32)],
+            num_scalar_prefetch=2,
+            grid=(2, 3),
+            in_specs=[field] * 4
+            + [pl.BlockSpec((CHUNK, 16, NH), lambda g, q, place, low: (q, g, 0))],
+            out_specs=[
+                pl.BlockSpec((8, 24, 32, 128), lambda g, q, place, low: (0, 0, g, 0)),
+                pl.BlockSpec((2, L + 16, NH), lambda g, q, place, low: (0, 0, 0)),
+            ],
+            scratch_shapes=[
+                pltpu.VMEM((4, 48 * PITCH, 128), f32),
+                pltpu.VMEM((2, 96 * PITCH, 128), f32),
+                pltpu.VMEM((2, (L + 1) * TABLE_PITCH + 7, 128), f32),
+            ],
         ),
-        out_shape=jax.ShapeDtypeStruct((8, 24, 64, 128), bf16),
-        compiler_params=pltpu.CompilerParams(vmem_limit_bytes=40 * MIB),
+        out_shape=[
+            jax.ShapeDtypeStruct((8, 24, 64, 128), bf16),
+            jax.ShapeDtypeStruct((2, L + 16, NH), bf16),
+        ],
+        compiler_params=pltpu.CompilerParams(vmem_limit_bytes=52 * MIB),
         cost_estimate=pl.CostEstimate(flops=int(1.6e9), bytes_accessed=15 * MIB, transcendentals=0),
         name="legendre_synthesis",
-    )(lower, velocity, vorticity, magnetic, current, table)
+    )(place, lower, velocity, vorticity, magnetic, current, table)
 
 
 def state_kernel(place, kappa, angular, vel, pot, *refs):
@@ -139,65 +179,57 @@
     )(place, kappa, angular, velocity, potential)
 
 
-def grid_kernel(lat, syn, ana, weight, out, wide, prod, acc):
+def grid_kernel(lat, syn, ana, weight, out, wide, prod):
     step = pl.program_id(0)
+    rows = 512
 
     @pl.when(step == 0)
     def _():
         for c in range(12):
             wide[:, c * 128 : c * 128 + 128] = lat[:, 2 * c : 2 * c + 2].reshape(1024, 128)
 
-    g = jnp.dot(syn[...], wide[...], preferred_element_type=f32)
-    x = [g[:, c * 128 : c * 128 + 128] for c in range(12)]
-    u, w, b, j = x[0:3], x[3:6], x[6:9], x[9:12]
-
-    def cross(p, q):
-        return [
-            p[1] * q[2] - p[2] * q[1],
-            p[2] * q[0] - p[0] * q[2],
-            p[0] * q[1] - p[1] * q[0],
-        ]
-
-    uw, jb, ub = cross(u, w), cross(j, b), cross(u, b)
-    terms = [uw[0] + jb[0] + 2.0 * u[1], uw[1] + jb[1] - 2.0 * u[0], uw[2] + jb[2]] + ub
-    for c in range(6):
-        prod[:, c * 128 : c * 128 + 128] = terms[c].astype(bf16)
-    part = jnp.dot(ana[...], prod[...], preferred_element_type=f32)
-
-    @pl.when(step == 0)
-    def _():
-        acc[...] = part
-
-    @pl.when(step > 0)
-    def _():
-        acc[...] += part
-
-    @pl.when(step == pl.num_programs(0) - 1)
-    def _():
-        wt = weight[...]
+    @pl.when(step < 2)
+    def _():
+        g = jnp.dot(syn[...], wide[...], preferred_element_type=f32)
+        x = [g[:, c * 128 : c * 128 + 128] for c in range(12)]
+        u, w, b, j = x[0:3], x[3:6], x[6:9], x[9:12]
+
+        def cross(p, q):
+            return [
+                p[1] * q[2] - p[2] * q[1],
+                p[2] * q[0] - p[0] * q[2],
+                p[0] * q[1] - p[1] * q[0],
+            ]
+
+        uw, jb, ub = cross(u, w), cross(j, b), cross(u, b)
+        terms = [uw[0] + jb[0] + 2.0 * u[1], uw[1] + jb[1] - 2.0 * u[0], uw[2] + jb[2]] + ub
+        at = pl.ds(pl.multiple_of(step * rows, rows), rows)
         for c in range(6):
-            out[:, c * 128 : c * 128 + 128] = (acc[:, c * 128 : c * 128 + 128] * wt).astype(bf16)
+            prod[at, c * 128 : c * 128 + 128] = terms[c].astype(bf16)
+
+    @pl.when(step >= 2)
+    def _():
+        sums = jnp.dot(ana[...], prod[...], preferred_element_type=f32)
+        for c in range(6):
+            part = sums[:, c * 128 : c * 128 + 128] * weight[...]
+            out[:, c * 128 : c * 128 + 128] = part.astype(bf16)
 
 
 def grid_stage(lat, syn, ana, weight):
-    rows = 256
+    rows = 512
     return pl.pallas_call(
         grid_kernel,
-        grid=(NPHI // rows,),
+        grid=(4,),
         in_specs=[
             pl.BlockSpec((8, 24, 64, 128), lambda i: (0, 0, 0, 0)),
-            pl.BlockSpec((rows, 1024), lambda i: (i, 0)),
-            pl.BlockSpec((1024, rows), lambda i: (0, i)),
+            pl.BlockSpec((rows, 1024), lambda i: (jnp.minimum(i, 1), 0)),
+            pl.BlockSpec((rows, 1024), lambda i: (jnp.maximum(i - 2, 0), 0)),
             pl.BlockSpec((1, 128), lambda i: (0, 0)),
         ],
-        out_specs=pl.BlockSpec((1024, 768), lambda i: (0, 0)),
+        out_specs=pl.BlockSpec((rows, 768), lambda i: (jnp.maximum(i - 2, 0), 0)),
         out_shape=jax.ShapeDtypeStruct((1024, 768), bf16),
-        scratch_shapes=[
-            pltpu.VMEM((1024, 1536), bf16),
-            pltpu.VMEM((rows, 768), bf16),
-            pltpu.VMEM((1024, 768), f32),
-        ],
-        compiler_params=pltpu.CompilerParams(vmem_limit_bytes=48 * MIB),
+        scratch_shapes=[pltpu.VMEM((1024, 1536), bf16), pltpu.VMEM((1024, 768), bf16)],
+        compiler_params=pltpu.CompilerParams(vmem_limit_bytes=32 * MIB),
         cost_estimate=pl.CostEstimate(flops=int(4.8e9), bytes_accessed=9 * MIB, transcendentals=0),
         name="grid_stage",
     )(lat, syn, ana, weight)
@@ -249,7 +281,7 @@
             num_scalar_prefetch=2,
             grid=(1,),
             in_specs=[
-                pl.BlockSpec((2, L + 1, NH), lambda g, place, low: (place[0], 0, 0)),
+                pl.BlockSpec((2, L + 16, NH), lambda g, place, low: (0, 0, 0)),
             ]
             + [pl.BlockSpec((112, L), lambda g, place, low: (0, 0))] * 16,
             out_specs=[
@@ -257,14 +289,14 @@
                 pl.BlockSpec((4, NH, L), lambda g, place, low: (0, 0, 0)),
                 pl.BlockSpec((3, 64, L), lambda g, place, low: (0, 0, 0)),
             ],
-            scratch_shapes=[pltpu.VMEM((L + 1, NH), f32), pltpu.VMEM((16, 16, L), f32)],
+            scratch_shapes=[pltpu.VMEM((L + 16, NH), f32), pltpu.VMEM((16, 16, L), f32)],
         ),
         out_shape=[
             jax.ShapeDtypeStruct((16, 96, L), bf16),
             jax.ShapeDtypeStruct((4, NH, L), bf16),
             jax.ShapeDtypeStruct((3, 64, L), f32),
         ],
-        compiler_params=pltpu.CompilerParams(vmem_limit_bytes=24 * MIB),
+        compiler_params=pltpu.CompilerParams(vmem_limit_bytes=60 * MIB),
         cost_estimate=pl.CostEstimate(flops=10**7, bytes_accessed=3 * MIB, transcendentals=0),
         name="prepare_solve",
     )(place, lower, table, *parts)
@@ -346,7 +378,7 @@
             ],
         ),
         out_shape=jax.ShapeDtypeStruct((16, 96, L), bf16),
-        compiler_params=pltpu.CompilerParams(vmem_limit_bytes=48 * MIB),
+        compiler_params=pltpu.CompilerParams(vmem_limit_bytes=32 * MIB),
         cost_estimate=pl.CostEstimate(flops=int(0.9e9), bytes_accessed=6 * MIB, transcendentals=0),
         name="analysis_and_solve",
     )(place, lower, coef, state, table, factors)
@@ -417,8 +449,14 @@
     colatitude = math.pi * (rows.astype(f32) + 0.5) / NLAT
     weight = (math.sqrt(2.0 * math.pi) * L * math.pi / NLAT * jnp.sin(colatitude))[None, :]
 
-    latitude = legendre_synthesis(
-        lower, velocity, vorticity, magnetic, current, legendre_values
+    latitude, pairs = legendre_synthesis(
+        place,
+        lower,
+        velocity,
+        vorticity,
+        magnetic,
+        current,
+        jnp.transpose(legendre_values, (1, 0, 2)),
     )
     incoming = lax.all_to_all(latitude, "order", 0, 0, tiled=True)
 
@@ -430,13 +468,13 @@
         lax.ppermute(parts[r], "shell", [(i, i ^ r) for i in range(16)]) for r in range(1, 16)
     ]
     syn, ana = fourier_tables(order_after)
-    early = 12
-    incoming, parts[1:early] = lax.optimization_barrier((incoming, parts[1:early]))
+    state, table, factors = prepare_solve(place, lower, pairs, parts)
+    incoming, state, table, factors = lax.optimization_barrier((incoming, state, table, factors))
+
     coefs = grid_stage(incoming, syn, ana, weight)
     coefs = lax.all_to_all(
         coefs.reshape(128, 8, 768), ("shell", "order"), 0, 0, tiled=True
     ).reshape(1024, 768)
-    state, table, factors = prepare_solve(place, lower, legendre_values, parts)
     solved = analysis_and_solve(place, lower, coefs, state, table, factors)
     solved = lax.all_to_all(solved, "shell", 0, 0, tiled=True)
     return tuple(unpack_solution(solved))

time: 180 us -> 154 us (0.86)
  blocking collectives: 27.3 us -> 58.2 us
  local copies, waits for them, and re-layouts: 33.4 us -> 7.08 us
  waiting for transfers between devices: 22.6 us -> 0.04 us
  starting transfers between devices: 45.2 us -> 40.2 us
  Pallas kernels: 37.9 us -> 35.2 us
    all_to_all x0 -> x1, blocking collectives: none -> 32.7 us  [body(): lax.all_to_all(coefs.reshape(128, 8, 768), ('shell', 'order'), 0, 0, tile...]
    unnamed x77 -> x60, local copies, waits for them, and re-layouts: 31.9 us -> 5.59 us
    ppermute x15, waiting for transfers between devices: 22.4 us -> 0.04 us  [body(): lax.ppermute(parts[r], 'shell', [(i, i ^ r) for i in range(16)])]
    all_to_all x1 -> x0, starting transfers between devices: 8.19 us -> none  [body(): lax.all_to_all(coefs.reshape(128, 8, 768), ('shell', 'order'), 0, 0, tile...]
    ppermute x15, starting transfers between devices: 31.4 us -> 34.7 us  [body(): lax.ppermute(parts[r], 'shell', [(i, i ^ r) for i in range(16)])]
    pallas_call x1, Pallas kernels: 11.6 us -> 8.36 us  [grid_stage(): pl.pallas_call(grid_kernel, grid=(4,), in_specs=[pl.BlockSpec((8, 24, 64,...]
    pallas_call x1, Pallas kernels: 1.6 us -> 4.82 us  [prepare_solve(): pl.pallas_call(prepare_kernel, grid_spec=pltpu.PrefetchScalarGridSpec(num...]
    pallas_call x1, Pallas kernels: 15.1 us -> 12.4 us  [legendre_synthesis(): pl.pallas_call(synthesis_kernel, grid_spec=pltpu.PrefetchScalarGridSpec(n...]
  transfers between devices with their start and end apart: 17 -> 16, of which waited for: 3 -> 0; matrix products, arithmetic and copies ran while one was open for 7% -> 8% of each run, Pallas kernels for 2% -> 4%
where the time goes in v3:
time: 154 us; the launch traced here: 153 us
  blocking collectives  58.2 us (38%)
  starting transfers between devices  40.2 us (26%)
  Pallas kernels  35.2 us (23%)
  matrix products  10.8 us (7%)
  local copies, waits for them, and re-layouts  7.08 us (5%)
    ppermute x15, starting transfers between devices, body(): lax.ppermute(parts[r], 'shell', [(i, i ^ r) for i in range(16)])  34.7 us
    all_to_all x1, blocking collectives, body(): lax.all_to_all(coefs.reshape(128, 8, 768), ('shell', 'order'), 0, 0, tile...  32.7 us
    all_to_all x1, blocking collectives, body(): solved = lax.all_to_all(solved, 'shell', 0, 0, tiled=True)  25.4 us
    pallas_call x1, Pallas kernels, legendre_synthesis(): pl.pallas_call(synthesis_kernel, grid_spec=pltpu.PrefetchScalarGridSpec(n...  12.4 us
    pallas_call x1, Pallas kernels, grid_stage(): pl.pallas_call(grid_kernel, grid=(4,), in_specs=[pl.BlockSpec((8, 24, 64,...  8.36 us
    pallas_call x1, Pallas kernels, analysis_and_solve(): pl.pallas_call(solve_kernel, grid_spec=pltpu.PrefetchScalarGridSpec(num_s...  5.64 us
    unnamed x60, local copies, waits for them, and re-layouts  5.59 us
    all_to_all x1, starting transfers between devices, body(): incoming = lax.all_to_all(latitude, 'order', 0, 0, tiled=True)  5.54 us
  transfers between devices with their start and end apart: 16, of which 0 were waited for; matrix products, arithmetic and copies ran while one was open for 8% of the time, Pallas kernels for 4%

profile of v3, /device:TPU:0, one launch (start us, length us, event | category | flops | bytes accessed | tf_op | source)
XLA Modules:
  0.0 153.1 jit_solution(4306382002320385919)
XLA Ops:
  0.6 0.8 dynamic_slice.3
  1.4 0.1 reshape.116
  1.5 0.1 slice_reduce_fusion.lower
  1.6 0.0 copy-start
  1.6 1.1 copy-done
  2.8 12.4 %legendre_synthesis.1 = (bf16[8,24,64,128]{3,2,1,0:T(8,128)(2,1)}, bf16[2,528,256]{2,1,0:T(8,128)(2,1)S(1)}) custom-call(s32[1]{0:T(128)} %bitcast.place, s32[32]{0:T(128)S(1)} %slice_reduce_fusion.lower, bf16[3,2,2,64,512]{4,3,2,1,0:T(8,128)(2,1)S(1)} %copy-done, bf16[3,2,2,64,512]{4,3,2,1,0:T(8,128)(2,1)} %vor.1, bf16[3,2,2,64,512]{4,3,2,1,0:T(8,128)(2,1)} %mag.1, ...), custom_call_target="tpu_custom_call" | custom-call | flops 1600000000 | bytes 15728640 | tf_op jit(solution)/shard_map/legendre_synthesis/pallas_call | solution.py:112
  15.1 0.8 copy-done.5
  16.0 0.0 copy-start.10
  16.0 0.0 copy-start.27
  16.0 5.5 %all-to-all-start = ((bf16[8,24,64,128]{3,2,1,0:T(8,128)(2,1)}), bf16[8,24,64,128]{3,2,1,0:T(8,128)(2,1)}, u32[]{:S(2)}, u32[]{:S(2)}) async-start(bf16[8,24,64,128]{3,2,1,0:T(8,128)(2,1)} %get-tuple-element.30), calls=%async_computation | async-start | bytes 6291456 | tf_op jit(solution)/shard_map/all_to_all | solution.py:461
  21.5 0.2 reduce-window.9
  21.7 0.2 compare_reduce_fusion
  21.9 1.1 state_to_send.1
  23.1 0.6 copy-done.7
  23.7 1.5 collective-permute-start
  25.2 2.7 %collective-permute-start.1 = (bf16[112,512]{1,0:T(8,128)(2,1)S(1)}, bf16[112,512]{1,0:T(8,128)(2,1)S(1)}, u32[]{:S(2)}, u32[]{:S(2)}) collective-permute-start(bf16[112,512]{1,0:T(8,128)(2,1)S(1)} %get-tuple-element.36), channel_id=1, source_target_pairs={{0,16},{8,24},{16,0},{24,8},{32,48},{40,56},{48,32},{56,40},{64,80... | collective-permute-start | bytes 344072 | tf_op jit(solution)/shard_map/ppermute | solution.py:468
  28.0 0.5 collective-permute-start.2
  28.4 1.6 %collective-permute-start.3 = (bf16[112,512]{1,0:T(8,128)(2,1)S(1)}, bf16[112,512]{1,0:T(8,128)(2,1)S(1)}, u32[]{:S(2)}, u32[]{:S(2)}) collective-permute-start(bf16[112,512]{1,0:T(8,128)(2,1)S(1)} %get-tuple-element.38), channel_id=1, source_target_pairs={{0,32},{8,40},{16,48},{24,56},{32,0},{40,8},{48,16},{56,24},{64,96... | collective-permute-start | bytes 344072 | tf_op jit(solution)/shard_map/ppermute | solution.py:468
  30.0 0.2 collective-permute-start.4
  30.2 0.1 mul.53
  30.3 0.2 iota_add_fusion
  30.5 0.2 add.89
  30.8 5.4 %fusion.4.ana = bf16[1024,1024]{1,0:T(8,128)(2,1)} fusion(bf16[1024,1024]{1,0:T(8,128)(2,1)} %constant.44.clone, s32[1024]{0:T(1024)S(1)} %add.89), kind=kOutput, calls=%fused_computation.7 | convolution fusion | flops 2149580800 | bytes 4198400 | tf_op jit(solution)/shard_map/dot_general | solution.py:424
  36.2 0.1 mul.52
  36.3 0.0 collective-permute-done.refs_1_
  36.3 5.0 %collective-permute-start.5 = (bf16[112,512]{1,0:T(8,128)(2,1)S(1)}, bf16[112,512]{1,0:T(8,128)(2,1)S(1)}, u32[]{:S(2)}, u32[]{:S(2)}) collective-permute-start(bf16[112,512]{1,0:T(8,128)(2,1)S(1)} %get-tuple-element.40), channel_id=1, source_target_pairs={{0,48},{8,56},{16,32},{24,40},{32,16},{40,24},{48,0},{56,8},{64,11... | collective-permute-start | bytes 344072 | tf_op jit(solution)/shard_map/ppermute | solution.py:468
  41.2 0.0 collective-permute-done.1.refs_2_
  41.2 0.4 collective-permute-start.6
  41.6 0.0 collective-permute-done.2.refs_3_
  41.6 3.2 %collective-permute-start.7 = (bf16[112,512]{1,0:T(8,128)(2,1)S(1)}, bf16[112,512]{1,0:T(8,128)(2,1)S(1)}, u32[]{:S(2)}, u32[]{:S(2)}) collective-permute-start(bf16[112,512]{1,0:T(8,128)(2,1)S(1)} %get-tuple-element.42), channel_id=1, source_target_pairs={{0,64},{8,72},{16,80},{24,88},{32,96},{40,104},{48,112},{56,120},{... | collective-permute-start | bytes 344072 | tf_op jit(solution)/shard_map/ppermute | solution.py:468
  44.8 0.0 collective-permute-done.3.refs_4_
  44.8 0.0 collective-permute-start.8
  44.8 0.0 collective-permute-done.4.refs_5_
  44.8 6.6 %collective-permute-start.9 = (bf16[112,512]{1,0:T(8,128)(2,1)S(1)}, bf16[112,512]{1,0:T(8,128)(2,1)S(1)}, u32[]{:S(2)}, u32[]{:S(2)}) collective-permute-start(bf16[112,512]{1,0:T(8,128)(2,1)S(1)} %get-tuple-element.44), channel_id=1, source_target_pairs={{0,80},{8,88},{16,64},{24,72},{32,112},{40,120},{48,96},{56,104},{... | collective-permute-start | bytes 344072 | tf_op jit(solution)/shard_map/ppermute | solution.py:468
  51.4 0.1 add.85
  51.5 0.0 collective-permute-done.5.refs_6_
  51.5 0.3 collective-permute-start.10
  51.8 0.0 collective-permute-done.6.refs_7_
  51.8 3.0 %collective-permute-start.11 = (bf16[112,512]{1,0:T(8,128)(2,1)S(1)}, bf16[112,512]{1,0:T(8,128)(2,1)S(1)}, u32[]{:S(2)}, u32[]{:S(2)}) collective-permute-start(bf16[112,512]{1,0:T(8,128)(2,1)S(1)} %get-tuple-element.46), channel_id=1, source_target_pairs={{0,96},{8,104},{16,112},{24,120},{32,64},{40,72},{48,80},{56,88},{... | collective-permute-start | bytes 344072 | tf_op jit(solution)/shard_map/ppermute | solution.py:468
  54.8 0.0 collective-permute-done.7.refs_8_
  54.8 4.3 %collective-permute-start.12 = (bf16[112,512]{1,0:T(8,128)(2,1)S(1)}, bf16[112,512]{1,0:T(8,128)(2,1)S(1)}, u32[]{:S(2)}, u32[]{:S(2)}) collective-permute-start(bf16[112,512]{1,0:T(8,128)(2,1)S(1)} %get-tuple-element.47), channel_id=1, source_target_pairs={{0,104},{8,96},{16,120},{24,112},{32,72},{40,64},{48,88},{56,80},{... | collective-permute-start | bytes 344072 | tf_op jit(solution)/shard_map/ppermute | solution.py:468
  59.1 0.0 collective-permute-done.8.refs_9_
  59.1 3.7 %collective-permute-start.13 = (bf16[112,512]{1,0:T(8,128)(2,1)S(1)}, bf16[112,512]{1,0:T(8,128)(2,1)S(1)}, u32[]{:S(2)}, u32[]{:S(2)}) collective-permute-start(bf16[112,512]{1,0:T(8,128)(2,1)S(1)} %get-tuple-element.48), channel_id=1, source_target_pairs={{0,112},{8,120},{16,96},{24,104},{32,80},{40,88},{48,64},{56,72},{... | collective-permute-start | bytes 344072 | tf_op jit(solution)/shard_map/ppermute | solution.py:468
  62.8 0.0 collective-permute-done.9.refs_10_
  62.8 1.9 %collective-permute-start.14 = (bf16[112,512]{1,0:T(8,128)(2,1)S(1)}, bf16[112,512]{1,0:T(8,128)(2,1)}, u32[]{:S(2)}, u32[]{:S(2)}) collective-permute-start(bf16[112,512]{1,0:T(8,128)(2,1)S(1)} %get-tuple-element.49), channel_id=1, source_target_pairs={{0,120},{8,112},{16,104},{24,96},{32,88},{40,80},{48,72},{56,64},{... | collective-permute-start | bytes 344072 | tf_op jit(solution)/shard_map/ppermute | solution.py:468
  64.7 5.4 %convert_bitcast_fusion.syn = bf16[1024,1024]{1,0:T(8,128)(2,1)} fusion(bf16[1024,1024]{1,0:T(8,128)(2,1)} %constant.43.clone, s32[1024]{0:T(1024)S(1)} %add.85), kind=kOutput, calls=%fused_computation.5 | convolution fusion | flops 2149580800 | bytes 4198400 | tf_op jit(solution)/shard_map/dot_general | solution.py:420
  70.2 0.0 collective-permute-done.10.refs_11_
  70.2 0.0 collective-permute-done.11.refs_12_
  70.3 0.0 collective-permute-done.13.refs_14_
  70.3 0.6 copy-done.23
  70.8 0.1 copy-done.24
  70.9 0.0 copy-done.25
  71.0 0.7 copy-done.26
  71.6 0.0 collective-permute-done.14.refs_15_
  71.6 4.8 %prepare_solve.1 = (bf16[16,96,512]{2,1,0:T(8,128)(2,1)}, bf16[4,256,512]{2,1,0:T(8,128)(2,1)}, f32[3,64,512]{2,1,0:T(8,128)}) custom-call(s32[1]{0:T(128)} %bitcast.place, s32[32]{0:T(128)} %copy-done.8, bf16[2,528,256]{2,1,0:T(8,128)(2,1)} %copy-done.5, bf16[112,512]{1,0:T(8,128)(2,1)} %copy-done.7, bf16[112,512]{1,0:T(8,128)(2,1)} %copy-done.13, ...), custom_call_target="tpu_custom_call" | custom-call | flops 10000000 | bytes 3145728 | tf_op jit(solution)/shard_map/prepare_solve/pallas_call | solution.py:278
  76.4 0.0 all-to-all-done.lat
  76.5 1.6 %copy-done.11 = bf16[1024,1024]{1,0:T(8,128)(2,1)S(1)} copy-done((bf16[1024,1024]{1,0:T(8,128)(2,1)S(1)}, bf16[1024,1024]{1,0:T(8,128)(2,1)}, u32[]{:S(2)}) %copy-start.11) | copy-done | bytes 2097176
  78.0 8.4 %grid_stage.1 = bf16[1024,768]{1,0:T(8,128)(2,1)S(1)} custom-call(bf16[8,24,64,128]{3,2,1,0:T(8,128)(2,1)} %all-to-all-done.lat, bf16[1024,1024]{1,0:T(8,128)(2,1)S(1)} %copy-done.12, bf16[1024,1024]{1,0:T(8,128)(2,1)S(1)} %copy-done.11, f32[1,128]{1,0:T(1,128)S(1)} %sine_multiply_fusion.weight), custom_call_target="tpu_custom_call" | custom-call | flops 4800000000 | bytes 9437184 | tf_op jit(solution)/shard_map/grid_stage/pallas_call | solution.py:220
  86.4 0.0 copy-start.2
  86.4 0.0 copy-start.3
  86.5 32.7 %all_to_all.15 = bf16[128,8,768]{2,1,0:T(8,128)(2,1)S(1)} all-to-all(bf16[128,8,768]{2,1,0:T(8,128)(2,1)S(1)} %bitcast.13), channel_id=1, replica_groups=mesh['shell'=16,'order'=8] {'shell','order'}, dimensions={0} | all-to-all | bytes 3145728 | tf_op jit(solution)/shard_map/all_to_all | solution.py:475
  119.2 5.6 %analysis_and_solve.1 = bf16[16,96,512]{2,1,0:T(8,128)(2,1)S(1)} custom-call(s32[1]{0:T(128)} %bitcast.place, s32[32]{0:T(128)S(1)} %copy-done.9, bf16[1024,768]{1,0:T(8,128)(2,1)S(1)} %bitcast.12, bf16[16,96,512]{2,1,0:T(8,128)(2,1)S(1)} %copy-done.2, bf16[4,256,512]{2,1,0:T(8,128)(2,1)S(1)} %copy-done.3, f32[3,64,512]{2,1,0:T(8,128)S(1)} %copy-done.6), custom_call_target="tpu_custom_call" | custom-call | flops 900000000 | bytes 6291456 | tf_op jit(solution)/shard_map/analysis_and_solve/pallas_call | solution.py:362
  124.8 25.4 %all_to_all.16.got = bf16[16,96,512]{2,1,0:T(8,128)(2,1)S(1)} all-to-all(bf16[16,96,512]{2,1,0:T(8,128)(2,1)S(1)} %analysis_and_solve.1), channel_id=1, replica_groups=mesh['shell'=16,'order'=8] {'shell'}, dimensions={0} | all-to-all | bytes 3145728 | tf_op jit(solution)/shard_map/all_to_all | solution.py:479
  150.3 2.8 %unpack_solution.1 = (f32[3,2,2,64,512]{4,3,2,1,0:T(8,128)}, f32[3,2,2,64,512]{4,3,2,1,0:T(8,128)}) custom-call(bf16[16,96,512]{2,1,0:T(8,128)(2,1)S(1)} %all_to_all.16.got), custom_call_target="tpu_custom_call" | custom-call | flops 1000000 | bytes 5242880 | tf_op jit(solution)/shard_map/unpack_solution/pallas_call | solution.py:401
  (55 shorter events, 0.2 us)
Async XLA Ops:
  1.6 13.5 %copy-start.8 = (s32[32]{0:T(128)}, s32[32]{0:T(128)S(1)}, u32[]{:S(2)}) copy-start(s32[32]{0:T(128)S(1)} %slice_reduce_fusion.lower) | copy-start | bytes 388
  1.6 1.1 copy-start
  15.1 0.8 copy-start.5
  15.9 5.6 %copy-start.29 = (s32[4]{0:T(128)S(1)}, s32[4]{0:T(128)}, u32[]{:S(2)}) copy-start(s32[4]{0:T(128)} %param.19) | copy-start | bytes 52
  15.9 6.0 %copy-start.28 = (f32[2,2]{1,0:T(2,128)S(1)}, f32[2,2]{1,0:T(2,128)}, u32[]{:S(2)}) copy-start(f32[2,2]{1,0:T(2,128)} %param.20) | copy-start | bytes 52
  15.9 6.0 %copy-start.1 = (bf16[3,2,2,64,512]{4,3,2,1,0:T(8,128)(2,1)S(1)}, bf16[3,2,2,64,512]{4,3,2,1,0:T(8,128)(2,1)}, u32[]{:S(2)}) copy-start(bf16[3,2,2,64,512]{4,3,2,1,0:T(8,128)(2,1)} %vel.2) | copy-start | bytes 2359300
  16.0 6.0 %copy-start.4 = (bf16[3,2,2,64,512]{4,3,2,1,0:T(8,128)(2,1)S(1)}, bf16[3,2,2,64,512]{4,3,2,1,0:T(8,128)(2,1)}, u32[]{:S(2)}) copy-start(bf16[3,2,2,64,512]{4,3,2,1,0:T(8,128)(2,1)} %pot) | copy-start | bytes 2359300
  16.0 6.0 %copy-start.10 = (f32[2,2]{1,0:T(2,128)S(1)}, f32[2,2]{1,0:T(2,128)}, u32[]{:S(2)}) copy-start(f32[2,2]{1,0:T(2,128)} %angular.1) | copy-start | bytes 52
  16.0 14.2 %copy-start.27 = (s32[512]{0:T(512)S(1)}, s32[512]{0:T(512)}, u32[]{:S(2)}) copy-start(s32[512]{0:T(512)} %param.17) | copy-start | bytes 6148
  16.0 60.5 %all-to-all-start = ((bf16[8,24,64,128]{3,2,1,0:T(8,128)(2,1)}), bf16[8,24,64,128]{3,2,1,0:T(8,128)(2,1)}, u32[]{:S(2)}, u32[]{:S(2)}) async-start(bf16[8,24,64,128]{3,2,1,0:T(8,128)(2,1)} %get-tuple-element.30), calls=%async_computation | async-start | bytes 6291456 | tf_op jit(solution)/shard_map/all_to_all | solution.py:461
  23.1 0.6 copy-start.7
  23.7 12.5 %collective-permute-start = (bf16[112,512]{1,0:T(8,128)(2,1)S(1)}, bf16[112,512]{1,0:T(8,128)(2,1)S(1)}, u32[]{:S(2)}, u32[]{:S(2)}) collective-permute-start(bf16[112,512]{1,0:T(8,128)(2,1)S(1)} %get-tuple-element.35), channel_id=1, source_target_pairs={{0,8},{8,0},{16,24},{24,16},{32,40},{40,32},{48,56},{56,48},{64,72... | collective-permute-start | bytes 344072 | tf_op jit(solution)/shard_map/ppermute | solution.py:468
  25.2 16.0 %collective-permute-start.1 = (bf16[112,512]{1,0:T(8,128)(2,1)S(1)}, bf16[112,512]{1,0:T(8,128)(2,1)S(1)}, u32[]{:S(2)}, u32[]{:S(2)}) collective-permute-start(bf16[112,512]{1,0:T(8,128)(2,1)S(1)} %get-tuple-element.36), channel_id=1, source_target_pairs={{0,16},{8,24},{16,0},{24,8},{32,48},{40,56},{48,32},{56,40},{64,80... | collective-permute-start | bytes 344072 | tf_op jit(solution)/shard_map/ppermute | solution.py:468
  28.0 13.6 %collective-permute-start.2 = (bf16[112,512]{1,0:T(8,128)(2,1)S(1)}, bf16[112,512]{1,0:T(8,128)(2,1)S(1)}, u32[]{:S(2)}, u32[]{:S(2)}) collective-permute-start(bf16[112,512]{1,0:T(8,128)(2,1)S(1)} %get-tuple-element.37), channel_id=1, source_target_pairs={{0,24},{8,16},{16,8},{24,0},{32,56},{40,48},{48,40},{56,32},{64,88... | collective-permute-start | bytes 344072 | tf_op jit(solution)/shard_map/ppermute | solution.py:468
  28.4 16.4 %collective-permute-start.3 = (bf16[112,512]{1,0:T(8,128)(2,1)S(1)}, bf16[112,512]{1,0:T(8,128)(2,1)S(1)}, u32[]{:S(2)}, u32[]{:S(2)}) collective-permute-start(bf16[112,512]{1,0:T(8,128)(2,1)S(1)} %get-tuple-element.38), channel_id=1, source_target_pairs={{0,32},{8,40},{16,48},{24,56},{32,0},{40,8},{48,16},{56,24},{64,96... | collective-permute-start | bytes 344072 | tf_op jit(solution)/shard_map/ppermute | solution.py:468
  30.0 14.8 %collective-permute-start.4 = (bf16[112,512]{1,0:T(8,128)(2,1)S(1)}, bf16[112,512]{1,0:T(8,128)(2,1)S(1)}, u32[]{:S(2)}, u32[]{:S(2)}) collective-permute-start(bf16[112,512]{1,0:T(8,128)(2,1)S(1)} %get-tuple-element.39), channel_id=1, source_target_pairs={{0,40},{8,32},{16,56},{24,48},{32,8},{40,0},{48,24},{56,16},{64,10... | collective-permute-start | bytes 344072 | tf_op jit(solution)/shard_map/ppermute | solution.py:468
  36.3 33.8 %copy-start.13 = (bf16[112,512]{1,0:T(8,128)(2,1)}, bf16[112,512]{1,0:T(8,128)(2,1)S(1)}, u32[]{:S(2)}) copy-start(bf16[112,512]{1,0:T(8,128)(2,1)S(1)} %collective-permute-done.refs_1_) | copy-start | bytes 344068
  36.3 15.3 %collective-permute-start.5 = (bf16[112,512]{1,0:T(8,128)(2,1)S(1)}, bf16[112,512]{1,0:T(8,128)(2,1)S(1)}, u32[]{:S(2)}, u32[]{:S(2)}) collective-permute-start(bf16[112,512]{1,0:T(8,128)(2,1)S(1)} %get-tuple-element.40), channel_id=1, source_target_pairs={{0,48},{8,56},{16,32},{24,40},{32,16},{40,24},{48,0},{56,8},{64,11... | collective-permute-start | bytes 344072 | tf_op jit(solution)/shard_map/ppermute | solution.py:468
  41.2 28.8 %copy-start.14 = (bf16[112,512]{1,0:T(8,128)(2,1)}, bf16[112,512]{1,0:T(8,128)(2,1)S(1)}, u32[]{:S(2)}) copy-start(bf16[112,512]{1,0:T(8,128)(2,1)S(1)} %collective-permute-done.1.refs_2_) | copy-start | bytes 344068
  41.2 10.6 %collective-permute-start.6 = (bf16[112,512]{1,0:T(8,128)(2,1)S(1)}, bf16[112,512]{1,0:T(8,128)(2,1)S(1)}, u32[]{:S(2)}, u32[]{:S(2)}) collective-permute-start(bf16[112,512]{1,0:T(8,128)(2,1)S(1)} %get-tuple-element.41), channel_id=1, source_target_pairs={{0,56},{8,48},{16,40},{24,32},{32,24},{40,16},{48,8},{56,0},{64,12... | collective-permute-start | bytes 344072 | tf_op jit(solution)/shard_map/ppermute | solution.py:468
  41.6 28.5 %copy-start.15 = (bf16[112,512]{1,0:T(8,128)(2,1)}, bf16[112,512]{1,0:T(8,128)(2,1)S(1)}, u32[]{:S(2)}) copy-start(bf16[112,512]{1,0:T(8,128)(2,1)S(1)} %collective-permute-done.2.refs_3_) | copy-start | bytes 344068
  41.6 13.2 %collective-permute-start.7 = (bf16[112,512]{1,0:T(8,128)(2,1)S(1)}, bf16[112,512]{1,0:T(8,128)(2,1)S(1)}, u32[]{:S(2)}, u32[]{:S(2)}) collective-permute-start(bf16[112,512]{1,0:T(8,128)(2,1)S(1)} %get-tuple-element.42), channel_id=1, source_target_pairs={{0,64},{8,72},{16,80},{24,88},{32,96},{40,104},{48,112},{56,120},{... | collective-permute-start | bytes 344072 | tf_op jit(solution)/shard_map/ppermute | solution.py:468
  44.8 25.3 %copy-start.16 = (bf16[112,512]{1,0:T(8,128)(2,1)}, bf16[112,512]{1,0:T(8,128)(2,1)S(1)}, u32[]{:S(2)}) copy-start(bf16[112,512]{1,0:T(8,128)(2,1)S(1)} %collective-permute-done.3.refs_4_) | copy-start | bytes 344068
  44.8 14.3 %collective-permute-start.8 = (bf16[112,512]{1,0:T(8,128)(2,1)S(1)}, bf16[112,512]{1,0:T(8,128)(2,1)S(1)}, u32[]{:S(2)}, u32[]{:S(2)}) collective-permute-start(bf16[112,512]{1,0:T(8,128)(2,1)S(1)} %get-tuple-element.43), channel_id=1, source_target_pairs={{0,72},{8,64},{16,88},{24,80},{32,104},{40,96},{48,120},{56,112},{... | collective-permute-start | bytes 344072 | tf_op jit(solution)/shard_map/ppermute | solution.py:468
  44.8 25.3 %copy-start.17 = (bf16[112,512]{1,0:T(8,128)(2,1)}, bf16[112,512]{1,0:T(8,128)(2,1)S(1)}, u32[]{:S(2)}) copy-start(bf16[112,512]{1,0:T(8,128)(2,1)S(1)} %collective-permute-done.4.refs_5_) | copy-start | bytes 344068
  44.8 17.9 %collective-permute-start.9 = (bf16[112,512]{1,0:T(8,128)(2,1)S(1)}, bf16[112,512]{1,0:T(8,128)(2,1)S(1)}, u32[]{:S(2)}, u32[]{:S(2)}) collective-permute-start(bf16[112,512]{1,0:T(8,128)(2,1)S(1)} %get-tuple-element.44), channel_id=1, source_target_pairs={{0,80},{8,88},{16,64},{24,72},{32,112},{40,120},{48,96},{56,104},{... | collective-permute-start | bytes 344072 | tf_op jit(solution)/shard_map/ppermute | solution.py:468
  51.5 18.6 %copy-start.18 = (bf16[112,512]{1,0:T(8,128)(2,1)}, bf16[112,512]{1,0:T(8,128)(2,1)S(1)}, u32[]{:S(2)}) copy-start(bf16[112,512]{1,0:T(8,128)(2,1)S(1)} %collective-permute-done.5.refs_6_) | copy-start | bytes 344068
  51.5 18.7 %collective-permute-start.10 = (bf16[112,512]{1,0:T(8,128)(2,1)S(1)}, bf16[112,512]{1,0:T(8,128)(2,1)S(1)}, u32[]{:S(2)}, u32[]{:S(2)}) collective-permute-start(bf16[112,512]{1,0:T(8,128)(2,1)S(1)} %get-tuple-element.45), channel_id=1, source_target_pairs={{0,88},{8,80},{16,72},{24,64},{32,120},{40,112},{48,104},{56,96},{... | collective-permute-start | bytes 344072 | tf_op jit(solution)/shard_map/ppermute | solution.py:468
  51.8 18.3 %copy-start.19 = (bf16[112,512]{1,0:T(8,128)(2,1)}, bf16[112,512]{1,0:T(8,128)(2,1)S(1)}, u32[]{:S(2)}) copy-start(bf16[112,512]{1,0:T(8,128)(2,1)S(1)} %collective-permute-done.6.refs_7_) | copy-start | bytes 344068
  51.8 18.4 %collective-permute-start.11 = (bf16[112,512]{1,0:T(8,128)(2,1)S(1)}, bf16[112,512]{1,0:T(8,128)(2,1)S(1)}, u32[]{:S(2)}, u32[]{:S(2)}) collective-permute-start(bf16[112,512]{1,0:T(8,128)(2,1)S(1)} %get-tuple-element.46), channel_id=1, source_target_pairs={{0,96},{8,104},{16,112},{24,120},{32,64},{40,72},{48,80},{56,88},{... | collective-permute-start | bytes 344072 | tf_op jit(solution)/shard_map/ppermute | solution.py:468
  54.8 15.3 %copy-start.20 = (bf16[112,512]{1,0:T(8,128)(2,1)}, bf16[112,512]{1,0:T(8,128)(2,1)S(1)}, u32[]{:S(2)}) copy-start(bf16[112,512]{1,0:T(8,128)(2,1)S(1)} %collective-permute-done.7.refs_8_) | copy-start | bytes 344068
  54.8 15.4 %collective-permute-start.12 = (bf16[112,512]{1,0:T(8,128)(2,1)S(1)}, bf16[112,512]{1,0:T(8,128)(2,1)S(1)}, u32[]{:S(2)}, u32[]{:S(2)}) collective-permute-start(bf16[112,512]{1,0:T(8,128)(2,1)S(1)} %get-tuple-element.47), channel_id=1, source_target_pairs={{0,104},{8,96},{16,120},{24,112},{32,72},{40,64},{48,88},{56,80},{... | collective-permute-start | bytes 344072 | tf_op jit(solution)/shard_map/ppermute | solution.py:468
  59.1 11.0 %copy-start.21 = (bf16[112,512]{1,0:T(8,128)(2,1)}, bf16[112,512]{1,0:T(8,128)(2,1)S(1)}, u32[]{:S(2)}) copy-start(bf16[112,512]{1,0:T(8,128)(2,1)S(1)} %collective-permute-done.8.refs_9_) | copy-start | bytes 344068
  59.1 11.2 %collective-permute-start.13 = (bf16[112,512]{1,0:T(8,128)(2,1)S(1)}, bf16[112,512]{1,0:T(8,128)(2,1)S(1)}, u32[]{:S(2)}, u32[]{:S(2)}) collective-permute-start(bf16[112,512]{1,0:T(8,128)(2,1)S(1)} %get-tuple-element.48), channel_id=1, source_target_pairs={{0,112},{8,120},{16,96},{24,104},{32,80},{40,88},{48,64},{56,72},{... | collective-permute-start | bytes 344072 | tf_op jit(solution)/shard_map/ppermute | solution.py:468
  62.8 7.4 %copy-start.22 = (bf16[112,512]{1,0:T(8,128)(2,1)}, bf16[112,512]{1,0:T(8,128)(2,1)S(1)}, u32[]{:S(2)}) copy-start(bf16[112,512]{1,0:T(8,128)(2,1)S(1)} %collective-permute-done.9.refs_10_) | copy-start | bytes 344068
  62.8 8.8 %collective-permute-start.14 = (bf16[112,512]{1,0:T(8,128)(2,1)S(1)}, bf16[112,512]{1,0:T(8,128)(2,1)}, u32[]{:S(2)}, u32[]{:S(2)}) collective-permute-start(bf16[112,512]{1,0:T(8,128)(2,1)S(1)} %get-tuple-element.49), channel_id=1, source_target_pairs={{0,120},{8,112},{16,104},{24,96},{32,88},{40,80},{48,72},{56,64},{... | collective-permute-start | bytes 344072 | tf_op jit(solution)/shard_map/ppermute | solution.py:468
  70.2 0.6 copy-start.23
  70.2 0.7 copy-start.24
  70.2 0.7 copy-start.25
  70.9 0.7 copy-start.26
  71.6 4.8 %copy-start.12 = (bf16[1024,1024]{1,0:T(8,128)(2,1)S(1)}, bf16[1024,1024]{1,0:T(8,128)(2,1)}, u32[]{:S(2)}) copy-start(bf16[1024,1024]{1,0:T(8,128)(2,1)} %convert_bitcast_fusion.syn) | copy-start | bytes 6291460
  76.4 1.6 %copy-start.11 = (bf16[1024,1024]{1,0:T(8,128)(2,1)S(1)}, bf16[1024,1024]{1,0:T(8,128)(2,1)}, u32[]{:S(2)}) copy-start(bf16[1024,1024]{1,0:T(8,128)(2,1)} %fusion.4.ana) | copy-start | bytes 6291460
  86.4 32.8 %copy-start.2 = (bf16[16,96,512]{2,1,0:T(8,128)(2,1)S(1)}, bf16[16,96,512]{2,1,0:T(8,128)(2,1)}, u32[]{:S(2)}) copy-start(bf16[16,96,512]{2,1,0:T(8,128)(2,1)} %get-tuple-element.55.state) | copy-start | bytes 4718596
  86.4 32.7 %copy-start.3 = (bf16[4,256,512]{2,1,0:T(8,128)(2,1)S(1)}, bf16[4,256,512]{2,1,0:T(8,128)(2,1)}, u32[]{:S(2)}) copy-start(bf16[4,256,512]{2,1,0:T(8,128)(2,1)} %get-tuple-element.56.table) | copy-start | bytes 3145732
  86.4 32.7 %copy-start.6 = (f32[3,64,512]{2,1,0:T(8,128)S(1)}, f32[3,64,512]{2,1,0:T(8,128)}, u32[]{:S(2)}) copy-start(f32[3,64,512]{2,1,0:T(8,128)} %get-tuple-element.57.factors) | copy-start | bytes 1179652
  86.4 32.7 %copy-start.9 = (s32[32]{0:T(128)S(1)}, s32[32]{0:T(128)}, u32[]{:S(2)}) copy-start(s32[32]{0:T(128)} %copy-done.8) | copy-start | bytes 388

commit v4 on v3

--- a/solution.py
+++ b/solution.py
@@ -20,11 +20,16 @@
 def natural_tables():
     phases = (np.arange(L)[:, None] * np.arange(NPHI)[None, :]) % NPHI
     angles = 2.0 * np.pi * phases / NPHI
-    rows = np.stack([np.cos(angles), -np.sin(angles)], axis=1)
+    rows = np.stack([np.cos(angles), -np.sin(angles)], axis=0)
     weight = np.where(np.arange(L) == 0, 1.0, 2.0) * (math.sqrt(2.0 * math.pi) / L)
-    synthesis = (rows * weight[:, None, None]).reshape(2 * L, NPHI)
+    synthesis = (rows * weight[None, :, None]).reshape(2 * L, NPHI)
     analysis = (rows / NPHI).reshape(2 * L, NPHI)
     return synthesis.T.astype(jnp.bfloat16), analysis.astype(jnp.bfloat16)
+
+
+def partner(place, odd, r):
+    swapped = (r & 3) * 4 + r // 4
+    return place ^ jnp.where(odd == 1, swapped, r)
 
 
 def load(ref, rows):
@@ -159,7 +164,7 @@
                 lines.append(jnp.where(lane < 128, high, jnp.where(lane < 256, mid, low)))
     extra = jnp.concatenate(lines + [jnp.zeros((8, L), f32)], axis=0).astype(bf16)
     for r in range(16):
-        outs[r][0:96, :] = scr[place[0] ^ r].astype(bf16)
+        outs[r][0:96, :] = scr[partner(place[0], place[1], r)].astype(bf16)
         outs[r][96:112, :] = extra
 
 
@@ -186,7 +191,9 @@
     @pl.when(step == 0)
     def _():
         for c in range(12):
-            wide[:, c * 128 : c * 128 + 128] = lat[:, 2 * c : 2 * c + 2].reshape(1024, 128)
+            for p in range(2):
+                rows_p = lat[:, 2 * c + p].reshape(512, 128)
+                wide[p * 512 : p * 512 + 512, c * 128 : c * 128 + 128] = rows_p
 
     @pl.when(step < 2)
     def _():
@@ -235,20 +242,62 @@
     )(lat, syn, ana, weight)
 
 
-def prepare_kernel(place, lower, table, *refs):
-    parts, (state_out, table_out, factors, scr, extra) = refs[:16], refs[16:]
-    for r in range(16):
-        state_out[place[0] ^ r] = parts[r][0:96, :]
-        extra[place[0] ^ r] = parts[r][96:112, :].astype(f32)
+def tables_kernel(lower, slots, targets, natural_s, natural_a, pairs, syn, ana, table_out, scr):
+    ids = lax.broadcasted_iota(jnp.int32, (L, L), 0)
+    pick = jnp.where(ids == slots[...], 1.0, 0.0).astype(bf16)
+    for p in range(2):
+        at = slice(p * L, p * L + L)
+        syn[:, at] = jnp.dot(natural_s[:, at], pick, preferred_element_type=f32).astype(bf16)
+    ids = lax.broadcasted_iota(jnp.int32, (2 * L, 2 * L), 0)
+    pick = jnp.where(ids == targets[...], 1.0, 0.0).astype(bf16)
+    ana[...] = lax.dot_general(
+        pick, natural_a[...], (((0,), (0,)), ((), ())), preferred_element_type=f32
+    ).astype(bf16)
     l_row = lax.broadcasted_iota(jnp.int32, (1, L), 1)
     for i in range(2):
-        m = lower[place[0] * 2 + i]
-        scr[...] = table[i].astype(f32)
+        m = lower[i]
+        scr[...] = pairs[i].astype(f32)
         a = jnp.transpose(scr[0:L, :])
         a = pltpu.roll(a, m, 1)
         table_out[2 * i] = jnp.where(l_row >= m, a, 0.0).astype(bf16)
         b = jnp.transpose(scr[1 : L + 1, :])
         table_out[2 * i + 1] = jnp.where(l_row >= L - 1 - m, b, 0.0).astype(bf16)
+
+
+def make_tables(own_lower, order_slots, pairs):
+    natural_s, natural_a = natural_tables()
+    slots = order_slots.reshape(8, 16, 4).transpose(1, 0, 2)[..., None]
+    targets = (slots + jnp.arange(2, dtype=jnp.int32) * L).reshape(1, 2 * L)
+    whole = lambda *shape: pl.BlockSpec(shape, lambda g: (0,) * len(shape))
+    return pl.pallas_call(
+        tables_kernel,
+        grid=(1,),
+        in_specs=[
+            pl.BlockSpec(memory_space=pltpu.SMEM),
+            whole(1, L),
+            whole(1, 2 * L),
+            whole(NPHI, 2 * L),
+            whole(2 * L, NPHI),
+            whole(2, L + 16, NH),
+        ],
+        out_specs=[whole(NPHI, 2 * L), whole(2 * L, NPHI), whole(4, NH, L)],
+        out_shape=[
+            jax.ShapeDtypeStruct((NPHI, 2 * L), bf16),
+            jax.ShapeDtypeStruct((2 * L, NPHI), bf16),
+            jax.ShapeDtypeStruct((4, NH, L), bf16),
+        ],
+        scratch_shapes=[pltpu.VMEM((L + 16, NH), f32)],
+        compiler_params=pltpu.CompilerParams(vmem_limit_bytes=40 * MIB),
+        cost_estimate=pl.CostEstimate(flops=int(4e9), bytes_accessed=12 * MIB, transcendentals=0),
+        name="make_tables",
+    )(own_lower, order_slots.reshape(1, L), targets, jnp.asarray(natural_s), jnp.asarray(natural_a), pairs)
+
+
+def factors_kernel(place, *refs):
+    parts, (factors, extra) = refs[:16], refs[16:]
+    for r in range(16):
+        extra[partner(place[0], place[1], r)] = parts[r][...].astype(f32)
+    l_row = lax.broadcasted_iota(jnp.int32, (1, L), 1)
     degree = l_row.astype(f32)
     degree_term = degree * (degree + 1.0)
     below, angle = [[], []], [[], []]
@@ -274,40 +323,30 @@
             factors[2, row : row + 1, :] = carried
 
 
-def prepare_solve(place, lower, table, parts):
-    return pl.pallas_call(
-        prepare_kernel,
-        grid_spec=pltpu.PrefetchScalarGridSpec(
-            num_scalar_prefetch=2,
-            grid=(1,),
-            in_specs=[
-                pl.BlockSpec((2, L + 16, NH), lambda g, place, low: (0, 0, 0)),
-            ]
-            + [pl.BlockSpec((112, L), lambda g, place, low: (0, 0))] * 16,
-            out_specs=[
-                pl.BlockSpec((16, 96, L), lambda g, place, low: (0, 0, 0)),
-                pl.BlockSpec((4, NH, L), lambda g, place, low: (0, 0, 0)),
-                pl.BlockSpec((3, 64, L), lambda g, place, low: (0, 0, 0)),
-            ],
-            scratch_shapes=[pltpu.VMEM((L + 16, NH), f32), pltpu.VMEM((16, 16, L), f32)],
-        ),
-        out_shape=[
-            jax.ShapeDtypeStruct((16, 96, L), bf16),
-            jax.ShapeDtypeStruct((4, NH, L), bf16),
-            jax.ShapeDtypeStruct((3, 64, L), f32),
-        ],
+def solve_factors(place, parts):
+    return pl.pallas_call(
+        factors_kernel,
+        grid=(1,),
+        in_specs=[pl.BlockSpec(memory_space=pltpu.SMEM)]
+        + [pl.BlockSpec((16, L), lambda g: (6, 0))] * 16,
+        out_specs=pl.BlockSpec((3, 64, L), lambda g: (0, 0, 0)),
+        out_shape=jax.ShapeDtypeStruct((3, 64, L), f32),
+        scratch_shapes=[pltpu.VMEM((16, 16, L), f32)],
         compiler_params=pltpu.CompilerParams(vmem_limit_bytes=60 * MIB),
-        cost_estimate=pl.CostEstimate(flops=10**7, bytes_accessed=3 * MIB, transcendentals=0),
-        name="prepare_solve",
-    )(place, lower, table, *parts)
-
-
-def solve_kernel(place, lower, coef, state, table, factors, out, cs, lhs, rhs):
+        cost_estimate=pl.CostEstimate(flops=10**6, bytes_accessed=MIB, transcendentals=0),
+        name="solve_factors",
+    )(place, *parts)
+
+
+def solve_kernel(place, lower, coef, table, factors, *refs):
+    parts, (out, cs, lhs, rhs, state) = refs[:16], refs[16:]
+    for r in range(16):
+        state[partner(place[0], place[1], r)] = parts[r][...]
     for c in range(6):
         cs[c] = coef[:, c * 128 : c * 128 + 128].astype(f32)
     l_row = lax.broadcasted_iota(jnp.int32, (1, L), 1)
     for k in range(4):
-        m = lower[place[0] * 2 + k // 2]
+        m = lower[k // 2]
         order = m if k % 2 == 0 else L - 1 - m
         half_sign = 0.5 * (1 - 2 * ((l_row + order) & 1)).astype(f32)
         for h in range(2):
@@ -358,30 +397,31 @@
     lax.fori_loop(0, 16, backward, (zero, zero))
 
 
-def analysis_and_solve(place, lower, coef, state, table, factors):
+def analysis_and_solve(place, own_lower, coef, table, factors, parts):
+    small = pl.BlockSpec(memory_space=pltpu.SMEM)
     return pl.pallas_call(
         solve_kernel,
-        grid_spec=pltpu.PrefetchScalarGridSpec(
-            num_scalar_prefetch=2,
-            grid=(1,),
-            in_specs=[
-                pl.BlockSpec((1024, 768), lambda g, place, low: (0, 0)),
-                pl.BlockSpec((16, 96, L), lambda g, place, low: (0, 0, 0)),
-                pl.BlockSpec((4, NH, L), lambda g, place, low: (0, 0, 0)),
-                pl.BlockSpec((3, 64, L), lambda g, place, low: (0, 0, 0)),
-            ],
-            out_specs=pl.BlockSpec((16, 96, L), lambda g, place, low: (0, 0, 0)),
-            scratch_shapes=[
-                pltpu.VMEM((6, 1024, 128), f32),
-                pltpu.VMEM((2, 768, NH), bf16),
-                pltpu.VMEM((4, 32 * 48, 128), f32),
-            ],
-        ),
+        grid=(1,),
+        in_specs=[
+            small,
+            small,
+            pl.BlockSpec((1024, 768), lambda g: (0, 0)),
+            pl.BlockSpec((4, NH, L), lambda g: (0, 0, 0)),
+            pl.BlockSpec((3, 64, L), lambda g: (0, 0, 0)),
+        ]
+        + [pl.BlockSpec((96, L), lambda g: (0, 0))] * 16,
+        out_specs=pl.BlockSpec((16, 96, L), lambda g: (0, 0, 0)),
         out_shape=jax.ShapeDtypeStruct((16, 96, L), bf16),
+        scratch_shapes=[
+            pltpu.VMEM((6, 1024, 128), f32),
+            pltpu.VMEM((2, 768, NH), bf16),
+            pltpu.VMEM((4, 32 * 48, 128), f32),
+            pltpu.VMEM((16, 96, L), bf16),
+        ],
         compiler_params=pltpu.CompilerParams(vmem_limit_bytes=32 * MIB),
         cost_estimate=pl.CostEstimate(flops=int(0.9e9), bytes_accessed=6 * MIB, transcendentals=0),
         name="analysis_and_solve",
-    )(place, lower, coef, state, table, factors)
+    )(place, own_lower, coef, table, factors, *parts)
 
 
 def unpack_kernel(got, out_v, out_p, scr, tmp):
@@ -409,20 +449,6 @@
         cost_estimate=pl.CostEstimate(flops=10**6, bytes_accessed=5 * MIB, transcendentals=0),
         name="unpack_solution",
     )(got)
-
-
-def fourier_tables(order_slots):
-    natural_s, natural_a = natural_tables()
-    ids = jnp.arange(2 * L, dtype=jnp.int32)
-    part = jnp.arange(2, dtype=jnp.int32)
-    by_source = order_slots.reshape(8, 1, 64) * 2 + part[None, :, None]
-    pick_s = (ids[:, None] == by_source.reshape(1, -1)).astype(bf16)
-    syn = jnp.dot(jnp.asarray(natural_s), pick_s, preferred_element_type=f32).astype(bf16)
-    slots = order_slots.reshape(8, 16, 4).transpose(1, 0, 2)
-    by_target = slots[..., None] * 2 + part
-    pick_a = (by_target.reshape(-1, 1) == ids[None, :]).astype(bf16)
-    ana = jnp.dot(pick_a, jnp.asarray(natural_a), preferred_element_type=f32).astype(bf16)
-    return syn, ana
 
 
 def body(
@@ -440,7 +466,8 @@
     order_rank = lax.axis_index("order")
     shell_rank = lax.axis_index("shell")
     lower = lax.dynamic_slice_in_dim(order_slots, order_rank * 64, 64).reshape(32, 2)[:, 0]
-    place = shell_rank.reshape(1)
+    place = jnp.stack([shell_rank, order_rank & 1]).astype(jnp.int32)
+    own_lower = lax.dynamic_slice_in_dim(lower, shell_rank * 2, 2)
     shell_ids = shell_rank * 2 + jnp.arange(2, dtype=jnp.int32)
     starts = jnp.cumsum(block_lengths) - block_lengths
     is_start = jnp.any(shell_ids[:, None] == starts[None, :], axis=1)
@@ -464,18 +491,24 @@
         (order_slots, velocity, potential, latitude)
     )
     parts = state_to_send(place, kappa, angular, vel_after, pot_after)
-    parts = [parts[0]] + [
-        lax.ppermute(parts[r], "shell", [(i, i ^ r) for i in range(16)]) for r in range(1, 16)
-    ]
-    syn, ana = fourier_tables(order_after)
-    state, table, factors = prepare_solve(place, lower, pairs, parts)
-    incoming, state, table, factors = lax.optimization_barrier((incoming, state, table, factors))
+    received = [parts[0]]
+    for r in range(1, 16):
+        swapped = (r & 3) * 4 + r // 4
+        pairs_r = [
+            (i * 8 + o, (i ^ (swapped if o & 1 else r)) * 8 + o) for i in range(16) for o in range(8)
+        ]
+        received.append(lax.ppermute(parts[r], ("shell", "order"), pairs_r))
+    syn, ana, table = make_tables(own_lower, order_after, pairs)
+    factors = solve_factors(place, received)
+    incoming, factors, table, received = lax.optimization_barrier(
+        (incoming, factors, table, received)
+    )
 
     coefs = grid_stage(incoming, syn, ana, weight)
     coefs = lax.all_to_all(
         coefs.reshape(128, 8, 768), ("shell", "order"), 0, 0, tiled=True
     ).reshape(1024, 768)
-    solved = analysis_and_solve(place, lower, coefs, state, table, factors)
+    solved = analysis_and_solve(place, own_lower, coefs, table, factors, received)
     solved = lax.all_to_all(solved, "shell", 0, 0, tiled=True)
     return tuple(unpack_solution(solved))
 

time: 154 us -> 152 us (0.987)
  matrix products: 10.8 us -> 0 us
  local copies, waits for them, and re-layouts: 7.08 us -> 14.4 us
  starting transfers between devices: 40.2 us -> 37.8 us
  Pallas kernels: 35.2 us -> 37.4 us
    dot_general x2 -> x0, matrix products: 10.8 us -> none  [the longest x1 5.39 us: fourier_tables(): jnp.dot(pick_a, jnp.asarray(natural_a), preferred_element_type=f32)]
    unnamed x60 -> x96, local copies, waits for them, and re-layouts: 5.59 us -> 11.7 us
    ppermute x15, starting transfers between devices: 34.7 us -> 32.3 us  [body(): received.append(lax.ppermute(parts[r], ('shell', 'order'), pairs_r))]
    pallas_call x2 -> x3, Pallas kernels: 10.5 us -> 12 us  [the longest x1 5.87 us: analysis_and_solve(): pl.pallas_call(solve_kernel, grid=(1,), in_specs=[small, small, pl.BlockS...]
  transfers between devices with their start and end apart: 16 -> 16, of which waited for: 0 -> 0; matrix products, arithmetic and copies ran while one was open for 8% -> 1% of each run, Pallas kernels for 4% -> 5%
where the time goes in v4:
time: 152 us; the launch traced here: 151 us
  blocking collectives  59.4 us (39%)
  starting transfers between devices  37.8 us (25%)
  Pallas kernels  37.4 us (25%)
  local copies, waits for them, and re-layouts  14.4 us (9%)
    all_to_all x1, blocking collectives, body(): lax.all_to_all(coefs.reshape(128, 8, 768), ('shell', 'order'), 0, 0, tile...  34 us
    ppermute x15, starting transfers between devices, body(): received.append(lax.ppermute(parts[r], ('shell', 'order'), pairs_r))  32.3 us
    all_to_all x1, blocking collectives, body(): solved = lax.all_to_all(solved, 'shell', 0, 0, tiled=True)  25.4 us
    pallas_call x1, Pallas kernels, legendre_synthesis(): pl.pallas_call(synthesis_kernel, grid_spec=pltpu.PrefetchScalarGridSpec(n...  12.4 us
    unnamed x96, local copies, waits for them, and re-layouts  11.7 us
    pallas_call x1, Pallas kernels, grid_stage(): pl.pallas_call(grid_kernel, grid=(4,), in_specs=[pl.BlockSpec((8, 24, 64,...  8.34 us
    pallas_call x1, Pallas kernels, analysis_and_solve(): pl.pallas_call(solve_kernel, grid=(1,), in_specs=[small, small, pl.BlockS...  5.87 us
    all_to_all x1, starting transfers between devices, body(): incoming = lax.all_to_all(latitude, 'order', 0, 0, tiled=True)  5.54 us
  transfers between devices with their start and end apart: 16, of which 0 were waited for; matrix products, arithmetic and copies ran while one was open for 1% of the time, Pallas kernels for 5%

profile of v4, /device:TPU:0, one launch (start us, length us, event | category | flops | bytes accessed | tf_op | source)
XLA Modules:
  0.0 151.1 jit_solution(2721490145709846578)
XLA Ops:
  0.6 0.8 dynamic_slice.8
  1.4 0.1 reshape.102
  1.5 0.7 slice_reduce_fusion
  2.2 0.1 pad_add_fusion.place
  2.3 1.1 copy-done
  3.4 12.4 %legendre_synthesis.1 = (bf16[8,24,64,128]{3,2,1,0:T(8,128)(2,1)}, bf16[2,528,256]{2,1,0:T(8,128)(2,1)S(1)}) custom-call(s32[2]{0:T(128)S(1)} %pad_add_fusion.place, s32[32]{0:T(128)S(1)} %get-tuple-element.88.lower, bf16[3,2,2,64,512]{4,3,2,1,0:T(8,128)(2,1)S(1)} %copy-done, bf16[3,2,2,64,512]{4,3,2,1,0:T(8,128)(2,1)} %vor.1, ...), custom_call_target="tpu_custom_call" | custom-call | flops 1600000000 | bytes 15728640 | tf_op jit(solution)/shard_map/legendre_synthesis/pallas_call | solution.py:117
  15.9 0.0 copy-start.3
  15.9 0.0 copy-start.39
  15.9 0.0 copy-start.38
  15.9 5.5 %all-to-all-start = ((bf16[8,24,64,128]{3,2,1,0:T(8,128)(2,1)}), bf16[8,24,64,128]{3,2,1,0:T(8,128)(2,1)}, u32[]{:S(2)}, u32[]{:S(2)}) async-start(bf16[8,24,64,128]{3,2,1,0:T(8,128)(2,1)} %get-tuple-element.45), calls=%async_computation | async-start | bytes 6291456 | tf_op jit(solution)/shard_map/all_to_all | solution.py:488
  21.4 0.2 reduce-window.9
  21.6 0.2 compare_reduce_fusion
  21.9 1.8 %state_to_send.1 = (bf16[112,512]{1,0:T(8,128)(2,1)S(1)}, bf16[112,512]{1,0:T(8,128)(2,1)S(1)}, bf16[112,512]{1,0:T(8,128)(2,1)S(1)}, bf16[112,512]{1,0:T(8,128)...) custom-call(s32[2]{0:T(128)S(1)} %pad_add_fusion.place, ...), custom_call_target="tpu_custom_call" | custom-call | flops 1000000 | bytes 4194304 | tf_op jit(solution)/shard_map/state_to_send/pallas_call | solution.py:174
  23.7 0.6 copy-done.4
  24.3 1.5 collective-permute-start
  25.8 2.7 %collective-permute-start.1 = (bf16[112,512]{1,0:T(8,128)(2,1)S(1)}, bf16[112,512]{1,0:T(8,128)(2,1)S(1)}, u32[]{:S(2)}, u32[]{:S(2)}) collective-permute-start(bf16[112,512]{1,0:T(8,128)(2,1)S(1)} %get-tuple-element.50), channel_id=1, source_target_pairs={{0,16},{1,65},{2,18},{3,67},{4,20},{5,69},{6,22},{7,71},{8,24},{9,... | collective-permute-start | bytes 344072 | tf_op jit(solution)/shard_map/ppermute | solution.py:500
  28.6 0.5 collective-permute-start.2
  29.0 1.6 %collective-permute-start.3 = (bf16[112,512]{1,0:T(8,128)(2,1)S(1)}, bf16[112,512]{1,0:T(8,128)(2,1)S(1)}, u32[]{:S(2)}, u32[]{:S(2)}) collective-permute-start(bf16[112,512]{1,0:T(8,128)(2,1)S(1)} %get-tuple-element.52), channel_id=1, source_target_pairs={{0,32},{1,9},{2,34},{3,11},{4,36},{5,13},{6,38},{7,15},{8,40},{9,1... | collective-permute-start | bytes 344072 | tf_op jit(solution)/shard_map/ppermute | solution.py:500
  30.6 0.2 collective-permute-start.4
  30.8 0.1 reshape.106
  30.9 0.0 collective-permute-done.refs_1_
  31.0 5.0 %collective-permute-start.5 = (bf16[112,512]{1,0:T(8,128)(2,1)S(1)}, bf16[112,512]{1,0:T(8,128)(2,1)S(1)}, u32[]{:S(2)}, u32[]{:S(2)}) collective-permute-start(bf16[112,512]{1,0:T(8,128)(2,1)S(1)} %get-tuple-element.54), channel_id=1, source_target_pairs={{0,48},{1,73},{2,50},{3,75},{4,52},{5,77},{6,54},{7,79},{8,56},{9,... | collective-permute-start | bytes 344072 | tf_op jit(solution)/shard_map/ppermute | solution.py:500
  36.0 0.0 collective-permute-done.1.refs_2_
  36.0 0.4 collective-permute-start.6
  36.4 0.0 collective-permute-done.2.refs_3_
  36.4 3.2 %collective-permute-start.7 = (bf16[112,512]{1,0:T(8,128)(2,1)S(1)}, bf16[112,512]{1,0:T(8,128)(2,1)S(1)}, u32[]{:S(2)}, u32[]{:S(2)}) collective-permute-start(bf16[112,512]{1,0:T(8,128)(2,1)S(1)} %get-tuple-element.56), channel_id=1, source_target_pairs={{0,64},{1,17},{2,66},{3,19},{4,68},{5,21},{6,70},{7,23},{8,72},{9,... | collective-permute-start | bytes 344072 | tf_op jit(solution)/shard_map/ppermute | solution.py:500
  39.6 0.0 collective-permute-done.3.refs_4_
  39.6 0.4 collective-permute-start.8
  40.0 0.0 collective-permute-done.4.refs_5_
  40.0 6.2 %collective-permute-start.9 = (bf16[112,512]{1,0:T(8,128)(2,1)S(1)}, bf16[112,512]{1,0:T(8,128)(2,1)S(1)}, u32[]{:S(2)}, u32[]{:S(2)}) collective-permute-start(bf16[112,512]{1,0:T(8,128)(2,1)S(1)} %get-tuple-element.58), channel_id=1, source_target_pairs={{0,80},{1,81},{2,82},{3,83},{4,84},{5,85},{6,86},{7,87},{8,88},{9,... | collective-permute-start | bytes 344072 | tf_op jit(solution)/shard_map/ppermute | solution.py:500
  46.2 0.2 broadcast_add_fusion
  46.4 0.3 add.72.targets
  46.7 0.8 dynamic-slice_reduce_fusion.lower
  47.5 0.0 collective-permute-done.5.refs_6_
  47.5 1.1 collective-permute-start.10
  48.6 0.0 collective-permute-done.6.refs_7_
  48.6 2.2 %collective-permute-start.11 = (bf16[112,512]{1,0:T(8,128)(2,1)}, bf16[112,512]{1,0:T(8,128)(2,1)S(1)}, u32[]{:S(2)}, u32[]{:S(2)}) collective-permute-start(bf16[112,512]{1,0:T(8,128)(2,1)} %get-tuple-element.60), channel_id=1, source_target_pairs={{0,96},{1,25},{2,98},{3,27},{4,100},{5,29},{6,102},{7,31},{8,104},... | collective-permute-start | bytes 344072 | tf_op jit(solution)/shard_map/ppermute | solution.py:500
  50.8 0.0 collective-permute-done.8.refs_9_
  50.9 6.3 %collective-permute-start.13 = (bf16[112,512]{1,0:T(8,128)(2,1)S(1)}, bf16[112,512]{1,0:T(8,128)(2,1)S(1)}, u32[]{:S(2)}, u32[]{:S(2)}) collective-permute-start(bf16[112,512]{1,0:T(8,128)(2,1)S(1)} %get-tuple-element.62), channel_id=1, source_target_pairs={{0,112},{1,89},{2,114},{3,91},{4,116},{5,93},{6,118},{7,95},{8,120... | collective-permute-start | bytes 344072 | tf_op jit(solution)/shard_map/ppermute | solution.py:500
  57.2 0.0 collective-permute-done.9.refs_10_
  57.2 0.9 collective-permute-start.14
  58.1 1.6 %copy-done.40 = bf16[1024,1024]{1,0:T(8,128)(2,1)S(1)} copy-done((bf16[1024,1024]{1,0:T(8,128)(2,1)S(1)}, bf16[1024,1024]{1,0:T(8,128)(2,1)}, u32[]{:S(2)}) %copy-start.40) | copy-done | bytes 2097176
  59.7 1.6 %copy-done.41 = bf16[1024,1024]{1,0:T(8,128)(2,1)S(1)} copy-done((bf16[1024,1024]{1,0:T(8,128)(2,1)S(1)}, bf16[1024,1024]{1,0:T(8,128)(2,1)}, u32[]{:S(2)}) %copy-start.41) | copy-done | bytes 2097176
  61.3 4.1 %make_tables.1 = (bf16[1024,1024]{1,0:T(8,128)(2,1)S(1)}, bf16[1024,1024]{1,0:T(8,128)(2,1)S(1)}, bf16[4,256,512]{2,1,0:T(8,128)(2,1)S(1)}) custom-call(s32[2]{0:T(128)S(1)} %dynamic-slice_reduce_fusion.lower, s32[1,512]{1,0:T(1,128)S(1)} %bitcast.12, s32[1,1024]{1,0:T(1,128)S(1)} %add.72.targets, bf16[1024,1024]{1,0:T(8,128)(2,1)S(1)} %copy-done.41, ...), custom_call_target="tpu_custom_call" | custom-call | flops 4000000000 | bytes 12582912 | tf_op jit(solution)/shard_map/make_tables/pallas_call | solution.py:272
  65.5 1.4 copy-done.42
  66.8 1.3 copy-done.44
  68.2 0.0 collective-permute-done.10.refs_11_
  68.2 0.0 copy-start.28
  68.3 0.0 collective-permute-done.12.refs_13_
  68.3 0.5 copy-done.26
  68.9 0.0 copy-done.28
  68.9 0.0 copy-done.30
  68.9 0.0 copy-done.32
  69.0 0.0 copy-done.34
  69.0 2.0 %solve_factors.1.factors = f32[3,64,512]{2,1,0:T(8,128)} custom-call(s32[2]{0:T(128)} %copy-done.36, bf16[112,512]{1,0:T(8,128)(2,1)} %copy-done.4, bf16[112,512]{1,0:T(8,128)(2,1)} %copy-done.6, bf16[112,512]{1,0:T(8,128)(2,1)} %copy-done.8, bf16[112,512]{1,0:T(8,128)(2,1)} %copy-done.10, bf16[112,512]{1,0:T(8,128)(2,1)} %copy-done.12, ...), custom_call_target="tpu_custom_call" | custom-call | flops 1000000 | bytes 1048576 | tf_op jit(solution)/shard_map/solve_factors/pallas_call | solution.py:327
  71.1 1.6 %copy-done.43 = bf16[1024,1024]{1,0:T(8,128)(2,1)S(1)} copy-done((bf16[1024,1024]{1,0:T(8,128)(2,1)S(1)}, bf16[1024,1024]{1,0:T(8,128)(2,1)}, u32[]{:S(2)}) %copy-start.43) | copy-done | bytes 2097176
  72.7 1.6 %copy-done.45 = bf16[1024,1024]{1,0:T(8,128)(2,1)S(1)} copy-done((bf16[1024,1024]{1,0:T(8,128)(2,1)S(1)}, bf16[1024,1024]{1,0:T(8,128)(2,1)}, u32[]{:S(2)}) %copy-start.45) | copy-done | bytes 2097176
  74.3 8.3 %grid_stage.1 = bf16[1024,768]{1,0:T(8,128)(2,1)S(1)} custom-call(bf16[8,24,64,128]{3,2,1,0:T(8,128)(2,1)} %all-to-all-done.lat, bf16[1024,1024]{1,0:T(8,128)(2,1)S(1)} %copy-done.43, bf16[1024,1024]{1,0:T(8,128)(2,1)S(1)} %copy-done.45, f32[1,128]{1,0:T(1,128)S(1)} %sine_multiply_fusion.weight), custom_call_target="tpu_custom_call" | custom-call | flops 4800000000 | bytes 9437184 | tf_op jit(solution)/shard_map/grid_stage/pallas_call | solution.py:227
  82.6 0.0 copy-start.2
  82.7 0.0 copy-start.29
  82.8 34.0 %all_to_all.15 = bf16[128,8,768]{2,1,0:T(8,128)(2,1)S(1)} all-to-all(bf16[128,8,768]{2,1,0:T(8,128)(2,1)S(1)} %bitcast.11), channel_id=1, replica_groups=mesh['shell'=16,'order'=8] {'shell','order'}, dimensions={0} | all-to-all | bytes 3145728 | tf_op jit(solution)/shard_map/all_to_all | solution.py:508
  116.9 5.9 %analysis_and_solve.1 = bf16[16,96,512]{2,1,0:T(8,128)(2,1)S(1)} custom-call(s32[2]{0:T(128)S(1)} %copy-done.37, s32[2]{0:T(128)S(1)} %dynamic-slice_reduce_fusion.lower, bf16[1024,768]{1,0:T(8,128)(2,1)S(1)} %bitcast.10, bf16[4,256,512]{2,1,0:T(8,128)(2,1)S(1)} %get-tuple-element.70.table, f32[3,64,512]{2,1,0:T(8,128)S(1)} %copy-done.2, ...), custom_call_target="tpu_custom_call" | custom-call | flops 900000000 | bytes 6291456 | tf_op jit(solution)/shard_map/analysis_and_solve/pallas_call | solution.py:402
  122.8 25.4 %all_to_all.16.got = bf16[16,96,512]{2,1,0:T(8,128)(2,1)S(1)} all-to-all(bf16[16,96,512]{2,1,0:T(8,128)(2,1)S(1)} %analysis_and_solve.1), channel_id=1, replica_groups=mesh['shell'=16,'order'=8] {'shell'}, dimensions={0} | all-to-all | bytes 3145728 | tf_op jit(solution)/shard_map/all_to_all | solution.py:512
  148.3 2.8 %unpack_solution.1 = (f32[3,2,2,64,512]{4,3,2,1,0:T(8,128)}, f32[3,2,2,64,512]{4,3,2,1,0:T(8,128)}) custom-call(bf16[16,96,512]{2,1,0:T(8,128)(2,1)S(1)} %all_to_all.16.got), custom_call_target="tpu_custom_call" | custom-call | flops 1000000 | bytes 5242880 | tf_op jit(solution)/shard_map/unpack_solution/pallas_call | solution.py:441
  (89 shorter events, 0.3 us)
Async XLA Ops:
  2.3 19.5 %copy-start.36 = (s32[2]{0:T(128)}, s32[2]{0:T(128)S(1)}, u32[]{:S(2)}) copy-start(s32[2]{0:T(128)S(1)} %pad_add_fusion.place) | copy-start | bytes 28
  2.3 1.1 copy-start
  15.8 5.6 %copy-start.47 = (s32[4]{0:T(128)S(1)}, s32[4]{0:T(128)}, u32[]{:S(2)}) copy-start(s32[4]{0:T(128)} %param.19) | copy-start | bytes 52
  15.8 6.0 %copy-start.46 = (f32[2,2]{1,0:T(2,128)S(1)}, f32[2,2]{1,0:T(2,128)}, u32[]{:S(2)}) copy-start(f32[2,2]{1,0:T(2,128)} %param.20) | copy-start | bytes 52
  15.8 6.0 %copy-start.1 = (bf16[3,2,2,64,512]{4,3,2,1,0:T(8,128)(2,1)S(1)}, bf16[3,2,2,64,512]{4,3,2,1,0:T(8,128)(2,1)}, u32[]{:S(2)}) copy-start(bf16[3,2,2,64,512]{4,3,2,1,0:T(8,128)(2,1)} %vel.2) | copy-start | bytes 2359300
  15.9 6.0 %copy-start.3 = (bf16[3,2,2,64,512]{4,3,2,1,0:T(8,128)(2,1)S(1)}, bf16[3,2,2,64,512]{4,3,2,1,0:T(8,128)(2,1)}, u32[]{:S(2)}) copy-start(bf16[3,2,2,64,512]{4,3,2,1,0:T(8,128)(2,1)} %pot) | copy-start | bytes 2359300
  15.9 6.0 %copy-start.39 = (f32[2,2]{1,0:T(2,128)S(1)}, f32[2,2]{1,0:T(2,128)}, u32[]{:S(2)}) copy-start(f32[2,2]{1,0:T(2,128)} %angular.1) | copy-start | bytes 52
  15.9 14.9 %copy-start.38 = (s32[512]{0:T(512)S(1)}, s32[512]{0:T(512)}, u32[]{:S(2)}) copy-start(s32[512]{0:T(512)} %param.17) | copy-start | bytes 6148
  15.9 55.2 %all-to-all-start = ((bf16[8,24,64,128]{3,2,1,0:T(8,128)(2,1)}), bf16[8,24,64,128]{3,2,1,0:T(8,128)(2,1)}, u32[]{:S(2)}, u32[]{:S(2)}) async-start(bf16[8,24,64,128]{3,2,1,0:T(8,128)(2,1)} %get-tuple-element.45), calls=%async_computation | async-start | bytes 6291456 | tf_op jit(solution)/shard_map/all_to_all | solution.py:488
  23.7 0.6 copy-start.4
  24.3 6.6 %collective-permute-start = (bf16[112,512]{1,0:T(8,128)(2,1)S(1)}, bf16[112,512]{1,0:T(8,128)(2,1)S(1)}, u32[]{:S(2)}, u32[]{:S(2)}) collective-permute-start(bf16[112,512]{1,0:T(8,128)(2,1)S(1)} %get-tuple-element.49), channel_id=1, source_target_pairs={{0,8},{1,33},{2,10},{3,35},{4,12},{5,37},{6,14},{7,39},{8,0},{9,41... | collective-permute-start | bytes 344072 | tf_op jit(solution)/shard_map/ppermute | solution.py:500
  25.8 10.2 %collective-permute-start.1 = (bf16[112,512]{1,0:T(8,128)(2,1)S(1)}, bf16[112,512]{1,0:T(8,128)(2,1)S(1)}, u32[]{:S(2)}, u32[]{:S(2)}) collective-permute-start(bf16[112,512]{1,0:T(8,128)(2,1)S(1)} %get-tuple-element.50), channel_id=1, source_target_pairs={{0,16},{1,65},{2,18},{3,67},{4,20},{5,69},{6,22},{7,71},{8,24},{9,... | collective-permute-start | bytes 344072 | tf_op jit(solution)/shard_map/ppermute | solution.py:500
  28.6 7.8 %collective-permute-start.2 = (bf16[112,512]{1,0:T(8,128)(2,1)S(1)}, bf16[112,512]{1,0:T(8,128)(2,1)S(1)}, u32[]{:S(2)}, u32[]{:S(2)}) collective-permute-start(bf16[112,512]{1,0:T(8,128)(2,1)S(1)} %get-tuple-element.51), channel_id=1, source_target_pairs={{0,24},{1,97},{2,26},{3,99},{4,28},{5,101},{6,30},{7,103},{8,16},{... | collective-permute-start | bytes 344072 | tf_op jit(solution)/shard_map/ppermute | solution.py:500
  29.0 10.5 %collective-permute-start.3 = (bf16[112,512]{1,0:T(8,128)(2,1)S(1)}, bf16[112,512]{1,0:T(8,128)(2,1)S(1)}, u32[]{:S(2)}, u32[]{:S(2)}) collective-permute-start(bf16[112,512]{1,0:T(8,128)(2,1)S(1)} %get-tuple-element.52), channel_id=1, source_target_pairs={{0,32},{1,9},{2,34},{3,11},{4,36},{5,13},{6,38},{7,15},{8,40},{9,1... | collective-permute-start | bytes 344072 | tf_op jit(solution)/shard_map/ppermute | solution.py:500
  30.6 9.4 %collective-permute-start.4 = (bf16[112,512]{1,0:T(8,128)(2,1)S(1)}, bf16[112,512]{1,0:T(8,128)(2,1)S(1)}, u32[]{:S(2)}, u32[]{:S(2)}) collective-permute-start(bf16[112,512]{1,0:T(8,128)(2,1)S(1)} %get-tuple-element.53), channel_id=1, source_target_pairs={{0,40},{1,41},{2,42},{3,43},{4,44},{5,45},{6,46},{7,47},{8,32},{9,... | collective-permute-start | bytes 344072 | tf_op jit(solution)/shard_map/ppermute | solution.py:500
  30.9 34.4 %copy-start.6 = (bf16[112,512]{1,0:T(8,128)(2,1)}, bf16[112,512]{1,0:T(8,128)(2,1)S(1)}, u32[]{:S(2)}) copy-start(bf16[112,512]{1,0:T(8,128)(2,1)S(1)} %collective-permute-done.refs_1_) | copy-start | bytes 344068
  31.0 16.5 %collective-permute-start.5 = (bf16[112,512]{1,0:T(8,128)(2,1)S(1)}, bf16[112,512]{1,0:T(8,128)(2,1)S(1)}, u32[]{:S(2)}, u32[]{:S(2)}) collective-permute-start(bf16[112,512]{1,0:T(8,128)(2,1)S(1)} %get-tuple-element.54), channel_id=1, source_target_pairs={{0,48},{1,73},{2,50},{3,75},{4,52},{5,77},{6,54},{7,79},{8,56},{9,... | collective-permute-start | bytes 344072 | tf_op jit(solution)/shard_map/ppermute | solution.py:500
  36.0 29.4 %copy-start.8 = (bf16[112,512]{1,0:T(8,128)(2,1)}, bf16[112,512]{1,0:T(8,128)(2,1)S(1)}, u32[]{:S(2)}) copy-start(bf16[112,512]{1,0:T(8,128)(2,1)S(1)} %collective-permute-done.1.refs_2_) | copy-start | bytes 344068
  36.0 12.6 %collective-permute-start.6 = (bf16[112,512]{1,0:T(8,128)(2,1)S(1)}, bf16[112,512]{1,0:T(8,128)(2,1)S(1)}, u32[]{:S(2)}, u32[]{:S(2)}) collective-permute-start(bf16[112,512]{1,0:T(8,128)(2,1)S(1)} %get-tuple-element.55), channel_id=1, source_target_pairs={{0,56},{1,105},{2,58},{3,107},{4,60},{5,109},{6,62},{7,111},{8,48}... | collective-permute-start | bytes 344072 | tf_op jit(solution)/shard_map/ppermute | solution.py:500
  36.4 29.0 %copy-start.10 = (bf16[112,512]{1,0:T(8,128)(2,1)}, bf16[112,512]{1,0:T(8,128)(2,1)S(1)}, u32[]{:S(2)}) copy-start(bf16[112,512]{1,0:T(8,128)(2,1)S(1)} %collective-permute-done.2.refs_3_) | copy-start | bytes 344068
  36.4 14.5 %collective-permute-start.7 = (bf16[112,512]{1,0:T(8,128)(2,1)S(1)}, bf16[112,512]{1,0:T(8,128)(2,1)S(1)}, u32[]{:S(2)}, u32[]{:S(2)}) collective-permute-start(bf16[112,512]{1,0:T(8,128)(2,1)S(1)} %get-tuple-element.56), channel_id=1, source_target_pairs={{0,64},{1,17},{2,66},{3,19},{4,68},{5,21},{6,70},{7,23},{8,72},{9,... | collective-permute-start | bytes 344072 | tf_op jit(solution)/shard_map/ppermute | solution.py:500
  39.6 25.8 %copy-start.12 = (bf16[112,512]{1,0:T(8,128)(2,1)}, bf16[112,512]{1,0:T(8,128)(2,1)S(1)}, u32[]{:S(2)}) copy-start(bf16[112,512]{1,0:T(8,128)(2,1)S(1)} %collective-permute-done.3.refs_4_) | copy-start | bytes 344068
  39.6 11.3 %collective-permute-start.8 = (bf16[112,512]{1,0:T(8,128)(2,1)S(1)}, bf16[112,512]{1,0:T(8,128)(2,1)S(1)}, u32[]{:S(2)}, u32[]{:S(2)}) collective-permute-start(bf16[112,512]{1,0:T(8,128)(2,1)S(1)} %get-tuple-element.57), channel_id=1, source_target_pairs={{0,72},{1,49},{2,74},{3,51},{4,76},{5,53},{6,78},{7,55},{8,64},{9,... | collective-permute-start | bytes 344072 | tf_op jit(solution)/shard_map/ppermute | solution.py:500
  40.0 25.4 %copy-start.14 = (bf16[112,512]{1,0:T(8,128)(2,1)}, bf16[112,512]{1,0:T(8,128)(2,1)S(1)}, u32[]{:S(2)}) copy-start(bf16[112,512]{1,0:T(8,128)(2,1)S(1)} %collective-permute-done.4.refs_5_) | copy-start | bytes 344068
  40.0 17.2 %collective-permute-start.9 = (bf16[112,512]{1,0:T(8,128)(2,1)S(1)}, bf16[112,512]{1,0:T(8,128)(2,1)S(1)}, u32[]{:S(2)}, u32[]{:S(2)}) collective-permute-start(bf16[112,512]{1,0:T(8,128)(2,1)S(1)} %get-tuple-element.58), channel_id=1, source_target_pairs={{0,80},{1,81},{2,82},{3,83},{4,84},{5,85},{6,86},{7,87},{8,88},{9,... | collective-permute-start | bytes 344072 | tf_op jit(solution)/shard_map/ppermute | solution.py:500
  47.5 18.0 %copy-start.16 = (bf16[112,512]{1,0:T(8,128)(2,1)}, bf16[112,512]{1,0:T(8,128)(2,1)S(1)}, u32[]{:S(2)}) copy-start(bf16[112,512]{1,0:T(8,128)(2,1)S(1)} %collective-permute-done.5.refs_6_) | copy-start | bytes 344068
  47.5 20.7 %collective-permute-start.10 = (bf16[112,512]{1,0:T(8,128)(2,1)}, bf16[112,512]{1,0:T(8,128)(2,1)S(1)}, u32[]{:S(2)}, u32[]{:S(2)}) collective-permute-start(bf16[112,512]{1,0:T(8,128)(2,1)} %get-tuple-element.59), channel_id=1, source_target_pairs={{0,88},{1,113},{2,90},{3,115},{4,92},{5,117},{6,94},{7,119},{8,80}... | collective-permute-start | bytes 344072 | tf_op jit(solution)/shard_map/ppermute | solution.py:500
  48.6 16.8 %copy-start.18 = (bf16[112,512]{1,0:T(8,128)(2,1)}, bf16[112,512]{1,0:T(8,128)(2,1)S(1)}, u32[]{:S(2)}) copy-start(bf16[112,512]{1,0:T(8,128)(2,1)S(1)} %collective-permute-done.6.refs_7_) | copy-start | bytes 344068
  48.6 19.6 %collective-permute-start.11 = (bf16[112,512]{1,0:T(8,128)(2,1)}, bf16[112,512]{1,0:T(8,128)(2,1)S(1)}, u32[]{:S(2)}, u32[]{:S(2)}) collective-permute-start(bf16[112,512]{1,0:T(8,128)(2,1)} %get-tuple-element.60), channel_id=1, source_target_pairs={{0,96},{1,25},{2,98},{3,27},{4,100},{5,29},{6,102},{7,31},{8,104},... | collective-permute-start | bytes 344072 | tf_op jit(solution)/shard_map/ppermute | solution.py:500
  50.8 14.6 %copy-start.20 = (bf16[112,512]{1,0:T(8,128)(2,1)}, bf16[112,512]{1,0:T(8,128)(2,1)S(1)}, u32[]{:S(2)}) copy-start(bf16[112,512]{1,0:T(8,128)(2,1)S(1)} %collective-permute-done.7.refs_8_) | copy-start | bytes 344068
  50.8 17.4 %collective-permute-start.12 = (bf16[112,512]{1,0:T(8,128)(2,1)}, bf16[112,512]{1,0:T(8,128)(2,1)S(1)}, u32[]{:S(2)}, u32[]{:S(2)}) collective-permute-start(bf16[112,512]{1,0:T(8,128)(2,1)} %get-tuple-element.61), channel_id=1, source_target_pairs={{0,104},{1,57},{2,106},{3,59},{4,108},{5,61},{6,110},{7,63},{8,96}... | collective-permute-start | bytes 344072 | tf_op jit(solution)/shard_map/ppermute | solution.py:500
  50.8 14.6 %copy-start.22 = (bf16[112,512]{1,0:T(8,128)(2,1)}, bf16[112,512]{1,0:T(8,128)(2,1)S(1)}, u32[]{:S(2)}) copy-start(bf16[112,512]{1,0:T(8,128)(2,1)S(1)} %collective-permute-done.8.refs_9_) | copy-start | bytes 344068
  50.9 17.4 %collective-permute-start.13 = (bf16[112,512]{1,0:T(8,128)(2,1)S(1)}, bf16[112,512]{1,0:T(8,128)(2,1)S(1)}, u32[]{:S(2)}, u32[]{:S(2)}) collective-permute-start(bf16[112,512]{1,0:T(8,128)(2,1)S(1)} %get-tuple-element.62), channel_id=1, source_target_pairs={{0,112},{1,89},{2,114},{3,91},{4,116},{5,93},{6,118},{7,95},{8,120... | collective-permute-start | bytes 344072 | tf_op jit(solution)/shard_map/ppermute | solution.py:500
  57.2 8.3 %copy-start.24 = (bf16[112,512]{1,0:T(8,128)(2,1)}, bf16[112,512]{1,0:T(8,128)(2,1)S(1)}, u32[]{:S(2)}) copy-start(bf16[112,512]{1,0:T(8,128)(2,1)S(1)} %collective-permute-done.9.refs_10_) | copy-start | bytes 344068
  57.2 11.1 %collective-permute-start.14 = (bf16[112,512]{1,0:T(8,128)(2,1)S(1)}, bf16[112,512]{1,0:T(8,128)(2,1)S(1)}, u32[]{:S(2)}, u32[]{:S(2)}) collective-permute-start(bf16[112,512]{1,0:T(8,128)(2,1)S(1)} %get-tuple-element.63), channel_id=1, source_target_pairs={{0,120},{1,121},{2,122},{3,123},{4,124},{5,125},{6,126},{7,127},{8... | collective-permute-start | bytes 344072 | tf_op jit(solution)/shard_map/ppermute | solution.py:500
  58.1 1.6 %copy-start.40 = (bf16[1024,1024]{1,0:T(8,128)(2,1)S(1)}, bf16[1024,1024]{1,0:T(8,128)(2,1)}, u32[]{:S(2)}) copy-start(bf16[1024,1024]{1,0:T(8,128)(2,1)} %constant.46.clone.natural_a) | copy-start | bytes 6291460
  59.7 1.6 %copy-start.41 = (bf16[1024,1024]{1,0:T(8,128)(2,1)S(1)}, bf16[1024,1024]{1,0:T(8,128)(2,1)}, u32[]{:S(2)}) copy-start(bf16[1024,1024]{1,0:T(8,128)(2,1)} %constant.45.clone.natural_s) | copy-start | bytes 6291460
  65.5 1.4 copy-start.42
  66.8 1.3 copy-start.44
  68.2 0.6 copy-start.26
  68.2 0.7 copy-start.28
  68.3 0.7 copy-start.30
  68.3 0.7 copy-start.32
  68.3 0.7 copy-start.34
  71.1 1.6 %copy-start.43 = (bf16[1024,1024]{1,0:T(8,128)(2,1)S(1)}, bf16[1024,1024]{1,0:T(8,128)(2,1)}, u32[]{:S(2)}) copy-start(bf16[1024,1024]{1,0:T(8,128)(2,1)} %copy-done.42) | copy-start | bytes 6291460
  72.7 1.6 %copy-start.45 = (bf16[1024,1024]{1,0:T(8,128)(2,1)S(1)}, bf16[1024,1024]{1,0:T(8,128)(2,1)}, u32[]{:S(2)}) copy-start(bf16[1024,1024]{1,0:T(8,128)(2,1)} %copy-done.44) | copy-start | bytes 6291460
  82.6 34.2 %copy-start.2 = (f32[3,64,512]{2,1,0:T(8,128)S(1)}, f32[3,64,512]{2,1,0:T(8,128)}, u32[]{:S(2)}) copy-start(f32[3,64,512]{2,1,0:T(8,128)} %solve_factors.1.factors) | copy-start | bytes 1179652
  82.6 34.1 %copy-start.5 = (bf16[112,512]{1,0:T(8,128)(2,1)S(1)}, bf16[112,512]{1,0:T(8,128)(2,1)}, u32[]{:S(2)}) copy-start(bf16[112,512]{1,0:T(8,128)(2,1)} %copy-done.4) | copy-start | bytes 344068
  82.6 34.1 %copy-start.7 = (bf16[112,512]{1,0:T(8,128)(2,1)S(1)}, bf16[112,512]{1,0:T(8,128)(2,1)}, u32[]{:S(2)}) copy-start(bf16[112,512]{1,0:T(8,128)(2,1)} %copy-done.6) | copy-start | bytes 344068
  82.6 34.1 %copy-start.9 = (bf16[112,512]{1,0:T(8,128)(2,1)S(1)}, bf16[112,512]{1,0:T(8,128)(2,1)}, u32[]{:S(2)}) copy-start(bf16[112,512]{1,0:T(8,128)(2,1)} %copy-done.8) | copy-start | bytes 344068
  82.7 34.1 %copy-start.11 = (bf16[112,512]{1,0:T(8,128)(2,1)S(1)}, bf16[112,512]{1,0:T(8,128)(2,1)}, u32[]{:S(2)}) copy-start(bf16[112,512]{1,0:T(8,128)(2,1)} %copy-done.10) | copy-start | bytes 344068
  82.7 34.1 %copy-start.13 = (bf16[112,512]{1,0:T(8,128)(2,1)S(1)}, bf16[112,512]{1,0:T(8,128)(2,1)}, u32[]{:S(2)}) copy-start(bf16[112,512]{1,0:T(8,128)(2,1)} %copy-done.12) | copy-start | bytes 344068
  82.7 34.1 %copy-start.15 = (bf16[112,512]{1,0:T(8,128)(2,1)S(1)}, bf16[112,512]{1,0:T(8,128)(2,1)}, u32[]{:S(2)}) copy-start(bf16[112,512]{1,0:T(8,128)(2,1)} %copy-done.14) | copy-start | bytes 344068
  82.7 34.1 %copy-start.17 = (bf16[112,512]{1,0:T(8,128)(2,1)S(1)}, bf16[112,512]{1,0:T(8,128)(2,1)}, u32[]{:S(2)}) copy-start(bf16[112,512]{1,0:T(8,128)(2,1)} %copy-done.16) | copy-start | bytes 344068
  82.7 34.1 %copy-start.19 = (bf16[112,512]{1,0:T(8,128)(2,1)S(1)}, bf16[112,512]{1,0:T(8,128)(2,1)}, u32[]{:S(2)}) copy-start(bf16[112,512]{1,0:T(8,128)(2,1)} %copy-done.18) | copy-start | bytes 344068
  82.7 34.1 %copy-start.21 = (bf16[112,512]{1,0:T(8,128)(2,1)S(1)}, bf16[112,512]{1,0:T(8,128)(2,1)}, u32[]{:S(2)}) copy-start(bf16[112,512]{1,0:T(8,128)(2,1)} %copy-done.20) | copy-start | bytes 344068
  82.7 34.1 %copy-start.23 = (bf16[112,512]{1,0:T(8,128)(2,1)S(1)}, bf16[112,512]{1,0:T(8,128)(2,1)}, u32[]{:S(2)}) copy-start(bf16[112,512]{1,0:T(8,128)(2,1)} %copy-done.22) | copy-start | bytes 344068
  82.7 34.1 %copy-start.25 = (bf16[112,512]{1,0:T(8,128)(2,1)S(1)}, bf16[112,512]{1,0:T(8,128)(2,1)}, u32[]{:S(2)}) copy-start(bf16[112,512]{1,0:T(8,128)(2,1)} %copy-done.24) | copy-start | bytes 344068
  82.7 34.1 %copy-start.27 = (bf16[112,512]{1,0:T(8,128)(2,1)S(1)}, bf16[112,512]{1,0:T(8,128)(2,1)}, u32[]{:S(2)}) copy-start(bf16[112,512]{1,0:T(8,128)(2,1)} %copy-done.26) | copy-start | bytes 344068
  82.7 34.1 %copy-start.29 = (bf16[112,512]{1,0:T(8,128)(2,1)S(1)}, bf16[112,512]{1,0:T(8,128)(2,1)}, u32[]{:S(2)}) copy-start(bf16[112,512]{1,0:T(8,128)(2,1)} %copy-done.28) | copy-start | bytes 344068
  82.8 34.1 %copy-start.31 = (bf16[112,512]{1,0:T(8,128)(2,1)S(1)}, bf16[112,512]{1,0:T(8,128)(2,1)}, u32[]{:S(2)}) copy-start(bf16[112,512]{1,0:T(8,128)(2,1)} %copy-done.30) | copy-start | bytes 344068
  82.8 34.1 %copy-start.33 = (bf16[112,512]{1,0:T(8,128)(2,1)S(1)}, bf16[112,512]{1,0:T(8,128)(2,1)}, u32[]{:S(2)}) copy-start(bf16[112,512]{1,0:T(8,128)(2,1)} %copy-done.32) | copy-start | bytes 344068
  82.8 34.1 %copy-start.35 = (bf16[112,512]{1,0:T(8,128)(2,1)S(1)}, bf16[112,512]{1,0:T(8,128)(2,1)}, u32[]{:S(2)}) copy-start(bf16[112,512]{1,0:T(8,128)(2,1)} %copy-done.34) | copy-start | bytes 344068
  82.8 34.1 %copy-start.37 = (s32[2]{0:T(128)S(1)}, s32[2]{0:T(128)}, u32[]{:S(2)}) copy-start(s32[2]{0:T(128)} %copy-done.36) | copy-start | bytes 28

commit v5 on v4

--- a/solution.py
+++ b/solution.py
@@ -27,9 +27,9 @@
     return synthesis.T.astype(jnp.bfloat16), analysis.astype(jnp.bfloat16)
 
 
-def partner(place, odd, r):
+def partner(place, r):
     swapped = (r & 3) * 4 + r // 4
-    return place ^ jnp.where(odd == 1, swapped, r)
+    return place[0] ^ jnp.where((place[1] & 1) == 1, swapped, r)
 
 
 def load(ref, rows):
@@ -46,7 +46,7 @@
 CHUNK = 171
 
 
-def synthesis_kernel(place, lower, vel, vor, mag, cur, table, out, pairs, xs, ys, ts):
+def synthesis_kernel(place, orders, vel, vor, mag, cur, table, out, pairs, xs, ys, ts):
     step = pl.program_id(0)
     chunk = pl.program_id(1)
 
@@ -70,7 +70,7 @@
     sign_a = (1 - 2 * (r & 1)).astype(f32)
 
     def one_pair(i, _):
-        m = lower[step * 16 + i]
+        m = orders[place[1] * 64 + step * 32 + 2 * i]
         a = load(xs, pl.ds(2 * i, 48, stride=PITCH))
         b = load(xs, pl.ds(2 * i + 1, 48, stride=PITCH))
         rows = load(ts, pl.ds(i, L, stride=TABLE_PITCH)).astype(bf16)
@@ -112,7 +112,7 @@
             pairs[i, L : L + 16, :] = jnp.broadcast_to(last, (16, NH)).astype(bf16)
 
 
-def legendre_synthesis(place, lower, velocity, vorticity, magnetic, current, table):
+def legendre_synthesis(place, orders, velocity, vorticity, magnetic, current, table):
     field = pl.BlockSpec((3, 2, 2, 32, L), lambda g, q, place, low: (0, 0, 0, g, 0))
     return pl.pallas_call(
         synthesis_kernel,
@@ -135,10 +135,10 @@
             jax.ShapeDtypeStruct((8, 24, 64, 128), bf16),
             jax.ShapeDtypeStruct((2, L + 16, NH), bf16),
         ],
-        compiler_params=pltpu.CompilerParams(vmem_limit_bytes=52 * MIB),
+        compiler_params=pltpu.CompilerParams(vmem_limit_bytes=60 * MIB),
         cost_estimate=pl.CostEstimate(flops=int(1.6e9), bytes_accessed=15 * MIB, transcendentals=0),
         name="legendre_synthesis",
-    )(place, lower, velocity, vorticity, magnetic, current, table)
+    )(place, orders, velocity, vorticity, magnetic, current, table)
 
 
 def state_kernel(place, kappa, angular, vel, pot, *refs):
@@ -164,7 +164,7 @@
                 lines.append(jnp.where(lane < 128, high, jnp.where(lane < 256, mid, low)))
     extra = jnp.concatenate(lines + [jnp.zeros((8, L), f32)], axis=0).astype(bf16)
     for r in range(16):
-        outs[r][0:96, :] = scr[partner(place[0], place[1], r)].astype(bf16)
+        outs[r][0:96, :] = scr[partner(place, r)].astype(bf16)
         outs[r][96:112, :] = extra
 
 
@@ -236,13 +236,13 @@
         out_specs=pl.BlockSpec((rows, 768), lambda i: (jnp.maximum(i - 2, 0), 0)),
         out_shape=jax.ShapeDtypeStruct((1024, 768), bf16),
         scratch_shapes=[pltpu.VMEM((1024, 1536), bf16), pltpu.VMEM((1024, 768), bf16)],
-        compiler_params=pltpu.CompilerParams(vmem_limit_bytes=32 * MIB),
+        compiler_params=pltpu.CompilerParams(vmem_limit_bytes=60 * MIB),
         cost_estimate=pl.CostEstimate(flops=int(4.8e9), bytes_accessed=9 * MIB, transcendentals=0),
         name="grid_stage",
     )(lat, syn, ana, weight)
 
 
-def tables_kernel(lower, slots, targets, natural_s, natural_a, pairs, syn, ana, table_out, scr):
+def tables_kernel(place, orders, slots, targets, natural_s, natural_a, pairs, syn, ana, table_out, scr):
     ids = lax.broadcasted_iota(jnp.int32, (L, L), 0)
     pick = jnp.where(ids == slots[...], 1.0, 0.0).astype(bf16)
     for p in range(2):
@@ -255,7 +255,7 @@
     ).astype(bf16)
     l_row = lax.broadcasted_iota(jnp.int32, (1, L), 1)
     for i in range(2):
-        m = lower[i]
+        m = orders[place[1] * 64 + place[0] * 4 + 2 * i]
         scr[...] = pairs[i].astype(f32)
         a = jnp.transpose(scr[0:L, :])
         a = pltpu.roll(a, m, 1)
@@ -264,7 +264,7 @@
         table_out[2 * i + 1] = jnp.where(l_row >= L - 1 - m, b, 0.0).astype(bf16)
 
 
-def make_tables(own_lower, order_slots, pairs):
+def make_tables(place, order_slots, pairs):
     natural_s, natural_a = natural_tables()
     slots = order_slots.reshape(8, 16, 4).transpose(1, 0, 2)[..., None]
     targets = (slots + jnp.arange(2, dtype=jnp.int32) * L).reshape(1, 2 * L)
@@ -273,6 +273,7 @@
         tables_kernel,
         grid=(1,),
         in_specs=[
+            pl.BlockSpec(memory_space=pltpu.SMEM),
             pl.BlockSpec(memory_space=pltpu.SMEM),
             whole(1, L),
             whole(1, 2 * L),
@@ -287,16 +288,24 @@
             jax.ShapeDtypeStruct((4, NH, L), bf16),
         ],
         scratch_shapes=[pltpu.VMEM((L + 16, NH), f32)],
-        compiler_params=pltpu.CompilerParams(vmem_limit_bytes=40 * MIB),
+        compiler_params=pltpu.CompilerParams(vmem_limit_bytes=60 * MIB),
         cost_estimate=pl.CostEstimate(flops=int(4e9), bytes_accessed=12 * MIB, transcendentals=0),
         name="make_tables",
-    )(own_lower, order_slots.reshape(1, L), targets, jnp.asarray(natural_s), jnp.asarray(natural_a), pairs)
+    )(
+        place,
+        order_slots,
+        order_slots.reshape(1, L),
+        targets,
+        jnp.asarray(natural_s),
+        jnp.asarray(natural_a),
+        pairs,
+    )
 
 
 def factors_kernel(place, *refs):
     parts, (factors, extra) = refs[:16], refs[16:]
     for r in range(16):
-        extra[partner(place[0], place[1], r)] = parts[r][...].astype(f32)
+        extra[partner(place, r)] = parts[r][...].astype(f32)
     l_row = lax.broadcasted_iota(jnp.int32, (1, L), 1)
     degree = l_row.astype(f32)
     degree_term = degree * (degree + 1.0)
@@ -338,15 +347,19 @@
     )(place, *parts)
 
 
-def solve_kernel(place, lower, coef, table, factors, *refs):
-    parts, (out, cs, lhs, rhs, state) = refs[:16], refs[16:]
+def solve_kernel(place, orders, coef, table, factors_hbm, *refs):
+    parts, (out, cs, lhs, rhs, state, factors, sems) = refs[:16], refs[16:]
+    copies = [pltpu.make_async_copy(factors_hbm, factors, sems.at[16])]
     for r in range(16):
-        state[partner(place[0], place[1], r)] = parts[r][...]
+        source = parts[r].at[pl.ds(0, 96)]
+        copies.append(pltpu.make_async_copy(source, state.at[partner(place, r)], sems.at[r]))
+    for copy in copies:
+        copy.start()
     for c in range(6):
         cs[c] = coef[:, c * 128 : c * 128 + 128].astype(f32)
     l_row = lax.broadcasted_iota(jnp.int32, (1, L), 1)
     for k in range(4):
-        m = lower[k // 2]
+        m = orders[place[1] * 64 + place[0] * 4 + k // 2 * 2]
         order = m if k % 2 == 0 else L - 1 - m
         half_sign = 0.5 * (1 - 2 * ((l_row + order) & 1)).astype(f32)
         for h in range(2):
@@ -363,6 +376,9 @@
         for cp in range(12):
             store(rhs, pl.ds(cp * 4 + k, 32, stride=48), half[cp * 32 : cp * 32 + 32])
 
+    for copy in copies:
+        copy.wait()
+
     def factor(kind, f, s):
         return factors[kind, pl.ds(f * 32 + s, 1), :]
 
@@ -397,7 +413,7 @@
     lax.fori_loop(0, 16, backward, (zero, zero))
 
 
-def analysis_and_solve(place, own_lower, coef, table, factors, parts):
+def analysis_and_solve(place, orders, coef, table, factors, parts):
     small = pl.BlockSpec(memory_space=pltpu.SMEM)
     return pl.pallas_call(
         solve_kernel,
@@ -407,9 +423,8 @@
             small,
             pl.BlockSpec((1024, 768), lambda g: (0, 0)),
             pl.BlockSpec((4, NH, L), lambda g: (0, 0, 0)),
-            pl.BlockSpec((3, 64, L), lambda g: (0, 0, 0)),
         ]
-        + [pl.BlockSpec((96, L), lambda g: (0, 0))] * 16,
+        + [pl.BlockSpec(memory_space=pltpu.HBM)] * 17,
         out_specs=pl.BlockSpec((16, 96, L), lambda g: (0, 0, 0)),
         out_shape=jax.ShapeDtypeStruct((16, 96, L), bf16),
         scratch_shapes=[
@@ -417,11 +432,13 @@
             pltpu.VMEM((2, 768, NH), bf16),
             pltpu.VMEM((4, 32 * 48, 128), f32),
             pltpu.VMEM((16, 96, L), bf16),
+            pltpu.VMEM((3, 64, L), f32),
+            pltpu.SemaphoreType.DMA((17,)),
         ],
-        compiler_params=pltpu.CompilerParams(vmem_limit_bytes=32 * MIB),
+        compiler_params=pltpu.CompilerParams(vmem_limit_bytes=60 * MIB),
         cost_estimate=pl.CostEstimate(flops=int(0.9e9), bytes_accessed=6 * MIB, transcendentals=0),
         name="analysis_and_solve",
-    )(place, own_lower, coef, table, factors, *parts)
+    )(place, orders, coef, table, factors, *parts)
 
 
 def unpack_kernel(got, out_v, out_p, scr, tmp):
@@ -465,9 +482,7 @@
 ):
     order_rank = lax.axis_index("order")
     shell_rank = lax.axis_index("shell")
-    lower = lax.dynamic_slice_in_dim(order_slots, order_rank * 64, 64).reshape(32, 2)[:, 0]
-    place = jnp.stack([shell_rank, order_rank & 1]).astype(jnp.int32)
-    own_lower = lax.dynamic_slice_in_dim(lower, shell_rank * 2, 2)
+    place = jnp.stack([shell_rank, order_rank]).astype(jnp.int32)
     shell_ids = shell_rank * 2 + jnp.arange(2, dtype=jnp.int32)
     starts = jnp.cumsum(block_lengths) - block_lengths
     is_start = jnp.any(shell_ids[:, None] == starts[None, :], axis=1)
@@ -478,7 +493,7 @@
 
     latitude, pairs = legendre_synthesis(
         place,
-        lower,
+        order_slots,
         velocity,
         vorticity,
         magnetic,
@@ -498,17 +513,16 @@
             (i * 8 + o, (i ^ (swapped if o & 1 else r)) * 8 + o) for i in range(16) for o in range(8)
         ]
         received.append(lax.ppermute(parts[r], ("shell", "order"), pairs_r))
-    syn, ana, table = make_tables(own_lower, order_after, pairs)
+    syn, ana, table = make_tables(place, order_after, pairs)
+    incoming, table, received = lax.optimization_barrier((incoming, table, received))
+
+    coefs = grid_stage(incoming, syn, ana, weight)
+    received, _ = lax.optimization_barrier((received, coefs))
     factors = solve_factors(place, received)
-    incoming, factors, table, received = lax.optimization_barrier(
-        (incoming, factors, table, received)
-    )
-
-    coefs = grid_stage(incoming, syn, ana, weight)
     coefs = lax.all_to_all(
         coefs.reshape(128, 8, 768), ("shell", "order"), 0, 0, tiled=True
     ).reshape(1024, 768)
-    solved = analysis_and_solve(place, own_lower, coefs, table, factors, received)
+    solved = analysis_and_solve(place, order_slots, coefs, table, factors, received)
     solved = lax.all_to_all(solved, "shell", 0, 0, tiled=True)
     return tuple(unpack_solution(solved))
 

time: 152 us -> 148 us (0.974)
  blocking collectives: 59.4 us -> 26.2 us
  waiting for transfers between devices: 0.04 us -> 22.8 us
  local copies, waits for them, and re-layouts: 14.4 us -> 2.85 us
  starting transfers between devices: 37.8 us -> 47 us
  Pallas kernels: 37.4 us -> 45.7 us
    all_to_all x1 -> x0, blocking collectives: 34 us -> none  [body(): lax.all_to_all(coefs.reshape(128, 8, 768), ('shell', 'order'), 0, 0, tile...]
    all_to_all x0 -> x1, waiting for transfers between devices: none -> 22.8 us  [body(): lax.all_to_all(coefs.reshape(128, 8, 768), ('shell', 'order'), 0, 0, tile...]
    unnamed x96 -> x48, local copies, waits for them, and re-layouts: 11.7 us -> 1.87 us
    all_to_all x0 -> x1, starting transfers between devices: none -> 9.29 us  [body(): lax.all_to_all(coefs.reshape(128, 8, 768), ('shell', 'order'), 0, 0, tile...]
    pallas_call x1, Pallas kernels: 4.06 us -> 7.49 us  [make_tables(): pl.pallas_call(tables_kernel, grid=(1,), in_specs=[pl.BlockSpec(memory_sp...]
    pallas_call x1, Pallas kernels: 5.87 us -> 9.25 us  [analysis_and_solve(): pl.pallas_call(solve_kernel, grid=(1,), in_specs=[small, small, pl.BlockS...]
    pallas_call x1, Pallas kernels: 8.34 us -> 10.2 us  [grid_stage(): pl.pallas_call(grid_kernel, grid=(4,), in_specs=[pl.BlockSpec((8, 24, 64,...]
    dynamic_slice x2 -> x0, local copies, waits for them, and re-layouts: 1.56 us -> none  [the longest x1 0.8 us: body(): own_lower = lax.dynamic_slice_in_dim(lower, shell_rank * 2, 2)]
  transfers between devices with their start and end apart: 16 -> 17, of which waited for: 0 -> 1; matrix products, arithmetic and copies ran while one was open for 1% -> 1% of each run, Pallas kernels for 5% -> 7%
where the time goes in v5:
time: 148 us; the launch traced here: 147 us
  starting transfers between devices  47 us (32%)
  Pallas kernels  45.7 us (31%)
  blocking collectives  26.2 us (18%)
  waiting for transfers between devices  22.8 us (15%)
  local copies, waits for them, and re-layouts  2.85 us (2%)
  other arithmetic  1.8 us (1%)
    ppermute x15, starting transfers between devices, body(): received.append(lax.ppermute(parts[r], ('shell', 'order'), pairs_r))  32.2 us
    all_to_all x1, blocking collectives, body(): solved = lax.all_to_all(solved, 'shell', 0, 0, tiled=True)  26.2 us
    all_to_all x1, waiting for transfers between devices, body(): lax.all_to_all(coefs.reshape(128, 8, 768), ('shell', 'order'), 0, 0, tile...  22.8 us
    pallas_call x1, Pallas kernels, legendre_synthesis(): pl.pallas_call(synthesis_kernel, grid_spec=pltpu.PrefetchScalarGridSpec(n...  12.7 us
    pallas_call x1, Pallas kernels, grid_stage(): pl.pallas_call(grid_kernel, grid=(4,), in_specs=[pl.BlockSpec((8, 24, 64,...  10.2 us
    all_to_all x1, starting transfers between devices, body(): lax.all_to_all(coefs.reshape(128, 8, 768), ('shell', 'order'), 0, 0, tile...  9.29 us
    pallas_call x1, Pallas kernels, analysis_and_solve(): pl.pallas_call(solve_kernel, grid=(1,), in_specs=[small, small, pl.BlockS...  9.25 us
    pallas_call x1, Pallas kernels, make_tables(): pl.pallas_call(tables_kernel, grid=(1,), in_specs=[pl.BlockSpec(memory_sp...  7.49 us
  transfers between devices with their start and end apart: 17, of which 1 were waited for; matrix products, arithmetic and copies ran while one was open for 1% of the time, Pallas kernels for 7%

profile of v5, /device:TPU:0, one launch (start us, length us, event | category | flops | bytes accessed | tf_op | source)
XLA Modules:
  0.0 147.4 jit_solution(10690131918255817666)
XLA Ops:
  0.6 0.7 pad_add_fusion.place
  1.3 12.7 %legendre_synthesis.1 = (bf16[8,24,64,128]{3,2,1,0:T(8,128)(2,1)}, bf16[2,528,256]{2,1,0:T(8,128)(2,1)}) custom-call(s32[2]{0:T(128)} %pad_add_fusion.place, s32[512]{0:T(512)} %orders.4, bf16[3,2,2,64,512]{4,3,2,1,0:T(8,128)(2,1)} %vel.2, bf16[3,2,2,64,512]{4,3,2,1,0:T(8,128)(2,1)} %vor.1, bf16[3,2,2,64,512]{4,3,2,1,0:T(8,128)(2,1)} %mag.1, ...), custom_call_target="tpu_custom_call" | custom-call | flops 1600000000 | bytes 15728640 | tf_op jit(solution)/shard_map/legendre_synthesis/pallas_call | solution.py:117
  14.0 0.0 copy-start
  14.0 0.0 copy-start.1
  14.1 0.0 copy-start.4
  14.1 0.0 copy-start.21
  14.1 5.5 %all-to-all-start = ((bf16[8,24,64,128]{3,2,1,0:T(8,128)(2,1)}), bf16[8,24,64,128]{3,2,1,0:T(8,128)(2,1)}, u32[]{:S(2)}, u32[]{:S(2)}) async-start(bf16[8,24,64,128]{3,2,1,0:T(8,128)(2,1)} %get-tuple-element.60), calls=%async_computation | async-start | bytes 6291456 | tf_op jit(solution)/shard_map/all_to_all | solution.py:503
  19.6 0.2 reduce-window.9
  19.8 0.2 compare_reduce_fusion
  20.1 1.2 state_to_send.1
  21.2 0.6 copy-done.2
  21.9 1.5 %collective-permute-start = (bf16[112,512]{1,0:T(8,128)(2,1)S(1)}, bf16[112,512]{1,0:T(8,128)(2,1)S(1)}, u32[]{:S(2)}, u32[]{:S(2)}) collective-permute-start(bf16[112,512]{1,0:T(8,128)(2,1)S(1)} %get-tuple-element.67), channel_id=1, source_target_pairs={{0,8},{1,33},{2,10},{3,35},{4,12},{5,37},{6,14},{7,39},{8,0},{9,41... | collective-permute-start | bytes 344072 | tf_op jit(solution)/shard_map/ppermute | solution.py:515
  23.3 2.7 %collective-permute-start.1 = (bf16[112,512]{1,0:T(8,128)(2,1)S(1)}, bf16[112,512]{1,0:T(8,128)(2,1)S(1)}, u32[]{:S(2)}, u32[]{:S(2)}) collective-permute-start(bf16[112,512]{1,0:T(8,128)(2,1)S(1)} %get-tuple-element.68), channel_id=1, source_target_pairs={{0,16},{1,65},{2,18},{3,67},{4,20},{5,69},{6,22},{7,71},{8,24},{9,... | collective-permute-start | bytes 344072 | tf_op jit(solution)/shard_map/ppermute | solution.py:515
  26.1 0.5 collective-permute-start.2
  26.6 1.6 %collective-permute-start.3 = (bf16[112,512]{1,0:T(8,128)(2,1)S(1)}, bf16[112,512]{1,0:T(8,128)(2,1)S(1)}, u32[]{:S(2)}, u32[]{:S(2)}) collective-permute-start(bf16[112,512]{1,0:T(8,128)(2,1)S(1)} %get-tuple-element.70), channel_id=1, source_target_pairs={{0,32},{1,9},{2,34},{3,11},{4,36},{5,13},{6,38},{7,15},{8,40},{9,1... | collective-permute-start | bytes 344072 | tf_op jit(solution)/shard_map/ppermute | solution.py:515
  28.1 0.2 collective-permute-start.4
  28.3 0.1 reshape.99
  28.5 0.0 collective-permute-done.refs_1_
  28.5 0.0 copy-start.6
  28.5 5.0 %collective-permute-start.5 = (bf16[112,512]{1,0:T(8,128)(2,1)S(1)}, bf16[112,512]{1,0:T(8,128)(2,1)S(1)}, u32[]{:S(2)}, u32[]{:S(2)}) collective-permute-start(bf16[112,512]{1,0:T(8,128)(2,1)S(1)} %get-tuple-element.72), channel_id=1, source_target_pairs={{0,48},{1,73},{2,50},{3,75},{4,52},{5,77},{6,54},{7,79},{8,56},{9,... | collective-permute-start | bytes 344072 | tf_op jit(solution)/shard_map/ppermute | solution.py:515
  33.5 0.0 collective-permute-done.1.refs_2_
  33.5 0.4 collective-permute-start.6
  33.9 0.0 collective-permute-done.2.refs_3_
  33.9 3.2 %collective-permute-start.7 = (bf16[112,512]{1,0:T(8,128)(2,1)S(1)}, bf16[112,512]{1,0:T(8,128)(2,1)S(1)}, u32[]{:S(2)}, u32[]{:S(2)}) collective-permute-start(bf16[112,512]{1,0:T(8,128)(2,1)S(1)} %get-tuple-element.74), channel_id=1, source_target_pairs={{0,64},{1,17},{2,66},{3,19},{4,68},{5,21},{6,70},{7,23},{8,72},{9,... | collective-permute-start | bytes 344072 | tf_op jit(solution)/shard_map/ppermute | solution.py:515
  37.1 0.0 collective-permute-done.3.refs_4_
  37.1 0.4 collective-permute-start.8
  37.5 0.0 collective-permute-done.4.refs_5_
  37.5 6.2 %collective-permute-start.9 = (bf16[112,512]{1,0:T(8,128)(2,1)S(1)}, bf16[112,512]{1,0:T(8,128)(2,1)S(1)}, u32[]{:S(2)}, u32[]{:S(2)}) collective-permute-start(bf16[112,512]{1,0:T(8,128)(2,1)S(1)} %get-tuple-element.76), channel_id=1, source_target_pairs={{0,80},{1,81},{2,82},{3,83},{4,84},{5,85},{6,86},{7,87},{8,88},{9,... | collective-permute-start | bytes 344072 | tf_op jit(solution)/shard_map/ppermute | solution.py:515
  43.7 0.2 broadcast_add_fusion
  43.9 0.9 add.62.targets
  44.8 0.0 collective-permute-done.5.refs_6_
  44.8 1.1 collective-permute-start.10
  45.8 0.0 collective-permute-done.6.refs_7_
  45.8 2.2 %collective-permute-start.11 = (bf16[112,512]{1,0:T(8,128)(2,1)S(1)}, bf16[112,512]{1,0:T(8,128)(2,1)S(1)}, u32[]{:S(2)}, u32[]{:S(2)}) collective-permute-start(bf16[112,512]{1,0:T(8,128)(2,1)S(1)} %get-tuple-element.78), channel_id=1, source_target_pairs={{0,96},{1,25},{2,98},{3,27},{4,100},{5,29},{6,102},{7,31},{8,104},... | collective-permute-start | bytes 344072 | tf_op jit(solution)/shard_map/ppermute | solution.py:515
  48.0 0.0 collective-permute-done.7.refs_8_
  48.1 0.0 collective-permute-start.12
  48.1 0.0 collective-permute-done.8.refs_9_
  48.1 0.0 copy-start.14
  48.1 6.3 %collective-permute-start.13 = (bf16[112,512]{1,0:T(8,128)(2,1)S(1)}, bf16[112,512]{1,0:T(8,128)(2,1)S(1)}, u32[]{:S(2)}, u32[]{:S(2)}) collective-permute-start(bf16[112,512]{1,0:T(8,128)(2,1)S(1)} %get-tuple-element.80), channel_id=1, source_target_pairs={{0,112},{1,89},{2,114},{3,91},{4,116},{5,93},{6,118},{7,95},{8,120... | collective-permute-start | bytes 344072 | tf_op jit(solution)/shard_map/ppermute | solution.py:515
  54.4 0.0 collective-permute-done.9.refs_10_
  54.4 0.9 collective-permute-start.14
  55.3 7.5 %make_tables.1 = (bf16[1024,1024]{1,0:T(8,128)(2,1)}, bf16[1024,1024]{1,0:T(8,128)(2,1)}, bf16[4,256,512]{2,1,0:T(8,128)(2,1)}) custom-call(s32[2]{0:T(128)} %pad_add_fusion.place, s32[512]{0:T(512)} %orders.4, s32[1,512]{1,0:T(1,128)} %bitcast.14, s32[1,1024]{1,0:T(1,128)} %add.62.targets, bf16[1024,1024]{1,0:T(8,128)(2,1)} %constant.38.clone.natural_s, ...), custom_call_target="tpu_custom_call" | custom-call | flops 4000000000 | bytes 12582912 | tf_op jit(solution)/shard_map/make_tables/pallas_call | solution.py:272
  62.8 0.0 copy-done.7
  62.8 0.0 copy-done.8
  62.9 0.0 copy-done.9
  62.9 0.0 copy-done.10
  62.9 0.0 copy-done.11
  62.9 0.0 copy-done.12
  62.9 0.0 copy-done.13
  62.9 0.6 sine_multiply_fusion.weight
  63.5 0.0 collective-permute-done.10.refs_11_
  63.5 0.0 collective-permute-done.11.refs_12_
  63.5 0.0 collective-permute-done.12.refs_13_
  63.5 0.0 collective-permute-done.13.refs_14_
  63.5 0.0 collective-permute-done.14.refs_15_
  63.6 0.0 all-to-all-done.lat
  63.6 10.2 %grid_stage.1 = bf16[1024,768]{1,0:T(8,128)(2,1)} custom-call(bf16[8,24,64,128]{3,2,1,0:T(8,128)(2,1)} %all-to-all-done.lat, bf16[1024,1024]{1,0:T(8,128)(2,1)} %get-tuple-element.83.syn, bf16[1024,1024]{1,0:T(8,128)(2,1)} %get-tuple-element.84.ana, f32[1,128]{1,0:T(1,128)} %sine_multiply_fusion.weight), custom_call_target="tpu_custom_call" | custom-call | flops 4800000000 | bytes 9437184 | tf_op jit(solution)/shard_map/grid_stage/pallas_call | solution.py:227
  73.8 9.3 %all-to-all-start.1 = ((bf16[128,8,768]{2,1,0:T(8,128)(2,1)}), bf16[128,8,768]{2,1,0:T(8,128)(2,1)S(1)}, u32[]{:S(2)}, u32[]{:S(2)}) async-start(bf16[128,8,768]{2,1,0:T(8,128)(2,1)} %bitcast.12), calls=%async_computation.1 | async-start | bytes 3145728 | tf_op jit(solution)/shard_map/all_to_all | solution.py:522
  83.1 2.1 %solve_factors.1.factors_hbm = f32[3,64,512]{2,1,0:T(8,128)} custom-call(s32[2]{0:T(128)} %pad_add_fusion.place, bf16[112,512]{1,0:T(8,128)(2,1)} %copy-done.2, bf16[112,512]{1,0:T(8,128)(2,1)} %copy-done.6, bf16[112,512]{1,0:T(8,128)(2,1)} %copy-done.7, bf16[112,512]{1,0:T(8,128)(2,1)} %copy-done.8, bf16[112,512]{1,0:T(8,128)(2,1)} %copy-done.9, ...), custom_call_target="tpu_custom_call" | custom-call | flops 1000000 | bytes 1048576 | tf_op jit(solution)/shard_map/solve_factors/pallas_call | solution.py:336
  85.2 22.8 %all-to-all-done.1 = bf16[128,8,768]{2,1,0:T(8,128)(2,1)S(1)} async-done(((bf16[128,8,768]{2,1,0:T(8,128)(2,1)}), bf16[128,8,768]{2,1,0:T(8,128)(2,1)S(1)}, u32[]{:S(2)}, u32[]{:S(2)}) %all-to-all-start.1) | async-done | bytes 1572896 | tf_op jit(solution)/shard_map/all_to_all | solution.py:522
  108.0 1.1 copy-done.5
  109.1 9.2 %analysis_and_solve.1 = bf16[16,96,512]{2,1,0:T(8,128)(2,1)} custom-call(s32[2]{0:T(128)} %pad_add_fusion.place, s32[512]{0:T(512)} %orders.4, bf16[1024,768]{1,0:T(8,128)(2,1)} %bitcast.11, bf16[4,256,512]{2,1,0:T(8,128)(2,1)} %get-tuple-element.85.table, f32[3,64,512]{2,1,0:T(8,128)} %solve_factors.1.factors_hbm, bf16[112,512]{1,0:T(8,128)(2,1)} %copy-done.2, ...), custom_call_target="tpu_custom_call" | custom-call | flops 900000000 | bytes 6291456 | tf_op jit(solution)/shard_map/analysis_and_solve/pallas_call | solution.py:418
  118.4 26.2 %all_to_all.15.got = bf16[16,96,512]{2,1,0:T(8,128)(2,1)S(1)} all-to-all(bf16[16,96,512]{2,1,0:T(8,128)(2,1)} %analysis_and_solve.1), channel_id=1, replica_groups=mesh['shell'=16,'order'=8] {'shell'}, dimensions={0} | all-to-all | bytes 3145728 | tf_op jit(solution)/shard_map/all_to_all | solution.py:526
  144.6 2.8 %unpack_solution.1 = (f32[3,2,2,64,512]{4,3,2,1,0:T(8,128)}, f32[3,2,2,64,512]{4,3,2,1,0:T(8,128)}) custom-call(bf16[16,96,512]{2,1,0:T(8,128)(2,1)S(1)} %all_to_all.15.got), custom_call_target="tpu_custom_call" | custom-call | flops 1000000 | bytes 5242880 | tf_op jit(solution)/shard_map/unpack_solution/pallas_call | solution.py:458
  (38 shorter events, 0.1 us)
Async XLA Ops:
  14.0 5.6 %copy-start.23 = (s32[4]{0:T(128)S(1)}, s32[4]{0:T(128)}, u32[]{:S(2)}) copy-start(s32[4]{0:T(128)} %param.19) | copy-start | bytes 52
  14.0 6.0 %copy-start.22 = (f32[2,2]{1,0:T(2,128)S(1)}, f32[2,2]{1,0:T(2,128)}, u32[]{:S(2)}) copy-start(f32[2,2]{1,0:T(2,128)} %param.20) | copy-start | bytes 52
  14.0 6.0 %copy-start = (bf16[3,2,2,64,512]{4,3,2,1,0:T(8,128)(2,1)S(1)}, bf16[3,2,2,64,512]{4,3,2,1,0:T(8,128)(2,1)}, u32[]{:S(2)}) copy-start(bf16[3,2,2,64,512]{4,3,2,1,0:T(8,128)(2,1)} %vel.2) | copy-start | bytes 2359300
  14.0 6.0 %copy-start.1 = (bf16[3,2,2,64,512]{4,3,2,1,0:T(8,128)(2,1)S(1)}, bf16[3,2,2,64,512]{4,3,2,1,0:T(8,128)(2,1)}, u32[]{:S(2)}) copy-start(bf16[3,2,2,64,512]{4,3,2,1,0:T(8,128)(2,1)} %pot) | copy-start | bytes 2359300
  14.0 6.0 %copy-start.3 = (s32[2]{0:T(128)S(1)}, s32[2]{0:T(128)}, u32[]{:S(2)}) copy-start(s32[2]{0:T(128)} %pad_add_fusion.place) | copy-start | bytes 28
  14.1 6.0 %copy-start.4 = (f32[2,2]{1,0:T(2,128)S(1)}, f32[2,2]{1,0:T(2,128)}, u32[]{:S(2)}) copy-start(f32[2,2]{1,0:T(2,128)} %angular.1) | copy-start | bytes 52
  14.1 14.2 %copy-start.21 = (s32[512]{0:T(512)S(1)}, s32[512]{0:T(512)}, u32[]{:S(2)}) copy-start(s32[512]{0:T(512)} %orders.4) | copy-start | bytes 6148
  14.1 49.5 %all-to-all-start = ((bf16[8,24,64,128]{3,2,1,0:T(8,128)(2,1)}), bf16[8,24,64,128]{3,2,1,0:T(8,128)(2,1)}, u32[]{:S(2)}, u32[]{:S(2)}) async-start(bf16[8,24,64,128]{3,2,1,0:T(8,128)(2,1)} %get-tuple-element.60), calls=%async_computation | async-start | bytes 6291456 | tf_op jit(solution)/shard_map/all_to_all | solution.py:503
  21.2 0.6 copy-start.2
  21.9 6.6 %collective-permute-start = (bf16[112,512]{1,0:T(8,128)(2,1)S(1)}, bf16[112,512]{1,0:T(8,128)(2,1)S(1)}, u32[]{:S(2)}, u32[]{:S(2)}) collective-permute-start(bf16[112,512]{1,0:T(8,128)(2,1)S(1)} %get-tuple-element.67), channel_id=1, source_target_pairs={{0,8},{1,33},{2,10},{3,35},{4,12},{5,37},{6,14},{7,39},{8,0},{9,41... | collective-permute-start | bytes 344072 | tf_op jit(solution)/shard_map/ppermute | solution.py:515
  23.3 10.2 %collective-permute-start.1 = (bf16[112,512]{1,0:T(8,128)(2,1)S(1)}, bf16[112,512]{1,0:T(8,128)(2,1)S(1)}, u32[]{:S(2)}, u32[]{:S(2)}) collective-permute-start(bf16[112,512]{1,0:T(8,128)(2,1)S(1)} %get-tuple-element.68), channel_id=1, source_target_pairs={{0,16},{1,65},{2,18},{3,67},{4,20},{5,69},{6,22},{7,71},{8,24},{9,... | collective-permute-start | bytes 344072 | tf_op jit(solution)/shard_map/ppermute | solution.py:515
  26.1 7.8 %collective-permute-start.2 = (bf16[112,512]{1,0:T(8,128)(2,1)S(1)}, bf16[112,512]{1,0:T(8,128)(2,1)S(1)}, u32[]{:S(2)}, u32[]{:S(2)}) collective-permute-start(bf16[112,512]{1,0:T(8,128)(2,1)S(1)} %get-tuple-element.69), channel_id=1, source_target_pairs={{0,24},{1,97},{2,26},{3,99},{4,28},{5,101},{6,30},{7,103},{8,16},{... | collective-permute-start | bytes 344072 | tf_op jit(solution)/shard_map/ppermute | solution.py:515
  26.6 10.5 %collective-permute-start.3 = (bf16[112,512]{1,0:T(8,128)(2,1)S(1)}, bf16[112,512]{1,0:T(8,128)(2,1)S(1)}, u32[]{:S(2)}, u32[]{:S(2)}) collective-permute-start(bf16[112,512]{1,0:T(8,128)(2,1)S(1)} %get-tuple-element.70), channel_id=1, source_target_pairs={{0,32},{1,9},{2,34},{3,11},{4,36},{5,13},{6,38},{7,15},{8,40},{9,1... | collective-permute-start | bytes 344072 | tf_op jit(solution)/shard_map/ppermute | solution.py:515
  28.1 9.4 %collective-permute-start.4 = (bf16[112,512]{1,0:T(8,128)(2,1)S(1)}, bf16[112,512]{1,0:T(8,128)(2,1)S(1)}, u32[]{:S(2)}, u32[]{:S(2)}) collective-permute-start(bf16[112,512]{1,0:T(8,128)(2,1)S(1)} %get-tuple-element.71), channel_id=1, source_target_pairs={{0,40},{1,41},{2,42},{3,43},{4,44},{5,45},{6,46},{7,47},{8,32},{9,... | collective-permute-start | bytes 344072 | tf_op jit(solution)/shard_map/ppermute | solution.py:515
  28.5 34.4 %copy-start.6 = (bf16[112,512]{1,0:T(8,128)(2,1)}, bf16[112,512]{1,0:T(8,128)(2,1)S(1)}, u32[]{:S(2)}) copy-start(bf16[112,512]{1,0:T(8,128)(2,1)S(1)} %collective-permute-done.refs_1_) | copy-start | bytes 344068
  28.5 16.3 %collective-permute-start.5 = (bf16[112,512]{1,0:T(8,128)(2,1)S(1)}, bf16[112,512]{1,0:T(8,128)(2,1)S(1)}, u32[]{:S(2)}, u32[]{:S(2)}) collective-permute-start(bf16[112,512]{1,0:T(8,128)(2,1)S(1)} %get-tuple-element.72), channel_id=1, source_target_pairs={{0,48},{1,73},{2,50},{3,75},{4,52},{5,77},{6,54},{7,79},{8,56},{9,... | collective-permute-start | bytes 344072 | tf_op jit(solution)/shard_map/ppermute | solution.py:515
  33.5 29.3 %copy-start.7 = (bf16[112,512]{1,0:T(8,128)(2,1)}, bf16[112,512]{1,0:T(8,128)(2,1)S(1)}, u32[]{:S(2)}) copy-start(bf16[112,512]{1,0:T(8,128)(2,1)S(1)} %collective-permute-done.1.refs_2_) | copy-start | bytes 344068
  33.5 12.3 %collective-permute-start.6 = (bf16[112,512]{1,0:T(8,128)(2,1)S(1)}, bf16[112,512]{1,0:T(8,128)(2,1)S(1)}, u32[]{:S(2)}, u32[]{:S(2)}) collective-permute-start(bf16[112,512]{1,0:T(8,128)(2,1)S(1)} %get-tuple-element.73), channel_id=1, source_target_pairs={{0,56},{1,105},{2,58},{3,107},{4,60},{5,109},{6,62},{7,111},{8,48}... | collective-permute-start | bytes 344072 | tf_op jit(solution)/shard_map/ppermute | solution.py:515
  33.9 29.0 %copy-start.8 = (bf16[112,512]{1,0:T(8,128)(2,1)}, bf16[112,512]{1,0:T(8,128)(2,1)S(1)}, u32[]{:S(2)}) copy-start(bf16[112,512]{1,0:T(8,128)(2,1)S(1)} %collective-permute-done.2.refs_3_) | copy-start | bytes 344068
  33.9 14.2 %collective-permute-start.7 = (bf16[112,512]{1,0:T(8,128)(2,1)S(1)}, bf16[112,512]{1,0:T(8,128)(2,1)S(1)}, u32[]{:S(2)}, u32[]{:S(2)}) collective-permute-start(bf16[112,512]{1,0:T(8,128)(2,1)S(1)} %get-tuple-element.74), channel_id=1, source_target_pairs={{0,64},{1,17},{2,66},{3,19},{4,68},{5,21},{6,70},{7,23},{8,72},{9,... | collective-permute-start | bytes 344072 | tf_op jit(solution)/shard_map/ppermute | solution.py:515
  37.1 25.8 %copy-start.9 = (bf16[112,512]{1,0:T(8,128)(2,1)}, bf16[112,512]{1,0:T(8,128)(2,1)S(1)}, u32[]{:S(2)}) copy-start(bf16[112,512]{1,0:T(8,128)(2,1)S(1)} %collective-permute-done.3.refs_4_) | copy-start | bytes 344068
  37.1 11.0 %collective-permute-start.8 = (bf16[112,512]{1,0:T(8,128)(2,1)S(1)}, bf16[112,512]{1,0:T(8,128)(2,1)S(1)}, u32[]{:S(2)}, u32[]{:S(2)}) collective-permute-start(bf16[112,512]{1,0:T(8,128)(2,1)S(1)} %get-tuple-element.75), channel_id=1, source_target_pairs={{0,72},{1,49},{2,74},{3,51},{4,76},{5,53},{6,78},{7,55},{8,64},{9,... | collective-permute-start | bytes 344072 | tf_op jit(solution)/shard_map/ppermute | solution.py:515
  37.5 25.4 %copy-start.10 = (bf16[112,512]{1,0:T(8,128)(2,1)}, bf16[112,512]{1,0:T(8,128)(2,1)S(1)}, u32[]{:S(2)}) copy-start(bf16[112,512]{1,0:T(8,128)(2,1)S(1)} %collective-permute-done.4.refs_5_) | copy-start | bytes 344068
  37.5 16.9 %collective-permute-start.9 = (bf16[112,512]{1,0:T(8,128)(2,1)S(1)}, bf16[112,512]{1,0:T(8,128)(2,1)S(1)}, u32[]{:S(2)}, u32[]{:S(2)}) collective-permute-start(bf16[112,512]{1,0:T(8,128)(2,1)S(1)} %get-tuple-element.76), channel_id=1, source_target_pairs={{0,80},{1,81},{2,82},{3,83},{4,84},{5,85},{6,86},{7,87},{8,88},{9,... | collective-permute-start | bytes 344072 | tf_op jit(solution)/shard_map/ppermute | solution.py:515
  44.8 18.1 %copy-start.11 = (bf16[112,512]{1,0:T(8,128)(2,1)}, bf16[112,512]{1,0:T(8,128)(2,1)S(1)}, u32[]{:S(2)}) copy-start(bf16[112,512]{1,0:T(8,128)(2,1)S(1)} %collective-permute-done.5.refs_6_) | copy-start | bytes 344068
  44.8 18.7 %collective-permute-start.10 = (bf16[112,512]{1,0:T(8,128)(2,1)S(1)}, bf16[112,512]{1,0:T(8,128)(2,1)S(1)}, u32[]{:S(2)}, u32[]{:S(2)}) collective-permute-start(bf16[112,512]{1,0:T(8,128)(2,1)S(1)} %get-tuple-element.77), channel_id=1, source_target_pairs={{0,88},{1,113},{2,90},{3,115},{4,92},{5,117},{6,94},{7,119},{8,80}... | collective-permute-start | bytes 344072 | tf_op jit(solution)/shard_map/ppermute | solution.py:515
  45.8 17.0 %copy-start.12 = (bf16[112,512]{1,0:T(8,128)(2,1)}, bf16[112,512]{1,0:T(8,128)(2,1)S(1)}, u32[]{:S(2)}) copy-start(bf16[112,512]{1,0:T(8,128)(2,1)S(1)} %collective-permute-done.6.refs_7_) | copy-start | bytes 344068
  45.8 17.7 %collective-permute-start.11 = (bf16[112,512]{1,0:T(8,128)(2,1)S(1)}, bf16[112,512]{1,0:T(8,128)(2,1)S(1)}, u32[]{:S(2)}, u32[]{:S(2)}) collective-permute-start(bf16[112,512]{1,0:T(8,128)(2,1)S(1)} %get-tuple-element.78), channel_id=1, source_target_pairs={{0,96},{1,25},{2,98},{3,27},{4,100},{5,29},{6,102},{7,31},{8,104},... | collective-permute-start | bytes 344072 | tf_op jit(solution)/shard_map/ppermute | solution.py:515
  48.1 14.8 %copy-start.13 = (bf16[112,512]{1,0:T(8,128)(2,1)}, bf16[112,512]{1,0:T(8,128)(2,1)S(1)}, u32[]{:S(2)}) copy-start(bf16[112,512]{1,0:T(8,128)(2,1)S(1)} %collective-permute-done.7.refs_8_) | copy-start | bytes 344068
  48.1 15.5 %collective-permute-start.12 = (bf16[112,512]{1,0:T(8,128)(2,1)S(1)}, bf16[112,512]{1,0:T(8,128)(2,1)S(1)}, u32[]{:S(2)}, u32[]{:S(2)}) collective-permute-start(bf16[112,512]{1,0:T(8,128)(2,1)S(1)} %get-tuple-element.79), channel_id=1, source_target_pairs={{0,104},{1,57},{2,106},{3,59},{4,108},{5,61},{6,110},{7,63},{8,96}... | collective-permute-start | bytes 344072 | tf_op jit(solution)/shard_map/ppermute | solution.py:515
  48.1 14.8 %copy-start.14 = (bf16[112,512]{1,0:T(8,128)(2,1)}, bf16[112,512]{1,0:T(8,128)(2,1)S(1)}, u32[]{:S(2)}) copy-start(bf16[112,512]{1,0:T(8,128)(2,1)S(1)} %collective-permute-done.8.refs_9_) | copy-start | bytes 344068
  48.1 15.5 %collective-permute-start.13 = (bf16[112,512]{1,0:T(8,128)(2,1)S(1)}, bf16[112,512]{1,0:T(8,128)(2,1)S(1)}, u32[]{:S(2)}, u32[]{:S(2)}) collective-permute-start(bf16[112,512]{1,0:T(8,128)(2,1)S(1)} %get-tuple-element.80), channel_id=1, source_target_pairs={{0,112},{1,89},{2,114},{3,91},{4,116},{5,93},{6,118},{7,95},{8,120... | collective-permute-start | bytes 344072 | tf_op jit(solution)/shard_map/ppermute | solution.py:515
  54.4 8.5 %copy-start.15 = (bf16[112,512]{1,0:T(8,128)(2,1)}, bf16[112,512]{1,0:T(8,128)(2,1)S(1)}, u32[]{:S(2)}) copy-start(bf16[112,512]{1,0:T(8,128)(2,1)S(1)} %collective-permute-done.9.refs_10_) | copy-start | bytes 344068
  54.4 9.2 %collective-permute-start.14 = (bf16[112,512]{1,0:T(8,128)(2,1)S(1)}, bf16[112,512]{1,0:T(8,128)(2,1)S(1)}, u32[]{:S(2)}, u32[]{:S(2)}) collective-permute-start(bf16[112,512]{1,0:T(8,128)(2,1)S(1)} %get-tuple-element.81), channel_id=1, source_target_pairs={{0,120},{1,121},{2,122},{3,123},{4,124},{5,125},{6,126},{7,127},{8... | collective-permute-start | bytes 344072 | tf_op jit(solution)/shard_map/ppermute | solution.py:515
  63.5 10.3 %copy-start.16 = (bf16[112,512]{1,0:T(8,128)(2,1)}, bf16[112,512]{1,0:T(8,128)(2,1)S(1)}, u32[]{:S(2)}) copy-start(bf16[112,512]{1,0:T(8,128)(2,1)S(1)} %collective-permute-done.10.refs_11_) | copy-start | bytes 344068
  63.5 10.3 %copy-start.17 = (bf16[112,512]{1,0:T(8,128)(2,1)}, bf16[112,512]{1,0:T(8,128)(2,1)S(1)}, u32[]{:S(2)}) copy-start(bf16[112,512]{1,0:T(8,128)(2,1)S(1)} %collective-permute-done.11.refs_12_) | copy-start | bytes 344068
  63.5 10.3 %copy-start.18 = (bf16[112,512]{1,0:T(8,128)(2,1)}, bf16[112,512]{1,0:T(8,128)(2,1)S(1)}, u32[]{:S(2)}) copy-start(bf16[112,512]{1,0:T(8,128)(2,1)S(1)} %collective-permute-done.12.refs_13_) | copy-start | bytes 344068
  63.5 10.3 %copy-start.19 = (bf16[112,512]{1,0:T(8,128)(2,1)}, bf16[112,512]{1,0:T(8,128)(2,1)S(1)}, u32[]{:S(2)}) copy-start(bf16[112,512]{1,0:T(8,128)(2,1)S(1)} %collective-permute-done.13.refs_14_) | copy-start | bytes 344068
  63.6 10.3 %copy-start.20 = (bf16[112,512]{1,0:T(8,128)(2,1)}, bf16[112,512]{1,0:T(8,128)(2,1)S(1)}, u32[]{:S(2)}) copy-start(bf16[112,512]{1,0:T(8,128)(2,1)S(1)} %collective-permute-done.14.refs_15_) | copy-start | bytes 344068
  73.8 34.2 %all-to-all-start.1 = ((bf16[128,8,768]{2,1,0:T(8,128)(2,1)}), bf16[128,8,768]{2,1,0:T(8,128)(2,1)S(1)}, u32[]{:S(2)}, u32[]{:S(2)}) async-start(bf16[128,8,768]{2,1,0:T(8,128)(2,1)} %bitcast.12), calls=%async_computation.1 | async-start | bytes 3145728 | tf_op jit(solution)/shard_map/all_to_all | solution.py:522
  108.0 1.1 copy-start.5

commit v6 on v5

--- a/solution.py
+++ b/solution.py
@@ -303,9 +303,10 @@
 
 
 def factors_kernel(place, *refs):
-    parts, (factors, extra) = refs[:16], refs[16:]
+    parts, (state, factors, extra) = refs[:16], refs[16:]
     for r in range(16):
-        extra[partner(place, r)] = parts[r][...].astype(f32)
+        state[partner(place, r)] = parts[r][0:96, :]
+        extra[partner(place, r)] = parts[r][96:112, :].astype(f32)
     l_row = lax.broadcasted_iota(jnp.int32, (1, L), 1)
     degree = l_row.astype(f32)
     degree_term = degree * (degree + 1.0)
@@ -337,26 +338,27 @@
         factors_kernel,
         grid=(1,),
         in_specs=[pl.BlockSpec(memory_space=pltpu.SMEM)]
-        + [pl.BlockSpec((16, L), lambda g: (6, 0))] * 16,
-        out_specs=pl.BlockSpec((3, 64, L), lambda g: (0, 0, 0)),
-        out_shape=jax.ShapeDtypeStruct((3, 64, L), f32),
+        + [pl.BlockSpec((112, L), lambda g: (0, 0))] * 16,
+        out_specs=[
+            pl.BlockSpec((16, 96, L), lambda g: (0, 0, 0)),
+            pl.BlockSpec((3, 64, L), lambda g: (0, 0, 0)),
+        ],
+        out_shape=[
+            jax.ShapeDtypeStruct((16, 96, L), bf16),
+            jax.ShapeDtypeStruct((3, 64, L), f32),
+        ],
         scratch_shapes=[pltpu.VMEM((16, 16, L), f32)],
-        compiler_params=pltpu.CompilerParams(vmem_limit_bytes=60 * MIB),
+        compiler_params=pltpu.CompilerParams(vmem_limit_bytes=16 * MIB),
         cost_estimate=pl.CostEstimate(flops=10**6, bytes_accessed=MIB, transcendentals=0),
         name="solve_factors",
     )(place, *parts)
 
 
-def solve_kernel(place, orders, coef, table, factors_hbm, *refs):
-    parts, (out, cs, lhs, rhs, state, factors, sems) = refs[:16], refs[16:]
-    copies = [pltpu.make_async_copy(factors_hbm, factors, sems.at[16])]
-    for r in range(16):
-        source = parts[r].at[pl.ds(0, 96)]
-        copies.append(pltpu.make_async_copy(source, state.at[partner(place, r)], sems.at[r]))
-    for copy in copies:
-        copy.start()
+def solve_kernel(place, orders, coef, table, factors, state, out, cs, lhs, rhs, reduced):
     for c in range(6):
-        cs[c] = coef[:, c * 128 : c * 128 + 128].astype(f32)
+        for ds in range(32):
+            piece = coef[ds * 32 : ds * 32 + 32, c * 128 : c * 128 + 128]
+            cs[c, ds * 33 : ds * 33 + 32, :] = piece.astype(f32)
     l_row = lax.broadcasted_iota(jnp.int32, (1, L), 1)
     for k in range(4):
         m = orders[place[1] * 64 + place[0] * 4 + k // 2 * 2]
@@ -369,33 +371,30 @@
                     for jh in range(2):
                         start = h * 16 + jh * 8 + k * 2 + p
                         lhs[k % 2, row : row + 32, jh * 128 : jh * 128 + 128] = cs[
-                            c, pl.ds(start, 32, stride=32), :
+                            c, pl.ds(start, 32, stride=33), :
                         ].astype(bf16)
         res = jnp.dot(lhs[k % 2], table[k], preferred_element_type=f32)
         half = 0.5 * res[0:384] + half_sign * res[384:768]
         for cp in range(12):
-            store(rhs, pl.ds(cp * 4 + k, 32, stride=48), half[cp * 32 : cp * 32 + 32])
-
-    for copy in copies:
-        copy.wait()
+            store(rhs, pl.ds(cp * 4 + k, 32, stride=49), half[cp * 32 : cp * 32 + 32])
 
     def factor(kind, f, s):
         return factors[kind, pl.ds(f * 32 + s, 1), :]
 
-    def forward(d, running):
+    def forward(step, running):
         running = list(running)
-        block = state[d].astype(f32)
-        for s2 in range(2):
-            s = 2 * d + s2
+        for t in range(8):
+            block = state[4 * step + t // 2, pl.ds(t % 2 * 48, 48), :].astype(f32)
+            s = 8 * step + t
             for f in range(2):
-                base = s * 48 + f * 24
-                value = load(rhs, pl.ds(base, 24)) + block[s2 * 48 + f * 24 : s2 * 48 + f * 24 + 24]
+                at = pl.ds(pl.multiple_of(step * 392, 8) + t * 49 + f * 24, 24)
+                value = load(rhs, at) + block[f * 24 : f * 24 + 24]
                 running[f] = factor(0, f, s) * value + factor(1, f, s) * running[f]
-                store(rhs, pl.ds(base, 24), running[f])
+                store(reduced, pl.ds(s * 48 + f * 24, 24), running[f])
         return tuple(running)
 
     zero = jnp.zeros((24, L), f32)
-    lax.fori_loop(0, 16, forward, (zero, zero))
+    lax.fori_loop(0, 4, forward, (zero, zero))
 
     def backward(step, carried):
         d = 15 - step
@@ -404,7 +403,7 @@
         for s2 in (1, 0):
             s = 2 * d + s2
             for f in range(2):
-                value = load(rhs, pl.ds(s * 48 + f * 24, 24))
+                value = load(reduced, pl.ds(s * 48 + f * 24, 24))
                 carried[f] = value + factor(2, f, s) * carried[f]
                 pieces[s2 * 2 + f] = carried[f]
         out[d] = jnp.concatenate(pieces, axis=0).astype(bf16)
@@ -413,7 +412,7 @@
     lax.fori_loop(0, 16, backward, (zero, zero))
 
 
-def analysis_and_solve(place, orders, coef, table, factors, parts):
+def analysis_and_solve(place, orders, coef, table, factors, state):
     small = pl.BlockSpec(memory_space=pltpu.SMEM)
     return pl.pallas_call(
         solve_kernel,
@@ -423,33 +422,33 @@
             small,
             pl.BlockSpec((1024, 768), lambda g: (0, 0)),
             pl.BlockSpec((4, NH, L), lambda g: (0, 0, 0)),
-        ]
-        + [pl.BlockSpec(memory_space=pltpu.HBM)] * 17,
+            pl.BlockSpec((3, 64, L), lambda g: (0, 0, 0)),
+            pl.BlockSpec((16, 96, L), lambda g: (0, 0, 0)),
+        ],
         out_specs=pl.BlockSpec((16, 96, L), lambda g: (0, 0, 0)),
         out_shape=jax.ShapeDtypeStruct((16, 96, L), bf16),
         scratch_shapes=[
-            pltpu.VMEM((6, 1024, 128), f32),
+            pltpu.VMEM((6, 32 * 33, 128), f32),
             pltpu.VMEM((2, 768, NH), bf16),
+            pltpu.VMEM((4, 32 * 49, 128), f32),
             pltpu.VMEM((4, 32 * 48, 128), f32),
-            pltpu.VMEM((16, 96, L), bf16),
-            pltpu.VMEM((3, 64, L), f32),
-            pltpu.SemaphoreType.DMA((17,)),
-        ],
-        compiler_params=pltpu.CompilerParams(vmem_limit_bytes=60 * MIB),
+        ],
+        compiler_params=pltpu.CompilerParams(vmem_limit_bytes=32 * MIB),
         cost_estimate=pl.CostEstimate(flops=int(0.9e9), bytes_accessed=6 * MIB, transcendentals=0),
         name="analysis_and_solve",
-    )(place, orders, coef, table, factors, *parts)
-
-
-def unpack_kernel(got, out_v, out_p, scr, tmp):
-    store(scr, pl.ds(0, 768), got[...].astype(f32).reshape(768, L))
+    )(place, orders, coef, table, factors, state)
+
+
+def unpack_kernel(got, out_v, out_p):
+    x = got[...].astype(f32)
+    low = lax.broadcasted_iota(jnp.int32, (1, 8, 1), 1) < 4
     for f, ref in enumerate((out_v, out_p)):
         for c in range(3):
-            for p in range(2):
-                for k in range(4):
-                    row = ((f * 3 + c) * 2 + p) * 4 + k
-                    store(tmp, pl.ds(k, 16, stride=4), load(scr, pl.ds(row, 16, stride=48)))
-                ref[c, 0, p] = load(tmp, pl.ds(0, 64))
+            row = (f * 3 + c) * 8
+            both = x[:, row : row + 8, :].reshape(8, 2, 8, L)
+            a, b = both[:, 0], both[:, 1]
+            ref[c, 0, 0] = jnp.where(low, a, pltpu.roll(b, 4, 1)).reshape(64, L)
+            ref[c, 0, 1] = jnp.where(low, pltpu.roll(a, 4, 1), b).reshape(64, L)
 
 
 def unpack_solution(got):
@@ -461,7 +460,6 @@
         in_specs=[pl.BlockSpec((16, 48, L), lambda s: (0, s, 0))],
         out_specs=[field, field],
         out_shape=[shape, shape],
-        scratch_shapes=[pltpu.VMEM((4, 768, 128), f32), pltpu.VMEM((4, 64, 128), f32)],
         compiler_params=pltpu.CompilerParams(vmem_limit_bytes=24 * MIB),
         cost_estimate=pl.CostEstimate(flops=10**6, bytes_accessed=5 * MIB, transcendentals=0),
         name="unpack_solution",
@@ -518,11 +516,11 @@
 
     coefs = grid_stage(incoming, syn, ana, weight)
     received, _ = lax.optimization_barrier((received, coefs))
-    factors = solve_factors(place, received)
+    state, factors = solve_factors(place, received)
     coefs = lax.all_to_all(
         coefs.reshape(128, 8, 768), ("shell", "order"), 0, 0, tiled=True
     ).reshape(1024, 768)
-    solved = analysis_and_solve(place, order_slots, coefs, table, factors, received)
+    solved = analysis_and_solve(place, order_slots, coefs, table, factors, state)
     solved = lax.all_to_all(solved, "shell", 0, 0, tiled=True)
     return tuple(unpack_solution(solved))
 

time: 148 us -> 141 us (0.953)
  local copies, waits for them, and re-layouts: 2.85 us -> 17.3 us
  waiting for transfers between devices: 22.8 us -> 9.47 us
  Pallas kernels: 45.7 us -> 37.5 us
    unnamed x48 -> x84, local copies, waits for them, and re-layouts: 1.87 us -> 16.3 us
    all_to_all x1, waiting for transfers between devices: 22.8 us -> 9.43 us  [body(): lax.all_to_all(coefs.reshape(128, 8, 768), ('shell', 'order'), 0, 0, tile...]
    pallas_call x1, Pallas kernels: 9.25 us -> 2.95 us  [analysis_and_solve(): pl.pallas_call(solve_kernel, grid=(1,), in_specs=[small, small, pl.BlockS...]
  transfers between devices with their start and end apart: 17 -> 17, of which waited for: 1 -> 1; matrix products, arithmetic and copies ran while one was open for 1% -> 2% of each run, Pallas kernels for 7% -> 7%
where the time goes in v6:
time: 141 us; the launch traced here: 140 us
  starting transfers between devices  47 us (33%)
  Pallas kernels  37.5 us (27%)
  blocking collectives  25.5 us (18%)
  local copies, waits for them, and re-layouts  17.3 us (12%)
  waiting for transfers between devices  9.47 us (7%)
  other arithmetic  1.75 us (1%)
    ppermute x15, starting transfers between devices, body(): received.append(lax.ppermute(parts[r], ('shell', 'order'), pairs_r))  32.2 us
    all_to_all x1, blocking collectives, body(): solved = lax.all_to_all(solved, 'shell', 0, 0, tiled=True)  25.5 us
    unnamed x84, local copies, waits for them, and re-layouts  16.3 us
    pallas_call x1, Pallas kernels, legendre_synthesis(): pl.pallas_call(synthesis_kernel, grid_spec=pltpu.PrefetchScalarGridSpec(n...  12.7 us
    pallas_call x1, Pallas kernels, grid_stage(): pl.pallas_call(grid_kernel, grid=(4,), in_specs=[pl.BlockSpec((8, 24, 64,...  10.2 us
    all_to_all x1, waiting for transfers between devices, body(): lax.all_to_all(coefs.reshape(128, 8, 768), ('shell', 'order'), 0, 0, tile...  9.43 us
    all_to_all x1, starting transfers between devices, body(): lax.all_to_all(coefs.reshape(128, 8, 768), ('shell', 'order'), 0, 0, tile...  9.29 us
    pallas_call x1, Pallas kernels, make_tables(): pl.pallas_call(tables_kernel, grid=(1,), in_specs=[pl.BlockSpec(memory_sp...  7.5 us
  transfers between devices with their start and end apart: 17, of which 1 were waited for; matrix products, arithmetic and copies ran while one was open for 2% of the time, Pallas kernels for 7%

profile of v6, /device:TPU:0, one launch (start us, length us, event | category | flops | bytes accessed | tf_op | source)
XLA Modules:
  0.0 139.6 jit_solution(2647509364940007479)
XLA Ops:
  0.6 0.6 pad_add_fusion.place
  1.2 12.7 %legendre_synthesis.1 = (bf16[8,24,64,128]{3,2,1,0:T(8,128)(2,1)}, bf16[2,528,256]{2,1,0:T(8,128)(2,1)}) custom-call(s32[2]{0:T(128)} %pad_add_fusion.place, s32[512]{0:T(512)} %orders.4, bf16[3,2,2,64,512]{4,3,2,1,0:T(8,128)(2,1)} %vel.2, bf16[3,2,2,64,512]{4,3,2,1,0:T(8,128)(2,1)} %vor.1, bf16[3,2,2,64,512]{4,3,2,1,0:T(8,128)(2,1)} %mag.1, ...), custom_call_target="tpu_custom_call" | custom-call | flops 1600000000 | bytes 15728640 | tf_op jit(solution)/shard_map/legendre_synthesis/pallas_call | solution.py:117
  14.0 0.0 copy-start
  14.0 0.0 copy-start.2
  14.0 0.0 copy-start.39
  14.0 0.0 copy-start.35
  14.0 5.5 %all-to-all-start = ((bf16[8,24,64,128]{3,2,1,0:T(8,128)(2,1)}), bf16[8,24,64,128]{3,2,1,0:T(8,128)(2,1)}, u32[]{:S(2)}, u32[]{:S(2)}) async-start(bf16[8,24,64,128]{3,2,1,0:T(8,128)(2,1)} %get-tuple-element.62), calls=%async_computation | async-start | bytes 6291456 | tf_op jit(solution)/shard_map/all_to_all | solution.py:501
  19.6 0.2 reduce-window.9
  19.8 0.2 compare_reduce_fusion
  20.0 1.2 state_to_send.1
  21.2 0.6 copy-done.3
  21.8 1.5 %collective-permute-start = (bf16[112,512]{1,0:T(8,128)(2,1)S(1)}, bf16[112,512]{1,0:T(8,128)(2,1)S(1)}, u32[]{:S(2)}, u32[]{:S(2)}) collective-permute-start(bf16[112,512]{1,0:T(8,128)(2,1)S(1)} %get-tuple-element.69), channel_id=1, source_target_pairs={{0,8},{1,33},{2,10},{3,35},{4,12},{5,37},{6,14},{7,39},{8,0},{9,41... | collective-permute-start | bytes 344072 | tf_op jit(solution)/shard_map/ppermute | solution.py:513
  23.3 2.7 %collective-permute-start.1 = (bf16[112,512]{1,0:T(8,128)(2,1)S(1)}, bf16[112,512]{1,0:T(8,128)(2,1)S(1)}, u32[]{:S(2)}, u32[]{:S(2)}) collective-permute-start(bf16[112,512]{1,0:T(8,128)(2,1)S(1)} %get-tuple-element.70), channel_id=1, source_target_pairs={{0,16},{1,65},{2,18},{3,67},{4,20},{5,69},{6,22},{7,71},{8,24},{9,... | collective-permute-start | bytes 344072 | tf_op jit(solution)/shard_map/ppermute | solution.py:513
  26.0 0.5 collective-permute-start.2
  26.5 1.6 %collective-permute-start.3 = (bf16[112,512]{1,0:T(8,128)(2,1)S(1)}, bf16[112,512]{1,0:T(8,128)(2,1)S(1)}, u32[]{:S(2)}, u32[]{:S(2)}) collective-permute-start(bf16[112,512]{1,0:T(8,128)(2,1)S(1)} %get-tuple-element.72), channel_id=1, source_target_pairs={{0,32},{1,9},{2,34},{3,11},{4,36},{5,13},{6,38},{7,15},{8,40},{9,1... | collective-permute-start | bytes 344072 | tf_op jit(solution)/shard_map/ppermute | solution.py:513
  28.1 0.2 collective-permute-start.4
  28.3 0.1 reshape.99
  28.4 0.0 collective-permute-done.refs_1_
  28.4 5.0 %collective-permute-start.5 = (bf16[112,512]{1,0:T(8,128)(2,1)S(1)}, bf16[112,512]{1,0:T(8,128)(2,1)S(1)}, u32[]{:S(2)}, u32[]{:S(2)}) collective-permute-start(bf16[112,512]{1,0:T(8,128)(2,1)S(1)} %get-tuple-element.74), channel_id=1, source_target_pairs={{0,48},{1,73},{2,50},{3,75},{4,52},{5,77},{6,54},{7,79},{8,56},{9,... | collective-permute-start | bytes 344072 | tf_op jit(solution)/shard_map/ppermute | solution.py:513
  33.5 0.0 collective-permute-done.1.refs_2_
  33.5 0.4 collective-permute-start.6
  33.8 0.0 collective-permute-done.2.refs_3_
  33.8 3.2 %collective-permute-start.7 = (bf16[112,512]{1,0:T(8,128)(2,1)S(1)}, bf16[112,512]{1,0:T(8,128)(2,1)S(1)}, u32[]{:S(2)}, u32[]{:S(2)}) collective-permute-start(bf16[112,512]{1,0:T(8,128)(2,1)S(1)} %get-tuple-element.76), channel_id=1, source_target_pairs={{0,64},{1,17},{2,66},{3,19},{4,68},{5,21},{6,70},{7,23},{8,72},{9,... | collective-permute-start | bytes 344072 | tf_op jit(solution)/shard_map/ppermute | solution.py:513
  37.0 0.0 collective-permute-done.3.refs_4_
  37.0 0.4 collective-permute-start.8
  37.5 6.2 %collective-permute-start.9 = (bf16[112,512]{1,0:T(8,128)(2,1)S(1)}, bf16[112,512]{1,0:T(8,128)(2,1)S(1)}, u32[]{:S(2)}, u32[]{:S(2)}) collective-permute-start(bf16[112,512]{1,0:T(8,128)(2,1)S(1)} %get-tuple-element.78), channel_id=1, source_target_pairs={{0,80},{1,81},{2,82},{3,83},{4,84},{5,85},{6,86},{7,87},{8,88},{9,... | collective-permute-start | bytes 344072 | tf_op jit(solution)/shard_map/ppermute | solution.py:513
  43.7 0.2 broadcast_add_fusion
  43.9 0.8 add.62.targets
  44.7 1.1 collective-permute-start.10
  45.8 2.2 %collective-permute-start.11 = (bf16[112,512]{1,0:T(8,128)(2,1)S(1)}, bf16[112,512]{1,0:T(8,128)(2,1)S(1)}, u32[]{:S(2)}, u32[]{:S(2)}) collective-permute-start(bf16[112,512]{1,0:T(8,128)(2,1)S(1)} %get-tuple-element.80), channel_id=1, source_target_pairs={{0,96},{1,25},{2,98},{3,27},{4,100},{5,29},{6,102},{7,31},{8,104},... | collective-permute-start | bytes 344072 | tf_op jit(solution)/shard_map/ppermute | solution.py:513
  48.0 0.0 collective-permute-done.7.refs_8_
  48.0 0.0 collective-permute-start.12
  48.0 6.3 %collective-permute-start.13 = (bf16[112,512]{1,0:T(8,128)(2,1)S(1)}, bf16[112,512]{1,0:T(8,128)(2,1)S(1)}, u32[]{:S(2)}, u32[]{:S(2)}) collective-permute-start(bf16[112,512]{1,0:T(8,128)(2,1)S(1)} %get-tuple-element.82), channel_id=1, source_target_pairs={{0,112},{1,89},{2,114},{3,91},{4,116},{5,93},{6,118},{7,95},{8,120... | collective-permute-start | bytes 344072 | tf_op jit(solution)/shard_map/ppermute | solution.py:513
  54.4 0.9 collective-permute-start.14
  55.3 7.5 %make_tables.1 = (bf16[1024,1024]{1,0:T(8,128)(2,1)}, bf16[1024,1024]{1,0:T(8,128)(2,1)}, bf16[4,256,512]{2,1,0:T(8,128)(2,1)}) custom-call(s32[2]{0:T(128)} %pad_add_fusion.place, s32[512]{0:T(512)} %orders.4, s32[1,512]{1,0:T(1,128)} %bitcast.11, s32[1,1024]{1,0:T(1,128)} %add.62.targets, bf16[1024,1024]{1,0:T(8,128)(2,1)} %constant.38.clone.natural_s, ...), custom_call_target="tpu_custom_call" | custom-call | flops 4000000000 | bytes 12582912 | tf_op jit(solution)/shard_map/make_tables/pallas_call | solution.py:272
  62.9 0.6 sine_multiply_fusion.weight
  63.5 0.0 collective-permute-done.12.refs_13_
  63.5 0.0 collective-permute-done.14.refs_15_
  63.5 0.0 all-to-all-done.lat
  63.6 10.2 %grid_stage.1 = bf16[1024,768]{1,0:T(8,128)(2,1)} custom-call(bf16[8,24,64,128]{3,2,1,0:T(8,128)(2,1)} %all-to-all-done.lat, bf16[1024,1024]{1,0:T(8,128)(2,1)} %get-tuple-element.85.syn, bf16[1024,1024]{1,0:T(8,128)(2,1)} %get-tuple-element.86.ana, f32[1,128]{1,0:T(1,128)} %sine_multiply_fusion.weight), custom_call_target="tpu_custom_call" | custom-call | flops 4800000000 | bytes 9437184 | tf_op jit(solution)/shard_map/grid_stage/pallas_call | solution.py:227
  73.8 0.0 copy-start.36
  73.8 9.3 %all-to-all-start.1 = ((bf16[128,8,768]{2,1,0:T(8,128)(2,1)}), bf16[128,8,768]{2,1,0:T(8,128)(2,1)S(1)}, u32[]{:S(2)}, u32[]{:S(2)}) async-start(bf16[128,8,768]{2,1,0:T(8,128)(2,1)} %bitcast.13), calls=%async_computation.1 | async-start | bytes 3145728 | tf_op jit(solution)/shard_map/all_to_all | solution.py:520
  83.2 0.9 copy-done.4
  84.0 0.9 copy-done.6
  84.9 0.9 copy-done.8
  85.8 0.9 copy-done.10
  86.7 0.9 copy-done.12
  87.6 0.9 copy-done.14
  88.5 0.9 copy-done.16
  89.4 0.9 copy-done.18
  90.3 0.9 copy-done.20
  91.2 0.9 copy-done.22
  92.1 0.9 copy-done.24
  93.0 0.9 copy-done.26
  93.9 0.9 copy-done.28
  94.8 0.9 copy-done.30
  95.7 0.9 copy-done.32
  96.6 0.9 copy-done.34
  97.5 1.0 solve_factors.1
  98.6 9.4 %all-to-all-done.1 = bf16[128,8,768]{2,1,0:T(8,128)(2,1)S(1)} async-done(((bf16[128,8,768]{2,1,0:T(8,128)(2,1)}), bf16[128,8,768]{2,1,0:T(8,128)(2,1)S(1)}, u32[]{:S(2)}, u32[]{:S(2)}) %all-to-all-start.1) | async-done | bytes 1572896 | tf_op jit(solution)/shard_map/all_to_all | solution.py:520
  108.0 1.2 copy-done.1
  109.2 3.0 %analysis_and_solve.1 = bf16[16,96,512]{2,1,0:T(8,128)(2,1)S(1)} custom-call(s32[2]{0:T(128)S(1)} %copy-done.38, s32[512]{0:T(512)S(1)} %copy-done.36, bf16[1024,768]{1,0:T(8,128)(2,1)S(1)} %bitcast.10, bf16[4,256,512]{2,1,0:T(8,128)(2,1)S(1)} %copy-done.1, f32[3,64,512]{2,1,0:T(8,128)S(1)} %get-tuple-element.120.factors, ...), custom_call_target="tpu_custom_call" | custom-call | flops 900000000 | bytes 6291456 | tf_op jit(solution)/shard_map/analysis_and_solve/pallas_call | solution.py:417
  112.2 25.5 %all_to_all.15.got = bf16[16,96,512]{2,1,0:T(8,128)(2,1)S(1)} all-to-all(bf16[16,96,512]{2,1,0:T(8,128)(2,1)S(1)} %analysis_and_solve.1), channel_id=1, replica_groups=mesh['shell'=16,'order'=8] {'shell'}, dimensions={0} | all-to-all | bytes 3145728 | tf_op jit(solution)/shard_map/all_to_all | solution.py:524
  137.6 2.0 %unpack_solution.1 = (f32[3,2,2,64,512]{4,3,2,1,0:T(8,128)}, f32[3,2,2,64,512]{4,3,2,1,0:T(8,128)}) custom-call(bf16[16,96,512]{2,1,0:T(8,128)(2,1)S(1)} %all_to_all.15.got), custom_call_target="tpu_custom_call" | custom-call | flops 1000000 | bytes 5242880 | tf_op jit(solution)/shard_map/unpack_solution/pallas_call | solution.py:457
  (74 shorter events, 0.2 us)
Async XLA Ops:
  14.0 5.6 %copy-start.41 = (s32[4]{0:T(128)S(1)}, s32[4]{0:T(128)}, u32[]{:S(2)}) copy-start(s32[4]{0:T(128)} %param.19) | copy-start | bytes 52
  14.0 6.0 %copy-start.40 = (f32[2,2]{1,0:T(2,128)S(1)}, f32[2,2]{1,0:T(2,128)}, u32[]{:S(2)}) copy-start(f32[2,2]{1,0:T(2,128)} %param.20) | copy-start | bytes 52
  14.0 6.0 %copy-start = (bf16[3,2,2,64,512]{4,3,2,1,0:T(8,128)(2,1)S(1)}, bf16[3,2,2,64,512]{4,3,2,1,0:T(8,128)(2,1)}, u32[]{:S(2)}) copy-start(bf16[3,2,2,64,512]{4,3,2,1,0:T(8,128)(2,1)} %vel.2) | copy-start | bytes 2359300
  14.0 6.0 %copy-start.2 = (bf16[3,2,2,64,512]{4,3,2,1,0:T(8,128)(2,1)S(1)}, bf16[3,2,2,64,512]{4,3,2,1,0:T(8,128)(2,1)}, u32[]{:S(2)}) copy-start(bf16[3,2,2,64,512]{4,3,2,1,0:T(8,128)(2,1)} %pot) | copy-start | bytes 2359300
  14.0 6.0 %copy-start.37 = (s32[2]{0:T(128)S(1)}, s32[2]{0:T(128)}, u32[]{:S(2)}) copy-start(s32[2]{0:T(128)} %pad_add_fusion.place) | copy-start | bytes 28
  14.0 6.0 %copy-start.39 = (f32[2,2]{1,0:T(2,128)S(1)}, f32[2,2]{1,0:T(2,128)}, u32[]{:S(2)}) copy-start(f32[2,2]{1,0:T(2,128)} %angular.1) | copy-start | bytes 52
  14.0 14.2 %copy-start.35 = (s32[512]{0:T(512)S(1)}, s32[512]{0:T(512)}, u32[]{:S(2)}) copy-start(s32[512]{0:T(512)} %orders.4) | copy-start | bytes 6148
  14.0 49.5 %all-to-all-start = ((bf16[8,24,64,128]{3,2,1,0:T(8,128)(2,1)}), bf16[8,24,64,128]{3,2,1,0:T(8,128)(2,1)}, u32[]{:S(2)}, u32[]{:S(2)}) async-start(bf16[8,24,64,128]{3,2,1,0:T(8,128)(2,1)} %get-tuple-element.62), calls=%async_computation | async-start | bytes 6291456 | tf_op jit(solution)/shard_map/all_to_all | solution.py:501
  21.2 0.6 copy-start.3
  21.8 6.6 %collective-permute-start = (bf16[112,512]{1,0:T(8,128)(2,1)S(1)}, bf16[112,512]{1,0:T(8,128)(2,1)S(1)}, u32[]{:S(2)}, u32[]{:S(2)}) collective-permute-start(bf16[112,512]{1,0:T(8,128)(2,1)S(1)} %get-tuple-element.69), channel_id=1, source_target_pairs={{0,8},{1,33},{2,10},{3,35},{4,12},{5,37},{6,14},{7,39},{8,0},{9,41... | collective-permute-start | bytes 344072 | tf_op jit(solution)/shard_map/ppermute | solution.py:513
  23.3 10.2 %collective-permute-start.1 = (bf16[112,512]{1,0:T(8,128)(2,1)S(1)}, bf16[112,512]{1,0:T(8,128)(2,1)S(1)}, u32[]{:S(2)}, u32[]{:S(2)}) collective-permute-start(bf16[112,512]{1,0:T(8,128)(2,1)S(1)} %get-tuple-element.70), channel_id=1, source_target_pairs={{0,16},{1,65},{2,18},{3,67},{4,20},{5,69},{6,22},{7,71},{8,24},{9,... | collective-permute-start | bytes 344072 | tf_op jit(solution)/shard_map/ppermute | solution.py:513
  26.0 7.8 %collective-permute-start.2 = (bf16[112,512]{1,0:T(8,128)(2,1)S(1)}, bf16[112,512]{1,0:T(8,128)(2,1)S(1)}, u32[]{:S(2)}, u32[]{:S(2)}) collective-permute-start(bf16[112,512]{1,0:T(8,128)(2,1)S(1)} %get-tuple-element.71), channel_id=1, source_target_pairs={{0,24},{1,97},{2,26},{3,99},{4,28},{5,101},{6,30},{7,103},{8,16},{... | collective-permute-start | bytes 344072 | tf_op jit(solution)/shard_map/ppermute | solution.py:513
  26.5 10.5 %collective-permute-start.3 = (bf16[112,512]{1,0:T(8,128)(2,1)S(1)}, bf16[112,512]{1,0:T(8,128)(2,1)S(1)}, u32[]{:S(2)}, u32[]{:S(2)}) collective-permute-start(bf16[112,512]{1,0:T(8,128)(2,1)S(1)} %get-tuple-element.72), channel_id=1, source_target_pairs={{0,32},{1,9},{2,34},{3,11},{4,36},{5,13},{6,38},{7,15},{8,40},{9,1... | collective-permute-start | bytes 344072 | tf_op jit(solution)/shard_map/ppermute | solution.py:513
  28.1 9.4 %collective-permute-start.4 = (bf16[112,512]{1,0:T(8,128)(2,1)S(1)}, bf16[112,512]{1,0:T(8,128)(2,1)S(1)}, u32[]{:S(2)}, u32[]{:S(2)}) collective-permute-start(bf16[112,512]{1,0:T(8,128)(2,1)S(1)} %get-tuple-element.73), channel_id=1, source_target_pairs={{0,40},{1,41},{2,42},{3,43},{4,44},{5,45},{6,46},{7,47},{8,32},{9,... | collective-permute-start | bytes 344072 | tf_op jit(solution)/shard_map/ppermute | solution.py:513
  28.4 34.4 %copy-start.5 = (bf16[112,512]{1,0:T(8,128)(2,1)}, bf16[112,512]{1,0:T(8,128)(2,1)S(1)}, u32[]{:S(2)}) copy-start(bf16[112,512]{1,0:T(8,128)(2,1)S(1)} %collective-permute-done.refs_1_) | copy-start | bytes 344068
  28.4 16.3 %collective-permute-start.5 = (bf16[112,512]{1,0:T(8,128)(2,1)S(1)}, bf16[112,512]{1,0:T(8,128)(2,1)S(1)}, u32[]{:S(2)}, u32[]{:S(2)}) collective-permute-start(bf16[112,512]{1,0:T(8,128)(2,1)S(1)} %get-tuple-element.74), channel_id=1, source_target_pairs={{0,48},{1,73},{2,50},{3,75},{4,52},{5,77},{6,54},{7,79},{8,56},{9,... | collective-permute-start | bytes 344072 | tf_op jit(solution)/shard_map/ppermute | solution.py:513
  33.5 29.3 %copy-start.7 = (bf16[112,512]{1,0:T(8,128)(2,1)}, bf16[112,512]{1,0:T(8,128)(2,1)S(1)}, u32[]{:S(2)}) copy-start(bf16[112,512]{1,0:T(8,128)(2,1)S(1)} %collective-permute-done.1.refs_2_) | copy-start | bytes 344068
  33.5 12.3 %collective-permute-start.6 = (bf16[112,512]{1,0:T(8,128)(2,1)S(1)}, bf16[112,512]{1,0:T(8,128)(2,1)S(1)}, u32[]{:S(2)}, u32[]{:S(2)}) collective-permute-start(bf16[112,512]{1,0:T(8,128)(2,1)S(1)} %get-tuple-element.75), channel_id=1, source_target_pairs={{0,56},{1,105},{2,58},{3,107},{4,60},{5,109},{6,62},{7,111},{8,48}... | collective-permute-start | bytes 344072 | tf_op jit(solution)/shard_map/ppermute | solution.py:513
  33.8 29.0 %copy-start.9 = (bf16[112,512]{1,0:T(8,128)(2,1)}, bf16[112,512]{1,0:T(8,128)(2,1)S(1)}, u32[]{:S(2)}) copy-start(bf16[112,512]{1,0:T(8,128)(2,1)S(1)} %collective-permute-done.2.refs_3_) | copy-start | bytes 344068
  33.8 14.2 %collective-permute-start.7 = (bf16[112,512]{1,0:T(8,128)(2,1)S(1)}, bf16[112,512]{1,0:T(8,128)(2,1)S(1)}, u32[]{:S(2)}, u32[]{:S(2)}) collective-permute-start(bf16[112,512]{1,0:T(8,128)(2,1)S(1)} %get-tuple-element.76), channel_id=1, source_target_pairs={{0,64},{1,17},{2,66},{3,19},{4,68},{5,21},{6,70},{7,23},{8,72},{9,... | collective-permute-start | bytes 344072 | tf_op jit(solution)/shard_map/ppermute | solution.py:513
  37.0 25.8 %copy-start.11 = (bf16[112,512]{1,0:T(8,128)(2,1)}, bf16[112,512]{1,0:T(8,128)(2,1)S(1)}, u32[]{:S(2)}) copy-start(bf16[112,512]{1,0:T(8,128)(2,1)S(1)} %collective-permute-done.3.refs_4_) | copy-start | bytes 344068
  37.0 11.0 %collective-permute-start.8 = (bf16[112,512]{1,0:T(8,128)(2,1)S(1)}, bf16[112,512]{1,0:T(8,128)(2,1)S(1)}, u32[]{:S(2)}, u32[]{:S(2)}) collective-permute-start(bf16[112,512]{1,0:T(8,128)(2,1)S(1)} %get-tuple-element.77), channel_id=1, source_target_pairs={{0,72},{1,49},{2,74},{3,51},{4,76},{5,53},{6,78},{7,55},{8,64},{9,... | collective-permute-start | bytes 344072 | tf_op jit(solution)/shard_map/ppermute | solution.py:513
  37.5 25.4 %copy-start.13 = (bf16[112,512]{1,0:T(8,128)(2,1)}, bf16[112,512]{1,0:T(8,128)(2,1)S(1)}, u32[]{:S(2)}) copy-start(bf16[112,512]{1,0:T(8,128)(2,1)S(1)} %collective-permute-done.4.refs_5_) | copy-start | bytes 344068
  37.5 16.9 %collective-permute-start.9 = (bf16[112,512]{1,0:T(8,128)(2,1)S(1)}, bf16[112,512]{1,0:T(8,128)(2,1)S(1)}, u32[]{:S(2)}, u32[]{:S(2)}) collective-permute-start(bf16[112,512]{1,0:T(8,128)(2,1)S(1)} %get-tuple-element.78), channel_id=1, source_target_pairs={{0,80},{1,81},{2,82},{3,83},{4,84},{5,85},{6,86},{7,87},{8,88},{9,... | collective-permute-start | bytes 344072 | tf_op jit(solution)/shard_map/ppermute | solution.py:513
  44.7 18.1 %copy-start.15 = (bf16[112,512]{1,0:T(8,128)(2,1)}, bf16[112,512]{1,0:T(8,128)(2,1)S(1)}, u32[]{:S(2)}) copy-start(bf16[112,512]{1,0:T(8,128)(2,1)S(1)} %collective-permute-done.5.refs_6_) | copy-start | bytes 344068
  44.7 18.7 %collective-permute-start.10 = (bf16[112,512]{1,0:T(8,128)(2,1)S(1)}, bf16[112,512]{1,0:T(8,128)(2,1)S(1)}, u32[]{:S(2)}, u32[]{:S(2)}) collective-permute-start(bf16[112,512]{1,0:T(8,128)(2,1)S(1)} %get-tuple-element.79), channel_id=1, source_target_pairs={{0,88},{1,113},{2,90},{3,115},{4,92},{5,117},{6,94},{7,119},{8,80}... | collective-permute-start | bytes 344072 | tf_op jit(solution)/shard_map/ppermute | solution.py:513
  45.8 17.1 %copy-start.17 = (bf16[112,512]{1,0:T(8,128)(2,1)}, bf16[112,512]{1,0:T(8,128)(2,1)S(1)}, u32[]{:S(2)}) copy-start(bf16[112,512]{1,0:T(8,128)(2,1)S(1)} %collective-permute-done.6.refs_7_) | copy-start | bytes 344068
  45.8 17.7 %collective-permute-start.11 = (bf16[112,512]{1,0:T(8,128)(2,1)S(1)}, bf16[112,512]{1,0:T(8,128)(2,1)S(1)}, u32[]{:S(2)}, u32[]{:S(2)}) collective-permute-start(bf16[112,512]{1,0:T(8,128)(2,1)S(1)} %get-tuple-element.80), channel_id=1, source_target_pairs={{0,96},{1,25},{2,98},{3,27},{4,100},{5,29},{6,102},{7,31},{8,104},... | collective-permute-start | bytes 344072 | tf_op jit(solution)/shard_map/ppermute | solution.py:513
  48.0 14.9 %copy-start.19 = (bf16[112,512]{1,0:T(8,128)(2,1)}, bf16[112,512]{1,0:T(8,128)(2,1)S(1)}, u32[]{:S(2)}) copy-start(bf16[112,512]{1,0:T(8,128)(2,1)S(1)} %collective-permute-done.7.refs_8_) | copy-start | bytes 344068
  48.0 15.5 %collective-permute-start.12 = (bf16[112,512]{1,0:T(8,128)(2,1)S(1)}, bf16[112,512]{1,0:T(8,128)(2,1)S(1)}, u32[]{:S(2)}, u32[]{:S(2)}) collective-permute-start(bf16[112,512]{1,0:T(8,128)(2,1)S(1)} %get-tuple-element.81), channel_id=1, source_target_pairs={{0,104},{1,57},{2,106},{3,59},{4,108},{5,61},{6,110},{7,63},{8,96}... | collective-permute-start | bytes 344072 | tf_op jit(solution)/shard_map/ppermute | solution.py:513
  48.0 14.8 %copy-start.21 = (bf16[112,512]{1,0:T(8,128)(2,1)}, bf16[112,512]{1,0:T(8,128)(2,1)S(1)}, u32[]{:S(2)}) copy-start(bf16[112,512]{1,0:T(8,128)(2,1)S(1)} %collective-permute-done.8.refs_9_) | copy-start | bytes 344068
  48.0 15.5 %collective-permute-start.13 = (bf16[112,512]{1,0:T(8,128)(2,1)S(1)}, bf16[112,512]{1,0:T(8,128)(2,1)S(1)}, u32[]{:S(2)}, u32[]{:S(2)}) collective-permute-start(bf16[112,512]{1,0:T(8,128)(2,1)S(1)} %get-tuple-element.82), channel_id=1, source_target_pairs={{0,112},{1,89},{2,114},{3,91},{4,116},{5,93},{6,118},{7,95},{8,120... | collective-permute-start | bytes 344072 | tf_op jit(solution)/shard_map/ppermute | solution.py:513
  54.3 8.5 %copy-start.23 = (bf16[112,512]{1,0:T(8,128)(2,1)}, bf16[112,512]{1,0:T(8,128)(2,1)S(1)}, u32[]{:S(2)}) copy-start(bf16[112,512]{1,0:T(8,128)(2,1)S(1)} %collective-permute-done.9.refs_10_) | copy-start | bytes 344068
  54.4 9.2 %collective-permute-start.14 = (bf16[112,512]{1,0:T(8,128)(2,1)S(1)}, bf16[112,512]{1,0:T(8,128)(2,1)S(1)}, u32[]{:S(2)}, u32[]{:S(2)}) collective-permute-start(bf16[112,512]{1,0:T(8,128)(2,1)S(1)} %get-tuple-element.83), channel_id=1, source_target_pairs={{0,120},{1,121},{2,122},{3,123},{4,124},{5,125},{6,126},{7,127},{8... | collective-permute-start | bytes 344072 | tf_op jit(solution)/shard_map/ppermute | solution.py:513
  63.5 10.3 %copy-start.25 = (bf16[112,512]{1,0:T(8,128)(2,1)}, bf16[112,512]{1,0:T(8,128)(2,1)S(1)}, u32[]{:S(2)}) copy-start(bf16[112,512]{1,0:T(8,128)(2,1)S(1)} %collective-permute-done.10.refs_11_) | copy-start | bytes 344068
  63.5 10.3 %copy-start.27 = (bf16[112,512]{1,0:T(8,128)(2,1)}, bf16[112,512]{1,0:T(8,128)(2,1)S(1)}, u32[]{:S(2)}) copy-start(bf16[112,512]{1,0:T(8,128)(2,1)S(1)} %collective-permute-done.11.refs_12_) | copy-start | bytes 344068
  63.5 10.3 %copy-start.29 = (bf16[112,512]{1,0:T(8,128)(2,1)}, bf16[112,512]{1,0:T(8,128)(2,1)S(1)}, u32[]{:S(2)}) copy-start(bf16[112,512]{1,0:T(8,128)(2,1)S(1)} %collective-permute-done.12.refs_13_) | copy-start | bytes 344068
  63.5 10.3 %copy-start.31 = (bf16[112,512]{1,0:T(8,128)(2,1)}, bf16[112,512]{1,0:T(8,128)(2,1)S(1)}, u32[]{:S(2)}) copy-start(bf16[112,512]{1,0:T(8,128)(2,1)S(1)} %collective-permute-done.13.refs_14_) | copy-start | bytes 344068
  63.5 10.3 %copy-start.33 = (bf16[112,512]{1,0:T(8,128)(2,1)}, bf16[112,512]{1,0:T(8,128)(2,1)S(1)}, u32[]{:S(2)}) copy-start(bf16[112,512]{1,0:T(8,128)(2,1)S(1)} %collective-permute-done.14.refs_15_) | copy-start | bytes 344068
  73.8 9.3 %copy-start.38 = (s32[2]{0:T(128)S(1)}, s32[2]{0:T(128)}, u32[]{:S(2)}) copy-start(s32[2]{0:T(128)} %pad_add_fusion.place) | copy-start | bytes 28
  73.8 34.2 %copy-start.36 = (s32[512]{0:T(512)S(1)}, s32[512]{0:T(512)}, u32[]{:S(2)}) copy-start(s32[512]{0:T(512)} %orders.4) | copy-start | bytes 6148
  73.8 34.2 %all-to-all-start.1 = ((bf16[128,8,768]{2,1,0:T(8,128)(2,1)}), bf16[128,8,768]{2,1,0:T(8,128)(2,1)S(1)}, u32[]{:S(2)}, u32[]{:S(2)}) async-start(bf16[128,8,768]{2,1,0:T(8,128)(2,1)} %bitcast.13), calls=%async_computation.1 | async-start | bytes 3145728 | tf_op jit(solution)/shard_map/all_to_all | solution.py:520
  83.1 0.9 copy-start.4
  84.0 0.9 copy-start.6
  84.9 0.9 copy-start.8
  85.8 0.9 copy-start.10
  86.7 0.9 copy-start.12
  87.6 0.9 copy-start.14
  88.5 0.9 copy-start.16
  89.4 0.9 copy-start.18
  90.3 0.9 copy-start.20
  91.2 0.9 copy-start.22
  92.1 0.9 copy-start.24
  93.0 0.9 copy-start.26
  93.9 0.9 copy-start.28
  94.8 0.9 copy-start.30
  95.7 0.9 copy-start.32
  96.6 0.9 copy-start.34
  108.0 1.2 copy-start.1

commit v7 on v6

--- a/solution.py
+++ b/solution.py
@@ -17,14 +17,21 @@
 MIB = 1 << 20
 
 
+FOLD = NPHI // 2
+
+
 def natural_tables():
-    phases = (np.arange(L)[:, None] * np.arange(NPHI)[None, :]) % NPHI
-    angles = 2.0 * np.pi * phases / NPHI
-    rows = np.stack([np.cos(angles), -np.sin(angles)], axis=0)
-    weight = np.where(np.arange(L) == 0, 1.0, 2.0) * (math.sqrt(2.0 * math.pi) / L)
-    synthesis = (rows * weight[None, :, None]).reshape(2 * L, NPHI)
-    analysis = (rows / NPHI).reshape(2 * L, NPHI)
-    return synthesis.T.astype(jnp.bfloat16), analysis.astype(jnp.bfloat16)
+    order = np.arange(L)[None, :]
+    angles = 2.0 * np.pi * ((np.arange(FOLD + 16)[:, None] * order) % NPHI) / NPHI
+    weight = np.where(order == 0, 1.0, 2.0) * (math.sqrt(2.0 * math.pi) / L)
+    syn_cos = np.cos(angles) * weight
+    syn_cos[FOLD + 1 :] = 0.0
+    syn_sin = (-np.sin(angles) * weight)[:FOLD]
+    ana_cos = np.cos(angles)[:FOLD].T / NPHI
+    ana_cos[:, 0] *= 0.5
+    ana_sin = -np.sin(angles)[:FOLD].T / NPHI
+    last = np.repeat(np.cos(np.pi * order).T / NPHI, 128, axis=1)
+    return [jnp.asarray(a.astype(jnp.bfloat16)) for a in (syn_cos, syn_sin, ana_cos, ana_sin, last)]
 
 
 def partner(place, r):
@@ -184,9 +191,22 @@
     )(place, kappa, angular, velocity, potential)
 
 
-def grid_kernel(lat, syn, ana, weight, out, wide, prod):
+def products(x):
+    u, w, b, j = x[0:3], x[3:6], x[6:9], x[9:12]
+
+    def cross(p, q):
+        return [
+            p[1] * q[2] - p[2] * q[1],
+            p[2] * q[0] - p[0] * q[2],
+            p[0] * q[1] - p[1] * q[0],
+        ]
+
+    uw, jb, ub = cross(u, w), cross(j, b), cross(u, b)
+    return [uw[0] + jb[0] + 2.0 * u[1], uw[1] + jb[1] - 2.0 * u[0], uw[2] + jb[2]] + ub
+
+
+def grid_kernel(lat, syn_cos, syn_sin, ana_cos, ana_sin, ana_last, weight, out, wide, even, odd, middle):
     step = pl.program_id(0)
-    rows = 512
 
     @pl.when(step == 0)
     def _():
@@ -194,65 +214,99 @@
             for p in range(2):
                 rows_p = lat[:, 2 * c + p].reshape(512, 128)
                 wide[p * 512 : p * 512 + 512, c * 128 : c * 128 + 128] = rows_p
-
-    @pl.when(step < 2)
+        g = jnp.dot(syn_cos[...], wide[0:512, :], preferred_element_type=f32)
+        d = jnp.dot(syn_sin[...], wide[512:1024, :], preferred_element_type=f32)
+        cols = [slice(c * 128, c * 128 + 128) for c in range(12)]
+        here = products([g[0:FOLD, at] + d[:, at] for at in cols])
+        mirror = products([g[0:FOLD, at] - d[:, at] for at in cols])
+        edge = products([g[FOLD : FOLD + 8, at] for at in cols])
+        for c in range(6):
+            even[:, cols[c]] = (here[c] + mirror[c]).astype(bf16)
+            odd[:, cols[c]] = (here[c] - mirror[c]).astype(bf16)
+            middle[:, cols[c]] = edge[c]
+
+    @pl.when(step > 0)
     def _():
-        g = jnp.dot(syn[...], wide[...], preferred_element_type=f32)
-        x = [g[:, c * 128 : c * 128 + 128] for c in range(12)]
-        u, w, b, j = x[0:3], x[3:6], x[6:9], x[9:12]
-
-        def cross(p, q):
-            return [
-                p[1] * q[2] - p[2] * q[1],
-                p[2] * q[0] - p[0] * q[2],
-                p[0] * q[1] - p[1] * q[0],
-            ]
-
-        uw, jb, ub = cross(u, w), cross(j, b), cross(u, b)
-        terms = [uw[0] + jb[0] + 2.0 * u[1], uw[1] + jb[1] - 2.0 * u[0], uw[2] + jb[2]] + ub
-        at = pl.ds(pl.multiple_of(step * rows, rows), rows)
+        real = jnp.dot(ana_cos[...], even[...], preferred_element_type=f32)
+        imag = jnp.dot(ana_sin[...], odd[...], preferred_element_type=f32)
+        sign = ana_last[...]
+        low = lax.broadcasted_iota(jnp.int32, (1, 8, 1), 1) < 4
         for c in range(6):
-            prod[at, c * 128 : c * 128 + 128] = terms[c].astype(bf16)
-
-    @pl.when(step >= 2)
-    def _():
-        sums = jnp.dot(ana[...], prod[...], preferred_element_type=f32)
-        for c in range(6):
-            part = sums[:, c * 128 : c * 128 + 128] * weight[...]
-            out[:, c * 128 : c * 128 + 128] = part.astype(bf16)
-
-
-def grid_stage(lat, syn, ana, weight):
-    rows = 512
+            at = slice(c * 128, c * 128 + 128)
+            a = (real[:, at] + sign * middle[0:1, at]) * weight[...]
+            b = imag[:, at] * weight[...]
+            a, b = a.reshape(32, 8, 128), b.reshape(32, 8, 128)
+            first = jnp.where(low, a, pltpu.roll(b, 4, 1))
+            second = jnp.where(low, pltpu.roll(a, 4, 1), b)
+            both = jnp.stack([first, second], axis=1).reshape(512, 128)
+            out[:, at] = both.astype(bf16)
+
+
+def grid_stage(lat, tables, weight):
+    rows = 256
+    by_slots = pl.BlockSpec((rows, FOLD), lambda i: (jnp.maximum(i - 1, 0), 0))
     return pl.pallas_call(
         grid_kernel,
-        grid=(4,),
+        grid=(3,),
         in_specs=[
             pl.BlockSpec((8, 24, 64, 128), lambda i: (0, 0, 0, 0)),
-            pl.BlockSpec((rows, 1024), lambda i: (jnp.minimum(i, 1), 0)),
-            pl.BlockSpec((rows, 1024), lambda i: (jnp.maximum(i - 2, 0), 0)),
+            pl.BlockSpec((FOLD + 16, L), lambda i: (0, 0)),
+            pl.BlockSpec((FOLD, L), lambda i: (0, 0)),
+            by_slots,
+            by_slots,
+            pl.BlockSpec((rows, 128), lambda i: (jnp.maximum(i - 1, 0), 0)),
             pl.BlockSpec((1, 128), lambda i: (0, 0)),
         ],
-        out_specs=pl.BlockSpec((rows, 768), lambda i: (jnp.maximum(i - 2, 0), 0)),
+        out_specs=pl.BlockSpec((2 * rows, 768), lambda i: (jnp.maximum(i - 1, 0), 0)),
         out_shape=jax.ShapeDtypeStruct((1024, 768), bf16),
-        scratch_shapes=[pltpu.VMEM((1024, 1536), bf16), pltpu.VMEM((1024, 768), bf16)],
+        scratch_shapes=[
+            pltpu.VMEM((1024, 1536), bf16),
+            pltpu.VMEM((FOLD, 768), bf16),
+            pltpu.VMEM((FOLD, 768), bf16),
+            pltpu.VMEM((8, 768), f32),
+        ],
         compiler_params=pltpu.CompilerParams(vmem_limit_bytes=60 * MIB),
-        cost_estimate=pl.CostEstimate(flops=int(4.8e9), bytes_accessed=9 * MIB, transcendentals=0),
+        cost_estimate=pl.CostEstimate(flops=int(2.4e9), bytes_accessed=7 * MIB, transcendentals=0),
         name="grid_stage",
-    )(lat, syn, ana, weight)
-
-
-def tables_kernel(place, orders, slots, targets, natural_s, natural_a, pairs, syn, ana, table_out, scr):
+    )(lat, *tables, weight)
+
+
+def tables_kernel(slots, targets, *refs):
+    natural, made = refs[:5], refs[5:]
     ids = lax.broadcasted_iota(jnp.int32, (L, L), 0)
     pick = jnp.where(ids == slots[...], 1.0, 0.0).astype(bf16)
-    for p in range(2):
-        at = slice(p * L, p * L + L)
-        syn[:, at] = jnp.dot(natural_s[:, at], pick, preferred_element_type=f32).astype(bf16)
-    ids = lax.broadcasted_iota(jnp.int32, (2 * L, 2 * L), 0)
+    for at in range(2):
+        made[at][...] = jnp.dot(natural[at][...], pick, preferred_element_type=f32).astype(bf16)
     pick = jnp.where(ids == targets[...], 1.0, 0.0).astype(bf16)
-    ana[...] = lax.dot_general(
-        pick, natural_a[...], (((0,), (0,)), ((), ())), preferred_element_type=f32
-    ).astype(bf16)
+    for at in range(2, 5):
+        made[at][...] = lax.dot_general(
+            pick, natural[at][...], (((0,), (0,)), ((), ())), preferred_element_type=f32
+        ).astype(made[at].dtype)
+
+
+def make_tables(order_slots):
+    natural = natural_tables()
+    targets = order_slots.reshape(8, 16, 4).transpose(1, 0, 2).reshape(1, L)
+    whole = lambda shape: pl.BlockSpec(shape, lambda g: (0, 0))
+    made = [jax.ShapeDtypeStruct(a.shape, bf16) for a in natural[:4]]
+    made.append(jax.ShapeDtypeStruct((L, 128), f32))
+    return pl.pallas_call(
+        tables_kernel,
+        grid=(1,),
+        in_specs=[whole((1, L)), whole((1, L))] + [whole(a.shape) for a in natural],
+        out_specs=[whole(a.shape) for a in made],
+        out_shape=made,
+        compiler_params=pltpu.CompilerParams(vmem_limit_bytes=60 * MIB),
+        cost_estimate=pl.CostEstimate(flops=int(1e9), bytes_accessed=5 * MIB, transcendentals=0),
+        name="make_tables",
+    )(order_slots.reshape(1, L), targets, *natural)
+
+
+def factors_kernel(place, orders, pairs, *refs):
+    parts, (state, factors, table_out, extra, scr) = refs[:16], refs[16:]
+    for r in range(16):
+        state[partner(place, r)] = parts[r][0:96, :]
+        extra[partner(place, r)] = parts[r][96:112, :].astype(f32)
     l_row = lax.broadcasted_iota(jnp.int32, (1, L), 1)
     for i in range(2):
         m = orders[place[1] * 64 + place[0] * 4 + 2 * i]
@@ -262,52 +316,6 @@
         table_out[2 * i] = jnp.where(l_row >= m, a, 0.0).astype(bf16)
         b = jnp.transpose(scr[1 : L + 1, :])
         table_out[2 * i + 1] = jnp.where(l_row >= L - 1 - m, b, 0.0).astype(bf16)
-
-
-def make_tables(place, order_slots, pairs):
-    natural_s, natural_a = natural_tables()
-    slots = order_slots.reshape(8, 16, 4).transpose(1, 0, 2)[..., None]
-    targets = (slots + jnp.arange(2, dtype=jnp.int32) * L).reshape(1, 2 * L)
-    whole = lambda *shape: pl.BlockSpec(shape, lambda g: (0,) * len(shape))
-    return pl.pallas_call(
-        tables_kernel,
-        grid=(1,),
-        in_specs=[
-            pl.BlockSpec(memory_space=pltpu.SMEM),
-            pl.BlockSpec(memory_space=pltpu.SMEM),
-            whole(1, L),
-            whole(1, 2 * L),
-            whole(NPHI, 2 * L),
-            whole(2 * L, NPHI),
-            whole(2, L + 16, NH),
-        ],
-        out_specs=[whole(NPHI, 2 * L), whole(2 * L, NPHI), whole(4, NH, L)],
-        out_shape=[
-            jax.ShapeDtypeStruct((NPHI, 2 * L), bf16),
-            jax.ShapeDtypeStruct((2 * L, NPHI), bf16),
-            jax.ShapeDtypeStruct((4, NH, L), bf16),
-        ],
-        scratch_shapes=[pltpu.VMEM((L + 16, NH), f32)],
-        compiler_params=pltpu.CompilerParams(vmem_limit_bytes=60 * MIB),
-        cost_estimate=pl.CostEstimate(flops=int(4e9), bytes_accessed=12 * MIB, transcendentals=0),
-        name="make_tables",
-    )(
-        place,
-        order_slots,
-        order_slots.reshape(1, L),
-        targets,
-        jnp.asarray(natural_s),
-        jnp.asarray(natural_a),
-        pairs,
-    )
-
-
-def factors_kernel(place, *refs):
-    parts, (state, factors, extra) = refs[:16], refs[16:]
-    for r in range(16):
-        state[partner(place, r)] = parts[r][0:96, :]
-        extra[partner(place, r)] = parts[r][96:112, :].astype(f32)
-    l_row = lax.broadcasted_iota(jnp.int32, (1, L), 1)
     degree = l_row.astype(f32)
     degree_term = degree * (degree + 1.0)
     below, angle = [[], []], [[], []]
@@ -333,25 +341,31 @@
             factors[2, row : row + 1, :] = carried
 
 
-def solve_factors(place, parts):
+def solve_factors(place, orders, pairs, parts):
     return pl.pallas_call(
         factors_kernel,
         grid=(1,),
-        in_specs=[pl.BlockSpec(memory_space=pltpu.SMEM)]
+        in_specs=[
+            pl.BlockSpec(memory_space=pltpu.SMEM),
+            pl.BlockSpec(memory_space=pltpu.SMEM),
+            pl.BlockSpec((2, L + 16, NH), lambda g: (0, 0, 0)),
+        ]
         + [pl.BlockSpec((112, L), lambda g: (0, 0))] * 16,
         out_specs=[
             pl.BlockSpec((16, 96, L), lambda g: (0, 0, 0)),
             pl.BlockSpec((3, 64, L), lambda g: (0, 0, 0)),
+            pl.BlockSpec((4, NH, L), lambda g: (0, 0, 0)),
         ],
         out_shape=[
             jax.ShapeDtypeStruct((16, 96, L), bf16),
             jax.ShapeDtypeStruct((3, 64, L), f32),
-        ],
-        scratch_shapes=[pltpu.VMEM((16, 16, L), f32)],
+            jax.ShapeDtypeStruct((4, NH, L), bf16),
+        ],
+        scratch_shapes=[pltpu.VMEM((16, 16, L), f32), pltpu.VMEM((L + 16, NH), f32)],
         compiler_params=pltpu.CompilerParams(vmem_limit_bytes=16 * MIB),
         cost_estimate=pl.CostEstimate(flops=10**6, bytes_accessed=MIB, transcendentals=0),
         name="solve_factors",
-    )(place, *parts)
+    )(place, orders, pairs, *parts)
 
 
 def solve_kernel(place, orders, coef, table, factors, state, out, cs, lhs, rhs, reduced):
@@ -369,7 +383,7 @@
                 for p in range(2):
                     row = ((h * 6 + c) * 2 + p) * 32
                     for jh in range(2):
-                        start = h * 16 + jh * 8 + k * 2 + p
+                        start = h * 16 + jh * 8 + p * 4 + k
                         lhs[k % 2, row : row + 32, jh * 128 : jh * 128 + 128] = cs[
                             c, pl.ds(start, 32, stride=33), :
                         ].astype(bf16)
@@ -511,12 +525,12 @@
             (i * 8 + o, (i ^ (swapped if o & 1 else r)) * 8 + o) for i in range(16) for o in range(8)
         ]
         received.append(lax.ppermute(parts[r], ("shell", "order"), pairs_r))
-    syn, ana, table = make_tables(place, order_after, pairs)
-    incoming, table, received = lax.optimization_barrier((incoming, table, received))
-
-    coefs = grid_stage(incoming, syn, ana, weight)
+    tables = make_tables(order_after)
+    incoming, received = lax.optimization_barrier((incoming, received))
+
+    coefs = grid_stage(incoming, tables, weight)
     received, _ = lax.optimization_barrier((received, coefs))
-    state, factors = solve_factors(place, received)
+    state, factors, table = solve_factors(place, order_slots, pairs, received)
     coefs = lax.all_to_all(
         coefs.reshape(128, 8, 768), ("shell", "order"), 0, 0, tiled=True
     ).reshape(1024, 768)

time: 141 us -> 138 us (0.979)
  Pallas kernels: 37.5 us -> 32.5 us
  local copies, waits for them, and re-layouts: 17.3 us -> 22.3 us
  starting transfers between devices: 47 us -> 43.7 us
    pallas_call x2, Pallas kernels: 17.7 us -> 12 us  [the longest x1 7.97 us: grid_stage(): pl.pallas_call(grid_kernel, grid=(3,), in_specs=[pl.BlockSpec((8, 24, 64,...]
    unnamed x84 -> x86, local copies, waits for them, and re-layouts: 16.3 us -> 21.5 us
    ppermute x15, waiting for transfers between devices: 0.04 us -> 3.34 us  [body(): received.append(lax.ppermute(parts[r], ('shell', 'order'), pairs_r))]
    all_to_all x1, waiting for transfers between devices: 9.43 us -> 6.81 us  [body(): lax.all_to_all(coefs.reshape(128, 8, 768), ('shell', 'order'), 0, 0, tile...]
    all_to_all x1, starting transfers between devices: 9.29 us -> 6.88 us  [body(): lax.all_to_all(coefs.reshape(128, 8, 768), ('shell', 'order'), 0, 0, tile...]
  transfers between devices with their start and end apart: 17 -> 17, of which waited for: 1 -> 2; matrix products, arithmetic and copies ran while one was open for 2% -> 1% of each run, Pallas kernels for 7% -> 5%
where the time goes in v7:
time: 138 us; the launch traced here: 137 us
  starting transfers between devices  43.7 us (32%)
  Pallas kernels  32.5 us (24%)
  blocking collectives  25.4 us (18%)
  local copies, waits for them, and re-layouts  22.3 us (16%)
  waiting for transfers between devices  10.2 us (7%)
  other arithmetic  1.61 us (1%)
    ppermute x15, starting transfers between devices, body(): received.append(lax.ppermute(parts[r], ('shell', 'order'), pairs_r))  31.3 us
    all_to_all x1, blocking collectives, body(): solved = lax.all_to_all(solved, 'shell', 0, 0, tiled=True)  25.4 us
    unnamed x86, local copies, waits for them, and re-layouts  21.5 us
    pallas_call x1, Pallas kernels, legendre_synthesis(): pl.pallas_call(synthesis_kernel, grid_spec=pltpu.PrefetchScalarGridSpec(n...  12.8 us
    pallas_call x1, Pallas kernels, grid_stage(): pl.pallas_call(grid_kernel, grid=(3,), in_specs=[pl.BlockSpec((8, 24, 64,...  7.97 us
    all_to_all x1, starting transfers between devices, body(): lax.all_to_all(coefs.reshape(128, 8, 768), ('shell', 'order'), 0, 0, tile...  6.88 us
    all_to_all x1, waiting for transfers between devices, body(): lax.all_to_all(coefs.reshape(128, 8, 768), ('shell', 'order'), 0, 0, tile...  6.81 us
    all_to_all x1, starting transfers between devices, body(): incoming = lax.all_to_all(latitude, 'order', 0, 0, tiled=True)  5.54 us
  transfers between devices with their start and end apart: 17, of which 2 were waited for; matrix products, arithmetic and copies ran while one was open for 1% of the time, Pallas kernels for 5%

profile of v7, /device:TPU:0, one launch (start us, length us, event | category | flops | bytes accessed | tf_op | source)
XLA Modules:
  0.0 136.7 jit_solution(5192722444114288468)
XLA Ops:
  0.6 0.7 pad_add_fusion.place
  1.3 12.8 %legendre_synthesis.1 = (bf16[8,24,64,128]{3,2,1,0:T(8,128)(2,1)}, bf16[2,528,256]{2,1,0:T(8,128)(2,1)}) custom-call(s32[2]{0:T(128)} %pad_add_fusion.place, s32[512]{0:T(512)} %orders.5, bf16[3,2,2,64,512]{4,3,2,1,0:T(8,128)(2,1)} %vel.2, bf16[3,2,2,64,512]{4,3,2,1,0:T(8,128)(2,1)} %vor.1, bf16[3,2,2,64,512]{4,3,2,1,0:T(8,128)(2,1)} %mag.1, ...), custom_call_target="tpu_custom_call" | custom-call | flops 1600000000 | bytes 15728640 | tf_op jit(solution)/shard_map/legendre_synthesis/pallas_call | solution.py:124
  14.1 0.0 copy-start
  14.1 0.0 copy-start.3
  14.1 0.0 copy-start.40
  14.1 5.5 %all-to-all-start = ((bf16[8,24,64,128]{3,2,1,0:T(8,128)(2,1)}), bf16[8,24,64,128]{3,2,1,0:T(8,128)(2,1)}, u32[]{:S(2)}, u32[]{:S(2)}) async-start(bf16[8,24,64,128]{3,2,1,0:T(8,128)(2,1)} %get-tuple-element.64), calls=%async_computation | async-start | bytes 6291456 | tf_op jit(solution)/shard_map/all_to_all | solution.py:515
  19.7 0.2 reduce-window.9
  19.9 0.2 compare_reduce_fusion
  20.1 1.2 state_to_send.1
  21.3 0.6 copy-done.5
  21.9 1.5 %collective-permute-start = (bf16[112,512]{1,0:T(8,128)(2,1)S(1)}, bf16[112,512]{1,0:T(8,128)(2,1)S(1)}, u32[]{:S(2)}, u32[]{:S(2)}) collective-permute-start(bf16[112,512]{1,0:T(8,128)(2,1)S(1)} %get-tuple-element.68), channel_id=1, source_target_pairs={{0,8},{1,33},{2,10},{3,35},{4,12},{5,37},{6,14},{7,39},{8,0},{9,41... | collective-permute-start | bytes 344072 | tf_op jit(solution)/shard_map/ppermute | solution.py:527
  23.4 2.7 %collective-permute-start.1 = (bf16[112,512]{1,0:T(8,128)(2,1)S(1)}, bf16[112,512]{1,0:T(8,128)(2,1)S(1)}, u32[]{:S(2)}, u32[]{:S(2)}) collective-permute-start(bf16[112,512]{1,0:T(8,128)(2,1)S(1)} %get-tuple-element.69), channel_id=1, source_target_pairs={{0,16},{1,65},{2,18},{3,67},{4,20},{5,69},{6,22},{7,71},{8,24},{9,... | collective-permute-start | bytes 344072 | tf_op jit(solution)/shard_map/ppermute | solution.py:527
  26.1 0.5 collective-permute-start.2
  26.6 1.6 %collective-permute-start.3 = (bf16[112,512]{1,0:T(8,128)(2,1)S(1)}, bf16[112,512]{1,0:T(8,128)(2,1)S(1)}, u32[]{:S(2)}, u32[]{:S(2)}) collective-permute-start(bf16[112,512]{1,0:T(8,128)(2,1)S(1)} %get-tuple-element.71), channel_id=1, source_target_pairs={{0,32},{1,9},{2,34},{3,11},{4,36},{5,13},{6,38},{7,15},{8,40},{9,1... | collective-permute-start | bytes 344072 | tf_op jit(solution)/shard_map/ppermute | solution.py:527
  28.2 0.2 collective-permute-start.4
  28.4 0.6 copy-done.7
  29.0 5.0 %collective-permute-start.5 = (bf16[112,512]{1,0:T(8,128)(2,1)S(1)}, bf16[112,512]{1,0:T(8,128)(2,1)S(1)}, u32[]{:S(2)}, u32[]{:S(2)}) collective-permute-start(bf16[112,512]{1,0:T(8,128)(2,1)S(1)} %get-tuple-element.73), channel_id=1, source_target_pairs={{0,48},{1,73},{2,50},{3,75},{4,52},{5,77},{6,54},{7,79},{8,56},{9,... | collective-permute-start | bytes 344072 | tf_op jit(solution)/shard_map/ppermute | solution.py:527
  33.9 0.0 collective-permute-done.1.refs_2_
  34.0 0.6 copy-done.9
  34.6 0.4 collective-permute-start.6
  35.0 0.6 copy-done.11
  35.6 3.2 %collective-permute-start.7 = (bf16[112,512]{1,0:T(8,128)(2,1)S(1)}, bf16[112,512]{1,0:T(8,128)(2,1)S(1)}, u32[]{:S(2)}, u32[]{:S(2)}) collective-permute-start(bf16[112,512]{1,0:T(8,128)(2,1)S(1)} %get-tuple-element.75), channel_id=1, source_target_pairs={{0,64},{1,17},{2,66},{3,19},{4,68},{5,21},{6,70},{7,23},{8,72},{9,... | collective-permute-start | bytes 344072 | tf_op jit(solution)/shard_map/ppermute | solution.py:527
  38.8 0.6 copy-done.13
  39.4 0.0 collective-permute-start.8
  39.5 0.6 copy-done.15
  40.1 6.6 %collective-permute-start.9 = (bf16[112,512]{1,0:T(8,128)(2,1)S(1)}, bf16[112,512]{1,0:T(8,128)(2,1)S(1)}, u32[]{:S(2)}, u32[]{:S(2)}) collective-permute-start(bf16[112,512]{1,0:T(8,128)(2,1)S(1)} %get-tuple-element.77), channel_id=1, source_target_pairs={{0,80},{1,81},{2,82},{3,83},{4,84},{5,85},{6,86},{7,87},{8,88},{9,... | collective-permute-start | bytes 344072 | tf_op jit(solution)/shard_map/ppermute | solution.py:527
  46.7 0.1 reshape.76
  46.8 0.7 reshape.77.targets
  47.5 0.2 collective-permute-start.10
  47.8 3.0 %collective-permute-start.11 = (bf16[112,512]{1,0:T(8,128)(2,1)S(1)}, bf16[112,512]{1,0:T(8,128)(2,1)S(1)}, u32[]{:S(2)}, u32[]{:S(2)}) collective-permute-start(bf16[112,512]{1,0:T(8,128)(2,1)S(1)} %get-tuple-element.79), channel_id=1, source_target_pairs={{0,96},{1,25},{2,98},{3,27},{4,100},{5,29},{6,102},{7,31},{8,104},... | collective-permute-start | bytes 344072 | tf_op jit(solution)/shard_map/ppermute | solution.py:527
  50.8 6.3 %collective-permute-start.13 = (bf16[112,512]{1,0:T(8,128)(2,1)S(1)}, bf16[112,512]{1,0:T(8,128)(2,1)S(1)}, u32[]{:S(2)}, u32[]{:S(2)}) collective-permute-start(bf16[112,512]{1,0:T(8,128)(2,1)S(1)} %get-tuple-element.81), channel_id=1, source_target_pairs={{0,112},{1,89},{2,114},{3,91},{4,116},{5,93},{6,118},{7,95},{8,120... | collective-permute-start | bytes 344072 | tf_op jit(solution)/shard_map/ppermute | solution.py:527
  57.2 0.1 collective-permute-start.14
  57.3 4.0 %make_tables.1 = (bf16[528,512]{1,0:T(8,128)(2,1)}, bf16[512,512]{1,0:T(8,128)(2,1)}, bf16[512,512]{1,0:T(8,128)(2,1)}, bf16[512,512]{1,0:T(8,128)(2,1)}, f32[512,128]{1,0:T(8,128)}) custom-call(s32[1,512]{1,0:T(1,128)} %bitcast.11, s32[1,512]{1,0:T(1,128)} %reshape.77.targets, bf16[528,512]{1,0:T(8,128)(2,1)} %constant.42.clone.refs_0_, ...), custom_call_target="tpu_custom_call" | custom-call | flops 1000000000 | bytes 5242880 | tf_op jit(solution)/shard_map/make_tables/pallas_call | solution.py:293
  61.3 0.6 sine_multiply_fusion.weight
  62.0 3.3 %collective-permute-done.14.refs_15_ = bf16[112,512]{1,0:T(8,128)(2,1)S(1)} collective-permute-done((bf16[112,512]{1,0:T(8,128)(2,1)S(1)}, bf16[112,512]{1,0:T(8,128)(2,1)S(1)}, u32[]{:S(2)}, u32[]{:S(2)}) %collective-permute-start.14) | collective-permute-done | bytes 114720 | tf_op jit(solution)/shard_map/ppermute | solution.py:527
  65.3 8.0 %grid_stage.1 = bf16[1024,768]{1,0:T(8,128)(2,1)} custom-call(bf16[8,24,64,128]{3,2,1,0:T(8,128)(2,1)} %all-to-all-done.lat, bf16[528,512]{1,0:T(8,128)(2,1)} %get-tuple-element.85.syn_cos, bf16[512,512]{1,0:T(8,128)(2,1)} %get-tuple-element.86.syn_sin, bf16[512,512]{1,0:T(8,128)(2,1)} %get-tuple-element.87.ana_cos, ...), custom_call_target="tpu_custom_call" | custom-call | flops 2400000000 | bytes 7340032 | tf_op jit(solution)/shard_map/grid_stage/pallas_call | solution.py:248
  73.3 0.0 copy-start.38
  73.3 6.9 %all-to-all-start.1 = ((bf16[128,8,768]{2,1,0:T(8,128)(2,1)}), bf16[128,8,768]{2,1,0:T(8,128)(2,1)S(1)}, u32[]{:S(2)}, u32[]{:S(2)}) async-start(bf16[128,8,768]{2,1,0:T(8,128)(2,1)} %bitcast.13), calls=%async_computation.1 | async-start | bytes 3145728 | tf_op jit(solution)/shard_map/all_to_all | solution.py:534
  80.2 0.0 copy-start.4
  80.2 1.0 copy-done.4
  81.3 0.9 copy-done.6
  82.2 0.9 copy-done.8
  83.0 0.9 copy-done.10
  83.9 0.9 copy-done.12
  84.8 0.9 copy-done.14
  85.7 0.9 copy-done.16
  86.6 0.9 copy-done.18
  87.5 0.9 copy-done.20
  88.4 0.9 copy-done.22
  89.3 0.9 copy-done.24
  90.2 0.9 copy-done.26
  91.1 0.9 copy-done.28
  92.0 0.9 copy-done.30
  92.9 0.9 copy-done.32
  93.8 0.9 copy-done.34
  94.7 0.9 copy-done.36
  95.6 1.6 %solve_factors.1 = (bf16[16,96,512]{2,1,0:T(8,128)(2,1)S(1)}, f32[3,64,512]{2,1,0:T(8,128)S(1)}, bf16[4,256,512]{2,1,0:T(8,128)(2,1)S(1)}) custom-call(s32[2]{0:T(128)S(1)} %copy-done.39, s32[512]{0:T(512)S(1)} %copy-done.38, bf16[2,528,256]{2,1,0:T(8,128)(2,1)S(1)} %copy-done.4, bf16[112,512]{1,0:T(8,128)(2,1)S(1)} %copy-done.6, ...), custom_call_target="tpu_custom_call" | custom-call | flops 1000000 | bytes 1048576 | tf_op jit(solution)/shard_map/solve_factors/pallas_call | solution.py:345
  97.3 0.0 copy-start.1
  97.3 1.0 copy-done.1
  98.2 6.8 %all-to-all-done.1 = bf16[128,8,768]{2,1,0:T(8,128)(2,1)S(1)} async-done(((bf16[128,8,768]{2,1,0:T(8,128)(2,1)}), bf16[128,8,768]{2,1,0:T(8,128)(2,1)S(1)}, u32[]{:S(2)}, u32[]{:S(2)}) %all-to-all-start.1) | async-done | bytes 1572896 | tf_op jit(solution)/shard_map/all_to_all | solution.py:534
  105.1 1.2 copy-done.2
  106.3 3.0 %analysis_and_solve.1 = bf16[16,96,512]{2,1,0:T(8,128)(2,1)S(1)} custom-call(s32[2]{0:T(128)S(1)} %copy-done.39, s32[512]{0:T(512)S(1)} %copy-done.38, bf16[1024,768]{1,0:T(8,128)(2,1)S(1)} %bitcast.10, bf16[4,256,512]{2,1,0:T(8,128)(2,1)S(1)} %copy-done.2, f32[3,64,512]{2,1,0:T(8,128)S(1)} %get-tuple-element.124.factors, ...), custom_call_target="tpu_custom_call" | custom-call | flops 900000000 | bytes 6291456 | tf_op jit(solution)/shard_map/analysis_and_solve/pallas_call | solution.py:431
  109.3 25.4 %all_to_all.15.got = bf16[16,96,512]{2,1,0:T(8,128)(2,1)S(1)} all-to-all(bf16[16,96,512]{2,1,0:T(8,128)(2,1)S(1)} %analysis_and_solve.1), channel_id=1, replica_groups=mesh['shell'=16,'order'=8] {'shell'}, dimensions={0} | all-to-all | bytes 3145728 | tf_op jit(solution)/shard_map/all_to_all | solution.py:538
  134.7 2.0 %unpack_solution.1 = (f32[3,2,2,64,512]{4,3,2,1,0:T(8,128)}, f32[3,2,2,64,512]{4,3,2,1,0:T(8,128)}) custom-call(bf16[16,96,512]{2,1,0:T(8,128)(2,1)S(1)} %all_to_all.15.got), custom_call_target="tpu_custom_call" | custom-call | flops 1000000 | bytes 5242880 | tf_op jit(solution)/shard_map/unpack_solution/pallas_call | solution.py:471
  (74 shorter events, 0.2 us)
Async XLA Ops:
  14.1 5.6 %copy-start.42 = (s32[4]{0:T(128)S(1)}, s32[4]{0:T(128)}, u32[]{:S(2)}) copy-start(s32[4]{0:T(128)} %param.22) | copy-start | bytes 52
  14.1 6.0 %copy-start.41 = (f32[2,2]{1,0:T(2,128)S(1)}, f32[2,2]{1,0:T(2,128)}, u32[]{:S(2)}) copy-start(f32[2,2]{1,0:T(2,128)} %param.23) | copy-start | bytes 52
  14.1 6.0 %copy-start = (bf16[3,2,2,64,512]{4,3,2,1,0:T(8,128)(2,1)S(1)}, bf16[3,2,2,64,512]{4,3,2,1,0:T(8,128)(2,1)}, u32[]{:S(2)}) copy-start(bf16[3,2,2,64,512]{4,3,2,1,0:T(8,128)(2,1)} %vel.2) | copy-start | bytes 2359300
  14.1 6.0 %copy-start.3 = (bf16[3,2,2,64,512]{4,3,2,1,0:T(8,128)(2,1)S(1)}, bf16[3,2,2,64,512]{4,3,2,1,0:T(8,128)(2,1)}, u32[]{:S(2)}) copy-start(bf16[3,2,2,64,512]{4,3,2,1,0:T(8,128)(2,1)} %pot) | copy-start | bytes 2359300
  14.1 6.0 %copy-start.39 = (s32[2]{0:T(128)S(1)}, s32[2]{0:T(128)}, u32[]{:S(2)}) copy-start(s32[2]{0:T(128)} %pad_add_fusion.place) | copy-start | bytes 28
  14.1 6.0 %copy-start.40 = (f32[2,2]{1,0:T(2,128)S(1)}, f32[2,2]{1,0:T(2,128)}, u32[]{:S(2)}) copy-start(f32[2,2]{1,0:T(2,128)} %angular.1) | copy-start | bytes 52
  14.1 51.2 %all-to-all-start = ((bf16[8,24,64,128]{3,2,1,0:T(8,128)(2,1)}), bf16[8,24,64,128]{3,2,1,0:T(8,128)(2,1)}, u32[]{:S(2)}, u32[]{:S(2)}) async-start(bf16[8,24,64,128]{3,2,1,0:T(8,128)(2,1)} %get-tuple-element.64), calls=%async_computation | async-start | bytes 6291456 | tf_op jit(solution)/shard_map/all_to_all | solution.py:515
  19.6 27.1 %copy-start.37 = (s32[512]{0:T(512)S(1)}, s32[512]{0:T(512)}, u32[]{:S(2)}) copy-start(s32[512]{0:T(512)} %orders.5) | copy-start | bytes 6148
  21.3 0.7 copy-start.5
  21.9 6.4 %collective-permute-start = (bf16[112,512]{1,0:T(8,128)(2,1)S(1)}, bf16[112,512]{1,0:T(8,128)(2,1)S(1)}, u32[]{:S(2)}, u32[]{:S(2)}) collective-permute-start(bf16[112,512]{1,0:T(8,128)(2,1)S(1)} %get-tuple-element.68), channel_id=1, source_target_pairs={{0,8},{1,33},{2,10},{3,35},{4,12},{5,37},{6,14},{7,39},{8,0},{9,41... | collective-permute-start | bytes 344072 | tf_op jit(solution)/shard_map/ppermute | solution.py:527
  23.4 10.6 %collective-permute-start.1 = (bf16[112,512]{1,0:T(8,128)(2,1)S(1)}, bf16[112,512]{1,0:T(8,128)(2,1)S(1)}, u32[]{:S(2)}, u32[]{:S(2)}) collective-permute-start(bf16[112,512]{1,0:T(8,128)(2,1)S(1)} %get-tuple-element.69), channel_id=1, source_target_pairs={{0,16},{1,65},{2,18},{3,67},{4,20},{5,69},{6,22},{7,71},{8,24},{9,... | collective-permute-start | bytes 344072 | tf_op jit(solution)/shard_map/ppermute | solution.py:527
  26.1 8.8 %collective-permute-start.2 = (bf16[112,512]{1,0:T(8,128)(2,1)S(1)}, bf16[112,512]{1,0:T(8,128)(2,1)S(1)}, u32[]{:S(2)}, u32[]{:S(2)}) collective-permute-start(bf16[112,512]{1,0:T(8,128)(2,1)S(1)} %get-tuple-element.70), channel_id=1, source_target_pairs={{0,24},{1,97},{2,26},{3,99},{4,28},{5,101},{6,30},{7,103},{8,16},{... | collective-permute-start | bytes 344072 | tf_op jit(solution)/shard_map/ppermute | solution.py:527
  26.6 12.2 %collective-permute-start.3 = (bf16[112,512]{1,0:T(8,128)(2,1)S(1)}, bf16[112,512]{1,0:T(8,128)(2,1)S(1)}, u32[]{:S(2)}, u32[]{:S(2)}) collective-permute-start(bf16[112,512]{1,0:T(8,128)(2,1)S(1)} %get-tuple-element.71), channel_id=1, source_target_pairs={{0,32},{1,9},{2,34},{3,11},{4,36},{5,13},{6,38},{7,15},{8,40},{9,1... | collective-permute-start | bytes 344072 | tf_op jit(solution)/shard_map/ppermute | solution.py:527
  28.2 11.3 %collective-permute-start.4 = (bf16[112,512]{1,0:T(8,128)(2,1)S(1)}, bf16[112,512]{1,0:T(8,128)(2,1)S(1)}, u32[]{:S(2)}, u32[]{:S(2)}) collective-permute-start(bf16[112,512]{1,0:T(8,128)(2,1)S(1)} %get-tuple-element.72), channel_id=1, source_target_pairs={{0,40},{1,41},{2,42},{3,43},{4,44},{5,45},{6,46},{7,47},{8,32},{9,... | collective-permute-start | bytes 344072 | tf_op jit(solution)/shard_map/ppermute | solution.py:527
  28.4 0.6 copy-start.7
  29.0 18.5 %collective-permute-start.5 = (bf16[112,512]{1,0:T(8,128)(2,1)S(1)}, bf16[112,512]{1,0:T(8,128)(2,1)S(1)}, u32[]{:S(2)}, u32[]{:S(2)}) collective-permute-start(bf16[112,512]{1,0:T(8,128)(2,1)S(1)} %get-tuple-element.73), channel_id=1, source_target_pairs={{0,48},{1,73},{2,50},{3,75},{4,52},{5,77},{6,54},{7,79},{8,56},{9,... | collective-permute-start | bytes 344072 | tf_op jit(solution)/shard_map/ppermute | solution.py:527
  34.0 0.6 copy-start.9
  34.6 13.2 %collective-permute-start.6 = (bf16[112,512]{1,0:T(8,128)(2,1)S(1)}, bf16[112,512]{1,0:T(8,128)(2,1)S(1)}, u32[]{:S(2)}, u32[]{:S(2)}) collective-permute-start(bf16[112,512]{1,0:T(8,128)(2,1)S(1)} %get-tuple-element.74), channel_id=1, source_target_pairs={{0,56},{1,105},{2,58},{3,107},{4,60},{5,109},{6,62},{7,111},{8,48}... | collective-permute-start | bytes 344072 | tf_op jit(solution)/shard_map/ppermute | solution.py:527
  35.0 0.6 copy-start.11
  35.6 15.2 %collective-permute-start.7 = (bf16[112,512]{1,0:T(8,128)(2,1)S(1)}, bf16[112,512]{1,0:T(8,128)(2,1)S(1)}, u32[]{:S(2)}, u32[]{:S(2)}) collective-permute-start(bf16[112,512]{1,0:T(8,128)(2,1)S(1)} %get-tuple-element.75), channel_id=1, source_target_pairs={{0,64},{1,17},{2,66},{3,19},{4,68},{5,21},{6,70},{7,23},{8,72},{9,... | collective-permute-start | bytes 344072 | tf_op jit(solution)/shard_map/ppermute | solution.py:527
  38.8 0.6 copy-start.13
  39.4 11.4 %collective-permute-start.8 = (bf16[112,512]{1,0:T(8,128)(2,1)S(1)}, bf16[112,512]{1,0:T(8,128)(2,1)S(1)}, u32[]{:S(2)}, u32[]{:S(2)}) collective-permute-start(bf16[112,512]{1,0:T(8,128)(2,1)S(1)} %get-tuple-element.76), channel_id=1, source_target_pairs={{0,72},{1,49},{2,74},{3,51},{4,76},{5,53},{6,78},{7,55},{8,64},{9,... | collective-permute-start | bytes 344072 | tf_op jit(solution)/shard_map/ppermute | solution.py:527
  39.5 0.6 copy-start.15
  40.1 17.1 %collective-permute-start.9 = (bf16[112,512]{1,0:T(8,128)(2,1)S(1)}, bf16[112,512]{1,0:T(8,128)(2,1)S(1)}, u32[]{:S(2)}, u32[]{:S(2)}) collective-permute-start(bf16[112,512]{1,0:T(8,128)(2,1)S(1)} %get-tuple-element.77), channel_id=1, source_target_pairs={{0,80},{1,81},{2,82},{3,83},{4,84},{5,85},{6,86},{7,87},{8,88},{9,... | collective-permute-start | bytes 344072 | tf_op jit(solution)/shard_map/ppermute | solution.py:527
  47.5 13.8 %copy-start.17 = (bf16[112,512]{1,0:T(8,128)(2,1)}, bf16[112,512]{1,0:T(8,128)(2,1)S(1)}, u32[]{:S(2)}) copy-start(bf16[112,512]{1,0:T(8,128)(2,1)S(1)} %collective-permute-done.5.refs_6_) | copy-start | bytes 344068
  47.5 14.4 %collective-permute-start.10 = (bf16[112,512]{1,0:T(8,128)(2,1)S(1)}, bf16[112,512]{1,0:T(8,128)(2,1)S(1)}, u32[]{:S(2)}, u32[]{:S(2)}) collective-permute-start(bf16[112,512]{1,0:T(8,128)(2,1)S(1)} %get-tuple-element.78), channel_id=1, source_target_pairs={{0,88},{1,113},{2,90},{3,115},{4,92},{5,117},{6,94},{7,119},{8,80}... | collective-permute-start | bytes 344072 | tf_op jit(solution)/shard_map/ppermute | solution.py:527
  47.8 13.5 %copy-start.19 = (bf16[112,512]{1,0:T(8,128)(2,1)}, bf16[112,512]{1,0:T(8,128)(2,1)S(1)}, u32[]{:S(2)}) copy-start(bf16[112,512]{1,0:T(8,128)(2,1)S(1)} %collective-permute-done.6.refs_7_) | copy-start | bytes 344068
  47.8 14.1 %collective-permute-start.11 = (bf16[112,512]{1,0:T(8,128)(2,1)S(1)}, bf16[112,512]{1,0:T(8,128)(2,1)S(1)}, u32[]{:S(2)}, u32[]{:S(2)}) collective-permute-start(bf16[112,512]{1,0:T(8,128)(2,1)S(1)} %get-tuple-element.79), channel_id=1, source_target_pairs={{0,96},{1,25},{2,98},{3,27},{4,100},{5,29},{6,102},{7,31},{8,104},... | collective-permute-start | bytes 344072 | tf_op jit(solution)/shard_map/ppermute | solution.py:527
  50.8 10.5 %copy-start.21 = (bf16[112,512]{1,0:T(8,128)(2,1)}, bf16[112,512]{1,0:T(8,128)(2,1)S(1)}, u32[]{:S(2)}) copy-start(bf16[112,512]{1,0:T(8,128)(2,1)S(1)} %collective-permute-done.7.refs_8_) | copy-start | bytes 344068
  50.8 11.1 %collective-permute-start.12 = (bf16[112,512]{1,0:T(8,128)(2,1)S(1)}, bf16[112,512]{1,0:T(8,128)(2,1)S(1)}, u32[]{:S(2)}, u32[]{:S(2)}) collective-permute-start(bf16[112,512]{1,0:T(8,128)(2,1)S(1)} %get-tuple-element.80), channel_id=1, source_target_pairs={{0,104},{1,57},{2,106},{3,59},{4,108},{5,61},{6,110},{7,63},{8,96}... | collective-permute-start | bytes 344072 | tf_op jit(solution)/shard_map/ppermute | solution.py:527
  50.8 10.5 %copy-start.23 = (bf16[112,512]{1,0:T(8,128)(2,1)}, bf16[112,512]{1,0:T(8,128)(2,1)S(1)}, u32[]{:S(2)}) copy-start(bf16[112,512]{1,0:T(8,128)(2,1)S(1)} %collective-permute-done.8.refs_9_) | copy-start | bytes 344068
  50.8 11.1 %collective-permute-start.13 = (bf16[112,512]{1,0:T(8,128)(2,1)S(1)}, bf16[112,512]{1,0:T(8,128)(2,1)S(1)}, u32[]{:S(2)}, u32[]{:S(2)}) collective-permute-start(bf16[112,512]{1,0:T(8,128)(2,1)S(1)} %get-tuple-element.81), channel_id=1, source_target_pairs={{0,112},{1,89},{2,114},{3,91},{4,116},{5,93},{6,118},{7,95},{8,120... | collective-permute-start | bytes 344072 | tf_op jit(solution)/shard_map/ppermute | solution.py:527
  57.2 4.2 %copy-start.25 = (bf16[112,512]{1,0:T(8,128)(2,1)}, bf16[112,512]{1,0:T(8,128)(2,1)S(1)}, u32[]{:S(2)}) copy-start(bf16[112,512]{1,0:T(8,128)(2,1)S(1)} %collective-permute-done.9.refs_10_) | copy-start | bytes 344068
  57.2 8.1 %collective-permute-start.14 = (bf16[112,512]{1,0:T(8,128)(2,1)S(1)}, bf16[112,512]{1,0:T(8,128)(2,1)S(1)}, u32[]{:S(2)}, u32[]{:S(2)}) collective-permute-start(bf16[112,512]{1,0:T(8,128)(2,1)S(1)} %get-tuple-element.82), channel_id=1, source_target_pairs={{0,120},{1,121},{2,122},{3,123},{4,124},{5,125},{6,126},{7,127},{8... | collective-permute-start | bytes 344072 | tf_op jit(solution)/shard_map/ppermute | solution.py:527
  61.9 11.3 %copy-start.27 = (bf16[112,512]{1,0:T(8,128)(2,1)}, bf16[112,512]{1,0:T(8,128)(2,1)S(1)}, u32[]{:S(2)}) copy-start(bf16[112,512]{1,0:T(8,128)(2,1)S(1)} %collective-permute-done.10.refs_11_) | copy-start | bytes 344068
  61.9 11.3 %copy-start.29 = (bf16[112,512]{1,0:T(8,128)(2,1)}, bf16[112,512]{1,0:T(8,128)(2,1)S(1)}, u32[]{:S(2)}) copy-start(bf16[112,512]{1,0:T(8,128)(2,1)S(1)} %collective-permute-done.11.refs_12_) | copy-start | bytes 344068
  61.9 11.3 %copy-start.31 = (bf16[112,512]{1,0:T(8,128)(2,1)}, bf16[112,512]{1,0:T(8,128)(2,1)S(1)}, u32[]{:S(2)}) copy-start(bf16[112,512]{1,0:T(8,128)(2,1)S(1)} %collective-permute-done.12.refs_13_) | copy-start | bytes 344068
  62.0 11.3 %copy-start.33 = (bf16[112,512]{1,0:T(8,128)(2,1)}, bf16[112,512]{1,0:T(8,128)(2,1)S(1)}, u32[]{:S(2)}) copy-start(bf16[112,512]{1,0:T(8,128)(2,1)S(1)} %collective-permute-done.13.refs_14_) | copy-start | bytes 344068
  65.3 8.0 %copy-start.35 = (bf16[112,512]{1,0:T(8,128)(2,1)}, bf16[112,512]{1,0:T(8,128)(2,1)S(1)}, u32[]{:S(2)}) copy-start(bf16[112,512]{1,0:T(8,128)(2,1)S(1)} %collective-permute-done.14.refs_15_) | copy-start | bytes 344068
  73.3 6.9 %copy-start.38 = (s32[512]{0:T(512)S(1)}, s32[512]{0:T(512)}, u32[]{:S(2)}) copy-start(s32[512]{0:T(512)} %orders.5) | copy-start | bytes 6148
  73.3 31.7 %all-to-all-start.1 = ((bf16[128,8,768]{2,1,0:T(8,128)(2,1)}), bf16[128,8,768]{2,1,0:T(8,128)(2,1)S(1)}, u32[]{:S(2)}, u32[]{:S(2)}) async-start(bf16[128,8,768]{2,1,0:T(8,128)(2,1)} %bitcast.13), calls=%async_computation.1 | async-start | bytes 3145728 | tf_op jit(solution)/shard_map/all_to_all | solution.py:534
  80.2 1.1 copy-start.4
  81.2 0.9 copy-start.6
  82.1 0.9 copy-start.8
  83.0 0.9 copy-start.10
  83.9 0.9 copy-start.12
  84.8 0.9 copy-start.14
  85.7 0.9 copy-start.16
  86.6 0.9 copy-start.18
  87.5 0.9 copy-start.20
  88.4 0.9 copy-start.22
  89.3 0.9 copy-start.24
  90.2 0.9 copy-start.26
  91.1 0.9 copy-start.28
  92.0 0.9 copy-start.30
  92.9 0.9 copy-start.32
  93.8 0.9 copy-start.34
  94.7 0.9 copy-start.36
  97.3 1.0 copy-start.1
  105.1 1.2 copy-start.2

commit v8 on v7

--- a/solution.py
+++ b/solution.py
@@ -53,25 +53,35 @@
 CHUNK = 171
 
 
-def synthesis_kernel(place, orders, vel, vor, mag, cur, table, out, pairs, xs, ys, ts):
+def synthesis_kernel(place, orders, vel, vor, mag, cur, table, out, pairs, xs, ys, ts, packed, sems):
     step = pl.program_id(0)
-    chunk = pl.program_id(1)
-
-    @pl.when(chunk == 0)
+
+    def arrival(g, q):
+        source = table.at[pl.ds(q * CHUNK, CHUNK), pl.ds(g * 16, 16)]
+        return pltpu.make_async_copy(source, packed.at[g, q], sems.at[g, q])
+
+    @pl.when(step == 0)
     def _():
-        for a, ref in enumerate((vel, vor, mag, cur)):
-            for c in range(3):
-                for s in range(2):
-                    for p in range(2):
-                        row = (s * 24 + (a * 3 + c) * 2 + p) * PITCH
-                        store(xs, pl.ds(row, 32), ref[c, s, p].astype(f32))
-
-    for q in range(3):
-
-        @pl.when(chunk == q)
+        for g in range(2):
+            for q in range(3):
+                arrival(g, q).start()
+
+    for a, ref in enumerate((vel, vor, mag, cur)):
+        for c in range(3):
+            for s in range(2):
+                for p in range(2):
+                    row = (s * 24 + (a * 3 + c) * 2 + p) * PITCH
+                    store(xs, pl.ds(row, 32), ref[c, s, p].astype(f32))
+
+    for g in range(2):
+
+        @pl.when(step == g)
         def _():
-            for d in range(CHUNK):
-                store(ts, pl.ds((q * CHUNK + d) * TABLE_PITCH, 16), table[d].astype(f32))
+            for q in range(3):
+                arrival(g, q).wait()
+                for d in range(CHUNK):
+                    at = pl.ds((q * CHUNK + d) * TABLE_PITCH, 16)
+                    store(ts, at, packed[g, q, d].astype(f32))
 
     r = lax.broadcasted_iota(jnp.int32, (1, L), 1)
     sign_a = (1 - 2 * (r & 1)).astype(f32)
@@ -101,16 +111,14 @@
                     store(ys, at, parts[h][s * 24 : s * 24 + 24])
         return 0
 
-    @pl.when(chunk == 2)
-    def _():
-        lax.fori_loop(0, 16, one_pair, 0, unroll=8)
-        for sh in range(4):
-            for jh in range(2):
-                for cp in range(24):
-                    row = (sh * 24 + cp) * PITCH
-                    out[sh * 2 + jh, cp] = ys[jh, row : row + 32, :].astype(bf16)
-
-    @pl.when((chunk == 2) & (step == place[0] // 8))
+    lax.fori_loop(0, 16, one_pair, 0, unroll=16)
+    for sh in range(4):
+        for jh in range(2):
+            for cp in range(24):
+                row = (sh * 24 + cp) * PITCH
+                out[sh * 2 + jh, cp] = ys[jh, row : row + 32, :].astype(bf16)
+
+    @pl.when(step == place[0] // 8)
     def _():
         for i in range(2):
             at = (place[0] & 7) * 2 + i
@@ -120,22 +128,23 @@
 
 
 def legendre_synthesis(place, orders, velocity, vorticity, magnetic, current, table):
-    field = pl.BlockSpec((3, 2, 2, 32, L), lambda g, q, place, low: (0, 0, 0, g, 0))
+    field = pl.BlockSpec((3, 2, 2, 32, L), lambda g, place, low: (0, 0, 0, g, 0))
     return pl.pallas_call(
         synthesis_kernel,
         grid_spec=pltpu.PrefetchScalarGridSpec(
             num_scalar_prefetch=2,
-            grid=(2, 3),
-            in_specs=[field] * 4
-            + [pl.BlockSpec((CHUNK, 16, NH), lambda g, q, place, low: (q, g, 0))],
+            grid=(2,),
+            in_specs=[field] * 4 + [pl.BlockSpec(memory_space=pl.ANY)],
             out_specs=[
-                pl.BlockSpec((8, 24, 32, 128), lambda g, q, place, low: (0, 0, g, 0)),
-                pl.BlockSpec((2, L + 16, NH), lambda g, q, place, low: (0, 0, 0)),
+                pl.BlockSpec((8, 24, 32, 128), lambda g, place, low: (0, 0, g, 0)),
+                pl.BlockSpec((2, L + 16, NH), lambda g, place, low: (0, 0, 0)),
             ],
             scratch_shapes=[
                 pltpu.VMEM((4, 48 * PITCH, 128), f32),
                 pltpu.VMEM((2, 96 * PITCH, 128), f32),
                 pltpu.VMEM((2, (L + 1) * TABLE_PITCH + 7, 128), f32),
+                pltpu.VMEM((2, 3, CHUNK, 16, NH), bf16),
+                pltpu.SemaphoreType.DMA((2, 3)),
             ],
         ),
         out_shape=[
@@ -185,7 +194,7 @@
         out_specs=[pl.BlockSpec((112, L), lambda g: (0, 0))] * 16,
         out_shape=[jax.ShapeDtypeStruct((112, L), bf16)] * 16,
         scratch_shapes=[pltpu.VMEM((16, 96, L), f32)],
-        compiler_params=pltpu.CompilerParams(vmem_limit_bytes=32 * MIB),
+        compiler_params=pltpu.CompilerParams(vmem_limit_bytes=60 * MIB),
         cost_estimate=pl.CostEstimate(flops=10**6, bytes_accessed=4 * MIB, transcendentals=0),
         name="state_to_send",
     )(place, kappa, angular, velocity, potential)

time: 138 us -> 136 us (0.986)
    pallas_call x1, Pallas kernels: 12.8 us -> 10 us  [legendre_synthesis(): pl.pallas_call(synthesis_kernel, grid_spec=pltpu.PrefetchScalarGridSpec(n...]
    pallas_call x1, Pallas kernels: 1.15 us -> 3.02 us  [state_to_send(): pl.pallas_call(state_kernel, grid=(1,), in_specs=[small, small, small, fi...]
    unnamed x86 -> x78, local copies, waits for them, and re-layouts: 21.5 us -> 20.9 us
  transfers between devices with their start and end apart: 17 -> 17, of which waited for: 2 -> 2; matrix products, arithmetic and copies ran while one was open for 1% -> 2% of each run, Pallas kernels for 5% -> 6%
where the time goes in v8:
time: 136 us
  starting transfers between devices  43.4 us (32%)
  Pallas kernels  31.6 us (23%)
  blocking collectives  25.4 us (19%)
  local copies, waits for them, and re-layouts  21.7 us (16%)
  waiting for transfers between devices  10.3 us (8%)
  other arithmetic  2.2 us (2%)
    ppermute x15, starting transfers between devices, body(): received.append(lax.ppermute(parts[r], ('shell', 'order'), pairs_r))  31.3 us
    all_to_all x1, blocking collectives, body(): solved = lax.all_to_all(solved, 'shell', 0, 0, tiled=True)  25.4 us
    unnamed x78, local copies, waits for them, and re-layouts  20.9 us
    pallas_call x1, Pallas kernels, legendre_synthesis(): pl.pallas_call(synthesis_kernel, grid_spec=pltpu.PrefetchScalarGridSpec(n...  10 us
    pallas_call x1, Pallas kernels, grid_stage(): pl.pallas_call(grid_kernel, grid=(3,), in_specs=[pl.BlockSpec((8, 24, 64,...  7.97 us
    all_to_all x1, waiting for transfers between devices, body(): lax.all_to_all(coefs.reshape(128, 8, 768), ('shell', 'order'), 0, 0, tile...  6.81 us
    all_to_all x1, starting transfers between devices, body(): lax.all_to_all(coefs.reshape(128, 8, 768), ('shell', 'order'), 0, 0, tile...  6.68 us
    all_to_all x1, starting transfers between devices, body(): incoming = lax.all_to_all(latitude, 'order', 0, 0, tiled=True)  5.41 us
  transfers between devices with their start and end apart: 17, of which 2 were waited for; matrix products, arithmetic and copies ran while one was open for 2% of the time, Pallas kernels for 6%

profile of v8, /device:TPU:0, one launch (start us, length us, event | category | flops | bytes accessed | tf_op | source)
XLA Modules:
  0.0 135.6 jit_solution(15534689295207226918)
XLA Ops:
  0.6 0.7 pad_add_fusion.place
  1.3 10.0 %legendre_synthesis.1 = (bf16[8,24,64,128]{3,2,1,0:T(8,128)(2,1)}, bf16[2,528,256]{2,1,0:T(8,128)(2,1)}) custom-call(s32[2]{0:T(128)} %pad_add_fusion.place, s32[512]{0:T(512)} %orders.5, bf16[3,2,2,64,512]{4,3,2,1,0:T(8,128)(2,1)} %vel.2, bf16[3,2,2,64,512]{4,3,2,1,0:T(8,128)(2,1)} %vor.1, bf16[3,2,2,64,512]{4,3,2,1,0:T(8,128)(2,1)} %mag.1, ...), custom_call_target="tpu_custom_call" | custom-call | flops 1600000000 | bytes 15728640 | tf_op jit(solution)/shard_map/legendre_synthesis/pallas_call | solution.py:132
  11.3 0.0 copy-start.38
  11.3 0.0 copy-start.37
  11.3 5.4 %all-to-all-start = ((bf16[8,24,64,128]{3,2,1,0:T(8,128)(2,1)}), bf16[8,24,64,128]{3,2,1,0:T(8,128)(2,1)}, u32[]{:S(2)}, u32[]{:S(2)}) async-start(bf16[8,24,64,128]{3,2,1,0:T(8,128)(2,1)} %get-tuple-element.64), calls=%async_computation | async-start | bytes 6291456 | tf_op jit(solution)/shard_map/all_to_all | solution.py:524
  16.8 0.2 reduce-window.9
  16.9 0.2 compare_reduce_fusion
  17.1 0.6 broadcast_select_fusion.kappa
  17.7 3.0 %state_to_send.1 = (bf16[112,512]{1,0:T(8,128)(2,1)}, bf16[112,512]{1,0:T(8,128)(2,1)}, bf16[112,512]{1,0:T(8,128)(2,1)}, bf16[112,512]{1,0:T(8,128)(2,1)}, bf16...) custom-call(s32[2]{0:T(128)} %pad_add_fusion.place, ...), custom_call_target="tpu_custom_call" | custom-call | flops 1000000 | bytes 4194304 | tf_op jit(solution)/shard_map/state_to_send/pallas_call | solution.py:190
  20.7 1.5 %collective-permute-start = (bf16[112,512]{1,0:T(8,128)(2,1)}, bf16[112,512]{1,0:T(8,128)(2,1)S(1)}, u32[]{:S(2)}, u32[]{:S(2)}) collective-permute-start(bf16[112,512]{1,0:T(8,128)(2,1)} %get-tuple-element.68), channel_id=1, source_target_pairs={{0,8},{1,33},{2,10},{3,35},{4,12},{5,37},{6,14},{7,39},{8,0},{9,41... | collective-permute-start | bytes 344072 | tf_op jit(solution)/shard_map/ppermute | solution.py:536
  22.3 2.7 %collective-permute-start.1 = (bf16[112,512]{1,0:T(8,128)(2,1)}, bf16[112,512]{1,0:T(8,128)(2,1)S(1)}, u32[]{:S(2)}, u32[]{:S(2)}) collective-permute-start(bf16[112,512]{1,0:T(8,128)(2,1)} %get-tuple-element.69), channel_id=1, source_target_pairs={{0,16},{1,65},{2,18},{3,67},{4,20},{5,69},{6,22},{7,71},{8,24},{9,... | collective-permute-start | bytes 344072 | tf_op jit(solution)/shard_map/ppermute | solution.py:536
  25.0 0.5 collective-permute-start.2
  25.5 1.6 %collective-permute-start.3 = (bf16[112,512]{1,0:T(8,128)(2,1)}, bf16[112,512]{1,0:T(8,128)(2,1)S(1)}, u32[]{:S(2)}, u32[]{:S(2)}) collective-permute-start(bf16[112,512]{1,0:T(8,128)(2,1)} %get-tuple-element.71), channel_id=1, source_target_pairs={{0,32},{1,9},{2,34},{3,11},{4,36},{5,13},{6,38},{7,15},{8,40},{9,1... | collective-permute-start | bytes 344072 | tf_op jit(solution)/shard_map/ppermute | solution.py:536
  27.0 0.2 collective-permute-start.4
  27.2 0.6 copy-done.4
  27.8 5.0 %collective-permute-start.5 = (bf16[112,512]{1,0:T(8,128)(2,1)}, bf16[112,512]{1,0:T(8,128)(2,1)S(1)}, u32[]{:S(2)}, u32[]{:S(2)}) collective-permute-start(bf16[112,512]{1,0:T(8,128)(2,1)} %get-tuple-element.73), channel_id=1, source_target_pairs={{0,48},{1,73},{2,50},{3,75},{4,52},{5,77},{6,54},{7,79},{8,56},{9,... | collective-permute-start | bytes 344072 | tf_op jit(solution)/shard_map/ppermute | solution.py:536
  32.8 0.7 copy-done.6
  33.5 0.4 collective-permute-start.6
  33.8 0.0 collective-permute-done.2.refs_3_
  33.8 0.6 copy-done.8
  34.5 3.2 %collective-permute-start.7 = (bf16[112,512]{1,0:T(8,128)(2,1)}, bf16[112,512]{1,0:T(8,128)(2,1)S(1)}, u32[]{:S(2)}, u32[]{:S(2)}) collective-permute-start(bf16[112,512]{1,0:T(8,128)(2,1)} %get-tuple-element.75), channel_id=1, source_target_pairs={{0,64},{1,17},{2,66},{3,19},{4,68},{5,21},{6,70},{7,23},{8,72},{9,... | collective-permute-start | bytes 344072 | tf_op jit(solution)/shard_map/ppermute | solution.py:536
  37.7 0.6 copy-done.10
  38.3 0.2 collective-permute-start.8
  38.5 0.0 collective-permute-done.4.refs_5_
  38.5 0.7 copy-done.12
  39.2 6.4 %collective-permute-start.9 = (bf16[112,512]{1,0:T(8,128)(2,1)}, bf16[112,512]{1,0:T(8,128)(2,1)S(1)}, u32[]{:S(2)}, u32[]{:S(2)}) collective-permute-start(bf16[112,512]{1,0:T(8,128)(2,1)} %get-tuple-element.77), channel_id=1, source_target_pairs={{0,80},{1,81},{2,82},{3,83},{4,84},{5,85},{6,86},{7,87},{8,88},{9,... | collective-permute-start | bytes 344072 | tf_op jit(solution)/shard_map/ppermute | solution.py:536
  45.6 0.1 reshape.76
  45.7 0.7 reshape.77.targets
  46.4 0.3 collective-permute-start.10
  46.7 3.0 %collective-permute-start.11 = (bf16[112,512]{1,0:T(8,128)(2,1)}, bf16[112,512]{1,0:T(8,128)(2,1)S(1)}, u32[]{:S(2)}, u32[]{:S(2)}) collective-permute-start(bf16[112,512]{1,0:T(8,128)(2,1)} %get-tuple-element.79), channel_id=1, source_target_pairs={{0,96},{1,25},{2,98},{3,27},{4,100},{5,29},{6,102},{7,31},{8,104},... | collective-permute-start | bytes 344072 | tf_op jit(solution)/shard_map/ppermute | solution.py:536
  49.7 6.3 %collective-permute-start.13 = (bf16[112,512]{1,0:T(8,128)(2,1)}, bf16[112,512]{1,0:T(8,128)(2,1)S(1)}, u32[]{:S(2)}, u32[]{:S(2)}) collective-permute-start(bf16[112,512]{1,0:T(8,128)(2,1)} %get-tuple-element.81), channel_id=1, source_target_pairs={{0,112},{1,89},{2,114},{3,91},{4,116},{5,93},{6,118},{7,95},{8,120... | collective-permute-start | bytes 344072 | tf_op jit(solution)/shard_map/ppermute | solution.py:536
  56.0 0.1 collective-permute-start.14
  56.2 4.0 %make_tables.1 = (bf16[528,512]{1,0:T(8,128)(2,1)}, bf16[512,512]{1,0:T(8,128)(2,1)}, bf16[512,512]{1,0:T(8,128)(2,1)}, bf16[512,512]{1,0:T(8,128)(2,1)}, f32[512,128]{1,0:T(8,128)}) custom-call(s32[1,512]{1,0:T(1,128)} %bitcast.11, s32[1,512]{1,0:T(1,128)} %reshape.77.targets, bf16[528,512]{1,0:T(8,128)(2,1)} %constant.42.clone.refs_0_, ...), custom_call_target="tpu_custom_call" | custom-call | flops 1000000000 | bytes 5242880 | tf_op jit(solution)/shard_map/make_tables/pallas_call | solution.py:302
  60.2 0.6 sine_multiply_fusion.weight
  60.9 3.5 %collective-permute-done.14.refs_15_ = bf16[112,512]{1,0:T(8,128)(2,1)S(1)} collective-permute-done((bf16[112,512]{1,0:T(8,128)(2,1)}, bf16[112,512]{1,0:T(8,128)(2,1)S(1)}, u32[]{:S(2)}, u32[]{:S(2)}) %collective-permute-start.14) | collective-permute-done | bytes 114720 | tf_op jit(solution)/shard_map/ppermute | solution.py:536
  64.4 8.0 %grid_stage.1 = bf16[1024,768]{1,0:T(8,128)(2,1)} custom-call(bf16[8,24,64,128]{3,2,1,0:T(8,128)(2,1)} %all-to-all-done.lat, bf16[528,512]{1,0:T(8,128)(2,1)} %get-tuple-element.85.syn_cos, bf16[512,512]{1,0:T(8,128)(2,1)} %get-tuple-element.86.syn_sin, bf16[512,512]{1,0:T(8,128)(2,1)} %get-tuple-element.87.ana_cos, ...), custom_call_target="tpu_custom_call" | custom-call | flops 2400000000 | bytes 7340032 | tf_op jit(solution)/shard_map/grid_stage/pallas_call | solution.py:257
  72.4 0.0 copy-start.35
  72.4 6.7 %all-to-all-start.1 = ((bf16[128,8,768]{2,1,0:T(8,128)(2,1)}), bf16[128,8,768]{2,1,0:T(8,128)(2,1)S(1)}, u32[]{:S(2)}, u32[]{:S(2)}) async-start(bf16[128,8,768]{2,1,0:T(8,128)(2,1)} %bitcast.13), calls=%async_computation.1 | async-start | bytes 3145728 | tf_op jit(solution)/shard_map/all_to_all | solution.py:543
  79.1 0.0 copy-start.2
  79.1 1.0 copy-done.2
  80.2 0.9 copy-done.3
  81.1 0.9 copy-done.5
  82.0 0.9 copy-done.7
  82.9 0.9 copy-done.9
  83.8 0.9 copy-done.11
  84.7 0.9 copy-done.13
  85.6 0.9 copy-done.15
  86.5 0.9 copy-done.17
  87.4 0.9 copy-done.19
  88.3 0.9 copy-done.21
  89.2 0.9 copy-done.23
  90.1 0.9 copy-done.25
  91.0 0.9 copy-done.27
  91.9 0.9 copy-done.29
  92.8 0.9 copy-done.31
  93.7 0.9 copy-done.33
  94.5 1.6 %solve_factors.1 = (bf16[16,96,512]{2,1,0:T(8,128)(2,1)S(1)}, f32[3,64,512]{2,1,0:T(8,128)S(1)}, bf16[4,256,512]{2,1,0:T(8,128)(2,1)S(1)}) custom-call(s32[2]{0:T(128)S(1)} %copy-done.36, s32[512]{0:T(512)S(1)} %copy-done.35, bf16[2,528,256]{2,1,0:T(8,128)(2,1)S(1)} %copy-done.2, bf16[112,512]{1,0:T(8,128)(2,1)S(1)} %copy-done.3, ...), custom_call_target="tpu_custom_call" | custom-call | flops 1000000 | bytes 1048576 | tf_op jit(solution)/shard_map/solve_factors/pallas_call | solution.py:354
  96.2 0.0 copy-start
  96.2 1.0 copy-done
  97.2 6.8 %all-to-all-done.1 = bf16[128,8,768]{2,1,0:T(8,128)(2,1)S(1)} async-done(((bf16[128,8,768]{2,1,0:T(8,128)(2,1)}), bf16[128,8,768]{2,1,0:T(8,128)(2,1)S(1)}, u32[]{:S(2)}, u32[]{:S(2)}) %all-to-all-start.1) | async-done | bytes 1572896 | tf_op jit(solution)/shard_map/all_to_all | solution.py:543
  104.0 1.2 copy-done.1
  105.2 3.0 %analysis_and_solve.1 = bf16[16,96,512]{2,1,0:T(8,128)(2,1)S(1)} custom-call(s32[2]{0:T(128)S(1)} %copy-done.36, s32[512]{0:T(512)S(1)} %copy-done.35, bf16[1024,768]{1,0:T(8,128)(2,1)S(1)} %bitcast.10, bf16[4,256,512]{2,1,0:T(8,128)(2,1)S(1)} %copy-done.1, f32[3,64,512]{2,1,0:T(8,128)S(1)} %get-tuple-element.124.factors, ...), custom_call_target="tpu_custom_call" | custom-call | flops 900000000 | bytes 6291456 | tf_op jit(solution)/shard_map/analysis_and_solve/pallas_call | solution.py:440
  108.2 25.4 %all_to_all.15.got = bf16[16,96,512]{2,1,0:T(8,128)(2,1)S(1)} all-to-all(bf16[16,96,512]{2,1,0:T(8,128)(2,1)S(1)} %analysis_and_solve.1), channel_id=1, replica_groups=mesh['shell'=16,'order'=8] {'shell'}, dimensions={0} | all-to-all | bytes 3145728 | tf_op jit(solution)/shard_map/all_to_all | solution.py:547
  133.6 2.0 %unpack_solution.1 = (f32[3,2,2,64,512]{4,3,2,1,0:T(8,128)}, f32[3,2,2,64,512]{4,3,2,1,0:T(8,128)}) custom-call(bf16[16,96,512]{2,1,0:T(8,128)(2,1)S(1)} %all_to_all.15.got), custom_call_target="tpu_custom_call" | custom-call | flops 1000000 | bytes 5242880 | tf_op jit(solution)/shard_map/unpack_solution/pallas_call | solution.py:480
  (66 shorter events, 0.2 us)
Async XLA Ops:
  11.3 5.4 %copy-start.38 = (s32[4]{0:T(128)S(1)}, s32[4]{0:T(128)}, u32[]{:S(2)}) copy-start(s32[4]{0:T(128)} %param.22) | copy-start | bytes 52
  11.3 5.8 %copy-start.37 = (f32[2,2]{1,0:T(2,128)S(1)}, f32[2,2]{1,0:T(2,128)}, u32[]{:S(2)}) copy-start(f32[2,2]{1,0:T(2,128)} %param.23) | copy-start | bytes 52
  11.3 53.1 %all-to-all-start = ((bf16[8,24,64,128]{3,2,1,0:T(8,128)(2,1)}), bf16[8,24,64,128]{3,2,1,0:T(8,128)(2,1)}, u32[]{:S(2)}, u32[]{:S(2)}) async-start(bf16[8,24,64,128]{3,2,1,0:T(8,128)(2,1)} %get-tuple-element.64), calls=%async_computation | async-start | bytes 6291456 | tf_op jit(solution)/shard_map/all_to_all | solution.py:524
  16.7 28.9 %copy-start.34 = (s32[512]{0:T(512)S(1)}, s32[512]{0:T(512)}, u32[]{:S(2)}) copy-start(s32[512]{0:T(512)} %orders.5) | copy-start | bytes 6148
  20.7 6.5 %collective-permute-start = (bf16[112,512]{1,0:T(8,128)(2,1)}, bf16[112,512]{1,0:T(8,128)(2,1)S(1)}, u32[]{:S(2)}, u32[]{:S(2)}) collective-permute-start(bf16[112,512]{1,0:T(8,128)(2,1)} %get-tuple-element.68), channel_id=1, source_target_pairs={{0,8},{1,33},{2,10},{3,35},{4,12},{5,37},{6,14},{7,39},{8,0},{9,41... | collective-permute-start | bytes 344072 | tf_op jit(solution)/shard_map/ppermute | solution.py:536
  22.3 10.5 %collective-permute-start.1 = (bf16[112,512]{1,0:T(8,128)(2,1)}, bf16[112,512]{1,0:T(8,128)(2,1)S(1)}, u32[]{:S(2)}, u32[]{:S(2)}) collective-permute-start(bf16[112,512]{1,0:T(8,128)(2,1)} %get-tuple-element.69), channel_id=1, source_target_pairs={{0,16},{1,65},{2,18},{3,67},{4,20},{5,69},{6,22},{7,71},{8,24},{9,... | collective-permute-start | bytes 344072 | tf_op jit(solution)/shard_map/ppermute | solution.py:536
  25.0 8.8 %collective-permute-start.2 = (bf16[112,512]{1,0:T(8,128)(2,1)}, bf16[112,512]{1,0:T(8,128)(2,1)S(1)}, u32[]{:S(2)}, u32[]{:S(2)}) collective-permute-start(bf16[112,512]{1,0:T(8,128)(2,1)} %get-tuple-element.70), channel_id=1, source_target_pairs={{0,24},{1,97},{2,26},{3,99},{4,28},{5,101},{6,30},{7,103},{8,16},{... | collective-permute-start | bytes 344072 | tf_op jit(solution)/shard_map/ppermute | solution.py:536
  25.5 12.2 %collective-permute-start.3 = (bf16[112,512]{1,0:T(8,128)(2,1)}, bf16[112,512]{1,0:T(8,128)(2,1)S(1)}, u32[]{:S(2)}, u32[]{:S(2)}) collective-permute-start(bf16[112,512]{1,0:T(8,128)(2,1)} %get-tuple-element.71), channel_id=1, source_target_pairs={{0,32},{1,9},{2,34},{3,11},{4,36},{5,13},{6,38},{7,15},{8,40},{9,1... | collective-permute-start | bytes 344072 | tf_op jit(solution)/shard_map/ppermute | solution.py:536
  27.0 11.5 %collective-permute-start.4 = (bf16[112,512]{1,0:T(8,128)(2,1)}, bf16[112,512]{1,0:T(8,128)(2,1)S(1)}, u32[]{:S(2)}, u32[]{:S(2)}) collective-permute-start(bf16[112,512]{1,0:T(8,128)(2,1)} %get-tuple-element.72), channel_id=1, source_target_pairs={{0,40},{1,41},{2,42},{3,43},{4,44},{5,45},{6,46},{7,47},{8,32},{9,... | collective-permute-start | bytes 344072 | tf_op jit(solution)/shard_map/ppermute | solution.py:536
  27.2 0.6 copy-start.4
  27.8 18.6 %collective-permute-start.5 = (bf16[112,512]{1,0:T(8,128)(2,1)}, bf16[112,512]{1,0:T(8,128)(2,1)S(1)}, u32[]{:S(2)}, u32[]{:S(2)}) collective-permute-start(bf16[112,512]{1,0:T(8,128)(2,1)} %get-tuple-element.73), channel_id=1, source_target_pairs={{0,48},{1,73},{2,50},{3,75},{4,52},{5,77},{6,54},{7,79},{8,56},{9,... | collective-permute-start | bytes 344072 | tf_op jit(solution)/shard_map/ppermute | solution.py:536
  32.8 0.7 copy-start.6
  33.5 13.2 %collective-permute-start.6 = (bf16[112,512]{1,0:T(8,128)(2,1)}, bf16[112,512]{1,0:T(8,128)(2,1)S(1)}, u32[]{:S(2)}, u32[]{:S(2)}) collective-permute-start(bf16[112,512]{1,0:T(8,128)(2,1)} %get-tuple-element.74), channel_id=1, source_target_pairs={{0,56},{1,105},{2,58},{3,107},{4,60},{5,109},{6,62},{7,111},{8,48}... | collective-permute-start | bytes 344072 | tf_op jit(solution)/shard_map/ppermute | solution.py:536
  33.8 0.6 copy-start.8
  34.5 15.2 %collective-permute-start.7 = (bf16[112,512]{1,0:T(8,128)(2,1)}, bf16[112,512]{1,0:T(8,128)(2,1)S(1)}, u32[]{:S(2)}, u32[]{:S(2)}) collective-permute-start(bf16[112,512]{1,0:T(8,128)(2,1)} %get-tuple-element.75), channel_id=1, source_target_pairs={{0,64},{1,17},{2,66},{3,19},{4,68},{5,21},{6,70},{7,23},{8,72},{9,... | collective-permute-start | bytes 344072 | tf_op jit(solution)/shard_map/ppermute | solution.py:536
  37.7 0.6 copy-start.10
  38.3 11.4 %collective-permute-start.8 = (bf16[112,512]{1,0:T(8,128)(2,1)}, bf16[112,512]{1,0:T(8,128)(2,1)S(1)}, u32[]{:S(2)}, u32[]{:S(2)}) collective-permute-start(bf16[112,512]{1,0:T(8,128)(2,1)} %get-tuple-element.76), channel_id=1, source_target_pairs={{0,72},{1,49},{2,74},{3,51},{4,76},{5,53},{6,78},{7,55},{8,64},{9,... | collective-permute-start | bytes 344072 | tf_op jit(solution)/shard_map/ppermute | solution.py:536
  38.5 0.7 copy-start.12
  39.2 16.9 %collective-permute-start.9 = (bf16[112,512]{1,0:T(8,128)(2,1)}, bf16[112,512]{1,0:T(8,128)(2,1)S(1)}, u32[]{:S(2)}, u32[]{:S(2)}) collective-permute-start(bf16[112,512]{1,0:T(8,128)(2,1)} %get-tuple-element.77), channel_id=1, source_target_pairs={{0,80},{1,81},{2,82},{3,83},{4,84},{5,85},{6,86},{7,87},{8,88},{9,... | collective-permute-start | bytes 344072 | tf_op jit(solution)/shard_map/ppermute | solution.py:536
  46.4 13.8 %copy-start.14 = (bf16[112,512]{1,0:T(8,128)(2,1)}, bf16[112,512]{1,0:T(8,128)(2,1)S(1)}, u32[]{:S(2)}) copy-start(bf16[112,512]{1,0:T(8,128)(2,1)S(1)} %collective-permute-done.5.refs_6_) | copy-start | bytes 344068
  46.4 14.4 %collective-permute-start.10 = (bf16[112,512]{1,0:T(8,128)(2,1)}, bf16[112,512]{1,0:T(8,128)(2,1)S(1)}, u32[]{:S(2)}, u32[]{:S(2)}) collective-permute-start(bf16[112,512]{1,0:T(8,128)(2,1)} %get-tuple-element.78), channel_id=1, source_target_pairs={{0,88},{1,113},{2,90},{3,115},{4,92},{5,117},{6,94},{7,119},{8,80}... | collective-permute-start | bytes 344072 | tf_op jit(solution)/shard_map/ppermute | solution.py:536
  46.7 13.5 %copy-start.16 = (bf16[112,512]{1,0:T(8,128)(2,1)}, bf16[112,512]{1,0:T(8,128)(2,1)S(1)}, u32[]{:S(2)}) copy-start(bf16[112,512]{1,0:T(8,128)(2,1)S(1)} %collective-permute-done.6.refs_7_) | copy-start | bytes 344068
  46.7 14.1 %collective-permute-start.11 = (bf16[112,512]{1,0:T(8,128)(2,1)}, bf16[112,512]{1,0:T(8,128)(2,1)S(1)}, u32[]{:S(2)}, u32[]{:S(2)}) collective-permute-start(bf16[112,512]{1,0:T(8,128)(2,1)} %get-tuple-element.79), channel_id=1, source_target_pairs={{0,96},{1,25},{2,98},{3,27},{4,100},{5,29},{6,102},{7,31},{8,104},... | collective-permute-start | bytes 344072 | tf_op jit(solution)/shard_map/ppermute | solution.py:536
  49.7 10.5 %copy-start.18 = (bf16[112,512]{1,0:T(8,128)(2,1)}, bf16[112,512]{1,0:T(8,128)(2,1)S(1)}, u32[]{:S(2)}) copy-start(bf16[112,512]{1,0:T(8,128)(2,1)S(1)} %collective-permute-done.7.refs_8_) | copy-start | bytes 344068
  49.7 11.1 %collective-permute-start.12 = (bf16[112,512]{1,0:T(8,128)(2,1)}, bf16[112,512]{1,0:T(8,128)(2,1)S(1)}, u32[]{:S(2)}, u32[]{:S(2)}) collective-permute-start(bf16[112,512]{1,0:T(8,128)(2,1)} %get-tuple-element.80), channel_id=1, source_target_pairs={{0,104},{1,57},{2,106},{3,59},{4,108},{5,61},{6,110},{7,63},{8,96}... | collective-permute-start | bytes 344072 | tf_op jit(solution)/shard_map/ppermute | solution.py:536
  49.7 10.5 %copy-start.20 = (bf16[112,512]{1,0:T(8,128)(2,1)}, bf16[112,512]{1,0:T(8,128)(2,1)S(1)}, u32[]{:S(2)}) copy-start(bf16[112,512]{1,0:T(8,128)(2,1)S(1)} %collective-permute-done.8.refs_9_) | copy-start | bytes 344068
  49.7 11.1 %collective-permute-start.13 = (bf16[112,512]{1,0:T(8,128)(2,1)}, bf16[112,512]{1,0:T(8,128)(2,1)S(1)}, u32[]{:S(2)}, u32[]{:S(2)}) collective-permute-start(bf16[112,512]{1,0:T(8,128)(2,1)} %get-tuple-element.81), channel_id=1, source_target_pairs={{0,112},{1,89},{2,114},{3,91},{4,116},{5,93},{6,118},{7,95},{8,120... | collective-permute-start | bytes 344072 | tf_op jit(solution)/shard_map/ppermute | solution.py:536
  56.0 4.2 %copy-start.22 = (bf16[112,512]{1,0:T(8,128)(2,1)}, bf16[112,512]{1,0:T(8,128)(2,1)S(1)}, u32[]{:S(2)}) copy-start(bf16[112,512]{1,0:T(8,128)(2,1)S(1)} %collective-permute-done.9.refs_10_) | copy-start | bytes 344068
  56.0 8.3 %collective-permute-start.14 = (bf16[112,512]{1,0:T(8,128)(2,1)}, bf16[112,512]{1,0:T(8,128)(2,1)S(1)}, u32[]{:S(2)}, u32[]{:S(2)}) collective-permute-start(bf16[112,512]{1,0:T(8,128)(2,1)} %get-tuple-element.82), channel_id=1, source_target_pairs={{0,120},{1,121},{2,122},{3,123},{4,124},{5,125},{6,126},{7,127},{8... | collective-permute-start | bytes 344072 | tf_op jit(solution)/shard_map/ppermute | solution.py:536
  60.8 11.5 %copy-start.24 = (bf16[112,512]{1,0:T(8,128)(2,1)}, bf16[112,512]{1,0:T(8,128)(2,1)S(1)}, u32[]{:S(2)}) copy-start(bf16[112,512]{1,0:T(8,128)(2,1)S(1)} %collective-permute-done.10.refs_11_) | copy-start | bytes 344068
  60.8 11.5 %copy-start.26 = (bf16[112,512]{1,0:T(8,128)(2,1)}, bf16[112,512]{1,0:T(8,128)(2,1)S(1)}, u32[]{:S(2)}) copy-start(bf16[112,512]{1,0:T(8,128)(2,1)S(1)} %collective-permute-done.11.refs_12_) | copy-start | bytes 344068
  60.8 11.5 %copy-start.28 = (bf16[112,512]{1,0:T(8,128)(2,1)}, bf16[112,512]{1,0:T(8,128)(2,1)S(1)}, u32[]{:S(2)}) copy-start(bf16[112,512]{1,0:T(8,128)(2,1)S(1)} %collective-permute-done.12.refs_13_) | copy-start | bytes 344068
  60.9 11.5 %copy-start.30 = (bf16[112,512]{1,0:T(8,128)(2,1)}, bf16[112,512]{1,0:T(8,128)(2,1)S(1)}, u32[]{:S(2)}) copy-start(bf16[112,512]{1,0:T(8,128)(2,1)S(1)} %collective-permute-done.13.refs_14_) | copy-start | bytes 344068
  64.4 8.0 %copy-start.32 = (bf16[112,512]{1,0:T(8,128)(2,1)}, bf16[112,512]{1,0:T(8,128)(2,1)S(1)}, u32[]{:S(2)}) copy-start(bf16[112,512]{1,0:T(8,128)(2,1)S(1)} %collective-permute-done.14.refs_15_) | copy-start | bytes 344068
  72.4 6.7 %copy-start.35 = (s32[512]{0:T(512)S(1)}, s32[512]{0:T(512)}, u32[]{:S(2)}) copy-start(s32[512]{0:T(512)} %orders.5) | copy-start | bytes 6148
  72.4 6.7 %copy-start.36 = (s32[2]{0:T(128)S(1)}, s32[2]{0:T(128)}, u32[]{:S(2)}) copy-start(s32[2]{0:T(128)} %pad_add_fusion.place) | copy-start | bytes 28
  72.4 31.6 %all-to-all-start.1 = ((bf16[128,8,768]{2,1,0:T(8,128)(2,1)}), bf16[128,8,768]{2,1,0:T(8,128)(2,1)S(1)}, u32[]{:S(2)}, u32[]{:S(2)}) async-start(bf16[128,8,768]{2,1,0:T(8,128)(2,1)} %bitcast.13), calls=%async_computation.1 | async-start | bytes 3145728 | tf_op jit(solution)/shard_map/all_to_all | solution.py:543
  79.1 1.1 copy-start.2
  80.2 0.9 copy-start.3
  81.1 0.9 copy-start.5
  82.0 0.9 copy-start.7
  82.9 0.9 copy-start.9
  83.8 0.9 copy-start.11
  84.7 0.9 copy-start.13
  85.6 0.9 copy-start.15
  86.5 0.9 copy-start.17
  87.4 0.9 copy-start.19
  88.3 0.9 copy-start.21
  89.2 0.9 copy-start.23
  90.1 0.9 copy-start.25
  91.0 0.9 copy-start.27
  91.9 0.9 copy-start.29
  92.8 0.9 copy-start.31
  93.7 0.9 copy-start.33
  96.2 1.0 copy-start
  104.0 1.2 copy-start.1

commit v9 on v8

--- a/solution.py
+++ b/solution.py
@@ -527,6 +527,9 @@
         (order_slots, velocity, potential, latitude)
     )
     parts = state_to_send(place, kappa, angular, vel_after, pot_after)
+    tables = make_tables(order_after)
+    parts = list(parts)
+    parts[6:], tables = lax.optimization_barrier((parts[6:], tables))
     received = [parts[0]]
     for r in range(1, 16):
         swapped = (r & 3) * 4 + r // 4
@@ -534,11 +537,11 @@
             (i * 8 + o, (i ^ (swapped if o & 1 else r)) * 8 + o) for i in range(16) for o in range(8)
         ]
         received.append(lax.ppermute(parts[r], ("shell", "order"), pairs_r))
-    tables = make_tables(order_after)
-    incoming, received = lax.optimization_barrier((incoming, received))
+    early = 12
+    incoming, received[:early] = lax.optimization_barrier((incoming, received[:early]))
 
     coefs = grid_stage(incoming, tables, weight)
-    received, _ = lax.optimization_barrier((received, coefs))
+    received, coefs = lax.optimization_barrier((received, coefs))
     state, factors, table = solve_factors(place, order_slots, pairs, received)
     coefs = lax.all_to_all(
         coefs.reshape(128, 8, 768), ("shell", "order"), 0, 0, tiled=True

time: 136 us -> 137 us (level)
  starting transfers between devices: 43.4 us -> 47.7 us
  waiting for transfers between devices: 10.3 us -> 6.85 us
    ppermute x15, waiting for transfers between devices: 3.53 us -> 0.04 us  [body(): received.append(lax.ppermute(parts[r], ('shell', 'order'), pairs_r))]
    all_to_all x1, starting transfers between devices: 6.68 us -> 10.1 us  [body(): lax.all_to_all(coefs.reshape(128, 8, 768), ('shell', 'order'), 0, 0, tile...]
    unnamed x78 -> x98, local copies, waits for them, and re-layouts: 20.9 us -> 20.9 us
  transfers between devices with their start and end apart: 17 -> 17, of which waited for: 2 -> 1; matrix products, arithmetic and copies ran while one was open for 2% -> 2% of each run, Pallas kernels for 6% -> 12%
where the time goes in v9:
time: 137 us; the launch traced here: 136 us
  starting transfers between devices  47.7 us (35%)
  Pallas kernels  31.6 us (23%)
  blocking collectives  25.4 us (19%)
  local copies, waits for them, and re-layouts  21.7 us (16%)
  waiting for transfers between devices  6.85 us (5%)
  other arithmetic  2.14 us (2%)
    ppermute x15, starting transfers between devices, body(): received.append(lax.ppermute(parts[r], ('shell', 'order'), pairs_r))  32.1 us
    all_to_all x1, blocking collectives, body(): solved = lax.all_to_all(solved, 'shell', 0, 0, tiled=True)  25.4 us
    unnamed x98, local copies, waits for them, and re-layouts  20.9 us
    all_to_all x1, starting transfers between devices, body(): lax.all_to_all(coefs.reshape(128, 8, 768), ('shell', 'order'), 0, 0, tile...  10.1 us
    pallas_call x1, Pallas kernels, legendre_synthesis(): pl.pallas_call(synthesis_kernel, grid_spec=pltpu.PrefetchScalarGridSpec(n...  10 us
    pallas_call x1, Pallas kernels, grid_stage(): pl.pallas_call(grid_kernel, grid=(3,), in_specs=[pl.BlockSpec((8, 24, 64,...  7.97 us
    all_to_all x1, waiting for transfers between devices, body(): lax.all_to_all(coefs.reshape(128, 8, 768), ('shell', 'order'), 0, 0, tile...  6.81 us
    all_to_all x1, starting transfers between devices, body(): incoming = lax.all_to_all(latitude, 'order', 0, 0, tiled=True)  5.41 us
  transfers between devices with their start and end apart: 17, of which 1 were waited for; matrix products, arithmetic and copies ran while one was open for 2% of the time, Pallas kernels for 12%

profile of v9, /device:TPU:0, one launch (start us, length us, event | category | flops | bytes accessed | tf_op | source)
XLA Modules:
  0.0 136.5 jit_solution(14191069273720732879)
XLA Ops:
  0.6 0.6 pad_add_fusion.place
  1.2 10.0 %legendre_synthesis.1 = (bf16[8,24,64,128]{3,2,1,0:T(8,128)(2,1)}, bf16[2,528,256]{2,1,0:T(8,128)(2,1)}) custom-call(s32[2]{0:T(128)} %pad_add_fusion.place, s32[512]{0:T(512)} %orders.5, bf16[3,2,2,64,512]{4,3,2,1,0:T(8,128)(2,1)} %vel.2, bf16[3,2,2,64,512]{4,3,2,1,0:T(8,128)(2,1)} %vor.1, bf16[3,2,2,64,512]{4,3,2,1,0:T(8,128)(2,1)} %mag.1, ...), custom_call_target="tpu_custom_call" | custom-call | flops 1600000000 | bytes 15728640 | tf_op jit(solution)/shard_map/legendre_synthesis/pallas_call | solution.py:132
  11.2 0.0 copy-start.48
  11.3 0.0 copy-start.37
  11.3 5.4 %all-to-all-start = ((bf16[8,24,64,128]{3,2,1,0:T(8,128)(2,1)}), bf16[8,24,64,128]{3,2,1,0:T(8,128)(2,1)}, u32[]{:S(2)}, u32[]{:S(2)}) async-start(bf16[8,24,64,128]{3,2,1,0:T(8,128)(2,1)} %get-tuple-element.76), calls=%async_computation | async-start | bytes 6291456 | tf_op jit(solution)/shard_map/all_to_all | solution.py:524
  16.7 0.2 reduce-window.9
  16.9 0.2 compare_reduce_fusion
  17.1 0.6 broadcast_select_fusion.kappa
  17.7 3.0 %state_to_send.1 = (bf16[112,512]{1,0:T(8,128)(2,1)}, bf16[112,512]{1,0:T(8,128)(2,1)}, bf16[112,512]{1,0:T(8,128)(2,1)}, bf16[112,512]{1,0:T(8,128)(2,1)}, bf16...) custom-call(s32[2]{0:T(128)} %pad_add_fusion.place, ...), custom_call_target="tpu_custom_call" | custom-call | flops 1000000 | bytes 4194304 | tf_op jit(solution)/shard_map/state_to_send/pallas_call | solution.py:190
  20.7 1.5 %collective-permute-start = (bf16[112,512]{1,0:T(8,128)(2,1)}, bf16[112,512]{1,0:T(8,128)(2,1)S(1)}, u32[]{:S(2)}, u32[]{:S(2)}) collective-permute-start(bf16[112,512]{1,0:T(8,128)(2,1)} %get-tuple-element.80), channel_id=1, source_target_pairs={{0,8},{1,33},{2,10},{3,35},{4,12},{5,37},{6,14},{7,39},{8,0},{9,41... | collective-permute-start | bytes 344072 | tf_op jit(solution)/shard_map/ppermute | solution.py:539
  22.2 2.7 %collective-permute-start.1 = (bf16[112,512]{1,0:T(8,128)(2,1)}, bf16[112,512]{1,0:T(8,128)(2,1)S(1)}, u32[]{:S(2)}, u32[]{:S(2)}) collective-permute-start(bf16[112,512]{1,0:T(8,128)(2,1)} %get-tuple-element.81), channel_id=1, source_target_pairs={{0,16},{1,65},{2,18},{3,67},{4,20},{5,69},{6,22},{7,71},{8,24},{9,... | collective-permute-start | bytes 344072 | tf_op jit(solution)/shard_map/ppermute | solution.py:539
  24.9 0.5 collective-permute-start.2
  25.4 1.6 %collective-permute-start.3 = (bf16[112,512]{1,0:T(8,128)(2,1)}, bf16[112,512]{1,0:T(8,128)(2,1)S(1)}, u32[]{:S(2)}, u32[]{:S(2)}) collective-permute-start(bf16[112,512]{1,0:T(8,128)(2,1)} %get-tuple-element.83), channel_id=1, source_target_pairs={{0,32},{1,9},{2,34},{3,11},{4,36},{5,13},{6,38},{7,15},{8,40},{9,1... | collective-permute-start | bytes 344072 | tf_op jit(solution)/shard_map/ppermute | solution.py:539
  27.0 0.2 collective-permute-start.4
  27.2 0.1 reshape.76
  27.3 0.7 reshape.77.targets
  28.1 4.1 %make_tables.1 = (bf16[528,512]{1,0:T(8,128)(2,1)}, bf16[512,512]{1,0:T(8,128)(2,1)}, bf16[512,512]{1,0:T(8,128)(2,1)}, bf16[512,512]{1,0:T(8,128)(2,1)}, f32[512,128]{1,0:T(8,128)}) custom-call(s32[1,512]{1,0:T(1,128)} %bitcast.11, s32[1,512]{1,0:T(1,128)} %reshape.77.targets, bf16[528,512]{1,0:T(8,128)(2,1)} %constant.42.clone.refs_0_, ...), custom_call_target="tpu_custom_call" | custom-call | flops 1000000000 | bytes 5242880 | tf_op jit(solution)/shard_map/make_tables/pallas_call | solution.py:302
  32.1 5.0 %collective-permute-start.5 = (bf16[112,512]{1,0:T(8,128)(2,1)S(1)}, bf16[112,512]{1,0:T(8,128)(2,1)S(1)}, u32[]{:S(2)}, u32[]{:S(2)}) collective-permute-start(bf16[112,512]{1,0:T(8,128)(2,1)S(1)} %copy-done.47), channel_id=1, source_target_pairs={{0,48},{1,73},{2,50},{3,75},{4,52},{5,77},{6,54},{7,79},{8,56},{9,... | collective-permute-start | bytes 344072 | tf_op jit(solution)/shard_map/ppermute | solution.py:539
  37.2 0.0 collective-permute-done.1.refs_2_
  37.2 0.4 collective-permute-start.6
  37.6 0.0 collective-permute-done.2.refs_3_
  37.6 3.3 %collective-permute-start.7 = (bf16[112,512]{1,0:T(8,128)(2,1)S(1)}, bf16[112,512]{1,0:T(8,128)(2,1)S(1)}, u32[]{:S(2)}, u32[]{:S(2)}) collective-permute-start(bf16[112,512]{1,0:T(8,128)(2,1)S(1)} %copy-done.45), channel_id=1, source_target_pairs={{0,64},{1,17},{2,66},{3,19},{4,68},{5,21},{6,70},{7,23},{8,72},{9,... | collective-permute-start | bytes 344072 | tf_op jit(solution)/shard_map/ppermute | solution.py:539
  40.9 0.0 collective-permute-done.3.refs_4_
  40.9 0.1 collective-permute-start.8
  41.0 6.7 %collective-permute-start.9 = (bf16[112,512]{1,0:T(8,128)(2,1)S(1)}, bf16[112,512]{1,0:T(8,128)(2,1)S(1)}, u32[]{:S(2)}, u32[]{:S(2)}) collective-permute-start(bf16[112,512]{1,0:T(8,128)(2,1)S(1)} %copy-done.43), channel_id=1, source_target_pairs={{0,80},{1,81},{2,82},{3,83},{4,84},{5,85},{6,86},{7,87},{8,88},{9,... | collective-permute-start | bytes 344072 | tf_op jit(solution)/shard_map/ppermute | solution.py:539
  47.7 0.6 copy-done.14
  48.3 0.2 collective-permute-start.10
  48.6 0.6 sine_multiply_fusion.weight
  49.2 3.1 %collective-permute-start.11 = (bf16[112,512]{1,0:T(8,128)(2,1)S(1)}, bf16[112,512]{1,0:T(8,128)(2,1)S(1)}, u32[]{:S(2)}, u32[]{:S(2)}) collective-permute-start(bf16[112,512]{1,0:T(8,128)(2,1)S(1)} %copy-done.41), channel_id=1, source_target_pairs={{0,96},{1,25},{2,98},{3,27},{4,100},{5,29},{6,102},{7,31},{8,104},... | collective-permute-start | bytes 344072 | tf_op jit(solution)/shard_map/ppermute | solution.py:539
  52.3 0.1 collective-permute-start.12
  52.4 6.4 %collective-permute-start.13 = (bf16[112,512]{1,0:T(8,128)(2,1)S(1)}, bf16[112,512]{1,0:T(8,128)(2,1)S(1)}, u32[]{:S(2)}, u32[]{:S(2)}) collective-permute-start(bf16[112,512]{1,0:T(8,128)(2,1)S(1)} %copy-done.39), channel_id=1, source_target_pairs={{0,112},{1,89},{2,114},{3,91},{4,116},{5,93},{6,118},{7,95},{8,120... | collective-permute-start | bytes 344072 | tf_op jit(solution)/shard_map/ppermute | solution.py:539
  58.8 0.4 collective-permute-start.14
  59.2 8.0 %grid_stage.1 = bf16[1024,768]{1,0:T(8,128)(2,1)} custom-call(bf16[8,24,64,128]{3,2,1,0:T(8,128)(2,1)} %all-to-all-done.lat, bf16[528,512]{1,0:T(8,128)(2,1)} %get-tuple-element.124.syn_cos, bf16[512,512]{1,0:T(8,128)(2,1)} %get-tuple-element.125.syn_sin, bf16[512,512]{1,0:T(8,128)(2,1)} %get-tuple-element.126.ana_cos, ...), custom_call_target="tpu_custom_call" | custom-call | flops 2400000000 | bytes 7340032 | tf_op jit(solution)/shard_map/grid_stage/pallas_call | solution.py:257
  67.3 0.6 copy-done.26
  67.9 0.7 copy-done.28
  68.6 0.6 copy-done.30
  69.2 0.6 copy-done.32
  69.9 10.1 %all-to-all-start.1 = ((bf16[128,8,768]{2,1,0:T(8,128)(2,1)}), bf16[128,8,768]{2,1,0:T(8,128)(2,1)S(1)}, u32[]{:S(2)}, u32[]{:S(2)}) async-start(bf16[128,8,768]{2,1,0:T(8,128)(2,1)} %bitcast.13), calls=%async_computation.1 | async-start | bytes 3145728 | tf_op jit(solution)/shard_map/all_to_all | solution.py:546
  80.0 0.0 copy-start.2
  80.0 1.0 copy-done.2
  81.0 0.9 copy-done.3
  81.9 0.9 copy-done.5
  82.8 0.9 copy-done.7
  83.7 0.9 copy-done.9
  84.6 0.9 copy-done.11
  85.5 0.9 copy-done.13
  86.4 0.9 copy-done.15
  87.3 0.9 copy-done.17
  88.2 0.9 copy-done.19
  89.1 0.9 copy-done.21
  90.0 0.9 copy-done.23
  90.9 0.9 copy-done.25
  91.8 0.9 copy-done.27
  92.7 0.9 copy-done.29
  93.6 0.9 copy-done.31
  94.5 0.9 copy-done.33
  95.4 1.6 %solve_factors.1 = (bf16[16,96,512]{2,1,0:T(8,128)(2,1)S(1)}, f32[3,64,512]{2,1,0:T(8,128)S(1)}, bf16[4,256,512]{2,1,0:T(8,128)(2,1)S(1)}) custom-call(s32[2]{0:T(128)S(1)} %copy-done.36, s32[512]{0:T(512)S(1)} %copy-done.35, bf16[2,528,256]{2,1,0:T(8,128)(2,1)S(1)} %copy-done.2, bf16[112,512]{1,0:T(8,128)(2,1)S(1)} %copy-done.3, ...), custom_call_target="tpu_custom_call" | custom-call | flops 1000000 | bytes 1048576 | tf_op jit(solution)/shard_map/solve_factors/pallas_call | solution.py:354
  97.0 0.0 copy-start
  97.1 1.0 copy-done
  98.0 6.8 %all-to-all-done.1 = bf16[128,8,768]{2,1,0:T(8,128)(2,1)S(1)} async-done(((bf16[128,8,768]{2,1,0:T(8,128)(2,1)}), bf16[128,8,768]{2,1,0:T(8,128)(2,1)S(1)}, u32[]{:S(2)}, u32[]{:S(2)}) %all-to-all-start.1) | async-done | bytes 1572896 | tf_op jit(solution)/shard_map/all_to_all | solution.py:546
  104.8 1.2 copy-done.1
  106.1 3.0 %analysis_and_solve.1 = bf16[16,96,512]{2,1,0:T(8,128)(2,1)S(1)} custom-call(s32[2]{0:T(128)S(1)} %copy-done.36, s32[512]{0:T(512)S(1)} %copy-done.35, bf16[1024,768]{1,0:T(8,128)(2,1)S(1)} %bitcast.10, bf16[4,256,512]{2,1,0:T(8,128)(2,1)S(1)} %copy-done.1, f32[3,64,512]{2,1,0:T(8,128)S(1)} %get-tuple-element.148.factors, ...), custom_call_target="tpu_custom_call" | custom-call | flops 900000000 | bytes 6291456 | tf_op jit(solution)/shard_map/analysis_and_solve/pallas_call | solution.py:440
  109.0 25.4 %all_to_all.15.got = bf16[16,96,512]{2,1,0:T(8,128)(2,1)S(1)} all-to-all(bf16[16,96,512]{2,1,0:T(8,128)(2,1)S(1)} %analysis_and_solve.1), channel_id=1, replica_groups=mesh['shell'=16,'order'=8] {'shell'}, dimensions={0} | all-to-all | bytes 3145728 | tf_op jit(solution)/shard_map/all_to_all | solution.py:550
  134.5 2.0 %unpack_solution.1 = (f32[3,2,2,64,512]{4,3,2,1,0:T(8,128)}, f32[3,2,2,64,512]{4,3,2,1,0:T(8,128)}) custom-call(bf16[16,96,512]{2,1,0:T(8,128)(2,1)S(1)} %all_to_all.15.got), custom_call_target="tpu_custom_call" | custom-call | flops 1000000 | bytes 5242880 | tf_op jit(solution)/shard_map/unpack_solution/pallas_call | solution.py:480
  (86 shorter events, 0.2 us)
Async XLA Ops:
  11.2 5.4 %copy-start.48 = (s32[4]{0:T(128)S(1)}, s32[4]{0:T(128)}, u32[]{:S(2)}) copy-start(s32[4]{0:T(128)} %param.22) | copy-start | bytes 52
  11.3 5.8 %copy-start.37 = (f32[2,2]{1,0:T(2,128)S(1)}, f32[2,2]{1,0:T(2,128)}, u32[]{:S(2)}) copy-start(f32[2,2]{1,0:T(2,128)} %param.23) | copy-start | bytes 52
  11.3 47.9 %all-to-all-start = ((bf16[8,24,64,128]{3,2,1,0:T(8,128)(2,1)}), bf16[8,24,64,128]{3,2,1,0:T(8,128)(2,1)}, u32[]{:S(2)}, u32[]{:S(2)}) async-start(bf16[8,24,64,128]{3,2,1,0:T(8,128)(2,1)} %get-tuple-element.76), calls=%async_computation | async-start | bytes 6291456 | tf_op jit(solution)/shard_map/all_to_all | solution.py:524
  16.7 10.5 %copy-start.34 = (s32[512]{0:T(512)S(1)}, s32[512]{0:T(512)}, u32[]{:S(2)}) copy-start(s32[512]{0:T(512)} %orders.5) | copy-start | bytes 6148
  20.7 11.5 %collective-permute-start = (bf16[112,512]{1,0:T(8,128)(2,1)}, bf16[112,512]{1,0:T(8,128)(2,1)S(1)}, u32[]{:S(2)}, u32[]{:S(2)}) collective-permute-start(bf16[112,512]{1,0:T(8,128)(2,1)} %get-tuple-element.80), channel_id=1, source_target_pairs={{0,8},{1,33},{2,10},{3,35},{4,12},{5,37},{6,14},{7,39},{8,0},{9,41... | collective-permute-start | bytes 344072 | tf_op jit(solution)/shard_map/ppermute | solution.py:539
  22.2 15.0 %collective-permute-start.1 = (bf16[112,512]{1,0:T(8,128)(2,1)}, bf16[112,512]{1,0:T(8,128)(2,1)S(1)}, u32[]{:S(2)}, u32[]{:S(2)}) collective-permute-start(bf16[112,512]{1,0:T(8,128)(2,1)} %get-tuple-element.81), channel_id=1, source_target_pairs={{0,16},{1,65},{2,18},{3,67},{4,20},{5,69},{6,22},{7,71},{8,24},{9,... | collective-permute-start | bytes 344072 | tf_op jit(solution)/shard_map/ppermute | solution.py:539
  24.9 12.7 %collective-permute-start.2 = (bf16[112,512]{1,0:T(8,128)(2,1)}, bf16[112,512]{1,0:T(8,128)(2,1)S(1)}, u32[]{:S(2)}, u32[]{:S(2)}) collective-permute-start(bf16[112,512]{1,0:T(8,128)(2,1)} %get-tuple-element.82), channel_id=1, source_target_pairs={{0,24},{1,97},{2,26},{3,99},{4,28},{5,101},{6,30},{7,103},{8,16},{... | collective-permute-start | bytes 344072 | tf_op jit(solution)/shard_map/ppermute | solution.py:539
  25.4 15.5 %collective-permute-start.3 = (bf16[112,512]{1,0:T(8,128)(2,1)}, bf16[112,512]{1,0:T(8,128)(2,1)S(1)}, u32[]{:S(2)}, u32[]{:S(2)}) collective-permute-start(bf16[112,512]{1,0:T(8,128)(2,1)} %get-tuple-element.83), channel_id=1, source_target_pairs={{0,32},{1,9},{2,34},{3,11},{4,36},{5,13},{6,38},{7,15},{8,40},{9,1... | collective-permute-start | bytes 344072 | tf_op jit(solution)/shard_map/ppermute | solution.py:539
  27.0 14.0 %collective-permute-start.4 = (bf16[112,512]{1,0:T(8,128)(2,1)}, bf16[112,512]{1,0:T(8,128)(2,1)S(1)}, u32[]{:S(2)}, u32[]{:S(2)}) collective-permute-start(bf16[112,512]{1,0:T(8,128)(2,1)} %get-tuple-element.84), channel_id=1, source_target_pairs={{0,40},{1,41},{2,42},{3,43},{4,44},{5,45},{6,46},{7,47},{8,32},{9,... | collective-permute-start | bytes 344072 | tf_op jit(solution)/shard_map/ppermute | solution.py:539
  28.0 4.1 %copy-start.47 = (bf16[112,512]{1,0:T(8,128)(2,1)S(1)}, bf16[112,512]{1,0:T(8,128)(2,1)}, u32[]{:S(2)}) copy-start(bf16[112,512]{1,0:T(8,128)(2,1)} %get-tuple-element.101) | copy-start | bytes 344068
  28.0 9.2 %copy-start.46 = (bf16[112,512]{1,0:T(8,128)(2,1)S(1)}, bf16[112,512]{1,0:T(8,128)(2,1)}, u32[]{:S(2)}) copy-start(bf16[112,512]{1,0:T(8,128)(2,1)} %get-tuple-element.102) | copy-start | bytes 344068
  28.0 9.6 %copy-start.45 = (bf16[112,512]{1,0:T(8,128)(2,1)S(1)}, bf16[112,512]{1,0:T(8,128)(2,1)}, u32[]{:S(2)}) copy-start(bf16[112,512]{1,0:T(8,128)(2,1)} %get-tuple-element.103) | copy-start | bytes 344068
  28.0 12.9 %copy-start.44 = (bf16[112,512]{1,0:T(8,128)(2,1)S(1)}, bf16[112,512]{1,0:T(8,128)(2,1)}, u32[]{:S(2)}) copy-start(bf16[112,512]{1,0:T(8,128)(2,1)} %get-tuple-element.104) | copy-start | bytes 344068
  28.0 13.0 %copy-start.43 = (bf16[112,512]{1,0:T(8,128)(2,1)S(1)}, bf16[112,512]{1,0:T(8,128)(2,1)}, u32[]{:S(2)}) copy-start(bf16[112,512]{1,0:T(8,128)(2,1)} %get-tuple-element.105) | copy-start | bytes 344068
  28.0 20.3 %copy-start.42 = (bf16[112,512]{1,0:T(8,128)(2,1)S(1)}, bf16[112,512]{1,0:T(8,128)(2,1)}, u32[]{:S(2)}) copy-start(bf16[112,512]{1,0:T(8,128)(2,1)} %get-tuple-element.106) | copy-start | bytes 344068
  28.0 21.2 %copy-start.41 = (bf16[112,512]{1,0:T(8,128)(2,1)S(1)}, bf16[112,512]{1,0:T(8,128)(2,1)}, u32[]{:S(2)}) copy-start(bf16[112,512]{1,0:T(8,128)(2,1)} %get-tuple-element.119) | copy-start | bytes 344068
  28.0 24.2 %copy-start.40 = (bf16[112,512]{1,0:T(8,128)(2,1)S(1)}, bf16[112,512]{1,0:T(8,128)(2,1)}, u32[]{:S(2)}) copy-start(bf16[112,512]{1,0:T(8,128)(2,1)} %get-tuple-element.120) | copy-start | bytes 344068
  28.1 24.3 %copy-start.39 = (bf16[112,512]{1,0:T(8,128)(2,1)S(1)}, bf16[112,512]{1,0:T(8,128)(2,1)}, u32[]{:S(2)}) copy-start(bf16[112,512]{1,0:T(8,128)(2,1)} %get-tuple-element.121) | copy-start | bytes 344068
  28.1 30.7 %copy-start.38 = (bf16[112,512]{1,0:T(8,128)(2,1)S(1)}, bf16[112,512]{1,0:T(8,128)(2,1)}, u32[]{:S(2)}) copy-start(bf16[112,512]{1,0:T(8,128)(2,1)} %get-tuple-element.122) | copy-start | bytes 344068
  32.1 35.0 %copy-start.4 = (bf16[112,512]{1,0:T(8,128)(2,1)}, bf16[112,512]{1,0:T(8,128)(2,1)S(1)}, u32[]{:S(2)}) copy-start(bf16[112,512]{1,0:T(8,128)(2,1)S(1)} %collective-permute-done.refs_1_) | copy-start | bytes 344068
  32.1 15.6 %collective-permute-start.5 = (bf16[112,512]{1,0:T(8,128)(2,1)S(1)}, bf16[112,512]{1,0:T(8,128)(2,1)S(1)}, u32[]{:S(2)}, u32[]{:S(2)}) collective-permute-start(bf16[112,512]{1,0:T(8,128)(2,1)S(1)} %copy-done.47), channel_id=1, source_target_pairs={{0,48},{1,73},{2,50},{3,75},{4,52},{5,77},{6,54},{7,79},{8,56},{9,... | collective-permute-start | bytes 344072 | tf_op jit(solution)/shard_map/ppermute | solution.py:539
  37.2 30.0 %copy-start.6 = (bf16[112,512]{1,0:T(8,128)(2,1)}, bf16[112,512]{1,0:T(8,128)(2,1)S(1)}, u32[]{:S(2)}) copy-start(bf16[112,512]{1,0:T(8,128)(2,1)S(1)} %collective-permute-done.1.refs_2_) | copy-start | bytes 344068
  37.2 12.0 %collective-permute-start.6 = (bf16[112,512]{1,0:T(8,128)(2,1)S(1)}, bf16[112,512]{1,0:T(8,128)(2,1)S(1)}, u32[]{:S(2)}, u32[]{:S(2)}) collective-permute-start(bf16[112,512]{1,0:T(8,128)(2,1)S(1)} %copy-done.46), channel_id=1, source_target_pairs={{0,56},{1,105},{2,58},{3,107},{4,60},{5,109},{6,62},{7,111},{8,48}... | collective-permute-start | bytes 344072 | tf_op jit(solution)/shard_map/ppermute | solution.py:539
  37.6 29.5 %copy-start.8 = (bf16[112,512]{1,0:T(8,128)(2,1)}, bf16[112,512]{1,0:T(8,128)(2,1)S(1)}, u32[]{:S(2)}) copy-start(bf16[112,512]{1,0:T(8,128)(2,1)S(1)} %collective-permute-done.2.refs_3_) | copy-start | bytes 344068
  37.6 14.7 %collective-permute-start.7 = (bf16[112,512]{1,0:T(8,128)(2,1)S(1)}, bf16[112,512]{1,0:T(8,128)(2,1)S(1)}, u32[]{:S(2)}, u32[]{:S(2)}) collective-permute-start(bf16[112,512]{1,0:T(8,128)(2,1)S(1)} %copy-done.45), channel_id=1, source_target_pairs={{0,64},{1,17},{2,66},{3,19},{4,68},{5,21},{6,70},{7,23},{8,72},{9,... | collective-permute-start | bytes 344072 | tf_op jit(solution)/shard_map/ppermute | solution.py:539
  40.9 26.3 %copy-start.10 = (bf16[112,512]{1,0:T(8,128)(2,1)}, bf16[112,512]{1,0:T(8,128)(2,1)S(1)}, u32[]{:S(2)}) copy-start(bf16[112,512]{1,0:T(8,128)(2,1)S(1)} %collective-permute-done.3.refs_4_) | copy-start | bytes 344068
  40.9 11.5 %collective-permute-start.8 = (bf16[112,512]{1,0:T(8,128)(2,1)S(1)}, bf16[112,512]{1,0:T(8,128)(2,1)S(1)}, u32[]{:S(2)}, u32[]{:S(2)}) collective-permute-start(bf16[112,512]{1,0:T(8,128)(2,1)S(1)} %copy-done.44), channel_id=1, source_target_pairs={{0,72},{1,49},{2,74},{3,51},{4,76},{5,53},{6,78},{7,55},{8,64},{9,... | collective-permute-start | bytes 344072 | tf_op jit(solution)/shard_map/ppermute | solution.py:539
  41.0 26.2 %copy-start.12 = (bf16[112,512]{1,0:T(8,128)(2,1)}, bf16[112,512]{1,0:T(8,128)(2,1)S(1)}, u32[]{:S(2)}) copy-start(bf16[112,512]{1,0:T(8,128)(2,1)S(1)} %collective-permute-done.4.refs_5_) | copy-start | bytes 344068
  41.0 17.8 %collective-permute-start.9 = (bf16[112,512]{1,0:T(8,128)(2,1)S(1)}, bf16[112,512]{1,0:T(8,128)(2,1)S(1)}, u32[]{:S(2)}, u32[]{:S(2)}) collective-permute-start(bf16[112,512]{1,0:T(8,128)(2,1)S(1)} %copy-done.43), channel_id=1, source_target_pairs={{0,80},{1,81},{2,82},{3,83},{4,84},{5,85},{6,86},{7,87},{8,88},{9,... | collective-permute-start | bytes 344072 | tf_op jit(solution)/shard_map/ppermute | solution.py:539
  48.3 10.8 %collective-permute-start.10 = (bf16[112,512]{1,0:T(8,128)(2,1)S(1)}, bf16[112,512]{1,0:T(8,128)(2,1)S(1)}, u32[]{:S(2)}, u32[]{:S(2)}) collective-permute-start(bf16[112,512]{1,0:T(8,128)(2,1)S(1)} %copy-done.42), channel_id=1, source_target_pairs={{0,88},{1,113},{2,90},{3,115},{4,92},{5,117},{6,94},{7,119},{8,80}... | collective-permute-start | bytes 344072 | tf_op jit(solution)/shard_map/ppermute | solution.py:539
  49.2 18.0 %copy-start.16 = (bf16[112,512]{1,0:T(8,128)(2,1)}, bf16[112,512]{1,0:T(8,128)(2,1)S(1)}, u32[]{:S(2)}) copy-start(bf16[112,512]{1,0:T(8,128)(2,1)S(1)} %collective-permute-done.6.refs_7_) | copy-start | bytes 344068
  49.2 18.1 %collective-permute-start.11 = (bf16[112,512]{1,0:T(8,128)(2,1)S(1)}, bf16[112,512]{1,0:T(8,128)(2,1)S(1)}, u32[]{:S(2)}, u32[]{:S(2)}) collective-permute-start(bf16[112,512]{1,0:T(8,128)(2,1)S(1)} %copy-done.41), channel_id=1, source_target_pairs={{0,96},{1,25},{2,98},{3,27},{4,100},{5,29},{6,102},{7,31},{8,104},... | collective-permute-start | bytes 344072 | tf_op jit(solution)/shard_map/ppermute | solution.py:539
  52.3 14.9 %copy-start.18 = (bf16[112,512]{1,0:T(8,128)(2,1)}, bf16[112,512]{1,0:T(8,128)(2,1)S(1)}, u32[]{:S(2)}) copy-start(bf16[112,512]{1,0:T(8,128)(2,1)S(1)} %collective-permute-done.7.refs_8_) | copy-start | bytes 344068
  52.3 15.6 %collective-permute-start.12 = (bf16[112,512]{1,0:T(8,128)(2,1)S(1)}, bf16[112,512]{1,0:T(8,128)(2,1)S(1)}, u32[]{:S(2)}, u32[]{:S(2)}) collective-permute-start(bf16[112,512]{1,0:T(8,128)(2,1)S(1)} %copy-done.40), channel_id=1, source_target_pairs={{0,104},{1,57},{2,106},{3,59},{4,108},{5,61},{6,110},{7,63},{8,96}... | collective-permute-start | bytes 344072 | tf_op jit(solution)/shard_map/ppermute | solution.py:539
  52.4 14.8 %copy-start.20 = (bf16[112,512]{1,0:T(8,128)(2,1)}, bf16[112,512]{1,0:T(8,128)(2,1)S(1)}, u32[]{:S(2)}) copy-start(bf16[112,512]{1,0:T(8,128)(2,1)S(1)} %collective-permute-done.8.refs_9_) | copy-start | bytes 344068
  52.4 16.1 %collective-permute-start.13 = (bf16[112,512]{1,0:T(8,128)(2,1)S(1)}, bf16[112,512]{1,0:T(8,128)(2,1)S(1)}, u32[]{:S(2)}, u32[]{:S(2)}) collective-permute-start(bf16[112,512]{1,0:T(8,128)(2,1)S(1)} %copy-done.39), channel_id=1, source_target_pairs={{0,112},{1,89},{2,114},{3,91},{4,116},{5,93},{6,118},{7,95},{8,120... | collective-permute-start | bytes 344072 | tf_op jit(solution)/shard_map/ppermute | solution.py:539
  58.8 8.4 %copy-start.22 = (bf16[112,512]{1,0:T(8,128)(2,1)}, bf16[112,512]{1,0:T(8,128)(2,1)S(1)}, u32[]{:S(2)}) copy-start(bf16[112,512]{1,0:T(8,128)(2,1)S(1)} %collective-permute-done.9.refs_10_) | copy-start | bytes 344068
  58.8 10.4 %collective-permute-start.14 = (bf16[112,512]{1,0:T(8,128)(2,1)S(1)}, bf16[112,512]{1,0:T(8,128)(2,1)S(1)}, u32[]{:S(2)}, u32[]{:S(2)}) collective-permute-start(bf16[112,512]{1,0:T(8,128)(2,1)S(1)} %copy-done.38), channel_id=1, source_target_pairs={{0,120},{1,121},{2,122},{3,123},{4,124},{5,125},{6,126},{7,127},{8... | collective-permute-start | bytes 344072 | tf_op jit(solution)/shard_map/ppermute | solution.py:539
  59.2 8.1 %copy-start.24 = (bf16[112,512]{1,0:T(8,128)(2,1)}, bf16[112,512]{1,0:T(8,128)(2,1)S(1)}, u32[]{:S(2)}) copy-start(bf16[112,512]{1,0:T(8,128)(2,1)S(1)} %collective-permute-done.10.refs_11_) | copy-start | bytes 344068
  67.9 0.7 copy-start.28
  68.6 0.6 copy-start.30
  69.2 0.7 copy-start.32
  69.9 10.1 %copy-start.35 = (s32[512]{0:T(512)S(1)}, s32[512]{0:T(512)}, u32[]{:S(2)}) copy-start(s32[512]{0:T(512)} %orders.5) | copy-start | bytes 6148
  69.9 10.1 %copy-start.36 = (s32[2]{0:T(128)S(1)}, s32[2]{0:T(128)}, u32[]{:S(2)}) copy-start(s32[2]{0:T(128)} %pad_add_fusion.place) | copy-start | bytes 28
  69.9 35.0 %all-to-all-start.1 = ((bf16[128,8,768]{2,1,0:T(8,128)(2,1)}), bf16[128,8,768]{2,1,0:T(8,128)(2,1)S(1)}, u32[]{:S(2)}, u32[]{:S(2)}) async-start(bf16[128,8,768]{2,1,0:T(8,128)(2,1)} %bitcast.13), calls=%async_computation.1 | async-start | bytes 3145728 | tf_op jit(solution)/shard_map/all_to_all | solution.py:546
  80.0 1.1 copy-start.2
  81.0 0.9 copy-start.3
  81.9 0.9 copy-start.5
  82.8 0.9 copy-start.7
  83.7 0.9 copy-start.9
  84.6 0.9 copy-start.11
  85.5 0.9 copy-start.13
  86.4 0.9 copy-start.15
  87.3 0.9 copy-start.17
  88.2 0.9 copy-start.19
  89.1 0.9 copy-start.21
  90.0 0.9 copy-start.23
  90.9 0.9 copy-start.25
  91.8 0.9 copy-start.27
  92.7 0.9 copy-start.29
  93.6 0.9 copy-start.31
  94.5 0.9 copy-start.33
  97.0 1.0 copy-start
  104.8 1.2 copy-start.1
  (2 other events, 1.3 us)

commit v10 on v9

--- a/solution.py
+++ b/solution.py
@@ -537,7 +537,7 @@
             (i * 8 + o, (i ^ (swapped if o & 1 else r)) * 8 + o) for i in range(16) for o in range(8)
         ]
         received.append(lax.ppermute(parts[r], ("shell", "order"), pairs_r))
-    early = 12
+    early = 15
     incoming, received[:early] = lax.optimization_barrier((incoming, received[:early]))
 
     coefs = grid_stage(incoming, tables, weight)

time: 137 us -> 139 us (1.015)
  waiting for transfers between devices: 6.85 us -> 9.12 us
    ppermute x15, waiting for transfers between devices: 0.04 us -> 2.31 us  [body(): received.append(lax.ppermute(parts[r], ('shell', 'order'), pairs_r))]
  transfers between devices with their start and end apart: 17 -> 17, of which waited for: 1 -> 2; matrix products, arithmetic and copies ran while one was open for 2% -> 2% of each run, Pallas kernels for 12% -> 12%
where the time goes in v10:
time: 139 us
  starting transfers between devices  47.4 us (34%)
  Pallas kernels  31.6 us (23%)
  blocking collectives  25.4 us (18%)
  local copies, waits for them, and re-layouts  21.7 us (16%)
  waiting for transfers between devices  9.12 us (7%)
  other arithmetic  2.19 us (2%)
    ppermute x15, starting transfers between devices, body(): received.append(lax.ppermute(parts[r], ('shell', 'order'), pairs_r))  32 us
    all_to_all x1, blocking collectives, body(): solved = lax.all_to_all(solved, 'shell', 0, 0, tiled=True)  25.4 us
    unnamed x98, local copies, waits for them, and re-layouts  20.9 us
    all_to_all x1, starting transfers between devices, body(): lax.all_to_all(coefs.reshape(128, 8, 768), ('shell', 'order'), 0, 0, tile...  10 us
    pallas_call x1, Pallas kernels, legendre_synthesis(): pl.pallas_call(synthesis_kernel, grid_spec=pltpu.PrefetchScalarGridSpec(n...  10 us
    pallas_call x1, Pallas kernels, grid_stage(): pl.pallas_call(grid_kernel, grid=(3,), in_specs=[pl.BlockSpec((8, 24, 64,...  7.97 us
    all_to_all x1, waiting for transfers between devices, body(): lax.all_to_all(coefs.reshape(128, 8, 768), ('shell', 'order'), 0, 0, tile...  6.81 us
    all_to_all x1, starting transfers between devices, body(): incoming = lax.all_to_all(latitude, 'order', 0, 0, tiled=True)  5.41 us
  transfers between devices with their start and end apart: 17, of which 2 were waited for; matrix products, arithmetic and copies ran while one was open for 2% of the time, Pallas kernels for 12%

profile of v10, /device:TPU:0, one launch (start us, length us, event | category | flops | bytes accessed | tf_op | source)
XLA Modules:
  0.0 138.5 jit_solution(15331748488444713464)
XLA Ops:
  0.6 0.6 pad_add_fusion.place
  1.2 10.0 %legendre_synthesis.1 = (bf16[8,24,64,128]{3,2,1,0:T(8,128)(2,1)}, bf16[2,528,256]{2,1,0:T(8,128)(2,1)}) custom-call(s32[2]{0:T(128)} %pad_add_fusion.place, s32[512]{0:T(512)} %orders.5, bf16[3,2,2,64,512]{4,3,2,1,0:T(8,128)(2,1)} %vel.2, bf16[3,2,2,64,512]{4,3,2,1,0:T(8,128)(2,1)} %vor.1, bf16[3,2,2,64,512]{4,3,2,1,0:T(8,128)(2,1)} %mag.1, ...), custom_call_target="tpu_custom_call" | custom-call | flops 1600000000 | bytes 15728640 | tf_op jit(solution)/shard_map/legendre_synthesis/pallas_call | solution.py:132
  11.2 0.0 copy-start.48
  11.3 0.0 copy-start.37
  11.3 5.4 %all-to-all-start = ((bf16[8,24,64,128]{3,2,1,0:T(8,128)(2,1)}), bf16[8,24,64,128]{3,2,1,0:T(8,128)(2,1)}, u32[]{:S(2)}, u32[]{:S(2)}) async-start(bf16[8,24,64,128]{3,2,1,0:T(8,128)(2,1)} %get-tuple-element.79), calls=%async_computation | async-start | bytes 6291456 | tf_op jit(solution)/shard_map/all_to_all | solution.py:524
  16.7 0.2 reduce-window.9
  16.9 0.2 compare_reduce_fusion
  17.1 0.6 broadcast_select_fusion.kappa
  17.7 3.0 %state_to_send.1 = (bf16[112,512]{1,0:T(8,128)(2,1)}, bf16[112,512]{1,0:T(8,128)(2,1)}, bf16[112,512]{1,0:T(8,128)(2,1)}, bf16[112,512]{1,0:T(8,128)(2,1)}, bf16...) custom-call(s32[2]{0:T(128)} %pad_add_fusion.place, ...), custom_call_target="tpu_custom_call" | custom-call | flops 1000000 | bytes 4194304 | tf_op jit(solution)/shard_map/state_to_send/pallas_call | solution.py:190
  20.7 1.5 %collective-permute-start = (bf16[112,512]{1,0:T(8,128)(2,1)}, bf16[112,512]{1,0:T(8,128)(2,1)S(1)}, u32[]{:S(2)}, u32[]{:S(2)}) collective-permute-start(bf16[112,512]{1,0:T(8,128)(2,1)} %get-tuple-element.83), channel_id=1, source_target_pairs={{0,8},{1,33},{2,10},{3,35},{4,12},{5,37},{6,14},{7,39},{8,0},{9,41... | collective-permute-start | bytes 344072 | tf_op jit(solution)/shard_map/ppermute | solution.py:539
  22.2 2.7 %collective-permute-start.1 = (bf16[112,512]{1,0:T(8,128)(2,1)}, bf16[112,512]{1,0:T(8,128)(2,1)S(1)}, u32[]{:S(2)}, u32[]{:S(2)}) collective-permute-start(bf16[112,512]{1,0:T(8,128)(2,1)} %get-tuple-element.84), channel_id=1, source_target_pairs={{0,16},{1,65},{2,18},{3,67},{4,20},{5,69},{6,22},{7,71},{8,24},{9,... | collective-permute-start | bytes 344072 | tf_op jit(solution)/shard_map/ppermute | solution.py:539
  24.9 0.5 collective-permute-start.2
  25.4 1.6 %collective-permute-start.3 = (bf16[112,512]{1,0:T(8,128)(2,1)}, bf16[112,512]{1,0:T(8,128)(2,1)S(1)}, u32[]{:S(2)}, u32[]{:S(2)}) collective-permute-start(bf16[112,512]{1,0:T(8,128)(2,1)} %get-tuple-element.86), channel_id=1, source_target_pairs={{0,32},{1,9},{2,34},{3,11},{4,36},{5,13},{6,38},{7,15},{8,40},{9,1... | collective-permute-start | bytes 344072 | tf_op jit(solution)/shard_map/ppermute | solution.py:539
  27.0 0.2 collective-permute-start.4
  27.2 0.1 reshape.76
  27.3 0.7 reshape.77.targets
  28.1 4.1 %make_tables.1 = (bf16[528,512]{1,0:T(8,128)(2,1)}, bf16[512,512]{1,0:T(8,128)(2,1)}, bf16[512,512]{1,0:T(8,128)(2,1)}, bf16[512,512]{1,0:T(8,128)(2,1)}, f32[512,128]{1,0:T(8,128)}) custom-call(s32[1,512]{1,0:T(1,128)} %bitcast.11, s32[1,512]{1,0:T(1,128)} %reshape.77.targets, bf16[528,512]{1,0:T(8,128)(2,1)} %constant.42.clone.refs_0_, ...), custom_call_target="tpu_custom_call" | custom-call | flops 1000000000 | bytes 5242880 | tf_op jit(solution)/shard_map/make_tables/pallas_call | solution.py:302
  32.1 5.0 %collective-permute-start.5 = (bf16[112,512]{1,0:T(8,128)(2,1)S(1)}, bf16[112,512]{1,0:T(8,128)(2,1)S(1)}, u32[]{:S(2)}, u32[]{:S(2)}) collective-permute-start(bf16[112,512]{1,0:T(8,128)(2,1)S(1)} %copy-done.47), channel_id=1, source_target_pairs={{0,48},{1,73},{2,50},{3,75},{4,52},{5,77},{6,54},{7,79},{8,56},{9,... | collective-permute-start | bytes 344072 | tf_op jit(solution)/shard_map/ppermute | solution.py:539
  37.2 0.0 collective-permute-done.1.refs_2_
  37.2 0.4 collective-permute-start.6
  37.6 0.0 collective-permute-done.2.refs_3_
  37.6 3.3 %collective-permute-start.7 = (bf16[112,512]{1,0:T(8,128)(2,1)S(1)}, bf16[112,512]{1,0:T(8,128)(2,1)S(1)}, u32[]{:S(2)}, u32[]{:S(2)}) collective-permute-start(bf16[112,512]{1,0:T(8,128)(2,1)S(1)} %copy-done.45), channel_id=1, source_target_pairs={{0,64},{1,17},{2,66},{3,19},{4,68},{5,21},{6,70},{7,23},{8,72},{9,... | collective-permute-start | bytes 344072 | tf_op jit(solution)/shard_map/ppermute | solution.py:539
  40.9 0.0 collective-permute-done.3.refs_4_
  40.9 0.1 collective-permute-start.8
  41.0 6.7 %collective-permute-start.9 = (bf16[112,512]{1,0:T(8,128)(2,1)S(1)}, bf16[112,512]{1,0:T(8,128)(2,1)S(1)}, u32[]{:S(2)}, u32[]{:S(2)}) collective-permute-start(bf16[112,512]{1,0:T(8,128)(2,1)S(1)} %copy-done.43), channel_id=1, source_target_pairs={{0,80},{1,81},{2,82},{3,83},{4,84},{5,85},{6,86},{7,87},{8,88},{9,... | collective-permute-start | bytes 344072 | tf_op jit(solution)/shard_map/ppermute | solution.py:539
  47.7 0.6 copy-done.14
  48.3 0.2 collective-permute-start.10
  48.6 0.7 copy-done.16
  49.3 3.0 %collective-permute-start.11 = (bf16[112,512]{1,0:T(8,128)(2,1)S(1)}, bf16[112,512]{1,0:T(8,128)(2,1)S(1)}, u32[]{:S(2)}, u32[]{:S(2)}) collective-permute-start(bf16[112,512]{1,0:T(8,128)(2,1)S(1)} %copy-done.41), channel_id=1, source_target_pairs={{0,96},{1,25},{2,98},{3,27},{4,100},{5,29},{6,102},{7,31},{8,104},... | collective-permute-start | bytes 344072 | tf_op jit(solution)/shard_map/ppermute | solution.py:539
  52.3 0.7 copy-done.18
  53.0 0.6 copy-done.20
  53.6 6.3 %collective-permute-start.13 = (bf16[112,512]{1,0:T(8,128)(2,1)S(1)}, bf16[112,512]{1,0:T(8,128)(2,1)S(1)}, u32[]{:S(2)}, u32[]{:S(2)}) collective-permute-start(bf16[112,512]{1,0:T(8,128)(2,1)S(1)} %copy-done.39), channel_id=1, source_target_pairs={{0,112},{1,89},{2,114},{3,91},{4,116},{5,93},{6,118},{7,95},{8,120... | collective-permute-start | bytes 344072 | tf_op jit(solution)/shard_map/ppermute | solution.py:539
  59.9 0.6 sine_multiply_fusion.weight
  60.6 0.4 collective-permute-start.14
  61.0 2.3 %collective-permute-done.13.refs_14_ = bf16[112,512]{1,0:T(8,128)(2,1)S(1)} collective-permute-done((bf16[112,512]{1,0:T(8,128)(2,1)S(1)}, bf16[112,512]{1,0:T(8,128)(2,1)S(1)}, u32[]{:S(2)}, u32[]{:S(2)}) %collective-permute-start.13) | collective-permute-done | bytes 114720 | tf_op jit(solution)/shard_map/ppermute | solution.py:539
  63.3 8.0 %grid_stage.1 = bf16[1024,768]{1,0:T(8,128)(2,1)} custom-call(bf16[8,24,64,128]{3,2,1,0:T(8,128)(2,1)} %all-to-all-done.lat, bf16[528,512]{1,0:T(8,128)(2,1)} %get-tuple-element.130.syn_cos, bf16[512,512]{1,0:T(8,128)(2,1)} %get-tuple-element.131.syn_sin, bf16[512,512]{1,0:T(8,128)(2,1)} %get-tuple-element.132.ana_cos, ...), custom_call_target="tpu_custom_call" | custom-call | flops 2400000000 | bytes 7340032 | tf_op jit(solution)/shard_map/grid_stage/pallas_call | solution.py:257
  71.3 0.6 copy-done.32
  72.0 10.0 %all-to-all-start.1 = ((bf16[128,8,768]{2,1,0:T(8,128)(2,1)}), bf16[128,8,768]{2,1,0:T(8,128)(2,1)S(1)}, u32[]{:S(2)}, u32[]{:S(2)}) async-start(bf16[128,8,768]{2,1,0:T(8,128)(2,1)} %bitcast.13), calls=%async_computation.1 | async-start | bytes 3145728 | tf_op jit(solution)/shard_map/all_to_all | solution.py:546
  82.1 0.0 copy-start.2
  82.1 1.0 copy-done.2
  83.1 0.9 copy-done.3
  84.0 0.9 copy-done.5
  84.9 0.9 copy-done.7
  85.8 0.9 copy-done.9
  86.7 0.9 copy-done.11
  87.6 0.9 copy-done.13
  88.5 0.9 copy-done.15
  89.4 0.9 copy-done.17
  90.3 0.9 copy-done.19
  91.2 0.9 copy-done.21
  92.1 0.9 copy-done.23
  93.0 0.9 copy-done.25
  93.9 0.9 copy-done.27
  94.8 0.9 copy-done.29
  95.7 0.9 copy-done.31
  96.6 0.9 copy-done.33
  97.5 1.6 %solve_factors.1 = (bf16[16,96,512]{2,1,0:T(8,128)(2,1)S(1)}, f32[3,64,512]{2,1,0:T(8,128)S(1)}, bf16[4,256,512]{2,1,0:T(8,128)(2,1)S(1)}) custom-call(s32[2]{0:T(128)S(1)} %copy-done.36, s32[512]{0:T(512)S(1)} %copy-done.35, bf16[2,528,256]{2,1,0:T(8,128)(2,1)S(1)} %copy-done.2, bf16[112,512]{1,0:T(8,128)(2,1)S(1)} %copy-done.3, ...), custom_call_target="tpu_custom_call" | custom-call | flops 1000000 | bytes 1048576 | tf_op jit(solution)/shard_map/solve_factors/pallas_call | solution.py:354
  99.1 0.0 copy-start
  99.1 1.0 copy-done
  100.1 6.8 %all-to-all-done.1 = bf16[128,8,768]{2,1,0:T(8,128)(2,1)S(1)} async-done(((bf16[128,8,768]{2,1,0:T(8,128)(2,1)}), bf16[128,8,768]{2,1,0:T(8,128)(2,1)S(1)}, u32[]{:S(2)}, u32[]{:S(2)}) %all-to-all-start.1) | async-done | bytes 1572896 | tf_op jit(solution)/shard_map/all_to_all | solution.py:546
  106.9 1.2 copy-done.1
  108.1 3.0 %analysis_and_solve.1 = bf16[16,96,512]{2,1,0:T(8,128)(2,1)S(1)} custom-call(s32[2]{0:T(128)S(1)} %copy-done.36, s32[512]{0:T(512)S(1)} %copy-done.35, bf16[1024,768]{1,0:T(8,128)(2,1)S(1)} %bitcast.10, bf16[4,256,512]{2,1,0:T(8,128)(2,1)S(1)} %copy-done.1, f32[3,64,512]{2,1,0:T(8,128)S(1)} %get-tuple-element.154.factors, ...), custom_call_target="tpu_custom_call" | custom-call | flops 900000000 | bytes 6291456 | tf_op jit(solution)/shard_map/analysis_and_solve/pallas_call | solution.py:440
  111.1 25.4 %all_to_all.15.got = bf16[16,96,512]{2,1,0:T(8,128)(2,1)S(1)} all-to-all(bf16[16,96,512]{2,1,0:T(8,128)(2,1)S(1)} %analysis_and_solve.1), channel_id=1, replica_groups=mesh['shell'=16,'order'=8] {'shell'}, dimensions={0} | all-to-all | bytes 3145728 | tf_op jit(solution)/shard_map/all_to_all | solution.py:550
  136.6 2.0 %unpack_solution.1 = (f32[3,2,2,64,512]{4,3,2,1,0:T(8,128)}, f32[3,2,2,64,512]{4,3,2,1,0:T(8,128)}) custom-call(bf16[16,96,512]{2,1,0:T(8,128)(2,1)S(1)} %all_to_all.15.got), custom_call_target="tpu_custom_call" | custom-call | flops 1000000 | bytes 5242880 | tf_op jit(solution)/shard_map/unpack_solution/pallas_call | solution.py:480
  (86 shorter events, 0.2 us)
Async XLA Ops:
  11.2 5.4 %copy-start.48 = (s32[4]{0:T(128)S(1)}, s32[4]{0:T(128)}, u32[]{:S(2)}) copy-start(s32[4]{0:T(128)} %param.22) | copy-start | bytes 52
  11.3 5.8 %copy-start.37 = (f32[2,2]{1,0:T(2,128)S(1)}, f32[2,2]{1,0:T(2,128)}, u32[]{:S(2)}) copy-start(f32[2,2]{1,0:T(2,128)} %param.23) | copy-start | bytes 52
  11.3 52.0 %all-to-all-start = ((bf16[8,24,64,128]{3,2,1,0:T(8,128)(2,1)}), bf16[8,24,64,128]{3,2,1,0:T(8,128)(2,1)}, u32[]{:S(2)}, u32[]{:S(2)}) async-start(bf16[8,24,64,128]{3,2,1,0:T(8,128)(2,1)} %get-tuple-element.79), calls=%async_computation | async-start | bytes 6291456 | tf_op jit(solution)/shard_map/all_to_all | solution.py:524
  16.7 10.5 %copy-start.34 = (s32[512]{0:T(512)S(1)}, s32[512]{0:T(512)}, u32[]{:S(2)}) copy-start(s32[512]{0:T(512)} %orders.5) | copy-start | bytes 6148
  20.7 11.5 %collective-permute-start = (bf16[112,512]{1,0:T(8,128)(2,1)}, bf16[112,512]{1,0:T(8,128)(2,1)S(1)}, u32[]{:S(2)}, u32[]{:S(2)}) collective-permute-start(bf16[112,512]{1,0:T(8,128)(2,1)} %get-tuple-element.83), channel_id=1, source_target_pairs={{0,8},{1,33},{2,10},{3,35},{4,12},{5,37},{6,14},{7,39},{8,0},{9,41... | collective-permute-start | bytes 344072 | tf_op jit(solution)/shard_map/ppermute | solution.py:539
  22.2 15.0 %collective-permute-start.1 = (bf16[112,512]{1,0:T(8,128)(2,1)}, bf16[112,512]{1,0:T(8,128)(2,1)S(1)}, u32[]{:S(2)}, u32[]{:S(2)}) collective-permute-start(bf16[112,512]{1,0:T(8,128)(2,1)} %get-tuple-element.84), channel_id=1, source_target_pairs={{0,16},{1,65},{2,18},{3,67},{4,20},{5,69},{6,22},{7,71},{8,24},{9,... | collective-permute-start | bytes 344072 | tf_op jit(solution)/shard_map/ppermute | solution.py:539
  24.9 12.7 %collective-permute-start.2 = (bf16[112,512]{1,0:T(8,128)(2,1)}, bf16[112,512]{1,0:T(8,128)(2,1)S(1)}, u32[]{:S(2)}, u32[]{:S(2)}) collective-permute-start(bf16[112,512]{1,0:T(8,128)(2,1)} %get-tuple-element.85), channel_id=1, source_target_pairs={{0,24},{1,97},{2,26},{3,99},{4,28},{5,101},{6,30},{7,103},{8,16},{... | collective-permute-start | bytes 344072 | tf_op jit(solution)/shard_map/ppermute | solution.py:539
  25.4 15.5 %collective-permute-start.3 = (bf16[112,512]{1,0:T(8,128)(2,1)}, bf16[112,512]{1,0:T(8,128)(2,1)S(1)}, u32[]{:S(2)}, u32[]{:S(2)}) collective-permute-start(bf16[112,512]{1,0:T(8,128)(2,1)} %get-tuple-element.86), channel_id=1, source_target_pairs={{0,32},{1,9},{2,34},{3,11},{4,36},{5,13},{6,38},{7,15},{8,40},{9,1... | collective-permute-start | bytes 344072 | tf_op jit(solution)/shard_map/ppermute | solution.py:539
  27.0 14.0 %collective-permute-start.4 = (bf16[112,512]{1,0:T(8,128)(2,1)}, bf16[112,512]{1,0:T(8,128)(2,1)S(1)}, u32[]{:S(2)}, u32[]{:S(2)}) collective-permute-start(bf16[112,512]{1,0:T(8,128)(2,1)} %get-tuple-element.87), channel_id=1, source_target_pairs={{0,40},{1,41},{2,42},{3,43},{4,44},{5,45},{6,46},{7,47},{8,32},{9,... | collective-permute-start | bytes 344072 | tf_op jit(solution)/shard_map/ppermute | solution.py:539
  28.0 4.1 %copy-start.47 = (bf16[112,512]{1,0:T(8,128)(2,1)S(1)}, bf16[112,512]{1,0:T(8,128)(2,1)}, u32[]{:S(2)}) copy-start(bf16[112,512]{1,0:T(8,128)(2,1)} %get-tuple-element.104) | copy-start | bytes 344068
  28.0 9.2 %copy-start.46 = (bf16[112,512]{1,0:T(8,128)(2,1)S(1)}, bf16[112,512]{1,0:T(8,128)(2,1)}, u32[]{:S(2)}) copy-start(bf16[112,512]{1,0:T(8,128)(2,1)} %get-tuple-element.105) | copy-start | bytes 344068
  28.0 9.6 %copy-start.45 = (bf16[112,512]{1,0:T(8,128)(2,1)S(1)}, bf16[112,512]{1,0:T(8,128)(2,1)}, u32[]{:S(2)}) copy-start(bf16[112,512]{1,0:T(8,128)(2,1)} %get-tuple-element.106) | copy-start | bytes 344068
  28.0 12.9 %copy-start.44 = (bf16[112,512]{1,0:T(8,128)(2,1)S(1)}, bf16[112,512]{1,0:T(8,128)(2,1)}, u32[]{:S(2)}) copy-start(bf16[112,512]{1,0:T(8,128)(2,1)} %get-tuple-element.107) | copy-start | bytes 344068
  28.0 13.0 %copy-start.43 = (bf16[112,512]{1,0:T(8,128)(2,1)S(1)}, bf16[112,512]{1,0:T(8,128)(2,1)}, u32[]{:S(2)}) copy-start(bf16[112,512]{1,0:T(8,128)(2,1)} %get-tuple-element.108) | copy-start | bytes 344068
  28.0 20.3 %copy-start.42 = (bf16[112,512]{1,0:T(8,128)(2,1)S(1)}, bf16[112,512]{1,0:T(8,128)(2,1)}, u32[]{:S(2)}) copy-start(bf16[112,512]{1,0:T(8,128)(2,1)} %get-tuple-element.109) | copy-start | bytes 344068
  28.0 21.2 %copy-start.41 = (bf16[112,512]{1,0:T(8,128)(2,1)S(1)}, bf16[112,512]{1,0:T(8,128)(2,1)}, u32[]{:S(2)}) copy-start(bf16[112,512]{1,0:T(8,128)(2,1)} %get-tuple-element.110) | copy-start | bytes 344068
  28.0 24.9 %copy-start.40 = (bf16[112,512]{1,0:T(8,128)(2,1)S(1)}, bf16[112,512]{1,0:T(8,128)(2,1)}, u32[]{:S(2)}) copy-start(bf16[112,512]{1,0:T(8,128)(2,1)} %get-tuple-element.111) | copy-start | bytes 344068
  28.1 25.5 %copy-start.39 = (bf16[112,512]{1,0:T(8,128)(2,1)S(1)}, bf16[112,512]{1,0:T(8,128)(2,1)}, u32[]{:S(2)}) copy-start(bf16[112,512]{1,0:T(8,128)(2,1)} %get-tuple-element.112) | copy-start | bytes 344068
  28.1 32.5 %copy-start.38 = (bf16[112,512]{1,0:T(8,128)(2,1)S(1)}, bf16[112,512]{1,0:T(8,128)(2,1)}, u32[]{:S(2)}) copy-start(bf16[112,512]{1,0:T(8,128)(2,1)} %get-tuple-element.128) | copy-start | bytes 344068
  32.1 39.1 %copy-start.4 = (bf16[112,512]{1,0:T(8,128)(2,1)}, bf16[112,512]{1,0:T(8,128)(2,1)S(1)}, u32[]{:S(2)}) copy-start(bf16[112,512]{1,0:T(8,128)(2,1)S(1)} %collective-permute-done.refs_1_) | copy-start | bytes 344068
  32.1 15.6 %collective-permute-start.5 = (bf16[112,512]{1,0:T(8,128)(2,1)S(1)}, bf16[112,512]{1,0:T(8,128)(2,1)S(1)}, u32[]{:S(2)}, u32[]{:S(2)}) collective-permute-start(bf16[112,512]{1,0:T(8,128)(2,1)S(1)} %copy-done.47), channel_id=1, source_target_pairs={{0,48},{1,73},{2,50},{3,75},{4,52},{5,77},{6,54},{7,79},{8,56},{9,... | collective-permute-start | bytes 344072 | tf_op jit(solution)/shard_map/ppermute | solution.py:539
  37.2 34.1 %copy-start.6 = (bf16[112,512]{1,0:T(8,128)(2,1)}, bf16[112,512]{1,0:T(8,128)(2,1)S(1)}, u32[]{:S(2)}) copy-start(bf16[112,512]{1,0:T(8,128)(2,1)S(1)} %collective-permute-done.1.refs_2_) | copy-start | bytes 344068
  37.2 11.4 %collective-permute-start.6 = (bf16[112,512]{1,0:T(8,128)(2,1)S(1)}, bf16[112,512]{1,0:T(8,128)(2,1)S(1)}, u32[]{:S(2)}, u32[]{:S(2)}) collective-permute-start(bf16[112,512]{1,0:T(8,128)(2,1)S(1)} %copy-done.46), channel_id=1, source_target_pairs={{0,56},{1,105},{2,58},{3,107},{4,60},{5,109},{6,62},{7,111},{8,48}... | collective-permute-start | bytes 344072 | tf_op jit(solution)/shard_map/ppermute | solution.py:539
  37.6 33.6 %copy-start.8 = (bf16[112,512]{1,0:T(8,128)(2,1)}, bf16[112,512]{1,0:T(8,128)(2,1)S(1)}, u32[]{:S(2)}) copy-start(bf16[112,512]{1,0:T(8,128)(2,1)S(1)} %collective-permute-done.2.refs_3_) | copy-start | bytes 344068
  37.6 14.6 %collective-permute-start.7 = (bf16[112,512]{1,0:T(8,128)(2,1)S(1)}, bf16[112,512]{1,0:T(8,128)(2,1)S(1)}, u32[]{:S(2)}, u32[]{:S(2)}) collective-permute-start(bf16[112,512]{1,0:T(8,128)(2,1)S(1)} %copy-done.45), channel_id=1, source_target_pairs={{0,64},{1,17},{2,66},{3,19},{4,68},{5,21},{6,70},{7,23},{8,72},{9,... | collective-permute-start | bytes 344072 | tf_op jit(solution)/shard_map/ppermute | solution.py:539
  40.9 30.4 %copy-start.10 = (bf16[112,512]{1,0:T(8,128)(2,1)}, bf16[112,512]{1,0:T(8,128)(2,1)S(1)}, u32[]{:S(2)}) copy-start(bf16[112,512]{1,0:T(8,128)(2,1)S(1)} %collective-permute-done.3.refs_4_) | copy-start | bytes 344068
  40.9 12.0 %collective-permute-start.8 = (bf16[112,512]{1,0:T(8,128)(2,1)S(1)}, bf16[112,512]{1,0:T(8,128)(2,1)S(1)}, u32[]{:S(2)}, u32[]{:S(2)}) collective-permute-start(bf16[112,512]{1,0:T(8,128)(2,1)S(1)} %copy-done.44), channel_id=1, source_target_pairs={{0,72},{1,49},{2,74},{3,51},{4,76},{5,53},{6,78},{7,55},{8,64},{9,... | collective-permute-start | bytes 344072 | tf_op jit(solution)/shard_map/ppermute | solution.py:539
  41.0 30.3 %copy-start.12 = (bf16[112,512]{1,0:T(8,128)(2,1)}, bf16[112,512]{1,0:T(8,128)(2,1)S(1)}, u32[]{:S(2)}) copy-start(bf16[112,512]{1,0:T(8,128)(2,1)S(1)} %collective-permute-done.4.refs_5_) | copy-start | bytes 344068
  41.0 19.5 %collective-permute-start.9 = (bf16[112,512]{1,0:T(8,128)(2,1)S(1)}, bf16[112,512]{1,0:T(8,128)(2,1)S(1)}, u32[]{:S(2)}, u32[]{:S(2)}) collective-permute-start(bf16[112,512]{1,0:T(8,128)(2,1)S(1)} %copy-done.43), channel_id=1, source_target_pairs={{0,80},{1,81},{2,82},{3,83},{4,84},{5,85},{6,86},{7,87},{8,88},{9,... | collective-permute-start | bytes 344072 | tf_op jit(solution)/shard_map/ppermute | solution.py:539
  47.7 0.7 copy-start.14
  48.3 12.6 %collective-permute-start.10 = (bf16[112,512]{1,0:T(8,128)(2,1)S(1)}, bf16[112,512]{1,0:T(8,128)(2,1)S(1)}, u32[]{:S(2)}, u32[]{:S(2)}) collective-permute-start(bf16[112,512]{1,0:T(8,128)(2,1)S(1)} %copy-done.42), channel_id=1, source_target_pairs={{0,88},{1,113},{2,90},{3,115},{4,92},{5,117},{6,94},{7,119},{8,80}... | collective-permute-start | bytes 344072 | tf_op jit(solution)/shard_map/ppermute | solution.py:539
  48.6 0.7 copy-start.16
  49.3 11.7 %collective-permute-start.11 = (bf16[112,512]{1,0:T(8,128)(2,1)S(1)}, bf16[112,512]{1,0:T(8,128)(2,1)S(1)}, u32[]{:S(2)}, u32[]{:S(2)}) collective-permute-start(bf16[112,512]{1,0:T(8,128)(2,1)S(1)} %copy-done.41), channel_id=1, source_target_pairs={{0,96},{1,25},{2,98},{3,27},{4,100},{5,29},{6,102},{7,31},{8,104},... | collective-permute-start | bytes 344072 | tf_op jit(solution)/shard_map/ppermute | solution.py:539
  52.3 0.7 copy-start.18
  52.9 8.0 %collective-permute-start.12 = (bf16[112,512]{1,0:T(8,128)(2,1)S(1)}, bf16[112,512]{1,0:T(8,128)(2,1)S(1)}, u32[]{:S(2)}, u32[]{:S(2)}) collective-permute-start(bf16[112,512]{1,0:T(8,128)(2,1)S(1)} %copy-done.40), channel_id=1, source_target_pairs={{0,104},{1,57},{2,106},{3,59},{4,108},{5,61},{6,110},{7,63},{8,96}... | collective-permute-start | bytes 344072 | tf_op jit(solution)/shard_map/ppermute | solution.py:539
  53.6 9.7 %collective-permute-start.13 = (bf16[112,512]{1,0:T(8,128)(2,1)S(1)}, bf16[112,512]{1,0:T(8,128)(2,1)S(1)}, u32[]{:S(2)}, u32[]{:S(2)}) collective-permute-start(bf16[112,512]{1,0:T(8,128)(2,1)S(1)} %copy-done.39), channel_id=1, source_target_pairs={{0,112},{1,89},{2,114},{3,91},{4,116},{5,93},{6,118},{7,95},{8,120... | collective-permute-start | bytes 344072 | tf_op jit(solution)/shard_map/ppermute | solution.py:539
  60.6 10.7 %copy-start.22 = (bf16[112,512]{1,0:T(8,128)(2,1)}, bf16[112,512]{1,0:T(8,128)(2,1)S(1)}, u32[]{:S(2)}) copy-start(bf16[112,512]{1,0:T(8,128)(2,1)S(1)} %collective-permute-done.9.refs_10_) | copy-start | bytes 344068
  60.6 10.8 %collective-permute-start.14 = (bf16[112,512]{1,0:T(8,128)(2,1)S(1)}, bf16[112,512]{1,0:T(8,128)(2,1)S(1)}, u32[]{:S(2)}, u32[]{:S(2)}) collective-permute-start(bf16[112,512]{1,0:T(8,128)(2,1)S(1)} %copy-done.38), channel_id=1, source_target_pairs={{0,120},{1,121},{2,122},{3,123},{4,124},{5,125},{6,126},{7,127},{8... | collective-permute-start | bytes 344072 | tf_op jit(solution)/shard_map/ppermute | solution.py:539
  61.0 10.3 %copy-start.24 = (bf16[112,512]{1,0:T(8,128)(2,1)}, bf16[112,512]{1,0:T(8,128)(2,1)S(1)}, u32[]{:S(2)}) copy-start(bf16[112,512]{1,0:T(8,128)(2,1)S(1)} %collective-permute-done.10.refs_11_) | copy-start | bytes 344068
  61.0 10.3 %copy-start.26 = (bf16[112,512]{1,0:T(8,128)(2,1)}, bf16[112,512]{1,0:T(8,128)(2,1)S(1)}, u32[]{:S(2)}) copy-start(bf16[112,512]{1,0:T(8,128)(2,1)S(1)} %collective-permute-done.11.refs_12_) | copy-start | bytes 344068
  61.0 10.3 %copy-start.28 = (bf16[112,512]{1,0:T(8,128)(2,1)}, bf16[112,512]{1,0:T(8,128)(2,1)S(1)}, u32[]{:S(2)}) copy-start(bf16[112,512]{1,0:T(8,128)(2,1)S(1)} %collective-permute-done.12.refs_13_) | copy-start | bytes 344068
  63.3 8.1 %copy-start.30 = (bf16[112,512]{1,0:T(8,128)(2,1)}, bf16[112,512]{1,0:T(8,128)(2,1)S(1)}, u32[]{:S(2)}) copy-start(bf16[112,512]{1,0:T(8,128)(2,1)S(1)} %collective-permute-done.13.refs_14_) | copy-start | bytes 344068
  72.0 10.1 %copy-start.35 = (s32[512]{0:T(512)S(1)}, s32[512]{0:T(512)}, u32[]{:S(2)}) copy-start(s32[512]{0:T(512)} %orders.5) | copy-start | bytes 6148
  72.0 10.1 %copy-start.36 = (s32[2]{0:T(128)S(1)}, s32[2]{0:T(128)}, u32[]{:S(2)}) copy-start(s32[2]{0:T(128)} %pad_add_fusion.place) | copy-start | bytes 28
  72.0 34.9 %all-to-all-start.1 = ((bf16[128,8,768]{2,1,0:T(8,128)(2,1)}), bf16[128,8,768]{2,1,0:T(8,128)(2,1)S(1)}, u32[]{:S(2)}, u32[]{:S(2)}) async-start(bf16[128,8,768]{2,1,0:T(8,128)(2,1)} %bitcast.13), calls=%async_computation.1 | async-start | bytes 3145728 | tf_op jit(solution)/shard_map/all_to_all | solution.py:546
  82.1 1.1 copy-start.2
  83.1 0.9 copy-start.3
  84.0 0.9 copy-start.5
  84.9 0.9 copy-start.7
  85.8 0.9 copy-start.9
  86.7 0.9 copy-start.11
  87.6 0.9 copy-start.13
  88.5 0.9 copy-start.15
  89.4 0.9 copy-start.17
  90.3 0.9 copy-start.19
  91.2 0.9 copy-start.21
  92.1 0.9 copy-start.23
  93.0 0.9 copy-start.25
  93.9 0.9 copy-start.27
  94.8 0.9 copy-start.29
  95.7 0.9 copy-start.31
  96.6 0.9 copy-start.33
  99.1 1.0 copy-start
  106.9 1.2 copy-start.1
  (2 other events, 1.3 us)
